TPU v7x, 32 devices: a whole 2x2x4 slice. The times are simulated.
32 devices in a mesh: rows: 8 (over z, y), dates: 4 (over x, core).
Axes of the slice: x: 2, y: 2, z: 4, core: 2. Of those that a mesh axis runs over, the one named last changes fastest.
Arguments:
- images: bfloat16 [16, 128, 128, 128], P('dates', 'rows'), may hold values from -12 to 12
- day_index: int32 [16], replicated, may hold values from 1 to 365
- valid: int32 [16, 64, 128], P(None, 'rows', 'dates'), may hold values from 0 to 1, as said below
- out_grad: bfloat16 [64, 128, 128], P('rows', 'dates'), may hold values from -6 to 6
- conv_weight: bfloat16 [3, 3, 64, 128], replicated, may hold values from -0.25 to 0.25
- first_gain: float32 [128], replicated, may hold values from 0.1 to 1.9
- first_shift: float32 [128], replicated, may hold values from -3 to 3
- block_weight: bfloat16 [3, 3, 128, 128], replicated, may hold values from -0.1875 to 0.1875
- gn_gain: float32 [128], replicated, may hold values from 0.1 to 1.9
- gn_shift: float32 [128], replicated, may hold values from -3 to 3
- key_weight: bfloat16 [128, 64], replicated, may hold values from -0.5 to 0.5
- queries: float32 [16, 4], replicated, may hold values from -4 to 4
Outputs:
- attended: bfloat16 [64, 128, 128], P('rows', 'dates')
- conv_grad: float32 [3, 3, 64, 128], replicated
- first_gain_grad: float32 [128], replicated
- first_shift_grad: float32 [128], replicated
- block_grad: float32 [3, 3, 128, 128], replicated
- gain_grad: float32 [128], replicated
- shift_grad: float32 [128], replicated
- key_grad: float32 [128, 64], replicated
- query_grad: float32 [16, 4], replicated
Inputs may be any that keep to these rules, and one draw needn't show every extreme that they name: Every pixel has at least one valid date.
All inputs are finite; a program needn't handle non-finite values.
Results may differ from a plain program's by a relative error of at most 0.018.
Values may be sent and summed in bfloat16 or wider, within the bound.
No kernel may reach another device: no remote copies, remote signals or barrier semaphores. Data moves between devices by JAX's collectives and lax.ppermute only.
A program may use at most 128 MiB of HBM per device.

v0:
```python
import functools

import jax
import jax.numpy as jnp
from jax import lax
from jax.experimental import pallas as pl
from jax.experimental.pallas import tpu as pltpu
from jax.sharding import PartitionSpec as P

GROUPS = 4


EPS = 1e-05


MIB = 1 << 20


F32 = jnp.float32


BF16 = jnp.bfloat16


def product(left, right, left_dim, right_dim):
    return lax.dot_general(
        left, right, (((left_dim,), (right_dim,)), ((), ())), preferred_element_type=F32
    )


def group_sum(values):
    width = values.shape[-1]
    lane_group = lax.broadcasted_iota(jnp.int32, values.shape, 1) // (width // GROUPS)
    spread = jnp.zeros_like(values)
    for group in range(GROUPS):
        inside = lane_group == group
        total = jnp.sum(jnp.where(inside, values, 0.0), axis=1, keepdims=True)
        spread = spread + jnp.where(inside, total, 0.0)
    return spread


def sigmoid(values):
    return 0.5 * jnp.tanh(0.5 * values) + 0.5


def from_left(values):
    column = lax.broadcasted_iota(jnp.int32, values.shape, 1)
    return jnp.where(column > 0, pltpu.roll(values, 1, 1), 0.0)


def from_right(values):
    count = values.shape[1]
    column = lax.broadcasted_iota(jnp.int32, values.shape, 1)
    return jnp.where(column < count - 1, pltpu.roll(values, count - 1, 1), 0.0)


def column_sum(values):
    return jnp.sum(jnp.sum(values, axis=0), axis=0, keepdims=True)


def split(values):
    high = values.astype(BF16)
    return high, (values - high.astype(F32)).astype(BF16)


def store_sums(sums_ref, date, dates, first, second):
    for copy in range(sums_ref.shape[0]):
        sums_ref[copy, pl.ds(date, 1), :] = first
        sums_ref[copy, pl.ds(dates + date, 1), :] = second


def norm_table(sums_ref, table_ref, dates, norm_count):
    means = group_sum(jnp.sum(sums_ref[...], axis=0)) / norm_count
    mean = means[:dates]
    table_ref[:dates] = mean
    table_ref[dates:] = 1.0 / jnp.sqrt(means[dates:] - mean * mean + EPS)


def down_kernel(dates, img_ref, above_ref, weight_ref, out_ref, top_ref, low_ref, sums_ref, table):
    date = pl.program_id(0)
    half = weight_ref.shape[2]

    @pl.when(date == 0)
    def _():
        for tap in range(3):
            base = tap * 2 * half
            table[base : base + half, : 2 * half] = weight_ref[tap, 1]
            table[base + half : base + 2 * half, : 2 * half] = weight_ref[tap, 2]
            table[base : base + half, 2 * half :] = jnp.zeros_like(weight_ref[tap, 0])
            table[base + half : base + 2 * half, 2 * half :] = weight_ref[tap, 0]

    even, odd = img_ref[0, :, 0], img_ref[0, :, 1]
    above = jnp.concatenate([above_ref[0][None], odd[:-1]], axis=0)
    rows, cols, width = even.shape
    taps = jnp.concatenate([above, even, odd], axis=-1).reshape(rows * cols, 3 * width)
    both = product(taps, table[...], 1, 0).reshape(rows, cols, 2 * width)
    stored = (both[..., :width] + from_left(both[..., width:])).astype(BF16)
    out_ref[0] = stored
    top_ref[0] = stored[0]
    low_ref[0] = stored[rows - 1]
    values = stored.astype(F32)
    store_sums(sums_ref, date, dates, column_sum(values), column_sum(values * values))


def block_kernel(
    dates,
    norm_count,
    edge_ref,
    conv_ref,
    up_ref,
    down_ref,
    stats_ref,
    gain_ref,
    weight_ref,
    out_ref,
    hidden_ref,
    norm_ref,
    sums_ref,
    table,
):
    date = pl.program_id(0)
    width = conv_ref.shape[-1]

    @pl.when(date == 0)
    def _():
        norm_table(stats_ref, norm_ref, dates, norm_count)
        for row_tap in range(3):
            for col_tap in range(3):
                table[
                    row_tap * width : (row_tap + 1) * width, col_tap * width : (col_tap + 1) * width
                ] = weight_ref[row_tap, col_tap]

    scale = norm_ref[pl.ds(dates + date, 1), :] * gain_ref[0:1]
    shift = gain_ref[1:2] - norm_ref[pl.ds(date, 1), :] * scale

    def activate(values):
        linear = values.astype(F32) * scale + shift
        return linear * sigmoid(linear)

    rows, cols = conv_ref.shape[1:3]
    hidden_ref[0, 0] = (activate(up_ref[0]) * edge_ref[0]).astype(BF16)
    hidden_ref[0, rows + 1] = (activate(down_ref[0]) * edge_ref[1]).astype(BF16)
    hidden_ref[0, 1 : rows + 1] = activate(conv_ref[0]).astype(BF16)
    taps = jnp.concatenate(
        [hidden_ref[0, tap : tap + rows] for tap in range(3)], axis=-1
    ).reshape(rows * cols, 3 * width)
    terms = product(taps, table[...], 1, 0).reshape(rows, cols, 3 * width)
    stored = (
        terms[..., width : 2 * width]
        + from_left(terms[..., :width])
        + from_right(terms[..., 2 * width :])
    ).astype(BF16)
    out_ref[0] = stored
    values = stored.astype(F32)
    store_sums(sums_ref, date, dates, column_sum(values), column_sum(values * values))


def score_kernel(
    dates,
    norm_count,
    grad_scale,
    block_ref,
    stats_ref,
    gain_ref,
    position_ref,
    grad_ref,
    valid_ref,
    score_ref,
    spread_ref,
    feat_ref,
    exp_ref,
    attn_ref,
    norm_ref,
    packed_ref,
    total,
    mean,
):
    date = pl.program_id(0)
    rows, cols, width = block_ref.shape[1:]

    @pl.when(date == 0)
    def _():
        norm_table(stats_ref, norm_ref, dates, norm_count)
        total[...] = jnp.zeros_like(total)
        mean[...] = jnp.zeros_like(mean)

    scale = norm_ref[pl.ds(dates + date, 1), :] * gain_ref[2:3]
    shift = gain_ref[3:4] - norm_ref[pl.ds(date, 1), :] * scale
    linear = block_ref[0].astype(F32) * scale + shift
    features = (linear * sigmoid(linear) + position_ref[pl.ds(date, 1), :]).astype(BF16)
    feat_ref[0] = features
    upstream = grad_ref[...]
    upstream = jnp.stack([upstream[:, row].reshape(cols, width) for row in range(rows)])
    parts = split(upstream.astype(F32) * features.astype(F32))
    parts = jnp.concatenate(parts, axis=-1).reshape(rows * cols, 2 * width)
    attn = product(parts, spread_ref[...], 1, 0).reshape(rows, cols, width) * grad_scale
    both = product(features.reshape(rows * cols, width), score_ref[...], 1, 0)
    scores = (both[:, :width] + both[:, width:]).reshape(rows, cols, width)
    diagonal = lax.broadcasted_iota(jnp.int32, (cols, cols), 0) == lax.broadcasted_iota(
        jnp.int32, (cols, cols), 1
    )
    ones = jnp.ones((cols, width), BF16)
    clear = jnp.concatenate(
        [jnp.where(diagonal, valid_ref[0, row : row + 1], 0.0) for row in range(rows)], axis=0
    ).astype(BF16)
    clear = product(clear, ones, 1, 0).reshape(rows, cols, width)
    exponent = clear * jnp.exp(scores)
    running = total[...] + exponent
    share = jnp.where(running > 0.0, exponent / running, 0.0)
    total[...] = running
    mean[...] += share * (attn - mean[...])
    exp_ref[0] = exponent
    attn_ref[0] = attn

    @pl.when(date == dates - 1)
    def _():
        place = lax.broadcasted_iota(jnp.int32, (cols, width), 1) % rows
        for index, source in enumerate((total, mean)):
            dense = jnp.zeros((cols, width), F32)
            for row in range(rows):
                dense = dense + jnp.where(place == row, source[row], 0.0)
            for copy in range(packed_ref.shape[0]):
                packed_ref[copy, index] = dense


def attend_kernel(
    dates,
    grad_scale,
    packed_ref,
    feat_ref,
    exp_ref,
    attn_ref,
    block_ref,
    norm_ref,
    gain_ref,
    query_ref,
    grad_ref,
    key_ref,
    spread_ref,
    grad_out_ref,
    up_ref,
    down_ref,
    part_ref,
    key_out_ref,
    vector_ref,
    sums_ref,
    inverse,
    average,
    attended,
):
    date = pl.program_id(0)
    rows, cols, width = block_ref.shape[1:]

    @pl.when(date == 0)
    def _():
        denominator = jnp.sum(packed_ref[:, 0], axis=0)
        reciprocal = 1.0 / denominator
        mean = jnp.sum(packed_ref[:, 0] * reciprocal * packed_ref[:, 1], axis=0)
        place = lax.broadcasted_iota(jnp.int32, (cols, width), 1) % rows
        for values, target in ((reciprocal, inverse), (mean, average)):
            parts = jnp.concatenate(split(values), axis=-1)
            wide_place = jnp.concatenate([place, place], axis=-1)
            picked = jnp.concatenate(
                [jnp.where(wide_place == row, parts, jnp.zeros_like(parts)) for row in range(rows)], axis=0
            )
            target[...] = product(picked, spread_ref[...], 1, 0).reshape(rows, cols, width)
        attended[...] = jnp.zeros_like(attended)
        key_out_ref[...] = jnp.zeros_like(key_out_ref)
        vector_ref[...] = jnp.zeros_like(vector_ref)

    features = feat_ref[0]
    weights = exp_ref[0] * inverse[...]
    rounded = weights.astype(BF16).astype(F32)
    attended[...] += rounded * features.astype(F32)
    score_grad = weights * (attn_ref[0] - average[...])
    spread_grad = score_grad * query_ref[0:1]
    rest = spread_grad - spread_grad.astype(BF16).astype(F32)
    lane = lax.broadcasted_iota(jnp.int32, spread_grad.shape, 2) % (width // 16)
    key_grads = jnp.where(lane == 5, rest, spread_grad).astype(BF16).reshape(rows * cols, width)
    key_out_ref[...] += product(features.reshape(rows * cols, width), key_grads, 0, 0)
    upstream = grad_ref[...]
    upstream = jnp.stack([upstream[:, row].reshape(cols, width) for row in range(rows)])
    feat_grad = rounded * (upstream.astype(F32) * grad_scale) + product(
        key_grads, key_ref[...], 1, 1
    ).reshape(rows, cols, width)
    gain = gain_ref[2:3]
    centred = (block_ref[0].astype(F32) - norm_ref[pl.ds(date, 1), :]) * norm_ref[
        pl.ds(dates + date, 1), :
    ]
    linear = centred * gain + gain_ref[3:4]
    part = sigmoid(linear)
    linear_grad = feat_grad * (part * (1.0 + linear * (1.0 - part)))
    first = column_sum(linear_grad)
    second = column_sum(linear_grad * centred)
    vector_ref[0:1] += second
    vector_ref[1:2] += first
    store_sums(sums_ref, date, dates, first * gain, second * gain)
    stored = (linear_grad * gain).astype(BF16)
    grad_out_ref[0] = stored
    up_ref[0, 0] = stored[0]
    up_ref[0, 1] = block_ref[0, 0]
    down_ref[0, 0] = stored[rows - 1]
    down_ref[0, 1] = block_ref[0, rows - 1]

    @pl.when(date == dates - 1)
    def _():
        devices, piece = part_ref.shape[0], part_ref.shape[2]
        for device in range(devices):
            part_ref[device] = attended[:, device * piece : (device + 1) * piece].astype(BF16)
        key_part = key_out_ref[...]
        place = lax.broadcasted_iota(jnp.int32, (width, width), 1) % (width // 16)
        both = pltpu.roll(key_part, width - 4, 1) + pltpu.roll(key_part, width - 5, 1)
        both = jnp.where(place == 0, both, 0.0)
        both = both + pltpu.roll(both, 1, 1)
        both = both + pltpu.roll(both, 2, 1)
        vector_ref[2:3] = 0.5 * jnp.sum(key_ref[...].astype(F32) * both, axis=0, keepdims=True)


def hidden_kernel(
    dates,
    norm_count,
    edge_ref,
    grad_ref,
    block_ref,
    up_ref,
    down_ref,
    tails_ref,
    norm_ref,
    weight_ref,
    conv_ref,
    first_norm_ref,
    gain_ref,
    pre_ref,
    out_ref,
    vector_ref,
    sums_ref,
    table,
    factors,
    padded,
):
    date = pl.program_id(0)
    rows, cols, width = block_ref.shape[1:]

    @pl.when(date == 0)
    def _():
        tails = group_sum(jnp.sum(tails_ref[...], axis=0)) / norm_count
        mean, inverse = norm_ref[:dates], norm_ref[dates:]
        slope = -inverse * inverse * tails[dates:]
        factors[0:dates] = slope
        factors[dates : 2 * dates] = -inverse * tails[:dates] - mean * slope
        vector_ref[...] = jnp.zeros_like(vector_ref)
        for row_tap in range(3):
            for col_tap in range(3):
                table[
                    col_tap * width : (col_tap + 1) * width, row_tap * width : (row_tap + 1) * width
                ] = weight_ref[2 - row_tap, col_tap]

    inverse = norm_ref[pl.ds(dates + date, 1), :]
    slope = factors[pl.ds(date, 1), :]
    constant = factors[pl.ds(dates + date, 1), :]

    def finish(grad, values):
        return grad.astype(F32) * inverse + (values.astype(F32) * slope + constant)

    stored = finish(grad_ref[0], block_ref[0]).astype(BF16)
    pre_ref[0] = stored
    padded[0] = (finish(up_ref[0, 0], up_ref[0, 1]) * edge_ref[0]).astype(BF16)
    padded[rows + 1] = (finish(down_ref[0, 0], down_ref[0, 1]) * edge_ref[1]).astype(BF16)
    padded[1 : rows + 1] = stored
    taps = jnp.concatenate([padded[tap : tap + rows] for tap in range(3)], axis=-1).reshape(
        rows * cols, 3 * width
    )
    terms = product(taps, table[...], 1, 1).reshape(rows, cols, 3 * width)
    hidden_grad = (
        terms[..., width : 2 * width]
        + from_right(terms[..., :width])
        + from_left(terms[..., 2 * width :])
    )
    gain = gain_ref[0:1]
    centred = (conv_ref[0].astype(F32) - first_norm_ref[pl.ds(date, 1), :]) * first_norm_ref[
        pl.ds(dates + date, 1), :
    ]
    linear = centred * gain + gain_ref[1:2]
    part = sigmoid(linear)
    linear_grad = hidden_grad * (part * (1.0 + linear * (1.0 - part)))
    out_ref[0] = linear_grad
    first = column_sum(linear_grad)
    second = column_sum(linear_grad * centred)
    vector_ref[0:1] += second
    vector_ref[1:2] += first
    store_sums(sums_ref, date, dates, first * gain, second * gain)


def block_grad_kernel(dates, hidden_ref, pre_ref, key_ref, vector_ref, out_ref, total):
    date = pl.program_id(0)
    rows, cols, width = pre_ref.shape[1:]

    @pl.when(date == 0)
    def _():
        total[...] = jnp.zeros_like(total)

    grads = pre_ref[0].astype(F32)
    grads = jnp.concatenate(
        [from_right(grads).astype(BF16), pre_ref[0], from_left(grads).astype(BF16)], axis=-1
    ).reshape(rows * cols, 3 * width)
    taps = jnp.concatenate(
        [hidden_ref[0, tap : tap + rows] for tap in range(3)], axis=-1
    ).reshape(rows * cols, 3 * width)
    total[...] += product(taps, grads, 0, 0)

    @pl.when(date == dates - 1)
    def _():
        for row_tap in range(3):
            for col_tap in range(3):
                base = (row_tap * 3 + col_tap) * width
                out_ref[base : base + width] = total[
                    row_tap * width : (row_tap + 1) * width, col_tap * width : (col_tap + 1) * width
                ].astype(BF16)
        high, low = split(key_ref[...])
        out_ref[9 * width : 10 * width] = high
        out_ref[10 * width : 11 * width] = low
        high, low = split(vector_ref[...])
        out_ref[11 * width : 11 * width + 16] = jnp.concatenate([high, low], axis=0)
        out_ref[11 * width + 16 :] = jnp.zeros_like(out_ref[11 * width + 16 :])


def conv_grad_kernel(
    dates,
    norm_count,
    img_ref,
    above_ref,
    conv_ref,
    grad_ref,
    tails_ref,
    norm_ref,
    gain_ref,
    vector_ref,
    out_ref,
    factors,
    total,
):
    date = pl.program_id(0)
    rows, cols, width = conv_ref.shape[1:]
    half = width // 2

    @pl.when(date == 0)
    def _():
        tails = group_sum(jnp.sum(tails_ref[...], axis=0)) / norm_count
        mean, inverse = norm_ref[:dates], norm_ref[dates:]
        slope = -inverse * inverse * tails[dates:]
        factors[0:dates] = slope
        factors[dates : 2 * dates] = -inverse * tails[:dates] - mean * slope
        total[...] = jnp.zeros_like(total)

    scale = norm_ref[pl.ds(dates + date, 1), :] * gain_ref[0:1]
    slope = factors[pl.ds(date, 1), :]
    constant = factors[pl.ds(dates + date, 1), :]
    stored = (grad_ref[0] * scale + (conv_ref[0].astype(F32) * slope + constant)).astype(BF16)
    moved = from_right(stored.astype(F32)).astype(BF16)
    grads = jnp.concatenate([stored, moved], axis=-1).reshape(rows * cols, 2 * width)
    even, odd = img_ref[0, :, 0], img_ref[0, :, 1]
    above = jnp.concatenate([above_ref[0][None], odd[:-1]], axis=0)
    taps = jnp.concatenate([above, even, odd], axis=-1).reshape(rows * cols, 3 * width)
    total[...] += product(taps, grads, 0, 0)

    @pl.when(date == dates - 1)
    def _():
        for tap in range(3):
            base = tap * width
            pair = total[base : base + width, :width].astype(BF16)
            left = total[base + half : base + width, width:].astype(BF16)
            start = tap * 3 * half
            out_ref[start : start + half] = left
            out_ref[start + half : start + 3 * half] = pair
        high, low = split(vector_ref[...])
        out_ref[9 * half : 9 * half + 16] = jnp.concatenate([high, low], axis=0)
        out_ref[9 * half + 16 :] = jnp.zeros_like(out_ref[9 * half + 16 :])


def total_kernel(in_ref, out_ref):
    total = jnp.sum(in_ref[...].astype(F32), axis=0).astype(BF16)
    for copy in range(out_ref.shape[0]):
        out_ref[copy] = total


def per_date(shape):
    zeros = (0,) * (len(shape) - 1)
    return pl.BlockSpec((1,) + tuple(shape[1:]), lambda date: (date,) + zeros)


def whole(shape):
    zeros = (0,) * len(shape)
    return pl.BlockSpec(tuple(shape), lambda date: zeros)


def call(kernel, dates, inputs, outputs, scratch, flops):
    in_specs, arrays = [], []
    for kind, array in inputs:
        arrays.append(array)
        if kind == "scalar":
            in_specs.append(pl.BlockSpec(memory_space=pltpu.SMEM))
        else:
            in_specs.append((per_date if kind == "date" else whole)(array.shape))
    out_specs = [(per_date if kind == "date" else whole)(shape) for kind, shape, _ in outputs]
    moved = sum(array.size * array.dtype.itemsize for array in arrays)
    return pl.pallas_call(
        kernel,
        grid=(dates,),
        in_specs=in_specs,
        out_specs=out_specs,
        out_shape=[jax.ShapeDtypeStruct(shape, dtype) for _, shape, dtype in outputs],
        scratch_shapes=scratch,
        compiler_params=pltpu.CompilerParams(vmem_limit_bytes=48 * MIB),
        cost_estimate=pl.CostEstimate(flops=flops, bytes_accessed=2 * moved, transcendentals=0),
    )(*arrays)


def encoding(day_index, feat_width):
    half_range = jnp.arange(feat_width // 2, dtype=F32)
    frequency = jnp.exp(half_range * (-2.0 * jnp.log(1000.0) / feat_width))
    angles = day_index.astype(F32)[:, None] * frequency[None, :]
    return jnp.stack([jnp.sin(angles), jnp.cos(angles)], axis=-1).reshape(
        day_index.shape[0], feat_width
    )


def neighbours(first_rows, last_rows):
    devices = lax.axis_size("rows")
    down = [(i, i + 1) for i in range(devices - 1)]
    up = [(i + 1, i) for i in range(devices - 1)]
    return lax.ppermute(last_rows, "rows", down), lax.ppermute(first_rows, "rows", up)


def exchange(pieces, axes):
    return lax.all_to_all(pieces, axes, split_axis=0, concat_axis=0, tiled=True)


def sum_over_all(rows_array):
    axes = ("rows", "dates")
    devices = lax.axis_size(axes)
    count, width = rows_array.shape
    pieces = exchange(rows_array.reshape(devices, count // devices, width), axes)
    spread = pl.pallas_call(
        total_kernel,
        out_shape=jax.ShapeDtypeStruct(pieces.shape, BF16),
        compiler_params=pltpu.CompilerParams(vmem_limit_bytes=32 * MIB),
    )(pieces)
    return exchange(spread, axes).reshape(count, width)


def padded_count(count, devices):
    step = 8 * devices
    return -(-count // step) * step


def local(
    images,
    day_index,
    valid,
    out_grad,
    conv_weight,
    first_gain,
    first_shift,
    block_weight,
    gn_gain,
    gn_shift,
    key_weight,
    queries,
):
    dates, rows_here, cols, pair_width = images.shape
    width = conv_weight.shape[-1]
    row_devs, date_devs = lax.axis_size("rows"), lax.axis_size("dates")
    devices = row_devs * date_devs
    rows = rows_here // 2
    heads, depth = queries.shape
    lanes = width // heads
    norm_count = float(rows * row_devs * cols * (width // GROUPS))
    grad_scale = float(rows * row_devs * cols) ** (-0.5)
    row_index = lax.axis_index("rows")
    date_start = lax.axis_index("dates") * dates
    frame = (dates, rows, cols, width)
    edge_rows = (dates, cols, width)
    tile = (row_devs, 2 * dates, width)
    flops = 2 * dates * rows * cols * width * width

    above = lax.ppermute(images[:, -1], "rows", [(i, i + 1) for i in range(row_devs - 1)])
    grads_here = lax.all_gather(out_grad, "dates")
    clear = lax.all_gather(valid.astype(BF16), "dates")
    clear = lax.dynamic_slice_in_dim(clear, date_start, dates, 1)
    clear = clear.transpose(1, 2, 0, 3).reshape(dates, rows, cols).astype(F32)
    edges = jnp.stack([row_index > 0, row_index < row_devs - 1]).astype(F32)
    gains = jnp.stack([first_gain, first_shift, gn_gain, gn_shift] * 2)
    position = lax.dynamic_slice_in_dim(encoding(day_index, width), date_start, dates, 0)
    position = jnp.concatenate([position, position], axis=0)
    half_queries = queries * (depth**-0.5)
    folded = jnp.sum(
        key_weight.astype(F32).reshape(width, heads, depth) * half_queries[None], axis=-1
    )
    folded = jnp.repeat(folded, lanes, axis=1)
    score_weight = jnp.concatenate(split(folded), axis=1)
    key_wide = jnp.pad(
        key_weight.reshape(width, heads, depth), ((0, 0), (0, 0), (0, lanes - depth))
    ).reshape(width, width)
    query_wide = jnp.concatenate(
        [half_queries, jnp.ones((heads, 2), F32), jnp.zeros((heads, lanes - depth - 2), F32)],
        axis=1,
    ).reshape(1, width)
    query_wide = jnp.broadcast_to(query_wide, (8, width))
    head_of = jnp.arange(width) // lanes
    spread = (head_of[:, None] == head_of[None, :]).astype(BF16)
    spread = jnp.concatenate([spread, spread], axis=0)

    paired = images.reshape(dates, rows, 2, cols, pair_width)
    conv_out, top, low, sums = call(
        functools.partial(down_kernel, dates),
        dates,
        [("date", paired), ("date", above), ("all", conv_weight)],
        [
            ("date", frame, BF16),
            ("date", edge_rows, BF16),
            ("date", edge_rows, BF16),
            ("all", tile, F32),
        ],
        [pltpu.VMEM((3 * pair_width, 2 * width), BF16)],
        6 * flops,
    )
    stats = exchange(sums, "rows")
    halo_up, halo_down = neighbours(top, low)
    block_out, hidden, first_norm, sums = call(
        functools.partial(block_kernel, dates, norm_count),
        dates,
        [
            ("scalar", edges),
            ("date", conv_out),
            ("date", halo_up),
            ("date", halo_down),
            ("all", stats),
            ("all", gains),
            ("all", block_weight),
        ],
        [
            ("date", frame, BF16),
            ("date", (dates, rows + 2, cols, width), BF16),
            ("all", (2 * dates, width), F32),
            ("all", tile, F32),
        ],
        [pltpu.VMEM((3 * width, 3 * width), BF16)],
        9 * flops,
    )
    stats = exchange(sums, "rows")
    features, exponent, attn, norm, packed = call(
        functools.partial(score_kernel, dates, norm_count, grad_scale),
        dates,
        [
            ("date", block_out),
            ("all", stats),
            ("all", gains),
            ("all", position),
            ("all", grads_here),
            ("date", clear),
            ("all", score_weight),
            ("all", spread),
        ],
        [
            ("date", frame, BF16),
            ("date", frame, F32),
            ("date", frame, F32),
            ("all", (2 * dates, width), F32),
            ("all", (date_devs, 2, cols, width), F32),
        ],
        [pltpu.VMEM(frame[1:], F32), pltpu.VMEM(frame[1:], F32)],
        5 * flops,
    )
    packed = exchange(packed, "dates")
    block_grad, up, low, attended, key_part, vectors, sums = call(
        functools.partial(attend_kernel, dates, grad_scale),
        dates,
        [
            ("all", packed),
            ("date", features),
            ("date", exponent),
            ("date", attn),
            ("date", block_out),
            ("all", norm),
            ("all", gains),
            ("all", query_wide),
            ("all", grads_here),
            ("all", key_wide),
            ("all", spread),
        ],
        [
            ("date", frame, BF16),
            ("date", (dates, 2, cols, width), BF16),
            ("date", (dates, 2, cols, width), BF16),
            ("all", (date_devs, rows, cols // date_devs, width), BF16),
            ("all", (width, width), F32),
            ("all", (8, width), F32),
            ("all", tile, F32),
        ],
        [pltpu.VMEM(frame[1:], F32)] * 3,
        5 * flops,
    )
    tails = exchange(sums, "rows")
    halo_up, halo_down = neighbours(up, low)
    attended = jnp.sum(exchange(attended, "dates").astype(F32), axis=0).astype(BF16)
    pre_grad, linear_grad, first_vectors, sums = call(
        functools.partial(hidden_kernel, dates, norm_count),
        dates,
        [
            ("scalar", edges),
            ("date", block_grad),
            ("date", block_out),
            ("date", halo_up),
            ("date", halo_down),
            ("all", tails),
            ("all", norm),
            ("all", block_weight),
            ("date", conv_out),
            ("all", first_norm),
            ("all", gains),
        ],
        [
            ("date", frame, BF16),
            ("date", frame, F32),
            ("all", (8, width), F32),
            ("all", tile, F32),
        ],
        [
            pltpu.VMEM((3 * width, 3 * width), BF16),
            pltpu.VMEM((2 * dates, width), F32),
            pltpu.VMEM((rows + 2, cols, width), BF16),
        ],
        9 * flops,
    )
    tails = exchange(sums, "rows")
    (block_rows,) = call(
        functools.partial(block_grad_kernel, dates),
        dates,
        [("date", hidden), ("date", pre_grad), ("all", key_part), ("all", vectors)],
        [("all", (padded_count(11 * width + 16, devices), width), BF16)],
        [pltpu.VMEM((3 * width, 3 * width), F32)],
        9 * flops,
    )
    block_rows = sum_over_all(block_rows)
    (conv_rows,) = call(
        functools.partial(conv_grad_kernel, dates, norm_count),
        dates,
        [
            ("date", paired),
            ("date", above),
            ("date", conv_out),
            ("date", linear_grad),
            ("all", tails),
            ("all", first_norm),
            ("all", gains),
            ("all", first_vectors),
        ],
        [("all", (padded_count(9 * pair_width // 2 + 16, devices), width), BF16)],
        [pltpu.VMEM((2 * dates, width), F32), pltpu.VMEM((3 * pair_width, 2 * width), F32)],
        6 * flops,
    )
    conv_rows = sum_over_all(conv_rows)

    conv_end = 9 * pair_width // 2
    conv_total = conv_rows[:conv_end].astype(F32).reshape(conv_weight.shape)
    first_sums = conv_rows[conv_end : conv_end + 16].astype(F32)
    first_sums = first_sums[:8] + first_sums[8:]
    block_total = block_rows[: 9 * width].astype(F32).reshape(block_weight.shape)
    key_sums = block_rows[9 * width : 11 * width].astype(F32)
    key_sums = key_sums[:width] + key_sums[width:]
    key_total = key_sums.reshape(width, heads, lanes)[:, :, :depth].reshape(width, heads * depth)
    sums = block_rows[11 * width : 11 * width + 16].astype(F32)
    sums = sums[:8] + sums[8:]
    query_total = sums[2].reshape(heads, lanes)[:, :depth]
    return (
        attended,
        conv_total,
        first_sums[0],
        first_sums[1],
        block_total,
        sums[0],
        sums[1],
        key_total,
        query_total,
    )


def solution(mesh):
    return jax.shard_map(
        local,
        mesh=mesh,
        in_specs=(
            P("dates", "rows", None, None),
            P(),
            P(None, "rows", "dates"),
            P("rows", "dates", None),
            P(),
            P(),
            P(),
            P(),
            P(),
            P(),
            P(),
            P(),
        ),
        out_specs=(P("rows", "dates", None), P(), P(), P(), P(), P(), P(), P(), P()),
        check_vma=False,
    )
```

profile of v0, /device:TPU:0, one launch (start us, length us, event | category | flops | bytes accessed | tf_op | source)
XLA Modules:
  0.0 183.3 jit_solution(9968543250966465004)
XLA Ops:
  0.6 0.9 slice_bitcast_fusion
  1.6 4.9 %collective-permute-start = (bf16[4,128,128]{2,1,0:T(8,128)(2,1)S(1)}, bf16[4,128,128]{2,1,0:T(8,128)(2,1)S(1)}, u32[]{:S(2)}, u32[]{:S(2)}) collective-permute-start(bf16[4,128,128]{2,1,0:T(8,128)(2,1)S(1)} %slice_bitcast_fusion), channel_id=1, source_target_pairs={{0,4},{4,8},{8,12},{12,16},{16,20},{20,24},{24,28},{1,5},{5,9},{9,... | collective-permute-start | bytes 393224 | tf_op jit(solution)/shard_map/ppermute | solution.py:586
  8.0 0.8 convert_element_type.56
  9.1 0.8 multiply_reduce_fusion
  10.1 5.4 %all-gather.1 = bf16[64,8,32]{2,1,0:T(8,128)(2,1)S(1)} all-gather(bf16[16,8,32]{2,1,0:T(8,128)(2,1)S(1)} %convert_element_type.56), channel_id=3, replica_groups=mesh['rows'=8,'dates'=4] {'dates'}, dimensions={0}, use_global_device_ids=true | all-gather | bytes 40960 | tf_op jit(solution)/shard_map/all_gather | solution.py:588
  15.8 1.6 copy-done
  17.3 0.9 copy-done.10
  18.3 2.5 %shard_map.187 = (bf16[4,8,128,128]{3,2,1,0:T(8,128)(2,1)S(1)}, bf16[4,128,128]{2,1,0:T(8,128)(2,1)S(1)}, bf16[4,128,128]{2,1,0:T(8,128)(2,1)S(1)}, f32[8,8,128]{2,1,0:T(8,128)}) custom-call(bf16[4,8,2,128,128]{4,3,2,1,0:T(8,128)(2,1)S(1)} %bitcast.42, bf16[4,128,128]{2,1,0:T(8,128)(2,1)S(1)} %collective-permute-done.above_ref, ...), custom_call_target="tpu_custom_call" | custom-call | flops 805306368 | bytes 4751360 | tf_op jit(solution)/shard_map/pallas_call | solution.py:506
  20.8 3.4 %collective-permute-start.1 = (bf16[4,128,128]{2,1,0:T(8,128)(2,1)S(1)}, bf16[4,128,128]{2,1,0:T(8,128)(2,1)S(1)}, u32[]{:S(2)}, u32[]{:S(2)}) collective-permute-start(bf16[4,128,128]{2,1,0:T(8,128)(2,1)S(1)} %get-tuple-element.34), channel_id=1, source_target_pairs={{0,4},{4,8},{8,12},{12,16},{16,20},{20,24},{24,28},{1,5},{5,9},{9,... | collective-permute-start | bytes 393224 | tf_op jit(solution)/shard_map/ppermute | solution.py:531
  24.2 1.3 collective-permute-start.2
  25.7 6.9 %all-to-all-start = ((f32[8,8,128]{2,1,0:T(8,128)}), f32[8,8,128]{2,1,0:T(8,128)S(1)}, u32[]{:S(2)}, u32[]{:S(2)}) async-start(f32[8,8,128]{2,1,0:T(8,128)} %get-tuple-element.36), calls=%async_computation | async-start | bytes 65536 | tf_op jit(solution)/shard_map/all_to_all | solution.py:535
  32.7 6.6 %all-to-all-done.stats_ref = f32[8,8,128]{2,1,0:T(8,128)S(1)} async-done(((f32[8,8,128]{2,1,0:T(8,128)}), f32[8,8,128]{2,1,0:T(8,128)S(1)}, u32[]{:S(2)}, u32[]{:S(2)}) %all-to-all-start) | async-done | bytes 32800 | tf_op jit(solution)/shard_map/all_to_all | solution.py:535
  39.4 4.3 %shard_map.188 = (bf16[4,8,128,128]{3,2,1,0:T(8,128)(2,1)S(1)}, bf16[4,10,128,128]{3,2,1,0:T(8,128)(2,1)S(1)}, f32[8,128]{1,0:T(8,128)S(1)}, f32[8,8,128]{2,1,0:T(8,128)}) custom-call(f32[2]{0:T(128)S(1)} %add_convert_fusion.1.edge_ref, bf16[4,8,128,128]{3,2,1,0:T(8,128)(2,1)S(1)} %get-tuple-element.33.conv_ref, ...), custom_call_target="tpu_custom_call" | custom-call | flops 1207959552 | bytes 3285008 | tf_op jit(solution)/shard_map/pallas_call | solution.py:506
  43.7 1.1 copy-done.13
  44.8 3.5 %all-to-all-start.1 = ((f32[8,8,128]{2,1,0:T(8,128)}), f32[8,8,128]{2,1,0:T(8,128)S(1)}, u32[]{:S(2)}, u32[]{:S(2)}) async-start(f32[8,8,128]{2,1,0:T(8,128)} %get-tuple-element.38), calls=%async_computation.1 | async-start | bytes 65536 | tf_op jit(solution)/shard_map/all_to_all | solution.py:535
  48.3 5.8 %all-gather = bf16[32,32,128]{2,1,0:T(8,128)(2,1)S(1)} all-gather(bf16[8,32,128]{2,1,0:T(8,128)(2,1)S(1)} %copy-done.15), channel_id=2, replica_groups=mesh['rows'=8,'dates'=4] {'dates'}, dimensions={0}, use_global_device_ids=true | all-gather | bytes 327680 | tf_op jit(solution)/shard_map/all_gather | solution.py:587
  54.1 0.8 all-to-all-done.1.stats_ref
  54.9 3.9 %shard_map.189 = (bf16[4,8,128,128]{3,2,1,0:T(8,128)(2,1)S(1)}, f32[4,8,128,128]{3,2,1,0:T(8,128)S(1)}, f32[4,8,128,128]{3,2,1,0:T(8,128)}, f32[8,128]{1,0:T(8,128)S(1)}, f32[4,2,128,128]{3,2,1,0:T(8,128)}) custom-call(bf16[4,8,128,128]{3,2,1,0:T(8,128)(2,1)S(1)} %get-tuple-element.37.block_ref, f32[8,8,128]{2,1,0:T(8,128)S(1)} %all-to-all-done.1.stats_ref, ...), custom_call_target="tpu_custom_call" | custom-call | flops 671088640 | bytes 2998272 | tf_op jit(solution)/shard_map/pallas_call | solution.py:506
  58.8 1.3 copy-done.3
  60.1 1.0 copy-done.6
  61.1 3.5 %all-to-all-start.2 = ((f32[4,2,128,128]{3,2,1,0:T(8,128)}), f32[4,2,128,128]{3,2,1,0:T(8,128)S(1)}, u32[]{:S(2)}, u32[]{:S(2)}) async-start(f32[4,2,128,128]{3,2,1,0:T(8,128)} %get-tuple-element.39), calls=%async_computation.2 | async-start | bytes 1048576 | tf_op jit(solution)/shard_map/all_to_all | solution.py:535
  65.2 8.3 %all-to-all-done.2.packed_ref = f32[4,2,128,128]{3,2,1,0:T(8,128)S(1)} async-done(((f32[4,2,128,128]{3,2,1,0:T(8,128)}), f32[4,2,128,128]{3,2,1,0:T(8,128)S(1)}, u32[]{:S(2)}, u32[]{:S(2)}) %all-to-all-start.2) | async-done | bytes 524320 | tf_op jit(solution)/shard_map/all_to_all | solution.py:535
  73.4 1.2 copy-done.7
  74.7 6.1 %shard_map.190 = (bf16[4,8,128,128]{3,2,1,0:T(8,128)(2,1)S(1)}, bf16[4,2,128,128]{3,2,1,0:T(8,128)(2,1)S(1)}, bf16[4,2,128,128]{3,2,1,0:T(8,128)(2,1)S(1)}, bf16...) custom-call(f32[4,2,128,128]{3,2,1,0:T(8,128)S(1)} %all-to-all-done.2.pac, ...), custom_call_target="tpu_custom_call" | custom-call | flops 671088640 | bytes 14376960 | tf_op jit(solution)/shard_map/pallas_call | solution.py:506
  80.8 3.0 %collective-permute-start.3 = (bf16[4,2,128,128]{3,2,1,0:T(8,128)(2,1)S(1)}, bf16[4,2,128,128]{3,2,1,0:T(8,128)(2,1)S(1)}, u32[]{:S(2)}, u32[]{:S(2)}) collective-permute-start(bf16[4,2,128,128]{3,2,1,0:T(8,128)(2,1)S(1)} %get-tuple-element.46), channel_id=1, source_target_pairs={{0,4},{4,8},{8,12},{12,16},{16,20},{20,24},{24,28},{1,5},{5,9},{9,... | collective-permute-start | bytes 786440 | tf_op jit(solution)/shard_map/ppermute | solution.py:531
  83.8 1.3 collective-permute-start.4
  85.1 13.1 %all_to_all.50.tails_ref = f32[8,8,128]{2,1,0:T(8,128)S(1)} all-to-all(f32[8,8,128]{2,1,0:T(8,128)S(1)} %get-tuple-element.48), channel_id=1, replica_groups=mesh['rows'=8,'dates'=4] {'rows'}, dimensions={0} | all-to-all | bytes 65536 | tf_op jit(solution)/shard_map/all_to_all | solution.py:535
  98.2 1.2 copy-done.5
  99.5 5.1 %shard_map.191 = (bf16[4,8,128,128]{3,2,1,0:T(8,128)(2,1)S(1)}, f32[4,8,128,128]{3,2,1,0:T(8,128)}, f32[8,128]{1,0:T(8,128)S(1)}, f32[8,8,128]{2,1,0:T(8,128)S(1)}) custom-call(f32[2]{0:T(128)S(1)} %add_convert_fusion.1.edge_ref, bf16[4,8,128,128]{3,2,1,0:T(8,128)(2,1)S(1)} %get-tuple-element.45.grad_ref, bf16[4,8,128,128]{3,2,1,0:T(8,128)(2,1)S(1)} %copy-done.5, ...), custom_call_target="tpu_custom_call" | custom-call | flops 1207959552 | bytes 8019984 | tf_op jit(solution)/shard_map/pallas_call | solution.py:506
  104.5 1.0 copy-done.11
  105.5 9.8 %all_to_all.51.tails_ref = f32[8,8,128]{2,1,0:T(8,128)S(1)} all-to-all(f32[8,8,128]{2,1,0:T(8,128)S(1)} %get-tuple-element.51), channel_id=1, replica_groups=mesh['rows'=8,'dates'=4] {'rows'}, dimensions={0} | all-to-all | bytes 65536 | tf_op jit(solution)/shard_map/all_to_all | solution.py:535
  115.3 4.0 %all-to-all-start.3 = ((bf16[4,8,32,128]{3,2,1,0:T(8,128)(2,1)}), bf16[4,8,32,128]{3,2,1,0:T(8,128)(2,1)}, u32[]{:S(2)}, u32[]{:S(2)}) async-start(bf16[4,8,32,128]{3,2,1,0:T(8,128)(2,1)} %get-tuple-element.44), calls=%async_computation.3 | async-start | bytes 524288 | tf_op jit(solution)/shard_map/all_to_all | solution.py:535
  119.4 1.6 copy-done.2
  121.0 2.5 %shard_map.192 = bf16[768,128]{1,0:T(8,128)(2,1)} custom-call(bf16[4,8,2,128,128]{4,3,2,1,0:T(8,128)(2,1)S(1)} %bitcast.43, bf16[4,128,128]{2,1,0:T(8,128)(2,1)S(1)} %collective-permute-done.above_ref, bf16[4,8,128,128]{3,2,1,0:T(8,128)(2,1)S(1)} %get-tuple-element.33.conv_ref, f32[4,8,128,128]{3,2,1,0:T(8,128)S(1)} %copy-done.2, ...), custom_call_target="tpu_custom_call" | custom-call | flops 805306368 | bytes 10838016 | tf_op jit(solution)/shard_map/pallas_call | solution.py:506
  123.5 1.9 %all-to-all-done.3 = bf16[4,8,32,128]{3,2,1,0:T(8,128)(2,1)} async-done(((bf16[4,8,32,128]{3,2,1,0:T(8,128)(2,1)}), bf16[4,8,32,128]{3,2,1,0:T(8,128)(2,1)}, u32[]{:S(2)}, u32[]{:S(2)}) %all-to-all-start.3) | async-done | bytes 262176 | tf_op jit(solution)/shard_map/all_to_all | solution.py:535
  125.5 2.6 %all-to-all-start.6 = ((bf16[32,24,128]{2,1,0:T(8,128)(2,1)}), bf16[32,24,128]{2,1,0:T(8,128)(2,1)S(1)}, u32[]{:S(2)}, u32[]{:S(2)}) async-start(bf16[32,24,128]{2,1,0:T(8,128)(2,1)} %bitcast.15), calls=%async_computation.6 | async-start | bytes 393216 | tf_op jit(solution)/shard_map/all_to_all | solution.py:535
  128.1 1.2 copy-done.12
  129.3 1.3 copy-done.14
  130.6 3.3 %shard_map.194 = bf16[1536,128]{1,0:T(8,128)(2,1)} custom-call(bf16[4,10,128,128]{3,2,1,0:T(8,128)(2,1)S(1)} %copy-done.14, bf16[4,8,128,128]{3,2,1,0:T(8,128)(2,1)S(1)} %copy-done.12, f32[128,128]{1,0:T(8,128)S(1)} %get-tuple-element.55.key_ref, f32[8,128]{1,0:T(8,128)S(1)} %get-tuple-element.56.vector_ref), custom_call_target="tpu_custom_call" | custom-call | flops 1207959552 | bytes 4857856 | tf_op jit(solution)/shard_map/pallas_call | solution.py:506
  133.9 3.1 %all-to-all-done.6.in_ref = bf16[32,24,128]{2,1,0:T(8,128)(2,1)S(1)} async-done(((bf16[32,24,128]{2,1,0:T(8,128)(2,1)}), bf16[32,24,128]{2,1,0:T(8,128)(2,1)S(1)}, u32[]{:S(2)}, u32[]{:S(2)}) %all-to-all-start.6) | async-done | bytes 196640 | tf_op jit(solution)/shard_map/all_to_all | solution.py:535
  137.0 2.8 %all-to-all-start.8 = ((bf16[32,48,128]{2,1,0:T(8,128)(2,1)}), bf16[32,48,128]{2,1,0:T(8,128)(2,1)S(1)}, u32[]{:S(2)}, u32[]{:S(2)}) async-start(bf16[32,48,128]{2,1,0:T(8,128)(2,1)} %bitcast.20), calls=%async_computation.8 | async-start | bytes 786432 | tf_op jit(solution)/shard_map/all_to_all | solution.py:535
  140.5 12.5 %all-to-all-done.8.in_ref = bf16[32,48,128]{2,1,0:T(8,128)(2,1)S(1)} async-done(((bf16[32,48,128]{2,1,0:T(8,128)(2,1)}), bf16[32,48,128]{2,1,0:T(8,128)(2,1)S(1)}, u32[]{:S(2)}, u32[]{:S(2)}) %all-to-all-start.8) | async-done | bytes 393248 | tf_op jit(solution)/shard_map/all_to_all | solution.py:535
  152.9 2.6 %all-to-all-start.7 = ((bf16[32,24,128]{2,1,0:T(8,128)(2,1)}), bf16[32,24,128]{2,1,0:T(8,128)(2,1)S(1)}, u32[]{:S(2)}, u32[]{:S(2)}) async-start(bf16[32,24,128]{2,1,0:T(8,128)(2,1)} %shard_map.193), calls=%async_computation.7 | async-start | bytes 393216 | tf_op jit(solution)/shard_map/all_to_all | solution.py:535
  156.4 8.1 %all-to-all-done.7 = bf16[32,24,128]{2,1,0:T(8,128)(2,1)S(1)} async-done(((bf16[32,24,128]{2,1,0:T(8,128)(2,1)}), bf16[32,24,128]{2,1,0:T(8,128)(2,1)S(1)}, u32[]{:S(2)}, u32[]{:S(2)}) %all-to-all-start.7) | async-done | bytes 196640 | tf_op jit(solution)/shard_map/all_to_all | solution.py:535
  164.4 2.7 %all-to-all-start.9 = ((bf16[32,48,128]{2,1,0:T(8,128)(2,1)}), bf16[32,48,128]{2,1,0:T(8,128)(2,1)S(1)}, u32[]{:S(2)}, u32[]{:S(2)}) async-start(bf16[32,48,128]{2,1,0:T(8,128)(2,1)} %shard_map.195), calls=%async_computation.9 | async-start | bytes 786432 | tf_op jit(solution)/shard_map/all_to_all | solution.py:535
  167.2 1.6 reduce_sum.22
  170.1 10.3 %all-to-all-done.9 = bf16[32,48,128]{2,1,0:T(8,128)(2,1)S(1)} async-done(((bf16[32,48,128]{2,1,0:T(8,128)(2,1)}), bf16[32,48,128]{2,1,0:T(8,128)(2,1)S(1)}, u32[]{:S(2)}, u32[]{:S(2)}) %all-to-all-start.9) | async-done | bytes 393248 | tf_op jit(solution)/shard_map/all_to_all | solution.py:535
  182.4 0.9 convert.8
  (86 shorter events, 7.8 us)
Async XLA Ops:
  1.6 14.2 %collective-permute-start = (bf16[4,128,128]{2,1,0:T(8,128)(2,1)S(1)}, bf16[4,128,128]{2,1,0:T(8,128)(2,1)S(1)}, u32[]{:S(2)}, u32[]{:S(2)}) collective-permute-start(bf16[4,128,128]{2,1,0:T(8,128)(2,1)S(1)} %slice_bitcast_fusion), channel_id=1, source_target_pairs={{0,4},{4,8},{8,12},{12,16},{16,20},{20,24},{24,28},{1,5},{5,9},{9,... | collective-permute-start | bytes 393224 | tf_op jit(solution)/shard_map/ppermute | solution.py:586
  9.1 16.6 %copy-start.17 = (f32[128]{0:T(128)S(1)}, f32[128]{0:T(128)}, u32[]{:S(2)}) copy-start(f32[128]{0:T(128)} %param.17) | copy-start | bytes 1540
  9.1 16.6 %copy-start.18 = (f32[128]{0:T(128)S(1)}, f32[128]{0:T(128)}, u32[]{:S(2)}) copy-start(f32[128]{0:T(128)} %param.18) | copy-start | bytes 1540
  9.1 16.6 %copy-start.19 = (f32[128]{0:T(128)S(1)}, f32[128]{0:T(128)}, u32[]{:S(2)}) copy-start(f32[128]{0:T(128)} %param.20) | copy-start | bytes 1540
  9.1 16.6 %copy-start.20 = (f32[128]{0:T(128)S(1)}, f32[128]{0:T(128)}, u32[]{:S(2)}) copy-start(f32[128]{0:T(128)} %param.21) | copy-start | bytes 1540
  10.0 29.3 %copy-start.8 = (bf16[3,3,128,128]{3,2,1,0:T(8,128)(2,1)S(1)}, bf16[3,3,128,128]{3,2,1,0:T(8,128)(2,1)}, u32[]{:S(2)}) copy-start(bf16[3,3,128,128]{3,2,1,0:T(8,128)(2,1)} %weight_ref.5) | copy-start | bytes 884740
  15.7 1.6 copy-start
  17.3 0.9 copy-start.10
  20.8 18.6 %collective-permute-start.1 = (bf16[4,128,128]{2,1,0:T(8,128)(2,1)S(1)}, bf16[4,128,128]{2,1,0:T(8,128)(2,1)S(1)}, u32[]{:S(2)}, u32[]{:S(2)}) collective-permute-start(bf16[4,128,128]{2,1,0:T(8,128)(2,1)S(1)} %get-tuple-element.34), channel_id=1, source_target_pairs={{0,4},{4,8},{8,12},{12,16},{16,20},{20,24},{24,28},{1,5},{5,9},{9,... | collective-permute-start | bytes 393224 | tf_op jit(solution)/shard_map/ppermute | solution.py:531
  24.2 15.1 %collective-permute-start.2 = (bf16[4,128,128]{2,1,0:T(8,128)(2,1)S(1)}, bf16[4,128,128]{2,1,0:T(8,128)(2,1)S(1)}, u32[]{:S(2)}, u32[]{:S(2)}) collective-permute-start(bf16[4,128,128]{2,1,0:T(8,128)(2,1)S(1)} %get-tuple-element.35), channel_id=1, source_target_pairs={{4,0},{8,4},{12,8},{16,12},{20,16},{24,20},{28,24},{5,1},{9,5},{13... | collective-permute-start | bytes 393224 | tf_op jit(solution)/shard_map/ppermute | solution.py:531
  25.7 13.6 %all-to-all-start = ((f32[8,8,128]{2,1,0:T(8,128)}), f32[8,8,128]{2,1,0:T(8,128)S(1)}, u32[]{:S(2)}, u32[]{:S(2)}) async-start(f32[8,8,128]{2,1,0:T(8,128)} %get-tuple-element.36), calls=%async_computation | async-start | bytes 65536 | tf_op jit(solution)/shard_map/all_to_all | solution.py:535
  39.3 8.9 %copy-start.15 = (bf16[8,32,128]{2,1,0:T(8,128)(2,1)S(1)}, bf16[8,32,128]{2,1,0:T(8,128)(2,1)}, u32[]{:S(2)}) copy-start(bf16[8,32,128]{2,1,0:T(8,128)(2,1)} %param.15) | copy-start | bytes 196612
  43.7 1.1 copy-start.13
  44.8 36.0 %copy-start.4 = (bf16[4,8,128,128]{3,2,1,0:T(8,128)(2,1)}, bf16[4,8,128,128]{3,2,1,0:T(8,128)(2,1)S(1)}, u32[]{:S(2)}) copy-start(bf16[4,8,128,128]{3,2,1,0:T(8,128)(2,1)S(1)} %get-tuple-element.37.block_ref) | copy-start | bytes 3145732
  44.8 20.3 %copy-start.16 = (bf16[128,64]{0,1:T(8,128)(2,1)S(1)}, bf16[128,64]{0,1:T(8,128)(2,1)}, u32[]{:S(2)}) copy-start(bf16[128,64]{0,1:T(8,128)(2,1)} %param.22) | copy-start | bytes 49156
  44.8 10.1 %all-to-all-start.1 = ((f32[8,8,128]{2,1,0:T(8,128)}), f32[8,8,128]{2,1,0:T(8,128)S(1)}, u32[]{:S(2)}, u32[]{:S(2)}) async-start(f32[8,8,128]{2,1,0:T(8,128)} %get-tuple-element.38), calls=%async_computation.1 | async-start | bytes 65536 | tf_op jit(solution)/shard_map/all_to_all | solution.py:535
  58.8 1.3 copy-start.3
  60.1 1.0 copy-start.6
  61.1 12.3 %all-to-all-start.2 = ((f32[4,2,128,128]{3,2,1,0:T(8,128)}), f32[4,2,128,128]{3,2,1,0:T(8,128)S(1)}, u32[]{:S(2)}, u32[]{:S(2)}) async-start(f32[4,2,128,128]{3,2,1,0:T(8,128)} %get-tuple-element.39), calls=%async_computation.2 | async-start | bytes 1048576 | tf_op jit(solution)/shard_map/all_to_all | solution.py:535
  73.4 1.2 copy-start.7
  74.7 23.6 %copy-start.9 = (bf16[3,3,128,128]{3,2,1,0:T(8,128)(2,1)S(1)}, bf16[3,3,128,128]{3,2,1,0:T(8,128)(2,1)}, u32[]{:S(2)}) copy-start(bf16[3,3,128,128]{3,2,1,0:T(8,128)(2,1)} %weight_ref.5) | copy-start | bytes 884740
  80.8 17.4 %collective-permute-start.3 = (bf16[4,2,128,128]{3,2,1,0:T(8,128)(2,1)S(1)}, bf16[4,2,128,128]{3,2,1,0:T(8,128)(2,1)S(1)}, u32[]{:S(2)}, u32[]{:S(2)}) collective-permute-start(bf16[4,2,128,128]{3,2,1,0:T(8,128)(2,1)S(1)} %get-tuple-element.46), channel_id=1, source_target_pairs={{0,4},{4,8},{8,12},{12,16},{16,20},{20,24},{24,28},{1,5},{5,9},{9,... | collective-permute-start | bytes 786440 | tf_op jit(solution)/shard_map/ppermute | solution.py:531
  83.8 14.4 %collective-permute-start.4 = (bf16[4,2,128,128]{3,2,1,0:T(8,128)(2,1)S(1)}, bf16[4,2,128,128]{3,2,1,0:T(8,128)(2,1)S(1)}, u32[]{:S(2)}, u32[]{:S(2)}) collective-permute-start(bf16[4,2,128,128]{3,2,1,0:T(8,128)(2,1)S(1)} %get-tuple-element.47), channel_id=1, source_target_pairs={{4,0},{8,4},{12,8},{16,12},{20,16},{24,20},{28,24},{5,1},{9,5},{13... | collective-permute-start | bytes 786440 | tf_op jit(solution)/shard_map/ppermute | solution.py:531
  98.2 1.2 copy-start.5
  99.5 19.9 %copy-start.1 = (bf16[4,16,128,128]{3,2,1,0:T(8,128)(2,1)S(1)}, bf16[4,16,128,128]{3,2,1,0:T(8,128)(2,1)}, u32[]{:S(2)}) copy-start(bf16[4,16,128,128]{3,2,1,0:T(8,128)(2,1)} %param.12) | copy-start | bytes 6291460
  104.5 1.0 copy-start.11
  115.3 10.1 %all-to-all-start.3 = ((bf16[4,8,32,128]{3,2,1,0:T(8,128)(2,1)}), bf16[4,8,32,128]{3,2,1,0:T(8,128)(2,1)}, u32[]{:S(2)}, u32[]{:S(2)}) async-start(bf16[4,8,32,128]{3,2,1,0:T(8,128)(2,1)} %get-tuple-element.44), calls=%async_computation.3 | async-start | bytes 524288 | tf_op jit(solution)/shard_map/all_to_all | solution.py:535
  119.4 1.6 copy-start.2
  125.5 11.5 %all-to-all-start.6 = ((bf16[32,24,128]{2,1,0:T(8,128)(2,1)}), bf16[32,24,128]{2,1,0:T(8,128)(2,1)S(1)}, u32[]{:S(2)}, u32[]{:S(2)}) async-start(bf16[32,24,128]{2,1,0:T(8,128)(2,1)} %bitcast.15), calls=%async_computation.6 | async-start | bytes 393216 | tf_op jit(solution)/shard_map/all_to_all | solution.py:535
  128.1 1.2 copy-start.12
  129.3 1.3 copy-start.14
  137.0 15.9 %all-to-all-start.8 = ((bf16[32,48,128]{2,1,0:T(8,128)(2,1)}), bf16[32,48,128]{2,1,0:T(8,128)(2,1)S(1)}, u32[]{:S(2)}, u32[]{:S(2)}) async-start(bf16[32,48,128]{2,1,0:T(8,128)(2,1)} %bitcast.20), calls=%async_computation.8 | async-start | bytes 786432 | tf_op jit(solution)/shard_map/all_to_all | solution.py:535
  152.9 11.5 %all-to-all-start.7 = ((bf16[32,24,128]{2,1,0:T(8,128)(2,1)}), bf16[32,24,128]{2,1,0:T(8,128)(2,1)S(1)}, u32[]{:S(2)}, u32[]{:S(2)}) async-start(bf16[32,24,128]{2,1,0:T(8,128)(2,1)} %shard_map.193), calls=%async_computation.7 | async-start | bytes 393216 | tf_op jit(solution)/shard_map/all_to_all | solution.py:535
  164.4 15.9 %all-to-all-start.9 = ((bf16[32,48,128]{2,1,0:T(8,128)(2,1)}), bf16[32,48,128]{2,1,0:T(8,128)(2,1)S(1)}, u32[]{:S(2)}, u32[]{:S(2)}) async-start(bf16[32,48,128]{2,1,0:T(8,128)(2,1)} %shard_map.195), calls=%async_computation.9 | async-start | bytes 786432 | tf_op jit(solution)/shard_map/all_to_all | solution.py:535
where the time goes:
time: 185 us; the launch traced here: 183 us
  waiting for transfers between devices  51.5 us (28%)
  starting transfers between devices  42.4 us (23%)
  blocking collectives  34.2 us (18%)
  Pallas kernels  29.3 us (16%)
  local copies, waits for them, and re-layouts  18 us (10%)
  other arithmetic  6.73 us (4%)
    all_to_all x8, waiting for transfers between devices, exchange(): return lax.all_to_all(pieces, axes, split_axis=0, concat_axis=0, tiled=True)  51.5 us
    all_to_all x8, starting transfers between devices, exchange(): return lax.all_to_all(pieces, axes, split_axis=0, concat_axis=0, tiled=True)  28.6 us
    pallas_call x7, Pallas kernels, call(): pl.pallas_call(kernel, grid=(dates,), in_specs=in_specs, out_specs=out_sp...  27.8 us
    all_to_all x2, blocking collectives, exchange(): return lax.all_to_all(pieces, axes, split_axis=0, concat_axis=0, tiled=True)  22.9 us
    unnamed x46, local copies, waits for them, and re-layouts  14.4 us
    ppermute x2, starting transfers between devices, neighbours(): lax.ppermute(last_rows, 'rows', down)  6.4 us
    all_gather x1, blocking collectives, local(): grads_here = lax.all_gather(out_grad, 'dates')  5.79 us
    all_gather x1, blocking collectives, local(): clear = lax.all_gather(valid.astype(BF16), 'dates')  5.43 us
  transfers between devices with their start and end apart: 13, of which 8 were waited for; matrix products, arithmetic and copies ran while one was open for 4% of the time, Pallas kernels for 4%

commit v1 on v0

--- a/solution.py
+++ b/solution.py
@@ -391,7 +391,7 @@
     store_sums(sums_ref, date, dates, first * gain, second * gain)
 
 
-def block_grad_kernel(dates, hidden_ref, pre_ref, key_ref, vector_ref, out_ref, total):
+def block_grad_kernel(dates, hidden_ref, pre_ref, key_ref, out_ref, total):
     date = pl.program_id(0)
     rows, cols, width = pre_ref.shape[1:]
 
@@ -416,12 +416,15 @@
                 out_ref[base : base + width] = total[
                     row_tap * width : (row_tap + 1) * width, col_tap * width : (col_tap + 1) * width
                 ].astype(BF16)
-        high, low = split(key_ref[...])
-        out_ref[9 * width : 10 * width] = high
-        out_ref[10 * width : 11 * width] = low
-        high, low = split(vector_ref[...])
-        out_ref[11 * width : 11 * width + 16] = jnp.concatenate([high, low], axis=0)
-        out_ref[11 * width + 16 :] = jnp.zeros_like(out_ref[11 * width + 16 :])
+        key_part = key_ref[...]
+        rest = key_part - key_part.astype(BF16).astype(F32)
+        lanes = width // 16
+        place = lax.broadcasted_iota(jnp.int32, key_part.shape, 1) % lanes
+        rest = pltpu.roll(rest, lanes // 2, 1)
+        key_rows = jnp.where(place < lanes // 2, key_part, rest).astype(BF16)
+        out_ref[9 * width : 10 * width] = key_rows
+        if out_ref.shape[0] > 10 * width:
+            out_ref[10 * width :] = jnp.zeros_like(out_ref[10 * width :])
 
 
 def conv_grad_kernel(
@@ -435,6 +438,7 @@
     norm_ref,
     gain_ref,
     vector_ref,
+    other_ref,
     out_ref,
     factors,
     total,
@@ -472,9 +476,13 @@
             start = tap * 3 * half
             out_ref[start : start + half] = left
             out_ref[start + half : start + 3 * half] = pair
-        high, low = split(vector_ref[...])
-        out_ref[9 * half : 9 * half + 16] = jnp.concatenate([high, low], axis=0)
-        out_ref[9 * half + 16 :] = jnp.zeros_like(out_ref[9 * half + 16 :])
+        start = 9 * half
+        for source in (vector_ref, other_ref):
+            high, low = split(source[...])
+            out_ref[start : start + 16] = jnp.concatenate([high, low], axis=0)
+            start += 16
+        if out_ref.shape[0] > start:
+            out_ref[start:] = jnp.zeros_like(out_ref[start:])
 
 
 def total_kernel(in_ref, out_ref):
@@ -510,7 +518,7 @@
         out_specs=out_specs,
         out_shape=[jax.ShapeDtypeStruct(shape, dtype) for _, shape, dtype in outputs],
         scratch_shapes=scratch,
-        compiler_params=pltpu.CompilerParams(vmem_limit_bytes=48 * MIB),
+        compiler_params=pltpu.CompilerParams(vmem_limit_bytes=60 * MIB),
         cost_estimate=pl.CostEstimate(flops=flops, bytes_accessed=2 * moved, transcendentals=0),
     )(*arrays)
 
@@ -535,17 +543,25 @@
     return lax.all_to_all(pieces, axes, split_axis=0, concat_axis=0, tiled=True)
 
 
-def sum_over_all(rows_array):
+def gather(array, axis):
+    return lax.all_gather(array, axis, axis=0, tiled=True)
+
+
+def scatter(rows_array):
     axes = ("rows", "dates")
     devices = lax.axis_size(axes)
     count, width = rows_array.shape
-    pieces = exchange(rows_array.reshape(devices, count // devices, width), axes)
+    return exchange(rows_array.reshape(devices, count // devices, width), axes)
+
+
+def collect(pieces):
     spread = pl.pallas_call(
         total_kernel,
         out_shape=jax.ShapeDtypeStruct(pieces.shape, BF16),
-        compiler_params=pltpu.CompilerParams(vmem_limit_bytes=32 * MIB),
+        compiler_params=pltpu.CompilerParams(vmem_limit_bytes=60 * MIB),
     )(pieces)
-    return exchange(spread, axes).reshape(count, width)
+    count, rows, width = pieces.shape
+    return exchange(spread, ("rows", "dates")).reshape(count * rows, width)
 
 
 def padded_count(count, devices):
@@ -584,8 +600,32 @@
     flops = 2 * dates * rows * cols * width * width
 
     above = lax.ppermute(images[:, -1], "rows", [(i, i + 1) for i in range(row_devs - 1)])
-    grads_here = lax.all_gather(out_grad, "dates")
-    clear = lax.all_gather(valid.astype(BF16), "dates")
+    paired = images.reshape(dates, rows, 2, cols, pair_width)
+    conv_out, top, low, sums = call(
+        functools.partial(down_kernel, dates),
+        dates,
+        [("date", paired), ("date", above), ("all", conv_weight)],
+        [
+            ("date", frame, BF16),
+            ("date", edge_rows, BF16),
+            ("date", edge_rows, BF16),
+            ("all", (1, 2 * dates, width), F32),
+        ],
+        [pltpu.VMEM((3 * pair_width, 2 * width), BF16)],
+        6 * flops,
+    )
+    sums, valid, out_grad, day_index, key_weight, queries = lax.optimization_barrier(
+        (sums, valid, out_grad, day_index, key_weight, queries)
+    )
+    halo_up, halo_down = neighbours(top, low)
+    stats = gather(sums, "rows")
+    grad_rows, valid_rows = out_grad.size // width, valid.size // width
+    packed = jnp.concatenate(
+        [out_grad.reshape(grad_rows, width), valid.astype(BF16).reshape(valid_rows, width)]
+    )
+    packed = gather(packed[None], "dates")
+    grads_here = packed[:, :grad_rows].reshape((date_devs,) + out_grad.shape)
+    clear = packed[:, grad_rows:].reshape((date_devs,) + valid.shape)
     clear = lax.dynamic_slice_in_dim(clear, date_start, dates, 1)
     clear = clear.transpose(1, 2, 0, 3).reshape(dates, rows, cols).astype(F32)
     edges = jnp.stack([row_index > 0, row_index < row_devs - 1]).astype(F32)
@@ -610,22 +650,6 @@
     spread = (head_of[:, None] == head_of[None, :]).astype(BF16)
     spread = jnp.concatenate([spread, spread], axis=0)
 
-    paired = images.reshape(dates, rows, 2, cols, pair_width)
-    conv_out, top, low, sums = call(
-        functools.partial(down_kernel, dates),
-        dates,
-        [("date", paired), ("date", above), ("all", conv_weight)],
-        [
-            ("date", frame, BF16),
-            ("date", edge_rows, BF16),
-            ("date", edge_rows, BF16),
-            ("all", tile, F32),
-        ],
-        [pltpu.VMEM((3 * pair_width, 2 * width), BF16)],
-        6 * flops,
-    )
-    stats = exchange(sums, "rows")
-    halo_up, halo_down = neighbours(top, low)
     block_out, hidden, first_norm, sums = call(
         functools.partial(block_kernel, dates, norm_count),
         dates,
@@ -666,12 +690,12 @@
             ("date", frame, F32),
             ("date", frame, F32),
             ("all", (2 * dates, width), F32),
-            ("all", (date_devs, 2, cols, width), F32),
+            ("all", (1, 2, cols, width), F32),
         ],
         [pltpu.VMEM(frame[1:], F32), pltpu.VMEM(frame[1:], F32)],
         5 * flops,
     )
-    packed = exchange(packed, "dates")
+    packed = gather(packed, "dates")
     block_grad, up, low, attended, key_part, vectors, sums = call(
         functools.partial(attend_kernel, dates, grad_scale),
         dates,
@@ -695,14 +719,13 @@
             ("all", (date_devs, rows, cols // date_devs, width), BF16),
             ("all", (width, width), F32),
             ("all", (8, width), F32),
-            ("all", tile, F32),
+            ("all", (1, 2 * dates, width), F32),
         ],
         [pltpu.VMEM(frame[1:], F32)] * 3,
         5 * flops,
     )
-    tails = exchange(sums, "rows")
     halo_up, halo_down = neighbours(up, low)
-    attended = jnp.sum(exchange(attended, "dates").astype(F32), axis=0).astype(BF16)
+    tails = gather(sums, "rows")
     pre_grad, linear_grad, first_vectors, sums = call(
         functools.partial(hidden_kernel, dates, norm_count),
         dates,
@@ -736,12 +759,13 @@
     (block_rows,) = call(
         functools.partial(block_grad_kernel, dates),
         dates,
-        [("date", hidden), ("date", pre_grad), ("all", key_part), ("all", vectors)],
-        [("all", (padded_count(11 * width + 16, devices), width), BF16)],
+        [("date", hidden), ("date", pre_grad), ("all", key_part)],
+        [("all", (padded_count(10 * width, devices), width), BF16)],
         [pltpu.VMEM((3 * width, 3 * width), F32)],
         9 * flops,
     )
-    block_rows = sum_over_all(block_rows)
+    tails, block_rows = lax.optimization_barrier((tails, block_rows))
+    block_pieces = scatter(block_rows)
     (conv_rows,) = call(
         functools.partial(conv_grad_kernel, dates, norm_count),
         dates,
@@ -754,23 +778,26 @@
             ("all", first_norm),
             ("all", gains),
             ("all", first_vectors),
-        ],
-        [("all", (padded_count(9 * pair_width // 2 + 16, devices), width), BF16)],
+            ("all", vectors),
+        ],
+        [("all", (padded_count(9 * pair_width // 2 + 32, devices), width), BF16)],
         [pltpu.VMEM((2 * dates, width), F32), pltpu.VMEM((3 * pair_width, 2 * width), F32)],
         6 * flops,
     )
-    conv_rows = sum_over_all(conv_rows)
+    conv_pieces = scatter(conv_rows)
+    conv_rows, attended = lax.optimization_barrier((conv_rows, attended))
+    attended = jnp.sum(exchange(attended, "dates").astype(F32), axis=0).astype(BF16)
+    block_pieces, conv_rows = lax.optimization_barrier((block_pieces, conv_rows))
+    block_rows = collect(block_pieces)
+    conv_rows = collect(conv_pieces)
 
     conv_end = 9 * pair_width // 2
     conv_total = conv_rows[:conv_end].astype(F32).reshape(conv_weight.shape)
-    first_sums = conv_rows[conv_end : conv_end + 16].astype(F32)
-    first_sums = first_sums[:8] + first_sums[8:]
+    vectors = conv_rows[conv_end : conv_end + 32].astype(F32).reshape(2, 2, 8, width)
+    first_sums, sums = vectors[:, 0] + vectors[:, 1]
     block_total = block_rows[: 9 * width].astype(F32).reshape(block_weight.shape)
-    key_sums = block_rows[9 * width : 11 * width].astype(F32)
-    key_sums = key_sums[:width] + key_sums[width:]
-    key_total = key_sums.reshape(width, heads, lanes)[:, :, :depth].reshape(width, heads * depth)
-    sums = block_rows[11 * width : 11 * width + 16].astype(F32)
-    sums = sums[:8] + sums[8:]
+    key_sums = block_rows[9 * width : 10 * width].astype(F32).reshape(width, heads, lanes)
+    key_total = (key_sums[..., :depth] + key_sums[..., depth:]).reshape(width, heads * depth)
     query_total = sums[2].reshape(heads, lanes)[:, :depth]
     return (
         attended,

time: 185 us -> 231 us (1.25)
  blocking collectives: 34.2 us -> 106 us
  waiting for transfers between devices: 51.5 us -> 34.6 us
  starting transfers between devices: 42.4 us -> 29.2 us
  Pallas kernels: 29.3 us -> 42.4 us
  local copies, waits for them, and re-layouts: 18 us -> 10.8 us
    all_gather x2 -> x4, blocking collectives: 11.2 us -> 85.5 us  [gather(): return lax.all_gather(array, axis, axis=0, tiled=True)]
    all_to_all x8 -> x5, waiting for transfers between devices: 51.5 us -> 34.6 us  [exchange(): return lax.all_to_all(pieces, axes, split_axis=0, concat_axis=0, tiled=True)]
    all_to_all x8 -> x5, starting transfers between devices: 28.6 us -> 15.1 us  [exchange(): return lax.all_to_all(pieces, axes, split_axis=0, concat_axis=0, tiled=True)]
    pallas_call x7, Pallas kernels: 27.8 us -> 39 us  [call(): pl.pallas_call(kernel, grid=(dates,), in_specs=in_specs, out_specs=out_sp...]
    unnamed x46 -> x34, local copies, waits for them, and re-layouts: 14.4 us -> 4.24 us
  transfers between devices with their start and end apart: 13 -> 10, of which waited for: 8 -> 5; matrix products, arithmetic and copies ran while one was open for 4% -> 4% of each run, Pallas kernels for 4% -> 4%
where the time goes in v1:
time: 231 us; the launch traced here: 230 us
  blocking collectives  106 us (46%)
  Pallas kernels  42.4 us (18%)
  waiting for transfers between devices  34.6 us (15%)
  starting transfers between devices  29.2 us (13%)
  local copies, waits for them, and re-layouts  10.8 us (5%)
  other arithmetic  5.8 us (3%)
    all_gather x4, blocking collectives, gather(): return lax.all_gather(array, axis, axis=0, tiled=True)  85.5 us
    pallas_call x7, Pallas kernels, call(): pl.pallas_call(kernel, grid=(dates,), in_specs=in_specs, out_specs=out_sp...  39 us
    all_to_all x5, waiting for transfers between devices, exchange(): return lax.all_to_all(pieces, axes, split_axis=0, concat_axis=0, tiled=True)  34.6 us
    all_to_all x2, blocking collectives, exchange(): return lax.all_to_all(pieces, axes, split_axis=0, concat_axis=0, tiled=True)  20.7 us
    all_to_all x5, starting transfers between devices, exchange(): return lax.all_to_all(pieces, axes, split_axis=0, concat_axis=0, tiled=True)  15.1 us
    ppermute x2, starting transfers between devices, neighbours(): lax.ppermute(last_rows, 'rows', down)  6.65 us
    ppermute x1, starting transfers between devices, local(): lax.ppermute(images[:, -1], 'rows', [(i, i + 1) for i in range(row_devs -...  4.88 us
  transfers between devices with their start and end apart: 10, of which 5 were waited for; matrix products, arithmetic and copies ran while one was open for 4% of the time, Pallas kernels for 4%

profile of v1, /device:TPU:0, one launch (start us, length us, event | category | flops | bytes accessed | tf_op | source)
XLA Modules:
  0.0 230.1 jit_solution(10980985167624446523)
XLA Ops:
  0.7 1.0 slice_bitcast_fusion
  1.7 4.9 %collective-permute-start = (bf16[4,128,128]{2,1,0:T(8,128)(2,1)S(1)}, bf16[4,128,128]{2,1,0:T(8,128)(2,1)S(1)}, u32[]{:S(2)}, u32[]{:S(2)}) collective-permute-start(bf16[4,128,128]{2,1,0:T(8,128)(2,1)S(1)} %slice_bitcast_fusion), channel_id=1, source_target_pairs={{0,4},{4,8},{8,12},{12,16},{16,20},{20,24},{24,28},{1,5},{5,9},{9,... | collective-permute-start | bytes 393224 | tf_op jit(solution)/shard_map/ppermute | solution.py:602
  7.4 1.4 stack.40.gain_ref
  8.8 0.6 add_convert_fusion.spread_ref
  9.4 0.6 copy-done.3
  10.1 4.5 %shard_map.187 = (bf16[4,8,128,128]{3,2,1,0:T(8,128)(2,1)}, bf16[4,128,128]{2,1,0:T(8,128)(2,1)}, bf16[4,128,128]{2,1,0:T(8,128)(2,1)}, f32[1,8,128]{2,1,0:T(8,128)}) custom-call(bf16[4,8,2,128,128]{4,3,2,1,0:T(8,128)(2,1)} %bitcast.48, bf16[4,128,128]{2,1,0:T(8,128)(2,1)} %copy-done.3, bf16[3,3,64,128]{3,2,1,0:T(8,128)(2,1)} %weight_ref.3), custom_call_target="tpu_custom_call" | custom-call | flops 805306368 | bytes 4751360 | tf_op jit(solution)/shard_map/pallas_call | solution.py:514
  15.3 4.3 %collective-permute-start.1 = (bf16[4,128,128]{2,1,0:T(8,128)(2,1)}, bf16[4,128,128]{2,1,0:T(8,128)(2,1)S(1)}, u32[]{:S(2)}, u32[]{:S(2)}) collective-permute-start(bf16[4,128,128]{2,1,0:T(8,128)(2,1)} %get-tuple-element.43), channel_id=1, source_target_pairs={{0,4},{4,8},{8,12},{12,16},{16,20},{20,24},{24,28},{1,5},{5,9},{9,... | collective-permute-start | bytes 393224 | tf_op jit(solution)/shard_map/ppermute | solution.py:539
  19.5 1.3 collective-permute-start.2
  20.8 5.9 %all-gather = bf16[1152,128]{1,0:T(8,128)(2,1)S(1)} all-gather(bf16[288,128]{1,0:T(8,128)(2,1)S(1)} %pad_maximum_fusion), channel_id=2, replica_groups=mesh['rows'=8,'dates'=4] {'dates'}, dimensions={0}, use_global_device_ids=true | all-gather | bytes 368640 | tf_op jit(solution)/shard_map/all_gather | solution.py:547
  27.1 0.7 slice.79
  28.0 0.7 copy.47.key_ref
  28.8 0.7 reshape.245.valid_ref
  29.5 35.2 %all_gather.12.stats_ref = f32[8,8,128]{2,1,0:T(8,128)} all-gather(f32[1,8,128]{2,1,0:T(8,128)S(1)} %copy-done.8), channel_id=1, replica_groups=mesh['rows'=8,'dates'=4] {'rows'}, dimensions={0}, use_global_device_ids=true | all-gather | bytes 36864 | tf_op jit(solution)/shard_map/all_gather | solution.py:547
  64.7 0.6 pad_maximum_fusion.1.score_ref
  65.4 0.6 copy-done.12
  66.0 5.3 %shard_map.188 = (bf16[4,8,128,128]{3,2,1,0:T(8,128)(2,1)}, bf16[4,10,128,128]{3,2,1,0:T(8,128)(2,1)}, f32[8,128]{1,0:T(8,128)}, f32[8,8,128]{2,1,0:T(8,128)}) custom-call(f32[2]{0:T(128)} %add_convert_fusion.1.edge_ref, bf16[4,8,128,128]{3,2,1,0:T(8,128)(2,1)} %get-tuple-element.42.conv_ref, bf16[4,128,128]{2,1,0:T(8,128)(2,1)} %copy-done.12, ...), custom_call_target="tpu_custom_call" | custom-call | flops 1207959552 | bytes 3285008 | tf_op jit(solution)/shard_map/pallas_call | solution.py:514
  71.3 3.9 %all-to-all-start = ((f32[8,8,128]{2,1,0:T(8,128)}), f32[8,8,128]{2,1,0:T(8,128)S(1)}, u32[]{:S(2)}, u32[]{:S(2)}) async-start(f32[8,8,128]{2,1,0:T(8,128)} %get-tuple-element.48), calls=%async_computation | async-start | bytes 65536 | tf_op jit(solution)/shard_map/all_to_all | solution.py:543
  75.2 0.6 pad_maximum_fusion.3.position_ref
  75.8 6.1 %all-to-all-done.stats_ref = f32[8,8,128]{2,1,0:T(8,128)S(1)} async-done(((f32[8,8,128]{2,1,0:T(8,128)}), f32[8,8,128]{2,1,0:T(8,128)S(1)}, u32[]{:S(2)}, u32[]{:S(2)}) %all-to-all-start) | async-done | bytes 32800 | tf_op jit(solution)/shard_map/all_to_all | solution.py:543
  81.9 0.6 copy-done.7
  82.5 5.7 %shard_map.189 = (bf16[4,8,128,128]{3,2,1,0:T(8,128)(2,1)}, f32[4,8,128,128]{3,2,1,0:T(8,128)}, f32[4,8,128,128]{3,2,1,0:T(8,128)}, f32[8,128]{1,0:T(8,128)}, f32[1,2,128,128]{3,2,1,0:T(8,128)}) custom-call(bf16[4,8,128,128]{3,2,1,0:T(8,128)(2,1)} %get-tuple-element.47.block_ref, f32[8,8,128]{2,1,0:T(8,128)} %copy-done.7, f32[8,128]{1,0:T(8,128)} %stack.40.gain_ref, ...), custom_call_target="tpu_custom_call" | custom-call | flops 671088640 | bytes 2998272 | tf_op jit(solution)/shard_map/pallas_call | solution.py:514
  88.2 8.1 %all_gather.14.packed_ref = f32[4,2,128,128]{3,2,1,0:T(8,128)} all-gather(f32[1,2,128,128]{3,2,1,0:T(8,128)} %get-tuple-element.54), channel_id=1, replica_groups=mesh['rows'=8,'dates'=4] {'dates'}, dimensions={0}, use_global_device_ids=true | all-gather | bytes 655360 | tf_op jit(solution)/shard_map/all_gather | solution.py:547
  96.9 7.3 %shard_map.190 = (bf16[4,8,128,128]{3,2,1,0:T(8,128)(2,1)}, bf16[4,2,128,128]{3,2,1,0:T(8,128)(2,1)}, bf16[4,2,128,128]{3,2,1,0:T(8,128)(2,1)}, bf16[4,8,32,128]...) custom-call(f32[4,2,128,128]{3,2,1,0:T(8,128)} %all_gather.14.packed_ref, ...), custom_call_target="tpu_custom_call" | custom-call | flops 671088640 | bytes 14376960 | tf_op jit(solution)/shard_map/pallas_call | solution.py:514
  104.1 2.4 %collective-permute-start.3 = (bf16[4,2,128,128]{3,2,1,0:T(8,128)(2,1)}, bf16[4,2,128,128]{3,2,1,0:T(8,128)(2,1)S(1)}, u32[]{:S(2)}, u32[]{:S(2)}) collective-permute-start(bf16[4,2,128,128]{3,2,1,0:T(8,128)(2,1)} %get-tuple-element.60), channel_id=1, source_target_pairs={{0,4},{4,8},{8,12},{12,16},{16,20},{20,24},{24,28},{1,5},{5,9},{9,... | collective-permute-start | bytes 786440 | tf_op jit(solution)/shard_map/ppermute | solution.py:539
  106.5 1.3 collective-permute-start.4
  107.8 36.3 %all_gather.15.tails_ref = f32[8,8,128]{2,1,0:T(8,128)} all-gather(f32[1,8,128]{2,1,0:T(8,128)} %get-tuple-element.62), channel_id=1, replica_groups=mesh['rows'=8,'dates'=4] {'rows'}, dimensions={0}, use_global_device_ids=true | all-gather | bytes 36864 | tf_op jit(solution)/shard_map/all_gather | solution.py:547
  144.2 0.7 copy-done.10
  144.9 6.5 %shard_map.191 = (bf16[4,8,128,128]{3,2,1,0:T(8,128)(2,1)}, f32[4,8,128,128]{3,2,1,0:T(8,128)}, f32[8,128]{1,0:T(8,128)}, f32[8,8,128]{2,1,0:T(8,128)}) custom-call(f32[2]{0:T(128)} %add_convert_fusion.1.edge_ref, bf16[4,8,128,128]{3,2,1,0:T(8,128)(2,1)} %get-tuple-element.59.grad_ref, bf16[4,8,128,128]{3,2,1,0:T(8,128)(2,1)} %get-tuple-element.47.block_ref, ...), custom_call_target="tpu_custom_call" | custom-call | flops 1207959552 | bytes 8019984 | tf_op jit(solution)/shard_map/pallas_call | solution.py:514
  151.4 3.4 %all-to-all-start.1 = ((f32[8,8,128]{2,1,0:T(8,128)}), f32[8,8,128]{2,1,0:T(8,128)S(1)}, u32[]{:S(2)}, u32[]{:S(2)}) async-start(f32[8,8,128]{2,1,0:T(8,128)} %get-tuple-element.65), calls=%async_computation.1 | async-start | bytes 65536 | tf_op jit(solution)/shard_map/all_to_all | solution.py:543
  154.8 4.8 %shard_map.192 = bf16[1280,128]{1,0:T(8,128)(2,1)} custom-call(bf16[4,10,128,128]{3,2,1,0:T(8,128)(2,1)} %get-tuple-element.66.hidden_ref, bf16[4,8,128,128]{3,2,1,0:T(8,128)(2,1)} %get-tuple-element.67.pre_ref, f32[128,128]{1,0:T(8,128)} %get-tuple-element.68.key_ref), custom_call_target="tpu_custom_call" | custom-call | flops 1207959552 | bytes 4849664 | tf_op jit(solution)/shard_map/pallas_call | solution.py:514
  159.6 1.8 all-to-all-done.1.tails_ref
  161.4 0.6 copy-done.2
  162.1 4.9 %shard_map.193 = bf16[768,128]{1,0:T(8,128)(2,1)} custom-call(bf16[4,8,2,128,128]{4,3,2,1,0:T(8,128)(2,1)} %bitcast.49, bf16[4,128,128]{2,1,0:T(8,128)(2,1)} %copy-done.3, bf16[4,8,128,128]{3,2,1,0:T(8,128)(2,1)} %get-tuple-element.42.conv_ref, f32[4,8,128,128]{3,2,1,0:T(8,128)} %get-tuple-element.64.grad_ref, f32[8,8,128]{2,1,0:T(8,128)} %copy-done.2, ...), custom_call_target="tpu_custom_call" | custom-call | flops 805306368 | bytes 10846208 | tf_op jit(solution)/shard_map/pallas_call | solution.py:514
  166.9 8.4 %all_to_all.35 = bf16[4,8,32,128]{3,2,1,0:T(8,128)(2,1)S(1)} all-to-all(bf16[4,8,32,128]{3,2,1,0:T(8,128)(2,1)S(1)} %copy-done.1), channel_id=1, replica_groups=mesh['rows'=8,'dates'=4] {'dates'}, dimensions={0} | all-to-all | bytes 524288 | tf_op jit(solution)/shard_map/all_to_all | solution.py:543
  175.4 12.2 %all_to_all.36.in_ref = bf16[32,24,128]{2,1,0:T(8,128)(2,1)} all-to-all(bf16[32,24,128]{2,1,0:T(8,128)(2,1)} %bitcast.57), channel_id=1, replica_groups=mesh['rows'=8,'dates'=4] {'rows','dates'}, dimensions={0} | all-to-all | bytes 393216 | tf_op jit(solution)/shard_map/all_to_all | solution.py:543
  187.6 2.7 %all-to-all-start.5 = ((bf16[32,40,128]{2,1,0:T(8,128)(2,1)}), bf16[32,40,128]{2,1,0:T(8,128)(2,1)S(1)}, u32[]{:S(2)}, u32[]{:S(2)}) async-start(bf16[32,40,128]{2,1,0:T(8,128)(2,1)} %bitcast.24), calls=%async_computation.5 | async-start | bytes 655360 | tf_op jit(solution)/shard_map/all_to_all | solution.py:543
  190.3 1.7 shard_map.194
  192.0 10.3 %all-to-all-done.5.in_ref = bf16[32,40,128]{2,1,0:T(8,128)(2,1)S(1)} async-done(((bf16[32,40,128]{2,1,0:T(8,128)(2,1)}), bf16[32,40,128]{2,1,0:T(8,128)(2,1)S(1)}, u32[]{:S(2)}, u32[]{:S(2)}) %all-to-all-start.5) | async-done | bytes 327712 | tf_op jit(solution)/shard_map/all_to_all | solution.py:543
  202.3 2.6 %all-to-all-start.4 = ((bf16[32,24,128]{2,1,0:T(8,128)(2,1)}), bf16[32,24,128]{2,1,0:T(8,128)(2,1)S(1)}, u32[]{:S(2)}, u32[]{:S(2)}) async-start(bf16[32,24,128]{2,1,0:T(8,128)(2,1)} %shard_map.194), calls=%async_computation.4 | async-start | bytes 393216 | tf_op jit(solution)/shard_map/all_to_all | solution.py:543
  204.9 1.8 shard_map.195
  206.7 7.1 %all-to-all-done.4 = bf16[32,24,128]{2,1,0:T(8,128)(2,1)S(1)} async-done(((bf16[32,24,128]{2,1,0:T(8,128)(2,1)}), bf16[32,24,128]{2,1,0:T(8,128)(2,1)S(1)}, u32[]{:S(2)}, u32[]{:S(2)}) %all-to-all-start.4) | async-done | bytes 196640 | tf_op jit(solution)/shard_map/all_to_all | solution.py:543
  213.8 2.6 %all-to-all-start.6 = ((bf16[32,40,128]{2,1,0:T(8,128)(2,1)}), bf16[32,40,128]{2,1,0:T(8,128)(2,1)S(1)}, u32[]{:S(2)}, u32[]{:S(2)}) async-start(bf16[32,40,128]{2,1,0:T(8,128)(2,1)} %shard_map.195), calls=%async_computation.6 | async-start | bytes 655360 | tf_op jit(solution)/shard_map/all_to_all | solution.py:543
  216.4 0.7 reduce_sum.22
  217.7 0.7 copy.49
  218.4 0.7 convert.11
  219.1 9.3 %all-to-all-done.6 = bf16[32,40,128]{2,1,0:T(8,128)(2,1)S(1)} async-done(((bf16[32,40,128]{2,1,0:T(8,128)(2,1)}), bf16[32,40,128]{2,1,0:T(8,128)(2,1)S(1)}, u32[]{:S(2)}, u32[]{:S(2)}) %all-to-all-start.6) | async-done | bytes 327712 | tf_op jit(solution)/shard_map/all_to_all | solution.py:543
  228.6 0.6 slice_add_fusion
  229.2 0.9 convert.12
  (72 shorter events, 3.6 us)
Async XLA Ops:
  0.6 13.9 %copy-start.9 = (f32[16,4]{0,1:T(4,128)S(1)}, f32[16,4]{0,1:T(4,128)}, u32[]{:S(2)}) copy-start(f32[16,4]{0,1:T(4,128)} %param.23) | copy-start | bytes 772
  0.7 14.4 %copy-start.4 = (bf16[128,64]{0,1:T(8,128)(2,1)S(1)}, bf16[128,64]{0,1:T(8,128)(2,1)}, u32[]{:S(2)}) copy-start(bf16[128,64]{0,1:T(8,128)(2,1)} %param.22) | copy-start | bytes 49156
  0.7 20.2 %copy-start.6 = (bf16[8,32,128]{2,1,0:T(8,128)(2,1)S(1)}, bf16[8,32,128]{2,1,0:T(8,128)(2,1)}, u32[]{:S(2)}) copy-start(bf16[8,32,128]{2,1,0:T(8,128)(2,1)} %param.15) | copy-start | bytes 196612
  0.7 14.0 %copy-start.5 = (s32[16,8,32]{2,1,0:T(8,128)S(1)}, s32[16,8,32]{2,1,0:T(8,128)}, u32[]{:S(2)}) copy-start(s32[16,8,32]{2,1,0:T(8,128)} %param.14) | copy-start | bytes 49156
  0.7 13.9 %copy-start.14 = (s32[16]{0:T(128)S(1)}, s32[16]{0:T(128)}, u32[]{:S(2)}) copy-start(s32[16]{0:T(128)} %param.13) | copy-start | bytes 196
  1.7 7.8 %collective-permute-start = (bf16[4,128,128]{2,1,0:T(8,128)(2,1)S(1)}, bf16[4,128,128]{2,1,0:T(8,128)(2,1)S(1)}, u32[]{:S(2)}, u32[]{:S(2)}) collective-permute-start(bf16[4,128,128]{2,1,0:T(8,128)(2,1)S(1)} %slice_bitcast_fusion), channel_id=1, source_target_pairs={{0,4},{4,8},{8,12},{12,16},{16,20},{20,24},{24,28},{1,5},{5,9},{9,... | collective-permute-start | bytes 393224 | tf_op jit(solution)/shard_map/ppermute | solution.py:602
  9.4 0.6 copy-start.3
  14.6 15.0 %copy-start.8 = (f32[1,8,128]{2,1,0:T(8,128)S(1)}, f32[1,8,128]{2,1,0:T(8,128)}, u32[]{:S(2)}) copy-start(f32[1,8,128]{2,1,0:T(8,128)} %get-tuple-element.46) | copy-start | bytes 12292
  15.3 50.1 %collective-permute-start.1 = (bf16[4,128,128]{2,1,0:T(8,128)(2,1)}, bf16[4,128,128]{2,1,0:T(8,128)(2,1)S(1)}, u32[]{:S(2)}, u32[]{:S(2)}) collective-permute-start(bf16[4,128,128]{2,1,0:T(8,128)(2,1)} %get-tuple-element.43), channel_id=1, source_target_pairs={{0,4},{4,8},{8,12},{12,16},{16,20},{20,24},{24,28},{1,5},{5,9},{9,... | collective-permute-start | bytes 393224 | tf_op jit(solution)/shard_map/ppermute | solution.py:539
  19.5 45.8 %collective-permute-start.2 = (bf16[4,128,128]{2,1,0:T(8,128)(2,1)}, bf16[4,128,128]{2,1,0:T(8,128)(2,1)S(1)}, u32[]{:S(2)}, u32[]{:S(2)}) collective-permute-start(bf16[4,128,128]{2,1,0:T(8,128)(2,1)} %get-tuple-element.44), channel_id=1, source_target_pairs={{4,0},{8,4},{12,8},{16,12},{20,16},{24,20},{28,24},{5,1},{9,5},{13... | collective-permute-start | bytes 393224 | tf_op jit(solution)/shard_map/ppermute | solution.py:539
  65.3 0.7 copy-start.12
  65.3 0.7 copy-start.13
  71.3 10.5 %all-to-all-start = ((f32[8,8,128]{2,1,0:T(8,128)}), f32[8,8,128]{2,1,0:T(8,128)S(1)}, u32[]{:S(2)}, u32[]{:S(2)}) async-start(f32[8,8,128]{2,1,0:T(8,128)} %get-tuple-element.48), calls=%async_computation | async-start | bytes 65536 | tf_op jit(solution)/shard_map/all_to_all | solution.py:543
  81.9 0.6 copy-start.7
  104.1 40.0 %collective-permute-start.3 = (bf16[4,2,128,128]{3,2,1,0:T(8,128)(2,1)}, bf16[4,2,128,128]{3,2,1,0:T(8,128)(2,1)S(1)}, u32[]{:S(2)}, u32[]{:S(2)}) collective-permute-start(bf16[4,2,128,128]{3,2,1,0:T(8,128)(2,1)} %get-tuple-element.60), channel_id=1, source_target_pairs={{0,4},{4,8},{8,12},{12,16},{16,20},{20,24},{24,28},{1,5},{5,9},{9,... | collective-permute-start | bytes 786440 | tf_op jit(solution)/shard_map/ppermute | solution.py:539
  106.5 37.6 %collective-permute-start.4 = (bf16[4,2,128,128]{3,2,1,0:T(8,128)(2,1)}, bf16[4,2,128,128]{3,2,1,0:T(8,128)(2,1)S(1)}, u32[]{:S(2)}, u32[]{:S(2)}) collective-permute-start(bf16[4,2,128,128]{3,2,1,0:T(8,128)(2,1)} %get-tuple-element.61), channel_id=1, source_target_pairs={{4,0},{8,4},{12,8},{16,12},{20,16},{24,20},{28,24},{5,1},{9,5},{13... | collective-permute-start | bytes 786440 | tf_op jit(solution)/shard_map/ppermute | solution.py:539
  144.1 0.7 copy-start.10
  144.2 0.8 copy-start.11
  151.4 10.0 %all-to-all-start.1 = ((f32[8,8,128]{2,1,0:T(8,128)}), f32[8,8,128]{2,1,0:T(8,128)S(1)}, u32[]{:S(2)}, u32[]{:S(2)}) async-start(f32[8,8,128]{2,1,0:T(8,128)} %get-tuple-element.65), calls=%async_computation.1 | async-start | bytes 65536 | tf_op jit(solution)/shard_map/all_to_all | solution.py:543
  161.4 0.6 copy-start.2
  162.1 4.9 %copy-start.1 = (bf16[4,8,32,128]{3,2,1,0:T(8,128)(2,1)S(1)}, bf16[4,8,32,128]{3,2,1,0:T(8,128)(2,1)}, u32[]{:S(2)}) copy-start(bf16[4,8,32,128]{3,2,1,0:T(8,128)(2,1)} %get-tuple-element.73) | copy-start | bytes 786436
  187.6 14.7 %all-to-all-start.5 = ((bf16[32,40,128]{2,1,0:T(8,128)(2,1)}), bf16[32,40,128]{2,1,0:T(8,128)(2,1)S(1)}, u32[]{:S(2)}, u32[]{:S(2)}) async-start(bf16[32,40,128]{2,1,0:T(8,128)(2,1)} %bitcast.24), calls=%async_computation.5 | async-start | bytes 655360 | tf_op jit(solution)/shard_map/all_to_all | solution.py:543
  202.3 2.6 %copy-start = (bf16[32,40,128]{2,1,0:T(8,128)(2,1)}, bf16[32,40,128]{2,1,0:T(8,128)(2,1)S(1)}, u32[]{:S(2)}) copy-start(bf16[32,40,128]{2,1,0:T(8,128)(2,1)S(1)} %all-to-all-done.5.in_ref) | copy-start | bytes 983044
  202.3 11.5 %all-to-all-start.4 = ((bf16[32,24,128]{2,1,0:T(8,128)(2,1)}), bf16[32,24,128]{2,1,0:T(8,128)(2,1)S(1)}, u32[]{:S(2)}, u32[]{:S(2)}) async-start(bf16[32,24,128]{2,1,0:T(8,128)(2,1)} %shard_map.194), calls=%async_computation.4 | async-start | bytes 393216 | tf_op jit(solution)/shard_map/all_to_all | solution.py:543
  213.8 14.6 %all-to-all-start.6 = ((bf16[32,40,128]{2,1,0:T(8,128)(2,1)}), bf16[32,40,128]{2,1,0:T(8,128)(2,1)S(1)}, u32[]{:S(2)}, u32[]{:S(2)}) async-start(bf16[32,40,128]{2,1,0:T(8,128)(2,1)} %shard_map.195), calls=%async_computation.6 | async-start | bytes 655360 | tf_op jit(solution)/shard_map/all_to_all | solution.py:543

commit v2 on v1

--- a/solution.py
+++ b/solution.py
@@ -1,4 +1,5 @@
 import functools
+import math
 
 import jax
 import jax.numpy as jnp
@@ -56,6 +57,17 @@
 
 def column_sum(values):
     return jnp.sum(jnp.sum(values, axis=0), axis=0, keepdims=True)
+
+
+def edges(place_ref, row_devs):
+    place = place_ref[0]
+    return (place > 0).astype(F32), (place < row_devs - 1).astype(F32)
+
+
+def head_spread(width):
+    lane = lax.broadcasted_iota(jnp.int32, (2 * width, width), 1) // (width // 16)
+    head = lax.broadcasted_iota(jnp.int32, (2 * width, width), 0) % width // (width // 16)
+    return (lane == head).astype(F32).astype(BF16)
 
 
 def split(values):
@@ -105,12 +117,14 @@
 def block_kernel(
     dates,
     norm_count,
+    row_devs,
     edge_ref,
     conv_ref,
     up_ref,
     down_ref,
     stats_ref,
     gain_ref,
+    shift_ref,
     weight_ref,
     out_ref,
     hidden_ref,
@@ -130,16 +144,17 @@
                     row_tap * width : (row_tap + 1) * width, col_tap * width : (col_tap + 1) * width
                 ] = weight_ref[row_tap, col_tap]
 
-    scale = norm_ref[pl.ds(dates + date, 1), :] * gain_ref[0:1]
-    shift = gain_ref[1:2] - norm_ref[pl.ds(date, 1), :] * scale
+    scale = norm_ref[pl.ds(dates + date, 1), :] * gain_ref[...]
+    shift = shift_ref[...] - norm_ref[pl.ds(date, 1), :] * scale
 
     def activate(values):
         linear = values.astype(F32) * scale + shift
         return linear * sigmoid(linear)
 
     rows, cols = conv_ref.shape[1:3]
-    hidden_ref[0, 0] = (activate(up_ref[0]) * edge_ref[0]).astype(BF16)
-    hidden_ref[0, rows + 1] = (activate(down_ref[0]) * edge_ref[1]).astype(BF16)
+    above_edge, below_edge = edges(edge_ref, row_devs)
+    hidden_ref[0, 0] = (activate(up_ref[0]) * above_edge).astype(BF16)
+    hidden_ref[0, rows + 1] = (activate(down_ref[0]) * below_edge).astype(BF16)
     hidden_ref[0, 1 : rows + 1] = activate(conv_ref[0]).astype(BF16)
     taps = jnp.concatenate(
         [hidden_ref[0, tap : tap + rows] for tap in range(3)], axis=-1
@@ -155,25 +170,60 @@
     store_sums(sums_ref, date, dates, column_sum(values), column_sum(values * values))
 
 
+def encoding(day, width):
+    lane = lax.broadcasted_iota(jnp.int32, (1, width), 1)
+    frequency = jnp.exp((lane // 2).astype(F32) * (-2.0 * math.log(1000.0) / width))
+    angles = day.astype(F32) * frequency
+    return jnp.where(lane % 2 == 0, jnp.sin(angles), jnp.cos(angles))
+
+
+def fold_keys(key_ref, query_ref, wide_ref, vector_ref, spread_ref, score_ref):
+    heads, depth = query_ref.shape
+    width = key_ref.shape[0]
+    lanes = width // heads
+    spread_ref[...] = head_spread(width)
+    row = lax.broadcasted_iota(jnp.int32, (heads * depth, width), 0)
+    lane = lax.broadcasted_iota(jnp.int32, (heads * depth, width), 1)
+    widen = (row // depth == lane // lanes) & (row % depth == lane % lanes)
+    wide = product(key_ref[...], widen.astype(F32).astype(BF16), 1, 0)
+    wide_ref[...] = wide.astype(BF16)
+    head = lax.broadcasted_iota(jnp.int32, (heads, width), 0)
+    lane = lax.broadcasted_iota(jnp.int32, (heads, width), 1)
+    queries = jnp.where((lane % lanes == depth) | (lane % lanes == depth + 1), 1.0, 0.0)
+    for step in range(depth):
+        scaled = query_ref[:, step : step + 1] * depth**-0.5
+        queries = queries + jnp.where(lane % lanes == step, scaled, 0.0)
+    queries = jnp.sum(jnp.where(lane // lanes == head, queries, 0.0), axis=0, keepdims=True)
+    vector_ref[...] = jnp.broadcast_to(queries, vector_ref.shape)
+    folded = jnp.concatenate(split(wide * queries), axis=-1)
+    folded = product(folded, spread_ref[...], 1, 0)
+    score_ref[...] = jnp.concatenate(split(folded), axis=-1)
+
+
 def score_kernel(
     dates,
     norm_count,
     grad_scale,
+    day_ref,
     block_ref,
     stats_ref,
     gain_ref,
-    position_ref,
+    shift_ref,
     grad_ref,
     valid_ref,
-    score_ref,
-    spread_ref,
+    key_ref,
+    query_ref,
     feat_ref,
     exp_ref,
     attn_ref,
     norm_ref,
     packed_ref,
+    wide_ref,
+    vector_ref,
     total,
     mean,
+    spread_ref,
+    score_ref,
 ):
     date = pl.program_id(0)
     rows, cols, width = block_ref.shape[1:]
@@ -181,13 +231,14 @@
     @pl.when(date == 0)
     def _():
         norm_table(stats_ref, norm_ref, dates, norm_count)
+        fold_keys(key_ref, query_ref, wide_ref, vector_ref, spread_ref, score_ref)
         total[...] = jnp.zeros_like(total)
         mean[...] = jnp.zeros_like(mean)
 
-    scale = norm_ref[pl.ds(dates + date, 1), :] * gain_ref[2:3]
-    shift = gain_ref[3:4] - norm_ref[pl.ds(date, 1), :] * scale
+    scale = norm_ref[pl.ds(dates + date, 1), :] * gain_ref[...]
+    shift = shift_ref[...] - norm_ref[pl.ds(date, 1), :] * scale
     linear = block_ref[0].astype(F32) * scale + shift
-    features = (linear * sigmoid(linear) + position_ref[pl.ds(date, 1), :]).astype(BF16)
+    features = (linear * sigmoid(linear) + encoding(day_ref[date], width)).astype(BF16)
     feat_ref[0] = features
     upstream = grad_ref[...]
     upstream = jnp.stack([upstream[:, row].reshape(cols, width) for row in range(rows)])
@@ -233,10 +284,10 @@
     block_ref,
     norm_ref,
     gain_ref,
+    shift_ref,
     query_ref,
     grad_ref,
     key_ref,
-    spread_ref,
     grad_out_ref,
     up_ref,
     down_ref,
@@ -263,7 +314,7 @@
             picked = jnp.concatenate(
                 [jnp.where(wide_place == row, parts, jnp.zeros_like(parts)) for row in range(rows)], axis=0
             )
-            target[...] = product(picked, spread_ref[...], 1, 0).reshape(rows, cols, width)
+            target[...] = product(picked, head_spread(width), 1, 0).reshape(rows, cols, width)
         attended[...] = jnp.zeros_like(attended)
         key_out_ref[...] = jnp.zeros_like(key_out_ref)
         vector_ref[...] = jnp.zeros_like(vector_ref)
@@ -283,11 +334,11 @@
     feat_grad = rounded * (upstream.astype(F32) * grad_scale) + product(
         key_grads, key_ref[...], 1, 1
     ).reshape(rows, cols, width)
-    gain = gain_ref[2:3]
+    gain = gain_ref[...]
     centred = (block_ref[0].astype(F32) - norm_ref[pl.ds(date, 1), :]) * norm_ref[
         pl.ds(dates + date, 1), :
     ]
-    linear = centred * gain + gain_ref[3:4]
+    linear = centred * gain + shift_ref[...]
     part = sigmoid(linear)
     linear_grad = feat_grad * (part * (1.0 + linear * (1.0 - part)))
     first = column_sum(linear_grad)
@@ -319,6 +370,7 @@
 def hidden_kernel(
     dates,
     norm_count,
+    row_devs,
     edge_ref,
     grad_ref,
     block_ref,
@@ -330,6 +382,7 @@
     conv_ref,
     first_norm_ref,
     gain_ref,
+    shift_ref,
     pre_ref,
     out_ref,
     vector_ref,
@@ -362,10 +415,11 @@
     def finish(grad, values):
         return grad.astype(F32) * inverse + (values.astype(F32) * slope + constant)
 
+    above_edge, below_edge = edges(edge_ref, row_devs)
     stored = finish(grad_ref[0], block_ref[0]).astype(BF16)
     pre_ref[0] = stored
-    padded[0] = (finish(up_ref[0, 0], up_ref[0, 1]) * edge_ref[0]).astype(BF16)
-    padded[rows + 1] = (finish(down_ref[0, 0], down_ref[0, 1]) * edge_ref[1]).astype(BF16)
+    padded[0] = (finish(up_ref[0, 0], up_ref[0, 1]) * above_edge).astype(BF16)
+    padded[rows + 1] = (finish(down_ref[0, 0], down_ref[0, 1]) * below_edge).astype(BF16)
     padded[1 : rows + 1] = stored
     taps = jnp.concatenate([padded[tap : tap + rows] for tap in range(3)], axis=-1).reshape(
         rows * cols, 3 * width
@@ -376,11 +430,11 @@
         + from_right(terms[..., :width])
         + from_left(terms[..., 2 * width :])
     )
-    gain = gain_ref[0:1]
+    gain = gain_ref[...]
     centred = (conv_ref[0].astype(F32) - first_norm_ref[pl.ds(date, 1), :]) * first_norm_ref[
         pl.ds(dates + date, 1), :
     ]
-    linear = centred * gain + gain_ref[1:2]
+    linear = centred * gain + shift_ref[...]
     part = sigmoid(linear)
     linear_grad = hidden_grad * (part * (1.0 + linear * (1.0 - part)))
     out_ref[0] = linear_grad
@@ -439,6 +493,7 @@
     gain_ref,
     vector_ref,
     other_ref,
+    block_rows_ref,
     out_ref,
     factors,
     total,
@@ -456,7 +511,7 @@
         factors[dates : 2 * dates] = -inverse * tails[:dates] - mean * slope
         total[...] = jnp.zeros_like(total)
 
-    scale = norm_ref[pl.ds(dates + date, 1), :] * gain_ref[0:1]
+    scale = norm_ref[pl.ds(dates + date, 1), :] * gain_ref[...]
     slope = factors[pl.ds(date, 1), :]
     constant = factors[pl.ds(dates + date, 1), :]
     stored = (grad_ref[0] * scale + (conv_ref[0].astype(F32) * slope + constant)).astype(BF16)
@@ -469,14 +524,16 @@
 
     @pl.when(date == dates - 1)
     def _():
+        begin = block_rows_ref.shape[0]
+        out_ref[:begin] = block_rows_ref[...]
         for tap in range(3):
             base = tap * width
             pair = total[base : base + width, :width].astype(BF16)
             left = total[base + half : base + width, width:].astype(BF16)
-            start = tap * 3 * half
+            start = begin + tap * 3 * half
             out_ref[start : start + half] = left
             out_ref[start + half : start + 3 * half] = pair
-        start = 9 * half
+        start = begin + 9 * half
         for source in (vector_ref, other_ref):
             high, low = split(source[...])
             out_ref[start : start + 16] = jnp.concatenate([high, low], axis=0)
@@ -491,6 +548,29 @@
         out_ref[copy] = total
 
 
+def final_kernel(depth, rows_ref, conv_ref, block_ref, key_ref, query_ref, *vector_refs):
+    conv_end, block_end, width = conv_ref.shape[0], block_ref.shape[0], block_ref.shape[1]
+    block_ref[...] = rows_ref[:block_end].astype(F32)
+    heads = key_ref.shape[1] // depth
+    lanes = width // heads
+    row = lax.broadcasted_iota(jnp.int32, (width, heads * depth), 0)
+    lane = lax.broadcasted_iota(jnp.int32, (width, heads * depth), 1)
+    narrow = (row // lanes == lane // depth) & (row % depth == lane % depth)
+    narrow = narrow.astype(F32).astype(BF16)
+    key_ref[...] = product(rows_ref[block_end : block_end + width], narrow, 1, 0)
+    start = block_end + width
+    conv_ref[...] = rows_ref[start : start + conv_end].astype(F32)
+    start += conv_end
+    for index in range(2):
+        both = rows_ref[start : start + 16].astype(F32)
+        both = both[:8] + both[8:]
+        vector_refs[2 * index][...] = both[0:1]
+        vector_refs[2 * index + 1][...] = both[1:2]
+        start += 16
+    query = product(rows_ref[start - 16 : start], narrow, 1, 0)
+    query_ref[...] = query[2:3] + query[10:11]
+
+
 def per_date(shape):
     zeros = (0,) * (len(shape) - 1)
     return pl.BlockSpec((1,) + tuple(shape[1:]), lambda date: (date,) + zeros)
@@ -501,7 +581,7 @@
     return pl.BlockSpec(tuple(shape), lambda date: zeros)
 
 
-def call(kernel, dates, inputs, outputs, scratch, flops):
+def call(kernel, dates, inputs, outputs, scratch, flops, memory=24):
     in_specs, arrays = [], []
     for kind, array in inputs:
         arrays.append(array)
@@ -518,18 +598,9 @@
         out_specs=out_specs,
         out_shape=[jax.ShapeDtypeStruct(shape, dtype) for _, shape, dtype in outputs],
         scratch_shapes=scratch,
-        compiler_params=pltpu.CompilerParams(vmem_limit_bytes=60 * MIB),
+        compiler_params=pltpu.CompilerParams(vmem_limit_bytes=memory * MIB),
         cost_estimate=pl.CostEstimate(flops=flops, bytes_accessed=2 * moved, transcendentals=0),
     )(*arrays)
-
-
-def encoding(day_index, feat_width):
-    half_range = jnp.arange(feat_width // 2, dtype=F32)
-    frequency = jnp.exp(half_range * (-2.0 * jnp.log(1000.0) / feat_width))
-    angles = day_index.astype(F32)[:, None] * frequency[None, :]
-    return jnp.stack([jnp.sin(angles), jnp.cos(angles)], axis=-1).reshape(
-        day_index.shape[0], feat_width
-    )
 
 
 def neighbours(first_rows, last_rows):
@@ -558,7 +629,7 @@
     spread = pl.pallas_call(
         total_kernel,
         out_shape=jax.ShapeDtypeStruct(pieces.shape, BF16),
-        compiler_params=pltpu.CompilerParams(vmem_limit_bytes=60 * MIB),
+        compiler_params=pltpu.CompilerParams(vmem_limit_bytes=16 * MIB),
     )(pieces)
     count, rows, width = pieces.shape
     return exchange(spread, ("rows", "dates")).reshape(count * rows, width)
@@ -567,6 +638,30 @@
 def padded_count(count, devices):
     step = 8 * devices
     return -(-count // step) * step
+
+
+def grouped(array, groups):
+    return lax.all_gather(array, "rows", axis_index_groups=groups, axis=0, tiled=True)
+
+
+def row_totals_by_squares(sums):
+    devices = lax.axis_size("rows")
+    near = [list(range(start, start + 4)) for start in range(0, devices, 4)]
+    far = [list(range(start, devices, 4)) for start in range(4)]
+    sums = jnp.sum(grouped(sums, near), axis=0, keepdims=True)
+    return grouped(sums, far)
+
+
+def row_totals_by_pairs(sums):
+    devices = lax.axis_size("rows")
+    step = 1
+    while step < devices:
+        pairs = [[i, i + step] for i in range(devices) if i // step % 2 == 0]
+        sums = grouped(sums, pairs)
+        step *= 2
+        if step < devices:
+            sums = jnp.sum(sums, axis=0, keepdims=True)
+    return sums
 
 
 def local(
@@ -589,16 +684,16 @@
     devices = row_devs * date_devs
     rows = rows_here // 2
     heads, depth = queries.shape
-    lanes = width // heads
     norm_count = float(rows * row_devs * cols * (width // GROUPS))
     grad_scale = float(rows * row_devs * cols) ** (-0.5)
-    row_index = lax.axis_index("rows")
     date_start = lax.axis_index("dates") * dates
     frame = (dates, rows, cols, width)
     edge_rows = (dates, cols, width)
-    tile = (row_devs, 2 * dates, width)
     flops = 2 * dates * rows * cols * width * width
 
+    rows_of = lambda vector: vector.reshape(1, width)
+    first_gain, first_shift = rows_of(first_gain), rows_of(first_shift)
+    gn_gain, gn_shift = rows_of(gn_gain), rows_of(gn_shift)
     above = lax.ppermute(images[:, -1], "rows", [(i, i + 1) for i in range(row_devs - 1)])
     paired = images.reshape(dates, rows, 2, cols, pair_width)
     conv_out, top, low, sums = call(
@@ -614,11 +709,9 @@
         [pltpu.VMEM((3 * pair_width, 2 * width), BF16)],
         6 * flops,
     )
-    sums, valid, out_grad, day_index, key_weight, queries = lax.optimization_barrier(
-        (sums, valid, out_grad, day_index, key_weight, queries)
-    )
+    sums, valid, out_grad = lax.optimization_barrier((sums, valid, out_grad))
     halo_up, halo_down = neighbours(top, low)
-    stats = gather(sums, "rows")
+    stats = row_totals_by_squares(sums)
     grad_rows, valid_rows = out_grad.size // width, valid.size // width
     packed = jnp.concatenate(
         [out_grad.reshape(grad_rows, width), valid.astype(BF16).reshape(valid_rows, width)]
@@ -628,62 +721,45 @@
     clear = packed[:, grad_rows:].reshape((date_devs,) + valid.shape)
     clear = lax.dynamic_slice_in_dim(clear, date_start, dates, 1)
     clear = clear.transpose(1, 2, 0, 3).reshape(dates, rows, cols).astype(F32)
-    edges = jnp.stack([row_index > 0, row_index < row_devs - 1]).astype(F32)
-    gains = jnp.stack([first_gain, first_shift, gn_gain, gn_shift] * 2)
-    position = lax.dynamic_slice_in_dim(encoding(day_index, width), date_start, dates, 0)
-    position = jnp.concatenate([position, position], axis=0)
-    half_queries = queries * (depth**-0.5)
-    folded = jnp.sum(
-        key_weight.astype(F32).reshape(width, heads, depth) * half_queries[None], axis=-1
-    )
-    folded = jnp.repeat(folded, lanes, axis=1)
-    score_weight = jnp.concatenate(split(folded), axis=1)
-    key_wide = jnp.pad(
-        key_weight.reshape(width, heads, depth), ((0, 0), (0, 0), (0, lanes - depth))
-    ).reshape(width, width)
-    query_wide = jnp.concatenate(
-        [half_queries, jnp.ones((heads, 2), F32), jnp.zeros((heads, lanes - depth - 2), F32)],
-        axis=1,
-    ).reshape(1, width)
-    query_wide = jnp.broadcast_to(query_wide, (8, width))
-    head_of = jnp.arange(width) // lanes
-    spread = (head_of[:, None] == head_of[None, :]).astype(BF16)
-    spread = jnp.concatenate([spread, spread], axis=0)
+    days = lax.dynamic_slice_in_dim(day_index, date_start, dates, 0)
+    place = lax.axis_index("rows").reshape(1)
 
     block_out, hidden, first_norm, sums = call(
-        functools.partial(block_kernel, dates, norm_count),
+        functools.partial(block_kernel, dates, norm_count, row_devs),
         dates,
         [
-            ("scalar", edges),
+            ("scalar", place),
             ("date", conv_out),
             ("date", halo_up),
             ("date", halo_down),
             ("all", stats),
-            ("all", gains),
+            ("all", first_gain),
+            ("all", first_shift),
             ("all", block_weight),
         ],
         [
             ("date", frame, BF16),
             ("date", (dates, rows + 2, cols, width), BF16),
             ("all", (2 * dates, width), F32),
-            ("all", tile, F32),
+            ("all", (row_devs, 2 * dates, width), F32),
         ],
         [pltpu.VMEM((3 * width, 3 * width), BF16)],
         9 * flops,
     )
     stats = exchange(sums, "rows")
-    features, exponent, attn, norm, packed = call(
+    features, exponent, attn, norm, packed, key_wide, query_wide = call(
         functools.partial(score_kernel, dates, norm_count, grad_scale),
         dates,
         [
+            ("scalar", days),
             ("date", block_out),
             ("all", stats),
-            ("all", gains),
-            ("all", position),
+            ("all", gn_gain),
+            ("all", gn_shift),
             ("all", grads_here),
             ("date", clear),
-            ("all", score_weight),
-            ("all", spread),
+            ("all", key_weight),
+            ("all", queries),
         ],
         [
             ("date", frame, BF16),
@@ -691,8 +767,15 @@
             ("date", frame, F32),
             ("all", (2 * dates, width), F32),
             ("all", (1, 2, cols, width), F32),
-        ],
-        [pltpu.VMEM(frame[1:], F32), pltpu.VMEM(frame[1:], F32)],
+            ("all", (width, width), BF16),
+            ("all", (8, width), F32),
+        ],
+        [
+            pltpu.VMEM(frame[1:], F32),
+            pltpu.VMEM(frame[1:], F32),
+            pltpu.VMEM((2 * width, width), BF16),
+            pltpu.VMEM((width, 2 * width), BF16),
+        ],
         5 * flops,
     )
     packed = gather(packed, "dates")
@@ -706,11 +789,11 @@
             ("date", attn),
             ("date", block_out),
             ("all", norm),
-            ("all", gains),
+            ("all", gn_gain),
+            ("all", gn_shift),
             ("all", query_wide),
             ("all", grads_here),
             ("all", key_wide),
-            ("all", spread),
         ],
         [
             ("date", frame, BF16),
@@ -725,12 +808,14 @@
         5 * flops,
     )
     halo_up, halo_down = neighbours(up, low)
-    tails = gather(sums, "rows")
+    tails = row_totals_by_pairs(sums)
+    attended, _ = lax.optimization_barrier((attended, tails))
+    attended = jnp.sum(exchange(attended, "dates").astype(F32), axis=0).astype(BF16)
     pre_grad, linear_grad, first_vectors, sums = call(
-        functools.partial(hidden_kernel, dates, norm_count),
+        functools.partial(hidden_kernel, dates, norm_count, row_devs),
         dates,
         [
-            ("scalar", edges),
+            ("scalar", place),
             ("date", block_grad),
             ("date", block_out),
             ("date", halo_up),
@@ -740,13 +825,14 @@
             ("all", block_weight),
             ("date", conv_out),
             ("all", first_norm),
-            ("all", gains),
+            ("all", first_gain),
+            ("all", first_shift),
         ],
         [
             ("date", frame, BF16),
             ("date", frame, F32),
             ("all", (8, width), F32),
-            ("all", tile, F32),
+            ("all", (row_devs, 2 * dates, width), F32),
         ],
         [
             pltpu.VMEM((3 * width, 3 * width), BF16),
@@ -755,18 +841,19 @@
         ],
         9 * flops,
     )
+    sums, attended = lax.optimization_barrier((sums, attended))
     tails = exchange(sums, "rows")
     (block_rows,) = call(
         functools.partial(block_grad_kernel, dates),
         dates,
         [("date", hidden), ("date", pre_grad), ("all", key_part)],
-        [("all", (padded_count(10 * width, devices), width), BF16)],
+        [("all", (10 * width, width), BF16)],
         [pltpu.VMEM((3 * width, 3 * width), F32)],
         9 * flops,
     )
     tails, block_rows = lax.optimization_barrier((tails, block_rows))
-    block_pieces = scatter(block_rows)
-    (conv_rows,) = call(
+    conv_count = 9 * pair_width // 2 + 32
+    (rows_all,) = call(
         functools.partial(conv_grad_kernel, dates, norm_count),
         dates,
         [
@@ -776,39 +863,38 @@
             ("date", linear_grad),
             ("all", tails),
             ("all", first_norm),
-            ("all", gains),
+            ("all", first_gain),
             ("all", first_vectors),
             ("all", vectors),
-        ],
-        [("all", (padded_count(9 * pair_width // 2 + 32, devices), width), BF16)],
+            ("all", block_rows),
+        ],
+        [("all", (padded_count(10 * width + conv_count, devices), width), BF16)],
         [pltpu.VMEM((2 * dates, width), F32), pltpu.VMEM((3 * pair_width, 2 * width), F32)],
         6 * flops,
     )
-    conv_pieces = scatter(conv_rows)
-    conv_rows, attended = lax.optimization_barrier((conv_rows, attended))
-    attended = jnp.sum(exchange(attended, "dates").astype(F32), axis=0).astype(BF16)
-    block_pieces, conv_rows = lax.optimization_barrier((block_pieces, conv_rows))
-    block_rows = collect(block_pieces)
-    conv_rows = collect(conv_pieces)
-
-    conv_end = 9 * pair_width // 2
-    conv_total = conv_rows[:conv_end].astype(F32).reshape(conv_weight.shape)
-    vectors = conv_rows[conv_end : conv_end + 32].astype(F32).reshape(2, 2, 8, width)
-    first_sums, sums = vectors[:, 0] + vectors[:, 1]
-    block_total = block_rows[: 9 * width].astype(F32).reshape(block_weight.shape)
-    key_sums = block_rows[9 * width : 10 * width].astype(F32).reshape(width, heads, lanes)
-    key_total = (key_sums[..., :depth] + key_sums[..., depth:]).reshape(width, heads * depth)
-    query_total = sums[2].reshape(heads, lanes)[:, :depth]
+    rows_all = collect(scatter(rows_all))
+    shapes = [
+        (9 * pair_width // 2, width),
+        (9 * width, width),
+        key_weight.shape,
+        (1, heads * depth),
+    ] + [(1, width)] * 4
+    conv_total, block_total, key_total, query_total, *totals = pl.pallas_call(
+        functools.partial(final_kernel, depth),
+        out_shape=[jax.ShapeDtypeStruct(shape, F32) for shape in shapes],
+        compiler_params=pltpu.CompilerParams(vmem_limit_bytes=16 * MIB),
+    )(rows_all)
+    totals = [total.reshape(width) for total in totals]
     return (
         attended,
-        conv_total,
-        first_sums[0],
-        first_sums[1],
-        block_total,
-        sums[0],
-        sums[1],
+        conv_total.reshape(conv_weight.shape),
+        totals[0],
+        totals[1],
+        block_total.reshape(block_weight.shape),
+        totals[2],
+        totals[3],
         key_total,
-        query_total,
+        query_total.reshape(heads, depth),
     )
 
 

time: 231 us -> 180 us (0.78)
  waiting for transfers between devices: 34.6 us -> 7.66 us
  Pallas kernels: 42.4 us -> 24.7 us
  local copies, waits for them, and re-layouts: 10.8 us -> 19.7 us
  starting transfers between devices: 29.2 us -> 23.2 us
  blocking collectives: 106 us -> 101 us
  other arithmetic: 5.8 us -> 2.33 us
    all_gather x4 -> x2, blocking collectives: 85.5 us -> 13 us  [gather(): return lax.all_gather(array, axis, axis=0, tiled=True)]
    all_gather x0 -> x5, blocking collectives: none -> 40.5 us  [grouped(): lax.all_gather(array, 'rows', axis_index_groups=groups, axis=0, tiled=True)]
    all_to_all x5 -> x2, waiting for transfers between devices: 34.6 us -> 7.25 us  [exchange(): return lax.all_to_all(pieces, axes, split_axis=0, concat_axis=0, tiled=True)]
    all_to_all x2 -> x3, blocking collectives: 20.7 us -> 47.3 us  [exchange(): return lax.all_to_all(pieces, axes, split_axis=0, concat_axis=0, tiled=True)]
    pallas_call x7, Pallas kernels: 39 us -> 23.6 us  [call(): pl.pallas_call(kernel, grid=(dates,), in_specs=in_specs, out_specs=out_sp...]
    unnamed x34 -> x49, local copies, waits for them, and re-layouts: 4.24 us -> 17.1 us
    all_to_all x5 -> x2, starting transfers between devices: 15.1 us -> 8.26 us  [exchange(): return lax.all_to_all(pieces, axes, split_axis=0, concat_axis=0, tiled=True)]
    pallas_call x2 -> x1, Pallas kernels: 3.41 us -> 0.1 us  [collect(): pl.pallas_call(total_kernel, out_shape=jax.ShapeDtypeStruct(pieces.shape,...]
  transfers between devices with their start and end apart: 10 -> 7, of which waited for: 5 -> 3; matrix products, arithmetic and copies ran while one was open for 4% -> 2% of each run, Pallas kernels for 4% -> 1%
where the time goes in v2:
time: 180 us; the launch traced here: 179 us
  blocking collectives  101 us (56%)
  Pallas kernels  24.7 us (14%)
  starting transfers between devices  23.2 us (13%)
  local copies, waits for them, and re-layouts  19.7 us (11%)
  waiting for transfers between devices  7.66 us (4%)
  other arithmetic  2.33 us (1%)
    all_to_all x3, blocking collectives, exchange(): return lax.all_to_all(pieces, axes, split_axis=0, concat_axis=0, tiled=True)  47.3 us
    all_gather x5, blocking collectives, grouped(): lax.all_gather(array, 'rows', axis_index_groups=groups, axis=0, tiled=True)  40.5 us
    pallas_call x7, Pallas kernels, call(): pl.pallas_call(kernel, grid=(dates,), in_specs=in_specs, out_specs=out_sp...  23.6 us
    unnamed x49, local copies, waits for them, and re-layouts  17.1 us
    all_gather x2, blocking collectives, gather(): return lax.all_gather(array, axis, axis=0, tiled=True)  13 us
    all_to_all x2, starting transfers between devices, exchange(): return lax.all_to_all(pieces, axes, split_axis=0, concat_axis=0, tiled=True)  8.26 us
    ppermute x2, starting transfers between devices, neighbours(): lax.ppermute(last_rows, 'rows', down)  7.47 us
    all_to_all x2, waiting for transfers between devices, exchange(): return lax.all_to_all(pieces, axes, split_axis=0, concat_axis=0, tiled=True)  7.25 us
  transfers between devices with their start and end apart: 7, of which 3 were waited for; matrix products, arithmetic and copies ran while one was open for 2% of the time, Pallas kernels for 1%

profile of v2, /device:TPU:0, one launch (start us, length us, event | category | flops | bytes accessed | tf_op | source)
XLA Modules:
  0.0 179.1 jit_solution(5352878046990127262)
XLA Ops:
  0.7 1.0 slice_bitcast_fusion
  1.6 4.9 %collective-permute-start = (bf16[4,128,128]{2,1,0:T(8,128)(2,1)S(1)}, bf16[4,128,128]{2,1,0:T(8,128)(2,1)S(1)}, u32[]{:S(2)}, u32[]{:S(2)}) collective-permute-start(bf16[4,128,128]{2,1,0:T(8,128)(2,1)S(1)} %slice_bitcast_fusion), channel_id=1, source_target_pairs={{0,4},{4,8},{8,12},{12,16},{16,20},{20,24},{24,28},{1,5},{5,9},{9,... | collective-permute-start | bytes 393224 | tf_op jit(solution)/shard_map/ppermute | solution.py:697
  6.5 0.8 copy.41.key_ref
  7.3 0.8 copy.42.query_ref
  8.1 0.7 dynamic_slice.6.day_ref
  9.2 1.6 copy-done
  10.9 0.9 copy-done.12
  11.8 1.9 %shard_map.187 = (bf16[4,8,128,128]{3,2,1,0:T(8,128)(2,1)S(1)}, bf16[4,128,128]{2,1,0:T(8,128)(2,1)S(1)}, bf16[4,128,128]{2,1,0:T(8,128)(2,1)S(1)}, f32[1,8,128]{2,1,0:T(8,128)S(1)}) custom-call(bf16[4,8,2,128,128]{4,3,2,1,0:T(8,128)(2,1)S(1)} %bitcast.28, bf16[4,128,128]{2,1,0:T(8,128)(2,1)S(1)} %collective-permute-done.above_ref, ...), custom_call_target="tpu_custom_call" | custom-call | flops 805306368 | bytes 4751360 | tf_op jit(solution)/shard_map/pallas_call | solution.py:594
  13.7 4.4 %collective-permute-start.1 = (bf16[4,128,128]{2,1,0:T(8,128)(2,1)S(1)}, bf16[4,128,128]{2,1,0:T(8,128)(2,1)S(1)}, u32[]{:S(2)}, u32[]{:S(2)}) collective-permute-start(bf16[4,128,128]{2,1,0:T(8,128)(2,1)S(1)} %get-tuple-element.52), channel_id=1, source_target_pairs={{0,4},{4,8},{8,12},{12,16},{16,20},{20,24},{24,28},{1,5},{5,9},{9,... | collective-permute-start | bytes 393224 | tf_op jit(solution)/shard_map/ppermute | solution.py:610
  18.1 1.3 collective-permute-start.2
  19.5 5.9 %all-gather.1 = bf16[1152,128]{1,0:T(8,128)(2,1)S(1)} all-gather(bf16[288,128]{1,0:T(8,128)(2,1)S(1)} %pad_maximum_fusion), channel_id=3, replica_groups=mesh['rows'=8,'dates'=4] {'dates'}, dimensions={0}, use_global_device_ids=true | all-gather | bytes 368640 | tf_op jit(solution)/shard_map/all_gather | solution.py:618
  25.6 14.4 %all_gather.21 = f32[4,8,128]{2,1,0:T(8,128)S(1)} all-gather(f32[1,8,128]{2,1,0:T(8,128)S(1)} %get-tuple-element.55), channel_id=1, replica_groups={{0,4,8,12},{16,20,24,28},{1,5,9,13},{17,21,25,29},{2,6,10,14},{18,22,26..., dimensions={0}, use_global_device_ids=true | all-gather | bytes 20480 | tf_op jit(solution)/shard_map/all_gather | solution.py:644
  40.0 5.2 %all-gather = f32[16,128]{1,0:T(8,128)S(1)} all-gather(f32[8,128]{1,0:T(8,128)S(1)} %reduce_sum.39), channel_id=2, replica_groups={{0,16},{4,20},{8,24},{12,28},{1,17},{5,21},{9,25},{13,29},{2,18},{6,22}..., dimensions={0}, use_global_device_ids=true | all-gather | bytes 12288 | tf_op jit(solution)/shard_map/all_gather | solution.py:644
  45.3 3.7 %shard_map.188 = (bf16[4,8,128,128]{3,2,1,0:T(8,128)(2,1)S(1)}, bf16[4,10,128,128]{3,2,1,0:T(8,128)(2,1)S(1)}, f32[8,128]{1,0:T(8,128)S(1)}, f32[8,8,128]{2,1,0:T(8,128)}) custom-call(s32[1]{0:T(128)} %bitcast.edge_ref, bf16[4,8,128,128]{3,2,1,0:T(8,128)(2,1)S(1)} %get-tuple-element.51.conv_ref, bf16[4,128,128]{2,1,0:T(8,128)(2,1)S(1)} %collective-permute-done.1.up_ref, ...), custom_call_target="tpu_custom_call" | custom-call | flops 1207959552 | bytes 3229704 | tf_op jit(solution)/shard_map/pallas_call | solution.py:594
  49.0 1.1 copy-done.18
  50.1 4.8 %all-to-all-start = ((f32[8,8,128]{2,1,0:T(8,128)}), f32[8,8,128]{2,1,0:T(8,128)S(1)}, u32[]{:S(2)}, u32[]{:S(2)}) async-start(f32[8,8,128]{2,1,0:T(8,128)} %get-tuple-element.57), calls=%async_computation | async-start | bytes 65536 | tf_op jit(solution)/shard_map/all_to_all | solution.py:614
  55.0 6.5 %all-to-all-done.stats_ref = f32[8,8,128]{2,1,0:T(8,128)S(1)} async-done(((f32[8,8,128]{2,1,0:T(8,128)}), f32[8,8,128]{2,1,0:T(8,128)S(1)}, u32[]{:S(2)}, u32[]{:S(2)}) %all-to-all-start) | async-done | bytes 32800 | tf_op jit(solution)/shard_map/all_to_all | solution.py:614
  61.5 3.8 %shard_map.189 = (bf16[4,8,128,128]{3,2,1,0:T(8,128)(2,1)S(1)}, f32[4,8,128,128]{3,2,1,0:T(8,128)S(1)}, f32[4,8,128,128]{3,2,1,0:T(8,128)S(1)}, f32[8,128]{1,0:T...) custom-call(s32[4]{0:T(128)S(1)} %dynamic_slice.6.day_ref, ...), custom_call_target="tpu_custom_call" | custom-call | flops 671088640 | bytes 2755104 | tf_op jit(solution)/shard_map/pallas_call | solution.py:594
  65.3 7.1 %all_gather.24.packed_ref = f32[4,2,128,128]{3,2,1,0:T(8,128)S(1)} all-gather(f32[1,2,128,128]{3,2,1,0:T(8,128)S(1)} %get-tuple-element.60), channel_id=1, replica_groups=mesh['rows'=8,'dates'=4] {'dates'}, dimensions={0}, use_global_device_ids=true | all-gather | bytes 655360 | tf_op jit(solution)/shard_map/all_gather | solution.py:618
  72.5 4.5 %shard_map.190 = (bf16[4,8,128,128]{3,2,1,0:T(8,128)(2,1)S(1)}, bf16[4,2,128,128]{3,2,1,0:T(8,128)(2,1)S(1)}, bf16[4,2,128,128]{3,2,1,0:T(8,128)(2,1)}, bf16[4,8...) custom-call(f32[4,2,128,128]{3,2,1,0:T(8,128)S(1)} %all_gather.24.packed_, ...), custom_call_target="tpu_custom_call" | custom-call | flops 671088640 | bytes 14239744 | tf_op jit(solution)/shard_map/pallas_call | solution.py:594
  76.9 1.0 copy-done.9
  77.9 3.1 %collective-permute-start.3 = (bf16[4,2,128,128]{3,2,1,0:T(8,128)(2,1)}, bf16[4,2,128,128]{3,2,1,0:T(8,128)(2,1)}, u32[]{:S(2)}, u32[]{:S(2)}) collective-permute-start(bf16[4,2,128,128]{3,2,1,0:T(8,128)(2,1)} %get-tuple-element.68), channel_id=1, source_target_pairs={{0,4},{4,8},{8,12},{12,16},{16,20},{20,24},{24,28},{1,5},{5,9},{9,... | collective-permute-start | bytes 786440 | tf_op jit(solution)/shard_map/ppermute | solution.py:610
  81.0 1.3 collective-permute-start.4
  82.3 10.0 %all_gather.25 = f32[2,8,128]{2,1,0:T(8,128)S(1)} all-gather(f32[1,8,128]{2,1,0:T(8,128)S(1)} %get-tuple-element.70), channel_id=1, replica_groups={{0,4},{8,12},{16,20},{24,28},{1,5},{9,13},{17,21},{25,29},{2,6},{10,14}..., dimensions={0}, use_global_device_ids=true | all-gather | bytes 12288 | tf_op jit(solution)/shard_map/all_gather | solution.py:644
  92.4 5.6 %all-gather.2 = f32[16,128]{1,0:T(8,128)S(1)} all-gather(f32[8,128]{1,0:T(8,128)S(1)} %reduce_sum.40), channel_id=4, replica_groups={{0,8},{4,12},{16,24},{20,28},{1,9},{5,13},{17,25},{21,29},{2,10},{6,14}..., dimensions={0}, use_global_device_ids=true | all-gather | bytes 12288 | tf_op jit(solution)/shard_map/all_gather | solution.py:644
  97.9 5.2 %all-gather.3 = f32[16,128]{1,0:T(8,128)S(1)} all-gather(f32[8,128]{1,0:T(8,128)S(1)} %bitcast_reduce_fusion), channel_id=5, replica_groups={{0,16},{4,20},{8,24},{12,28},{1,17},{5,21},{9,25},{13,29},{2,18},{6,22}..., dimensions={0}, use_global_device_ids=true | all-gather | bytes 12288 | tf_op jit(solution)/shard_map/all_gather | solution.py:644
  103.2 9.1 %all_to_all.25 = bf16[4,8,32,128]{3,2,1,0:T(8,128)(2,1)} all-to-all(bf16[4,8,32,128]{3,2,1,0:T(8,128)(2,1)S(1)} %get-tuple-element.74), channel_id=1, replica_groups=mesh['rows'=8,'dates'=4] {'dates'}, dimensions={0} | all-to-all | bytes 524288 | tf_op jit(solution)/shard_map/all_to_all | solution.py:614
  112.3 1.6 reduce_sum.42
  113.9 1.2 copy-done.10
  115.1 5.2 %shard_map.191 = (bf16[4,8,128,128]{3,2,1,0:T(8,128)(2,1)S(1)}, f32[4,8,128,128]{3,2,1,0:T(8,128)S(1)}, f32[8,128]{1,0:T(8,128)S(1)}, f32[8,8,128]{2,1,0:T(8,128)}) custom-call(s32[1]{0:T(128)} %bitcast.edge_ref, bf16[4,8,128,128]{3,2,1,0:T(8,128)(2,1)S(1)} %copy-done.10, bf16[4,8,128,128]{3,2,1,0:T(8,128)(2,1)S(1)} %get-tuple-element.56.block_ref, ...), custom_call_target="tpu_custom_call" | custom-call | flops 1207959552 | bytes 7964680 | tf_op jit(solution)/shard_map/pallas_call | solution.py:594
  120.3 1.3 copy-done.2
  121.7 1.0 copy-done.16
  122.6 3.5 %all-to-all-start.2 = ((f32[8,8,128]{2,1,0:T(8,128)}), f32[8,8,128]{2,1,0:T(8,128)S(1)}, u32[]{:S(2)}, u32[]{:S(2)}) async-start(f32[8,8,128]{2,1,0:T(8,128)} %get-tuple-element.77), calls=%async_computation.2 | async-start | bytes 65536 | tf_op jit(solution)/shard_map/all_to_all | solution.py:614
  126.1 0.8 copy-done.14
  127.0 1.2 copy-done.17
  128.2 1.3 copy-done.19
  129.5 2.6 %shard_map.192.block_rows_ref = bf16[1280,128]{1,0:T(8,128)(2,1)S(1)} custom-call(bf16[4,10,128,128]{3,2,1,0:T(8,128)(2,1)S(1)} %copy-done.19, bf16[4,8,128,128]{3,2,1,0:T(8,128)(2,1)S(1)} %copy-done.17, f32[128,128]{1,0:T(8,128)S(1)} %copy-done.14), custom_call_target="tpu_custom_call" | custom-call | flops 1207959552 | bytes 4849664 | tf_op jit(solution)/shard_map/pallas_call | solution.py:594
  132.1 0.7 all-to-all-done.2.tails_ref
  132.8 1.6 copy-done.3
  134.4 0.9 copy-done.5
  135.3 1.9 %shard_map.193 = bf16[2048,128]{1,0:T(8,128)(2,1)S(1)} custom-call(bf16[4,8,2,128,128]{4,3,2,1,0:T(8,128)(2,1)S(1)} %bitcast.29, bf16[4,128,128]{2,1,0:T(8,128)(2,1)S(1)} %copy-done.5, bf16[4,8,128,128]{3,2,1,0:T(8,128)(2,1)S(1)} %get-tuple-element.51.conv_ref, f32[4,8,128,128]{3,2,1,0:T(8,128)S(1)} %copy-done.3, f32[8,8,128]{2,1,0:T(8,128)S(1)} %all-to-all-done.2.tails_ref, ...), custom_call_target="tpu_custom_call" | custom-call | flops 805306368 | bytes 11494400 | tf_op jit(solution)/shard_map/pallas_call | solution.py:594
  137.2 19.7 %all_to_all.26.in_ref = bf16[32,64,128]{2,1,0:T(8,128)(2,1)S(1)} all-to-all(bf16[32,64,128]{2,1,0:T(8,128)(2,1)S(1)} %bitcast.31), channel_id=1, replica_groups=mesh['rows'=8,'dates'=4] {'rows','dates'}, dimensions={0} | all-to-all | bytes 1048576 | tf_op jit(solution)/shard_map/all_to_all | solution.py:614
  157.1 18.4 %all_to_all.27 = bf16[32,64,128]{2,1,0:T(8,128)(2,1)S(1)} all-to-all(bf16[32,64,128]{2,1,0:T(8,128)(2,1)S(1)} %shard_map.194), channel_id=1, replica_groups=mesh['rows'=8,'dates'=4] {'rows','dates'}, dimensions={0} | all-to-all | bytes 1048576 | tf_op jit(solution)/shard_map/all_to_all | solution.py:614
  175.5 1.0 shard_map.195
  176.5 0.7 copy.43
  177.2 0.5 broadcast.3
  177.7 0.7 reduce.4
  178.4 0.7 copy.44
  (51 shorter events, 1.0 us)
Async XLA Ops:
  0.6 18.8 %copy-start.20 = (s32[16,8,32]{2,1,0:T(8,128)S(1)}, s32[16,8,32]{2,1,0:T(8,128)}, u32[]{:S(2)}) copy-start(s32[16,8,32]{2,1,0:T(8,128)} %param.14) | copy-start | bytes 49156
  0.7 18.9 %copy-start.21 = (bf16[8,32,128]{2,1,0:T(8,128)(2,1)S(1)}, bf16[8,32,128]{2,1,0:T(8,128)(2,1)}, u32[]{:S(2)}) copy-start(bf16[8,32,128]{2,1,0:T(8,128)(2,1)} %param.15) | copy-start | bytes 196612
  1.6 7.6 %collective-permute-start = (bf16[4,128,128]{2,1,0:T(8,128)(2,1)S(1)}, bf16[4,128,128]{2,1,0:T(8,128)(2,1)S(1)}, u32[]{:S(2)}, u32[]{:S(2)}) collective-permute-start(bf16[4,128,128]{2,1,0:T(8,128)(2,1)S(1)} %slice_bitcast_fusion), channel_id=1, source_target_pairs={{0,4},{4,8},{8,12},{12,16},{16,20},{20,24},{24,28},{1,5},{5,9},{9,... | collective-permute-start | bytes 393224 | tf_op jit(solution)/shard_map/ppermute | solution.py:697
  9.2 16.2 %copy-start.4 = (bf16[4,128,128]{2,1,0:T(8,128)(2,1)}, bf16[4,128,128]{2,1,0:T(8,128)(2,1)S(1)}, u32[]{:S(2)}) copy-start(bf16[4,128,128]{2,1,0:T(8,128)(2,1)S(1)} %collective-permute-done.above_ref) | copy-start | bytes 393220
  9.2 1.6 copy-start
  10.9 0.9 copy-start.12
  11.8 33.4 %copy-start.8 = (f32[128]{0:T(128)S(1)}, f32[128]{0:T(128)}, u32[]{:S(2)}) copy-start(f32[128]{0:T(128)} %param.17) | copy-start | bytes 1540
  11.8 33.4 %copy-start.11 = (bf16[3,3,128,128]{3,2,1,0:T(8,128)(2,1)S(1)}, bf16[3,3,128,128]{3,2,1,0:T(8,128)(2,1)}, u32[]{:S(2)}) copy-start(bf16[3,3,128,128]{3,2,1,0:T(8,128)(2,1)} %weight_ref.5) | copy-start | bytes 884740
  11.8 33.4 %copy-start.15 = (f32[128]{0:T(128)S(1)}, f32[128]{0:T(128)}, u32[]{:S(2)}) copy-start(f32[128]{0:T(128)} %param.18) | copy-start | bytes 1540
  13.7 31.5 %collective-permute-start.1 = (bf16[4,128,128]{2,1,0:T(8,128)(2,1)S(1)}, bf16[4,128,128]{2,1,0:T(8,128)(2,1)S(1)}, u32[]{:S(2)}, u32[]{:S(2)}) collective-permute-start(bf16[4,128,128]{2,1,0:T(8,128)(2,1)S(1)} %get-tuple-element.52), channel_id=1, source_target_pairs={{0,4},{4,8},{8,12},{12,16},{16,20},{20,24},{24,28},{1,5},{5,9},{9,... | collective-permute-start | bytes 393224 | tf_op jit(solution)/shard_map/ppermute | solution.py:610
  18.1 27.1 %collective-permute-start.2 = (bf16[4,128,128]{2,1,0:T(8,128)(2,1)S(1)}, bf16[4,128,128]{2,1,0:T(8,128)(2,1)S(1)}, u32[]{:S(2)}, u32[]{:S(2)}) collective-permute-start(bf16[4,128,128]{2,1,0:T(8,128)(2,1)S(1)} %get-tuple-element.53), channel_id=1, source_target_pairs={{4,0},{8,4},{12,8},{16,12},{20,16},{24,20},{28,24},{5,1},{9,5},{13... | collective-permute-start | bytes 393224 | tf_op jit(solution)/shard_map/ppermute | solution.py:610
  45.2 16.3 %copy-start.6 = (f32[128]{0:T(128)S(1)}, f32[128]{0:T(128)}, u32[]{:S(2)}) copy-start(f32[128]{0:T(128)} %param.20) | copy-start | bytes 1540
  45.2 16.3 %copy-start.7 = (f32[128]{0:T(128)S(1)}, f32[128]{0:T(128)}, u32[]{:S(2)}) copy-start(f32[128]{0:T(128)} %param.21) | copy-start | bytes 1540
  49.0 1.1 copy-start.18
  50.1 11.4 %all-to-all-start = ((f32[8,8,128]{2,1,0:T(8,128)}), f32[8,8,128]{2,1,0:T(8,128)S(1)}, u32[]{:S(2)}, u32[]{:S(2)}) async-start(f32[8,8,128]{2,1,0:T(8,128)} %get-tuple-element.57), calls=%async_computation | async-start | bytes 65536 | tf_op jit(solution)/shard_map/all_to_all | solution.py:614
  76.9 1.0 copy-start.9
  77.9 42.4 %copy-start.13 = (f32[128,128]{1,0:T(8,128)}, f32[128,128]{1,0:T(8,128)S(1)}, u32[]{:S(2)}) copy-start(f32[128,128]{1,0:T(8,128)S(1)} %get-tuple-element.80.key_ref) | copy-start | bytes 196612
  77.9 36.0 %collective-permute-start.3 = (bf16[4,2,128,128]{3,2,1,0:T(8,128)(2,1)}, bf16[4,2,128,128]{3,2,1,0:T(8,128)(2,1)}, u32[]{:S(2)}, u32[]{:S(2)}) collective-permute-start(bf16[4,2,128,128]{3,2,1,0:T(8,128)(2,1)} %get-tuple-element.68), channel_id=1, source_target_pairs={{0,4},{4,8},{8,12},{12,16},{16,20},{20,24},{24,28},{1,5},{5,9},{9,... | collective-permute-start | bytes 786440 | tf_op jit(solution)/shard_map/ppermute | solution.py:610
  81.0 32.9 %collective-permute-start.4 = (bf16[4,2,128,128]{3,2,1,0:T(8,128)(2,1)S(1)}, bf16[4,2,128,128]{3,2,1,0:T(8,128)(2,1)}, u32[]{:S(2)}, u32[]{:S(2)}) collective-permute-start(bf16[4,2,128,128]{3,2,1,0:T(8,128)(2,1)S(1)} %get-tuple-element.69), channel_id=1, source_target_pairs={{4,0},{8,4},{12,8},{16,12},{20,16},{24,20},{28,24},{5,1},{9,5},{13... | collective-permute-start | bytes 786440 | tf_op jit(solution)/shard_map/ppermute | solution.py:610
  113.9 1.2 copy-start.10
  120.3 1.3 copy-start.2
  121.7 1.0 copy-start.16
  122.6 10.2 %all-to-all-start.2 = ((f32[8,8,128]{2,1,0:T(8,128)}), f32[8,8,128]{2,1,0:T(8,128)S(1)}, u32[]{:S(2)}, u32[]{:S(2)}) async-start(f32[8,8,128]{2,1,0:T(8,128)} %get-tuple-element.77), calls=%async_computation.2 | async-start | bytes 65536 | tf_op jit(solution)/shard_map/all_to_all | solution.py:614
  126.1 0.8 copy-start.14
  127.0 1.2 copy-start.17
  128.2 1.3 copy-start.19
  129.5 3.3 %copy-start.1 = (bf16[4,16,128,128]{3,2,1,0:T(8,128)(2,1)S(1)}, bf16[4,16,128,128]{3,2,1,0:T(8,128)(2,1)}, u32[]{:S(2)}) copy-start(bf16[4,16,128,128]{3,2,1,0:T(8,128)(2,1)} %param.12) | copy-start | bytes 6291460
  132.8 1.6 copy-start.3
  134.4 0.9 copy-start.5

commit v3 on v2

--- a/solution.py
+++ b/solution.py
@@ -15,6 +15,9 @@
 
 
 MIB = 1 << 20
+
+
+MEMORY = 60
 
 
 F32 = jnp.float32
@@ -88,30 +91,49 @@
     table_ref[dates:] = 1.0 / jnp.sqrt(means[dates:] - mean * mean + EPS)
 
 
-def down_kernel(dates, img_ref, above_ref, weight_ref, out_ref, top_ref, low_ref, sums_ref, table):
+def down_table(weight_ref, table):
+    half = weight_ref.shape[2]
+    for tap in range(3):
+        base = tap * 2 * half
+        table[base : base + half, : 2 * half] = weight_ref[tap, 1]
+        table[base + half : base + 2 * half, : 2 * half] = weight_ref[tap, 2]
+        table[base : base + half, 2 * half :] = jnp.zeros_like(weight_ref[tap, 0])
+        table[base + half : base + 2 * half, 2 * half :] = weight_ref[tap, 0]
+
+
+def down_rows(taps, table):
+    rows, cols, width = taps[0].shape
+    taps = jnp.concatenate(taps, axis=-1).reshape(rows * cols, 3 * width)
+    both = product(taps, table[...], 1, 0).reshape(rows, cols, 2 * width)
+    return (both[..., :width] + from_left(both[..., width:])).astype(BF16)
+
+
+def down_kernel(dates, img_ref, above_ref, weight_ref, out_ref, sums_ref, table):
     date = pl.program_id(0)
-    half = weight_ref.shape[2]
 
     @pl.when(date == 0)
     def _():
-        for tap in range(3):
-            base = tap * 2 * half
-            table[base : base + half, : 2 * half] = weight_ref[tap, 1]
-            table[base + half : base + 2 * half, : 2 * half] = weight_ref[tap, 2]
-            table[base : base + half, 2 * half :] = jnp.zeros_like(weight_ref[tap, 0])
-            table[base + half : base + 2 * half, 2 * half :] = weight_ref[tap, 0]
+        down_table(weight_ref, table)
 
     even, odd = img_ref[0, :, 0], img_ref[0, :, 1]
     above = jnp.concatenate([above_ref[0][None], odd[:-1]], axis=0)
-    rows, cols, width = even.shape
-    taps = jnp.concatenate([above, even, odd], axis=-1).reshape(rows * cols, 3 * width)
-    both = product(taps, table[...], 1, 0).reshape(rows, cols, 2 * width)
-    stored = (both[..., :width] + from_left(both[..., width:])).astype(BF16)
+    stored = down_rows([above, even, odd], table)
     out_ref[0] = stored
-    top_ref[0] = stored[0]
-    low_ref[0] = stored[rows - 1]
     values = stored.astype(F32)
     store_sums(sums_ref, date, dates, column_sum(values), column_sum(values * values))
+
+
+def edge_kernel(high_ref, above_ref, last_ref, below_ref, weight_ref, up_ref, down_ref, table):
+    dates = above_ref.shape[0]
+    down_table(weight_ref, table)
+    taps = [
+        jnp.concatenate([high_ref[:, 0], last_ref[...]], axis=0),
+        jnp.concatenate([high_ref[:, 1], below_ref[:, 0]], axis=0),
+        jnp.concatenate([above_ref[...], below_ref[:, 1]], axis=0),
+    ]
+    stored = down_rows(taps, table)
+    up_ref[...] = stored[:dates]
+    down_ref[...] = stored[dates:]
 
 
 def block_kernel(
@@ -178,22 +200,26 @@
 
 
 def fold_keys(key_ref, query_ref, wide_ref, vector_ref, spread_ref, score_ref):
-    heads, depth = query_ref.shape
-    width = key_ref.shape[0]
+    depth, heads = query_ref.shape
+    width = key_ref.shape[1]
     lanes = width // heads
     spread_ref[...] = head_spread(width)
     row = lax.broadcasted_iota(jnp.int32, (heads * depth, width), 0)
     lane = lax.broadcasted_iota(jnp.int32, (heads * depth, width), 1)
     widen = (row // depth == lane // lanes) & (row % depth == lane % lanes)
-    wide = product(key_ref[...], widen.astype(F32).astype(BF16), 1, 0)
+    wide = product(key_ref[...], widen.astype(F32).astype(BF16), 0, 0)
     wide_ref[...] = wide.astype(BF16)
     head = lax.broadcasted_iota(jnp.int32, (heads, width), 0)
     lane = lax.broadcasted_iota(jnp.int32, (heads, width), 1)
-    queries = jnp.where((lane % lanes == depth) | (lane % lanes == depth + 1), 1.0, 0.0)
-    for step in range(depth):
-        scaled = query_ref[:, step : step + 1] * depth**-0.5
-        queries = queries + jnp.where(lane % lanes == step, scaled, 0.0)
-    queries = jnp.sum(jnp.where(lane // lanes == head, queries, 0.0), axis=0, keepdims=True)
+    inside = (lane // lanes == head).astype(F32).astype(BF16)
+    high, low = split(query_ref[...])
+    lower = (query_ref[...] - high.astype(F32) - low.astype(F32)).astype(BF16)
+    spread = sum(product(part, inside, 1, 0) for part in (high, low, lower))
+    step = lax.broadcasted_iota(jnp.int32, (depth, width), 0)
+    place = lax.broadcasted_iota(jnp.int32, (depth, width), 1) % lanes
+    queries = jnp.sum(jnp.where(step == place, spread * depth**-0.5, 0.0), axis=0, keepdims=True)
+    place = lax.broadcasted_iota(jnp.int32, (1, width), 1) % lanes
+    queries = queries + jnp.where((place == depth) | (place == depth + 1), 1.0, 0.0)
     vector_ref[...] = jnp.broadcast_to(queries, vector_ref.shape)
     folded = jnp.concatenate(split(wide * queries), axis=-1)
     folded = product(folded, spread_ref[...], 1, 0)
@@ -289,8 +315,6 @@
     grad_ref,
     key_ref,
     grad_out_ref,
-    up_ref,
-    down_ref,
     part_ref,
     key_out_ref,
     vector_ref,
@@ -346,12 +370,7 @@
     vector_ref[0:1] += second
     vector_ref[1:2] += first
     store_sums(sums_ref, date, dates, first * gain, second * gain)
-    stored = (linear_grad * gain).astype(BF16)
-    grad_out_ref[0] = stored
-    up_ref[0, 0] = stored[0]
-    up_ref[0, 1] = block_ref[0, 0]
-    down_ref[0, 0] = stored[rows - 1]
-    down_ref[0, 1] = block_ref[0, rows - 1]
+    grad_out_ref[0] = (linear_grad * gain).astype(BF16)
 
     @pl.when(date == dates - 1)
     def _():
@@ -374,12 +393,12 @@
     edge_ref,
     grad_ref,
     block_ref,
-    up_ref,
-    down_ref,
     tails_ref,
     norm_ref,
     weight_ref,
     conv_ref,
+    up_ref,
+    down_ref,
     first_norm_ref,
     gain_ref,
     shift_ref,
@@ -402,6 +421,8 @@
         factors[0:dates] = slope
         factors[dates : 2 * dates] = -inverse * tails[:dates] - mean * slope
         vector_ref[...] = jnp.zeros_like(vector_ref)
+        padded[:2] = jnp.zeros_like(padded[:2])
+        padded[rows + 2 :] = jnp.zeros_like(padded[rows + 2 :])
         for row_tap in range(3):
             for col_tap in range(3):
                 table[
@@ -412,32 +433,39 @@
     slope = factors[pl.ds(date, 1), :]
     constant = factors[pl.ds(dates + date, 1), :]
 
-    def finish(grad, values):
-        return grad.astype(F32) * inverse + (values.astype(F32) * slope + constant)
-
     above_edge, below_edge = edges(edge_ref, row_devs)
-    stored = finish(grad_ref[0], block_ref[0]).astype(BF16)
+    stored = (
+        grad_ref[0].astype(F32) * inverse + (block_ref[0].astype(F32) * slope + constant)
+    ).astype(BF16)
     pre_ref[0] = stored
-    padded[0] = (finish(up_ref[0, 0], up_ref[0, 1]) * above_edge).astype(BF16)
-    padded[rows + 1] = (finish(down_ref[0, 0], down_ref[0, 1]) * below_edge).astype(BF16)
-    padded[1 : rows + 1] = stored
-    taps = jnp.concatenate([padded[tap : tap + rows] for tap in range(3)], axis=-1).reshape(
-        rows * cols, 3 * width
-    )
-    terms = product(taps, table[...], 1, 1).reshape(rows, cols, 3 * width)
+    padded[2 : rows + 2] = stored
+    reach = rows + 2
+    taps = jnp.concatenate([padded[tap : tap + reach] for tap in range(3)], axis=-1).reshape(
+        reach * cols, 3 * width
+    )
+    terms = product(taps, table[...], 1, 1).reshape(reach, cols, 3 * width)
     hidden_grad = (
         terms[..., width : 2 * width]
         + from_right(terms[..., :width])
         + from_left(terms[..., 2 * width :])
     )
     gain = gain_ref[...]
-    centred = (conv_ref[0].astype(F32) - first_norm_ref[pl.ds(date, 1), :]) * first_norm_ref[
+    conv = jnp.concatenate([up_ref[0][None], conv_ref[0], down_ref[0][None]], axis=0)
+    centred = (conv.astype(F32) - first_norm_ref[pl.ds(date, 1), :]) * first_norm_ref[
         pl.ds(dates + date, 1), :
     ]
     linear = centred * gain + shift_ref[...]
     part = sigmoid(linear)
     linear_grad = hidden_grad * (part * (1.0 + linear * (1.0 - part)))
-    out_ref[0] = linear_grad
+    linear_grad = jnp.concatenate(
+        [
+            linear_grad[:1] * above_edge,
+            linear_grad[1 : rows + 1],
+            linear_grad[rows + 1 :] * below_edge,
+        ],
+        axis=0,
+    )
+    out_ref[0] = linear_grad.astype(BF16)
     first = column_sum(linear_grad)
     second = column_sum(linear_grad * centred)
     vector_ref[0:1] += second
@@ -486,6 +514,8 @@
     norm_count,
     img_ref,
     above_ref,
+    high_ref,
+    below_ref,
     conv_ref,
     grad_ref,
     tails_ref,
@@ -514,12 +544,22 @@
     scale = norm_ref[pl.ds(dates + date, 1), :] * gain_ref[...]
     slope = factors[pl.ds(date, 1), :]
     constant = factors[pl.ds(dates + date, 1), :]
-    stored = (grad_ref[0] * scale + (conv_ref[0].astype(F32) * slope + constant)).astype(BF16)
+    own = conv_ref[0].astype(F32) * slope + constant
+    scaled = grad_ref[0].astype(F32) * scale
+    stored = jnp.concatenate(
+        [scaled[:1], scaled[1 : rows + 1] + own, scaled[rows + 1 :]], axis=0
+    ).astype(BF16)
     moved = from_right(stored.astype(F32)).astype(BF16)
-    grads = jnp.concatenate([stored, moved], axis=-1).reshape(rows * cols, 2 * width)
+    reach = rows + 2
+    grads = jnp.concatenate([stored, moved], axis=-1).reshape(reach * cols, 2 * width)
     even, odd = img_ref[0, :, 0], img_ref[0, :, 1]
-    above = jnp.concatenate([above_ref[0][None], odd[:-1]], axis=0)
-    taps = jnp.concatenate([above, even, odd], axis=-1).reshape(rows * cols, 3 * width)
+    above = above_ref[0][None]
+    taps = [
+        jnp.concatenate([high_ref[0, :1], above, odd], axis=0),
+        jnp.concatenate([high_ref[0, 1:], even, below_ref[0, :1]], axis=0),
+        jnp.concatenate([above, odd, below_ref[0, 1:]], axis=0),
+    ]
+    taps = jnp.concatenate(taps, axis=-1).reshape(reach * cols, 3 * width)
     total[...] += product(taps, grads, 0, 0)
 
     @pl.when(date == dates - 1)
@@ -551,13 +591,14 @@
 def final_kernel(depth, rows_ref, conv_ref, block_ref, key_ref, query_ref, *vector_refs):
     conv_end, block_end, width = conv_ref.shape[0], block_ref.shape[0], block_ref.shape[1]
     block_ref[...] = rows_ref[:block_end].astype(F32)
-    heads = key_ref.shape[1] // depth
+    wide = key_ref.shape[0]
+    heads = wide // depth
     lanes = width // heads
-    row = lax.broadcasted_iota(jnp.int32, (width, heads * depth), 0)
-    lane = lax.broadcasted_iota(jnp.int32, (width, heads * depth), 1)
-    narrow = (row // lanes == lane // depth) & (row % depth == lane % depth)
+    row = lax.broadcasted_iota(jnp.int32, (wide, width), 0)
+    lane = lax.broadcasted_iota(jnp.int32, (wide, width), 1)
+    narrow = (row // depth == lane // lanes) & (row % depth == lane % depth)
     narrow = narrow.astype(F32).astype(BF16)
-    key_ref[...] = product(rows_ref[block_end : block_end + width], narrow, 1, 0)
+    key_ref[...] = product(narrow, rows_ref[block_end : block_end + width], 1, 1)
     start = block_end + width
     conv_ref[...] = rows_ref[start : start + conv_end].astype(F32)
     start += conv_end
@@ -567,8 +608,18 @@
         vector_refs[2 * index][...] = both[0:1]
         vector_refs[2 * index + 1][...] = both[1:2]
         start += 16
-    query = product(rows_ref[start - 16 : start], narrow, 1, 0)
-    query_ref[...] = query[2:3] + query[10:11]
+    both = rows_ref[start - 16 : start]
+    row = lax.broadcasted_iota(jnp.int32, (heads, width), 0)
+    lane = lax.broadcasted_iota(jnp.int32, (heads, width), 1)
+    inside = row == lane // lanes
+    step = lax.broadcasted_iota(jnp.int32, (8, width), 0)
+    place = lax.broadcasted_iota(jnp.int32, (8, width), 1) % lanes
+    steps = step == place
+    query = jnp.zeros((8, heads), F32)
+    for index in (2, 10):
+        picked = jnp.where(steps, both[index : index + 1].astype(F32), 0.0).astype(BF16)
+        query = query + product(picked, inside.astype(F32).astype(BF16), 1, 1)
+    query_ref[...] = query[:depth]
 
 
 def per_date(shape):
@@ -576,38 +627,83 @@
     return pl.BlockSpec((1,) + tuple(shape[1:]), lambda date: (date,) + zeros)
 
 
+def streamed(kernel, dates, kinds, out_count):
+    count = kinds.count("date")
+
+    def body(*refs):
+        inputs, rest = list(refs[: len(kinds)]), refs[len(kinds) :]
+        outputs, scratch = rest[:out_count], rest[out_count:]
+        buffers, ready, scratch = scratch[:count], scratch[count], scratch[count + 1 :]
+        date = pl.program_id(0)
+        places = [place for place, kind in enumerate(kinds) if kind == "date"]
+
+        def copy(index, step):
+            return pltpu.make_async_copy(
+                inputs[places[index]].at[step], buffers[index].at[step], ready.at[index, step]
+            )
+
+        @pl.when(date == 0)
+        def _():
+            for step in range(dates):
+                for index in range(count):
+                    copy(index, step).start()
+
+        for index in range(count):
+            copy(index, date).wait()
+        views = list(inputs)
+        for index, place in enumerate(places):
+            views[place] = buffers[index].at[pl.ds(date, 1)]
+        kernel(*views, *outputs, *scratch)
+
+    return body
+
+
 def whole(shape):
     zeros = (0,) * len(shape)
     return pl.BlockSpec(tuple(shape), lambda date: zeros)
 
 
-def call(kernel, dates, inputs, outputs, scratch, flops, memory=24):
-    in_specs, arrays = [], []
+def call(kernel, dates, inputs, outputs, scratch, flops, memory=MEMORY):
+    in_specs, arrays, buffers = [], [], []
     for kind, array in inputs:
         arrays.append(array)
         if kind == "scalar":
             in_specs.append(pl.BlockSpec(memory_space=pltpu.SMEM))
+        elif kind == "date":
+            in_specs.append(pl.BlockSpec(memory_space=pl.ANY))
+            buffers.append(pltpu.VMEM(array.shape, array.dtype))
         else:
-            in_specs.append((per_date if kind == "date" else whole)(array.shape))
+            in_specs.append(whole(array.shape))
     out_specs = [(per_date if kind == "date" else whole)(shape) for kind, shape, _ in outputs]
     moved = sum(array.size * array.dtype.itemsize for array in arrays)
+    ready = pltpu.SemaphoreType.DMA((len(buffers), dates))
     return pl.pallas_call(
-        kernel,
+        streamed(kernel, dates, [kind for kind, _ in inputs], len(outputs)),
         grid=(dates,),
         in_specs=in_specs,
         out_specs=out_specs,
         out_shape=[jax.ShapeDtypeStruct(shape, dtype) for _, shape, dtype in outputs],
-        scratch_shapes=scratch,
+        scratch_shapes=buffers + [ready] + scratch,
         compiler_params=pltpu.CompilerParams(vmem_limit_bytes=memory * MIB),
         cost_estimate=pl.CostEstimate(flops=flops, bytes_accessed=2 * moved, transcendentals=0),
     )(*arrays)
 
 
-def neighbours(first_rows, last_rows):
+def shifted(array, by):
     devices = lax.axis_size("rows")
-    down = [(i, i + 1) for i in range(devices - 1)]
-    up = [(i + 1, i) for i in range(devices - 1)]
-    return lax.ppermute(last_rows, "rows", down), lax.ppermute(first_rows, "rows", up)
+    pairs = [(i, i + by) for i in range(devices) if 0 <= i + by < devices]
+    return lax.ppermute(array, "rows", pairs)
+
+
+def sum_of_parts(parts):
+    devices = lax.axis_size("dates")
+    place = lax.axis_index("dates")
+    total = lax.dynamic_index_in_dim(parts, place, 0, keepdims=False).astype(F32)
+    for step in range(1, devices):
+        piece = lax.dynamic_index_in_dim(parts, (place + step) % devices, 0, keepdims=False)
+        pairs = [(i, (i + step) % devices) for i in range(devices)]
+        total = total + lax.ppermute(piece, "dates", pairs).astype(F32)
+    return total.astype(BF16)
 
 
 def exchange(pieces, axes):
@@ -629,7 +725,7 @@
     spread = pl.pallas_call(
         total_kernel,
         out_shape=jax.ShapeDtypeStruct(pieces.shape, BF16),
-        compiler_params=pltpu.CompilerParams(vmem_limit_bytes=16 * MIB),
+        compiler_params=pltpu.CompilerParams(vmem_limit_bytes=MEMORY * MIB),
     )(pieces)
     count, rows, width = pieces.shape
     return exchange(spread, ("rows", "dates")).reshape(count * rows, width)
@@ -638,30 +734,6 @@
 def padded_count(count, devices):
     step = 8 * devices
     return -(-count // step) * step
-
-
-def grouped(array, groups):
-    return lax.all_gather(array, "rows", axis_index_groups=groups, axis=0, tiled=True)
-
-
-def row_totals_by_squares(sums):
-    devices = lax.axis_size("rows")
-    near = [list(range(start, start + 4)) for start in range(0, devices, 4)]
-    far = [list(range(start, devices, 4)) for start in range(4)]
-    sums = jnp.sum(grouped(sums, near), axis=0, keepdims=True)
-    return grouped(sums, far)
-
-
-def row_totals_by_pairs(sums):
-    devices = lax.axis_size("rows")
-    step = 1
-    while step < devices:
-        pairs = [[i, i + step] for i in range(devices) if i // step % 2 == 0]
-        sums = grouped(sums, pairs)
-        step *= 2
-        if step < devices:
-            sums = jnp.sum(sums, axis=0, keepdims=True)
-    return sums
 
 
 def local(
@@ -694,33 +766,27 @@
     rows_of = lambda vector: vector.reshape(1, width)
     first_gain, first_shift = rows_of(first_gain), rows_of(first_shift)
     gn_gain, gn_shift = rows_of(gn_gain), rows_of(gn_shift)
-    above = lax.ppermute(images[:, -1], "rows", [(i, i + 1) for i in range(row_devs - 1)])
+    last = images[:, -1]
+    above = shifted(last, 1)
+    high = shifted(images[:, -3:-1], 1)
+    below = shifted(images[:, :2], -1)
     paired = images.reshape(dates, rows, 2, cols, pair_width)
-    conv_out, top, low, sums = call(
+    conv_out, sums = call(
         functools.partial(down_kernel, dates),
         dates,
         [("date", paired), ("date", above), ("all", conv_weight)],
-        [
-            ("date", frame, BF16),
-            ("date", edge_rows, BF16),
-            ("date", edge_rows, BF16),
-            ("all", (1, 2 * dates, width), F32),
-        ],
+        [("date", frame, BF16), ("all", (row_devs, 2 * dates, width), F32)],
         [pltpu.VMEM((3 * pair_width, 2 * width), BF16)],
         6 * flops,
     )
-    sums, valid, out_grad = lax.optimization_barrier((sums, valid, out_grad))
-    halo_up, halo_down = neighbours(top, low)
-    stats = row_totals_by_squares(sums)
-    grad_rows, valid_rows = out_grad.size // width, valid.size // width
-    packed = jnp.concatenate(
-        [out_grad.reshape(grad_rows, width), valid.astype(BF16).reshape(valid_rows, width)]
-    )
-    packed = gather(packed[None], "dates")
-    grads_here = packed[:, :grad_rows].reshape((date_devs,) + out_grad.shape)
-    clear = packed[:, grad_rows:].reshape((date_devs,) + valid.shape)
-    clear = lax.dynamic_slice_in_dim(clear, date_start, dates, 1)
-    clear = clear.transpose(1, 2, 0, 3).reshape(dates, rows, cols).astype(F32)
+    stats = exchange(sums, "rows")
+    high, below, last, _ = lax.optimization_barrier((high, below, last, sums))
+    halo_up, halo_down = pl.pallas_call(
+        edge_kernel,
+        out_shape=[jax.ShapeDtypeStruct(edge_rows, BF16)] * 2,
+        scratch_shapes=[pltpu.VMEM((3 * pair_width, 2 * width), BF16)],
+        compiler_params=pltpu.CompilerParams(vmem_limit_bytes=MEMORY * MIB),
+    )(high, above, last, below, conv_weight)
     days = lax.dynamic_slice_in_dim(day_index, date_start, dates, 0)
     place = lax.axis_index("rows").reshape(1)
 
@@ -747,6 +813,16 @@
         9 * flops,
     )
     stats = exchange(sums, "rows")
+    sums, valid, out_grad = lax.optimization_barrier((sums, valid, out_grad))
+    grad_rows, valid_rows = out_grad.size // width, valid.size // width
+    packed = jnp.concatenate(
+        [out_grad.reshape(grad_rows, width), valid.astype(BF16).reshape(valid_rows, width)]
+    )
+    packed = gather(packed[None], "dates")
+    grads_here = packed[:, :grad_rows].reshape((date_devs,) + out_grad.shape)
+    clear = packed[:, grad_rows:].reshape((date_devs,) + valid.shape)
+    clear = lax.dynamic_slice_in_dim(clear, date_start, dates, 1)
+    clear = clear.transpose(1, 2, 0, 3).reshape(dates, rows, cols).astype(F32)
     features, exponent, attn, norm, packed, key_wide, query_wide = call(
         functools.partial(score_kernel, dates, norm_count, grad_scale),
         dates,
@@ -758,8 +834,8 @@
             ("all", gn_shift),
             ("all", grads_here),
             ("date", clear),
-            ("all", key_weight),
-            ("all", queries),
+            ("all", key_weight.T),
+            ("all", queries.T),
         ],
         [
             ("date", frame, BF16),
@@ -777,9 +853,10 @@
             pltpu.VMEM((width, 2 * width), BF16),
         ],
         5 * flops,
+        24,
     )
     packed = gather(packed, "dates")
-    block_grad, up, low, attended, key_part, vectors, sums = call(
+    block_grad, attended, key_part, vectors, sums = call(
         functools.partial(attend_kernel, dates, grad_scale),
         dates,
         [
@@ -797,20 +874,16 @@
         ],
         [
             ("date", frame, BF16),
-            ("date", (dates, 2, cols, width), BF16),
-            ("date", (dates, 2, cols, width), BF16),
             ("all", (date_devs, rows, cols // date_devs, width), BF16),
             ("all", (width, width), F32),
             ("all", (8, width), F32),
-            ("all", (1, 2 * dates, width), F32),
+            ("all", (row_devs, 2 * dates, width), F32),
         ],
         [pltpu.VMEM(frame[1:], F32)] * 3,
         5 * flops,
-    )
-    halo_up, halo_down = neighbours(up, low)
-    tails = row_totals_by_pairs(sums)
-    attended, _ = lax.optimization_barrier((attended, tails))
-    attended = jnp.sum(exchange(attended, "dates").astype(F32), axis=0).astype(BF16)
+        24,
+    )
+    tails = exchange(sums, "rows")
     pre_grad, linear_grad, first_vectors, sums = call(
         functools.partial(hidden_kernel, dates, norm_count, row_devs),
         dates,
@@ -818,30 +891,29 @@
             ("scalar", place),
             ("date", block_grad),
             ("date", block_out),
-            ("date", halo_up),
-            ("date", halo_down),
             ("all", tails),
             ("all", norm),
             ("all", block_weight),
             ("date", conv_out),
+            ("date", halo_up),
+            ("date", halo_down),
             ("all", first_norm),
             ("all", first_gain),
             ("all", first_shift),
         ],
         [
             ("date", frame, BF16),
-            ("date", frame, F32),
+            ("date", (dates, rows + 2, cols, width), BF16),
             ("all", (8, width), F32),
             ("all", (row_devs, 2 * dates, width), F32),
         ],
         [
             pltpu.VMEM((3 * width, 3 * width), BF16),
             pltpu.VMEM((2 * dates, width), F32),
-            pltpu.VMEM((rows + 2, cols, width), BF16),
+            pltpu.VMEM((rows + 4, cols, width), BF16),
         ],
         9 * flops,
     )
-    sums, attended = lax.optimization_barrier((sums, attended))
     tails = exchange(sums, "rows")
     (block_rows,) = call(
         functools.partial(block_grad_kernel, dates),
@@ -859,6 +931,8 @@
         [
             ("date", paired),
             ("date", above),
+            ("date", high),
+            ("date", below),
             ("date", conv_out),
             ("date", linear_grad),
             ("all", tails),
@@ -872,17 +946,20 @@
         [pltpu.VMEM((2 * dates, width), F32), pltpu.VMEM((3 * pair_width, 2 * width), F32)],
         6 * flops,
     )
-    rows_all = collect(scatter(rows_all))
+    pieces = scatter(rows_all)
+    attended, _ = lax.optimization_barrier((attended, rows_all))
+    attended = sum_of_parts(attended)
+    rows_all = collect(pieces)
     shapes = [
         (9 * pair_width // 2, width),
         (9 * width, width),
-        key_weight.shape,
-        (1, heads * depth),
+        (heads * depth, width),
+        (depth, heads),
     ] + [(1, width)] * 4
     conv_total, block_total, key_total, query_total, *totals = pl.pallas_call(
         functools.partial(final_kernel, depth),
         out_shape=[jax.ShapeDtypeStruct(shape, F32) for shape in shapes],
-        compiler_params=pltpu.CompilerParams(vmem_limit_bytes=16 * MIB),
+        compiler_params=pltpu.CompilerParams(vmem_limit_bytes=MEMORY * MIB),
     )(rows_all)
     totals = [total.reshape(width) for total in totals]
     return (
@@ -893,8 +970,8 @@
         block_total.reshape(block_weight.shape),
         totals[2],
         totals[3],
-        key_total,
-        query_total.reshape(heads, depth),
+        key_total.T,
+        query_total.T,
     )
 
 

time: 180 us -> 150 us (0.83)
  blocking collectives: 101 us -> 42.4 us
  Pallas kernels: 24.7 us -> 44.1 us
  waiting for transfers between devices: 7.66 us -> 22.1 us
  local copies, waits for them, and re-layouts: 19.7 us -> 9.36 us
  starting transfers between devices: 23.2 us -> 29.7 us
    all_gather x5 -> x0, blocking collectives: 40.5 us -> none  [grouped(): lax.all_gather(array, 'rows', axis_index_groups=groups, axis=0, tiled=True)]
    all_to_all x3 -> x2, blocking collectives: 47.3 us -> 29.4 us  [exchange(): return lax.all_to_all(pieces, axes, split_axis=0, concat_axis=0, tiled=True)]
    pallas_call x7 -> x8, Pallas kernels: 23.6 us -> 40.1 us  [the longest x7 37.8 us: call(): pl.pallas_call(streamed(kernel, dates, [kind for kind, _ in inputs], len(...]
    unnamed x49 -> x39, local copies, waits for them, and re-layouts: 17.1 us -> 6.95 us
    all_to_all x2 -> x4, waiting for transfers between devices: 7.25 us -> 16.5 us  [exchange(): return lax.all_to_all(pieces, axes, split_axis=0, concat_axis=0, tiled=True)]
    all_to_all x2 -> x4, starting transfers between devices: 8.26 us -> 16.7 us  [exchange(): return lax.all_to_all(pieces, axes, split_axis=0, concat_axis=0, tiled=True)]
    ppermute x5 -> x6, waiting for transfers between devices: 0.41 us -> 5.59 us  [the longest x3 5.59 us: sum_of_parts(): total = total + lax.ppermute(piece, 'dates', pairs).astype(F32)]
    ppermute x5 -> x6, starting transfers between devices: 14.9 us -> 13 us  [the longest x3 9.74 us: shifted(): return lax.ppermute(array, 'rows', pairs)]
  transfers between devices with their start and end apart: 7 -> 10, of which waited for: 3 -> 6; matrix products, arithmetic and copies ran while one was open for 2% -> 1% of each run, Pallas kernels for 1% -> 8%
where the time goes in v3:
time: 150 us; the launch traced here: 149 us
  Pallas kernels  44.1 us (29%)
  blocking collectives  42.4 us (28%)
  starting transfers between devices  29.7 us (20%)
  waiting for transfers between devices  22.1 us (15%)
  local copies, waits for them, and re-layouts  9.36 us (6%)
    pallas_call x7, Pallas kernels, call(): pl.pallas_call(streamed(kernel, dates, [kind for kind, _ in inputs], len(...  37.8 us
    all_to_all x2, blocking collectives, exchange(): return lax.all_to_all(pieces, axes, split_axis=0, concat_axis=0, tiled=True)  29.4 us
    all_to_all x4, starting transfers between devices, exchange(): return lax.all_to_all(pieces, axes, split_axis=0, concat_axis=0, tiled=True)  16.7 us
    all_to_all x4, waiting for transfers between devices, exchange(): return lax.all_to_all(pieces, axes, split_axis=0, concat_axis=0, tiled=True)  16.5 us
    all_gather x2, blocking collectives, gather(): return lax.all_gather(array, axis, axis=0, tiled=True)  13.1 us
    ppermute x3, starting transfers between devices, shifted(): return lax.ppermute(array, 'rows', pairs)  9.74 us
    unnamed x39, local copies, waits for them, and re-layouts  6.95 us
    ppermute x3, waiting for transfers between devices, sum_of_parts(): total = total + lax.ppermute(piece, 'dates', pairs).astype(F32)  5.59 us
  transfers between devices with their start and end apart: 10, of which 6 were waited for; matrix products, arithmetic and copies ran while one was open for 1% of the time, Pallas kernels for 8%

profile of v3, /device:TPU:0, one launch (start us, length us, event | category | flops | bytes accessed | tf_op | source)
XLA Modules:
  0.0 149.3 jit_solution(13825191787194059687)
XLA Ops:
  0.6 0.9 slice_bitcast_fusion.last_ref
  1.6 0.0 copy-start.13
  1.6 0.0 copy-start.18
  1.6 5.0 %collective-permute-start = (bf16[4,128,128]{2,1,0:T(8,128)(2,1)S(1)}, bf16[4,128,128]{2,1,0:T(8,128)(2,1)S(1)}, u32[]{:S(2)}, u32[]{:S(2)}) collective-permute-start(bf16[4,128,128]{2,1,0:T(8,128)(2,1)S(1)} %slice_bitcast_fusion.last_ref), channel_id=1, source_target_pairs={{0,4},{4,8},{8,12},{12,16},{16,20},{20,24},{24,28},{1,5},{5,9},{9,... | collective-permute-start | bytes 393224 | tf_op jit(solution)/shard_map/ppermute | solution.py:695
  6.6 1.1 fusion.3
  7.7 3.4 %collective-permute-start.1 = (bf16[4,2,128,128]{3,2,1,0:T(8,128)(2,1)S(1)}, bf16[4,2,128,128]{3,2,1,0:T(8,128)(2,1)S(1)}, u32[]{:S(2)}, u32[]{:S(2)}) collective-permute-start(bf16[4,2,128,128]{3,2,1,0:T(8,128)(2,1)S(1)} %get-tuple-element.90), channel_id=1, source_target_pairs={{0,4},{4,8},{8,12},{12,16},{16,20},{20,24},{24,28},{1,5},{5,9},{9,... | collective-permute-start | bytes 786440 | tf_op jit(solution)/shard_map/ppermute | solution.py:695
  11.1 1.3 collective-permute-start.2
  12.4 0.6 copy-done.12
  13.1 4.8 %shard_map.187 = (bf16[4,8,128,128]{3,2,1,0:T(8,128)(2,1)}, f32[8,8,128]{2,1,0:T(8,128)}) custom-call(bf16[4,8,2,128,128]{4,3,2,1,0:T(8,128)(2,1)} %bitcast.45, bf16[4,128,128]{2,1,0:T(8,128)(2,1)} %copy-done.12, bf16[3,3,64,128]{3,2,1,0:T(8,128)(2,1)} %weight_ref.1), custom_call_target="tpu_custom_call" | custom-call | flops 805306368 | bytes 4751360 | tf_op jit(solution)/shard_map/pallas_call | solution.py:680
  17.9 6.9 %all-to-all-start = ((f32[8,8,128]{2,1,0:T(8,128)}), f32[8,8,128]{2,1,0:T(8,128)S(1)}, u32[]{:S(2)}, u32[]{:S(2)}) async-start(f32[8,8,128]{2,1,0:T(8,128)} %get-tuple-element.50), calls=%async_computation | async-start | bytes 65536 | tf_op jit(solution)/shard_map/all_to_all | solution.py:710
  24.8 0.1 dynamic_slice.19.refs_0_
  24.9 0.7 copy-done.10
  25.6 0.7 copy-done.11
  26.3 2.3 %shard_map.188 = (bf16[4,128,128]{2,1,0:T(8,128)(2,1)}, bf16[4,128,128]{2,1,0:T(8,128)(2,1)}) custom-call(bf16[4,2,128,128]{3,2,1,0:T(8,128)(2,1)} %copy-done.10, bf16[4,128,128]{2,1,0:T(8,128)(2,1)} %copy-done.12, bf16[4,128,128]{2,1,0:T(8,128)(2,1)} %copy-done.13, bf16[4,2,128,128]{3,2,1,0:T(8,128)(2,1)} %copy-done.11, bf16[3,3,64,128]{3,2,1,0:T(8,128)(2,1)} %weight_ref.1), custom_call_target="tpu_custom_call" | custom-call | tf_op jit(solution)/shard_map/pallas_call | solution.py:784
  28.6 2.9 %all-to-all-done.refs_4_ = f32[8,8,128]{2,1,0:T(8,128)S(1)} async-done(((f32[8,8,128]{2,1,0:T(8,128)}), f32[8,8,128]{2,1,0:T(8,128)S(1)}, u32[]{:S(2)}, u32[]{:S(2)}) %all-to-all-start) | async-done | bytes 32800 | tf_op jit(solution)/shard_map/all_to_all | solution.py:710
  31.5 0.6 copy-done.17
  32.1 6.0 %shard_map.189 = (bf16[4,8,128,128]{3,2,1,0:T(8,128)(2,1)}, bf16[4,10,128,128]{3,2,1,0:T(8,128)(2,1)}, f32[8,128]{1,0:T(8,128)}, f32[8,8,128]{2,1,0:T(8,128)}) custom-call(s32[1]{0:T(128)} %bitcast.refs_0_, bf16[4,8,128,128]{3,2,1,0:T(8,128)(2,1)} %get-tuple-element.49.refs_1_.refs_6_.refs_4_, bf16[4,128,128]{2,1,0:T(8,128)(2,1)} %get-tuple-element.54.refs_2_.refs_7_, ...), custom_call_target="tpu_custom_call" | custom-call | flops 1207959552 | bytes 3278856 | tf_op jit(solution)/shard_map/pallas_call | solution.py:680
  38.2 0.1 reshape.84
  38.3 5.9 %all-gather = bf16[1152,128]{1,0:T(8,128)(2,1)S(1)} all-gather(bf16[288,128]{1,0:T(8,128)(2,1)S(1)} %pad_maximum_fusion), channel_id=2, replica_groups=mesh['rows'=8,'dates'=4] {'dates'}, dimensions={0}, use_global_device_ids=true | all-gather | bytes 368640 | tf_op jit(solution)/shard_map/all_gather | solution.py:714
  44.3 3.4 %all-to-all-start.1 = ((f32[8,8,128]{2,1,0:T(8,128)}), f32[8,8,128]{2,1,0:T(8,128)S(1)}, u32[]{:S(2)}, u32[]{:S(2)}) async-start(f32[8,8,128]{2,1,0:T(8,128)} %get-tuple-element.57), calls=%async_computation.1 | async-start | bytes 65536 | tf_op jit(solution)/shard_map/all_to_all | solution.py:710
  47.6 0.1 reshape.86
  47.8 0.1 reshape.95.refs_6_
  47.9 6.3 %all-to-all-done.1.refs_2_ = f32[8,8,128]{2,1,0:T(8,128)S(1)} async-done(((f32[8,8,128]{2,1,0:T(8,128)}), f32[8,8,128]{2,1,0:T(8,128)S(1)}, u32[]{:S(2)}, u32[]{:S(2)}) %all-to-all-start.1) | async-done | bytes 32800 | tf_op jit(solution)/shard_map/all_to_all | solution.py:710
  54.3 1.2 copy-done
  55.5 4.0 %shard_map.190 = (bf16[4,8,128,128]{3,2,1,0:T(8,128)(2,1)S(1)}, f32[4,8,128,128]{3,2,1,0:T(8,128)S(1)}, f32[4,8,128,128]{3,2,1,0:T(8,128)S(1)}, f32[8,128]{1,0:T...) custom-call(s32[4]{0:T(128)S(1)} %dynamic_slice.19.refs_0_, ...), custom_call_target="tpu_custom_call" | custom-call | flops 671088640 | bytes 2755104 | tf_op jit(solution)/shard_map/pallas_call | solution.py:680
  59.6 7.1 %all_gather.7.refs_0_ = f32[4,2,128,128]{3,2,1,0:T(8,128)S(1)} all-gather(f32[1,2,128,128]{3,2,1,0:T(8,128)S(1)} %get-tuple-element.60), channel_id=1, replica_groups=mesh['rows'=8,'dates'=4] {'dates'}, dimensions={0}, use_global_device_ids=true | all-gather | bytes 655360 | tf_op jit(solution)/shard_map/all_gather | solution.py:714
  66.7 4.3 %shard_map.191 = (bf16[4,8,128,128]{3,2,1,0:T(8,128)(2,1)S(1)}, bf16[4,8,32,128]{3,2,1,0:T(8,128)(2,1)S(1)}, f32[128,128]{1,0:T(8,128)S(1)}, f32[8,128]{1,0:T(8,128)S(1)}, f32[8,8,128]{2,1,0:T(8,128)S(1)}) custom-call(f32[4,2,128,128]{3,2,1,0:T(8,128)S(1)} %all_gather.7.refs_0_, bf16[4,8,128,128]{3,2,1,0:T(8,128)(2,1)S(1)} %get-tuple-element.61.refs_1_, ...), custom_call_target="tpu_custom_call" | custom-call | flops 671088640 | bytes 14239744 | tf_op jit(solution)/shard_map/pallas_call | solution.py:680
  71.0 1.0 copy-done.5
  72.0 0.6 copy-done.6
  72.6 9.7 %all_to_all.30.refs_3_ = f32[8,8,128]{2,1,0:T(8,128)} all-to-all(f32[8,8,128]{2,1,0:T(8,128)S(1)} %get-tuple-element.69), channel_id=1, replica_groups=mesh['rows'=8,'dates'=4] {'rows'}, dimensions={0} | all-to-all | bytes 65536 | tf_op jit(solution)/shard_map/all_to_all | solution.py:710
  82.3 7.8 %shard_map.192 = (bf16[4,8,128,128]{3,2,1,0:T(8,128)(2,1)}, bf16[4,10,128,128]{3,2,1,0:T(8,128)(2,1)}, f32[8,128]{1,0:T(8,128)}, f32[8,8,128]{2,1,0:T(8,128)}) custom-call(s32[1]{0:T(128)} %bitcast.refs_0_, bf16[4,8,128,128]{3,2,1,0:T(8,128)(2,1)} %copy-done.5, bf16[4,8,128,128]{3,2,1,0:T(8,128)(2,1)} %get-tuple-element.56.refs_1_.refs_4_.refs_2_, ...), custom_call_target="tpu_custom_call" | custom-call | flops 1207959552 | bytes 7489544 | tf_op jit(solution)/shard_map/pallas_call | solution.py:680
  90.1 3.4 %all-to-all-start.3 = ((f32[8,8,128]{2,1,0:T(8,128)}), f32[8,8,128]{2,1,0:T(8,128)S(1)}, u32[]{:S(2)}, u32[]{:S(2)}) async-start(f32[8,8,128]{2,1,0:T(8,128)} %get-tuple-element.72), calls=%async_computation.3 | async-start | bytes 65536 | tf_op jit(solution)/shard_map/all_to_all | solution.py:710
  93.5 5.3 %shard_map.193.refs_11_ = bf16[1280,128]{1,0:T(8,128)(2,1)} custom-call(bf16[4,10,128,128]{3,2,1,0:T(8,128)(2,1)} %get-tuple-element.73.refs_0_, bf16[4,8,128,128]{3,2,1,0:T(8,128)(2,1)} %get-tuple-element.74.refs_1_, f32[128,128]{1,0:T(8,128)} %copy-done.6), custom_call_target="tpu_custom_call" | custom-call | flops 1207959552 | bytes 4849664 | tf_op jit(solution)/shard_map/pallas_call | solution.py:680
  98.8 1.3 all-to-all-done.3.refs_6_
  100.1 0.6 copy-done.14
  100.7 5.6 %shard_map.194 = bf16[2048,128]{1,0:T(8,128)(2,1)} custom-call(bf16[4,8,2,128,128]{4,3,2,1,0:T(8,128)(2,1)} %bitcast.46, bf16[4,128,128]{2,1,0:T(8,128)(2,1)} %copy-done.12, bf16[4,2,128,128]{3,2,1,0:T(8,128)(2,1)} %copy-done.10, bf16[4,2,128,128]{3,2,1,0:T(8,128)(2,1)} %copy-done.11, bf16[4,8,128,128]{3,2,1,0:T(8,128)(2,1)} %get-tuple-element.49.refs_1_.refs_6_.refs_4_, ...), custom_call_target="tpu_custom_call" | custom-call | flops 805306368 | bytes 10970112 | tf_op jit(solution)/shard_map/pallas_call | solution.py:680
  106.3 19.6 %all_to_all.31.in_ref = bf16[32,64,128]{2,1,0:T(8,128)(2,1)} all-to-all(bf16[32,64,128]{2,1,0:T(8,128)(2,1)} %bitcast.48), channel_id=1, replica_groups=mesh['rows'=8,'dates'=4] {'rows','dates'}, dimensions={0} | all-to-all | bytes 1048576 | tf_op jit(solution)/shard_map/all_to_all | solution.py:710
  126.0 1.9 %shard_map.195 = bf16[32,64,128]{2,1,0:T(8,128)(2,1)} custom-call(bf16[32,64,128]{2,1,0:T(8,128)(2,1)} %all_to_all.31.in_ref), custom_call_target="tpu_custom_call" | custom-call | tf_op jit(solution)/shard_map/pallas_call | solution.py:725
  127.9 3.1 %all-to-all-start.5 = ((bf16[32,64,128]{2,1,0:T(8,128)(2,1)}), bf16[32,64,128]{2,1,0:T(8,128)(2,1)S(1)}, u32[]{:S(2)}, u32[]{:S(2)}) async-start(bf16[32,64,128]{2,1,0:T(8,128)(2,1)} %shard_map.195), calls=%async_computation.5 | async-start | bytes 1048576 | tf_op jit(solution)/shard_map/all_to_all | solution.py:710
  131.1 0.3 collective-permute-start.3
  131.4 1.7 %collective-permute-start.4 = (bf16[8,32,128]{2,1,0:T(8,128)(2,1)S(1)}, bf16[8,32,128]{2,1,0:T(8,128)(2,1)S(1)}, u32[]{:S(2)}, u32[]{:S(2)}) collective-permute-start(bf16[8,32,128]{2,1,0:T(8,128)(2,1)S(1)} %get-tuple-element.93), channel_id=1, source_target_pairs={{0,2},{1,3},{2,0},{3,1},{4,6},{5,7},{6,4},{7,5},{8,10},{9,11},{10,... | collective-permute-start | bytes 196616 | tf_op jit(solution)/shard_map/ppermute | solution.py:705
  133.0 1.3 collective-permute-start.5
  134.4 2.7 %collective-permute-done.3 = bf16[8,32,128]{2,1,0:T(8,128)(2,1)S(1)} collective-permute-done((bf16[8,32,128]{2,1,0:T(8,128)(2,1)S(1)}, bf16[8,32,128]{2,1,0:T(8,128)(2,1)S(1)}, u32[]{:S(2)}, u32[]{:S(2)}) %collective-permute-start.3) | collective-permute-done | bytes 65568 | tf_op jit(solution)/shard_map/ppermute | solution.py:705
  137.1 2.9 %collective-permute-done.4 = bf16[8,32,128]{2,1,0:T(8,128)(2,1)S(1)} collective-permute-done((bf16[8,32,128]{2,1,0:T(8,128)(2,1)S(1)}, bf16[8,32,128]{2,1,0:T(8,128)(2,1)S(1)}, u32[]{:S(2)}, u32[]{:S(2)}) %collective-permute-start.4) | collective-permute-done | bytes 65568 | tf_op jit(solution)/shard_map/ppermute | solution.py:705
  139.9 0.7 fusion.2
  140.6 5.9 %all-to-all-done.5 = bf16[32,64,128]{2,1,0:T(8,128)(2,1)S(1)} async-done(((bf16[32,64,128]{2,1,0:T(8,128)(2,1)}), bf16[32,64,128]{2,1,0:T(8,128)(2,1)S(1)}, u32[]{:S(2)}, u32[]{:S(2)}) %all-to-all-start.5) | async-done | bytes 524320 | tf_op jit(solution)/shard_map/all_to_all | solution.py:710
  146.5 0.8 copy-done.9
  147.3 2.0 %shard_map.196 = (f32[576,128]{1,0:T(8,128)}, f32[1152,128]{1,0:T(8,128)}, f32[64,128]{1,0:T(8,128)}, f32[4,16]{1,0:T(4,128)}, f32[1,128]{1,0:T(1,128)}, /*index...) custom-call(bf16[2048,128]{1,0:T(8,128)(2,1)} %bitcast.47), custom_call_target="tpu_custom_call" | custom-call | tf_op jit(solution)/shard_map/pallas_call | solution.py:959
  (38 shorter events, 0.2 us)
Async XLA Ops:
  1.6 23.3 %copy-start.13 = (bf16[4,128,128]{2,1,0:T(8,128)(2,1)}, bf16[4,128,128]{2,1,0:T(8,128)(2,1)S(1)}, u32[]{:S(2)}) copy-start(bf16[4,128,128]{2,1,0:T(8,128)(2,1)S(1)} %slice_bitcast_fusion.last_ref) | copy-start | bytes 393220
  1.6 23.2 %copy-start.18 = (s32[16]{0:T(128)S(1)}, s32[16]{0:T(128)}, u32[]{:S(2)}) copy-start(s32[16]{0:T(128)} %param.13) | copy-start | bytes 196
  1.6 10.8 %collective-permute-start = (bf16[4,128,128]{2,1,0:T(8,128)(2,1)S(1)}, bf16[4,128,128]{2,1,0:T(8,128)(2,1)S(1)}, u32[]{:S(2)}, u32[]{:S(2)}) collective-permute-start(bf16[4,128,128]{2,1,0:T(8,128)(2,1)S(1)} %slice_bitcast_fusion.last_ref), channel_id=1, source_target_pairs={{0,4},{4,8},{8,12},{12,16},{16,20},{20,24},{24,28},{1,5},{5,9},{9,... | collective-permute-start | bytes 393224 | tf_op jit(solution)/shard_map/ppermute | solution.py:695
  7.7 17.2 %collective-permute-start.1 = (bf16[4,2,128,128]{3,2,1,0:T(8,128)(2,1)S(1)}, bf16[4,2,128,128]{3,2,1,0:T(8,128)(2,1)S(1)}, u32[]{:S(2)}, u32[]{:S(2)}) collective-permute-start(bf16[4,2,128,128]{3,2,1,0:T(8,128)(2,1)S(1)} %get-tuple-element.90), channel_id=1, source_target_pairs={{0,4},{4,8},{8,12},{12,16},{16,20},{20,24},{24,28},{1,5},{5,9},{9,... | collective-permute-start | bytes 786440 | tf_op jit(solution)/shard_map/ppermute | solution.py:695
  11.1 13.8 %collective-permute-start.2 = (bf16[4,2,128,128]{3,2,1,0:T(8,128)(2,1)S(1)}, bf16[4,2,128,128]{3,2,1,0:T(8,128)(2,1)S(1)}, u32[]{:S(2)}, u32[]{:S(2)}) collective-permute-start(bf16[4,2,128,128]{3,2,1,0:T(8,128)(2,1)S(1)} %get-tuple-element.89), channel_id=1, source_target_pairs={{4,0},{8,4},{12,8},{16,12},{20,16},{24,20},{28,24},{5,1},{9,5},{13... | collective-permute-start | bytes 786440 | tf_op jit(solution)/shard_map/ppermute | solution.py:695
  12.4 0.6 copy-start.12
  17.9 13.6 %all-to-all-start = ((f32[8,8,128]{2,1,0:T(8,128)}), f32[8,8,128]{2,1,0:T(8,128)S(1)}, u32[]{:S(2)}, u32[]{:S(2)}) async-start(f32[8,8,128]{2,1,0:T(8,128)} %get-tuple-element.50), calls=%async_computation | async-start | bytes 65536 | tf_op jit(solution)/shard_map/all_to_all | solution.py:710
  24.9 0.7 copy-start.10
  25.6 0.7 copy-start.11
  31.5 0.6 copy-start.17
  32.1 6.1 %copy-start.15 = (s32[16,8,32]{2,1,0:T(8,128)S(1)}, s32[16,8,32]{2,1,0:T(8,128)}, u32[]{:S(2)}) copy-start(s32[16,8,32]{2,1,0:T(8,128)} %param.14) | copy-start | bytes 49156
  32.1 6.2 %copy-start.16 = (bf16[8,32,128]{2,1,0:T(8,128)(2,1)S(1)}, bf16[8,32,128]{2,1,0:T(8,128)(2,1)}, u32[]{:S(2)}) copy-start(bf16[8,32,128]{2,1,0:T(8,128)(2,1)} %param.15) | copy-start | bytes 196612
  32.1 22.1 %copy-start.3 = (f32[128]{0:T(128)S(1)}, f32[128]{0:T(128)}, u32[]{:S(2)}) copy-start(f32[128]{0:T(128)} %param.20) | copy-start | bytes 1540
  32.1 22.1 %copy-start.4 = (f32[128]{0:T(128)S(1)}, f32[128]{0:T(128)}, u32[]{:S(2)}) copy-start(f32[128]{0:T(128)} %param.21) | copy-start | bytes 1540
  32.1 22.1 %copy-start.7 = (bf16[128,64]{0,1:T(8,128)(2,1)S(1)}, bf16[128,64]{0,1:T(8,128)(2,1)}, u32[]{:S(2)}) copy-start(bf16[128,64]{0,1:T(8,128)(2,1)} %param.22) | copy-start | bytes 49156
  32.1 22.1 %copy-start.8 = (f32[16,4]{0,1:T(4,128)S(1)}, f32[16,4]{0,1:T(4,128)}, u32[]{:S(2)}) copy-start(f32[16,4]{0,1:T(4,128)} %param.23) | copy-start | bytes 772
  44.3 10.0 %all-to-all-start.1 = ((f32[8,8,128]{2,1,0:T(8,128)}), f32[8,8,128]{2,1,0:T(8,128)S(1)}, u32[]{:S(2)}, u32[]{:S(2)}) async-start(f32[8,8,128]{2,1,0:T(8,128)} %get-tuple-element.57), calls=%async_computation.1 | async-start | bytes 65536 | tf_op jit(solution)/shard_map/all_to_all | solution.py:710
  54.3 1.2 copy-start
  59.5 11.4 %copy-start.1 = (f32[8,128]{1,0:T(8,128)}, f32[8,128]{1,0:T(8,128)S(1)}, u32[]{:S(2)}) copy-start(f32[8,128]{1,0:T(8,128)S(1)} %get-tuple-element.64.refs_5_.refs_4_) | copy-start | bytes 12292
  71.0 1.0 copy-start.5
  72.0 0.6 copy-start.6
  72.6 9.7 %copy-start.2 = (f32[8,128]{1,0:T(8,128)}, f32[8,128]{1,0:T(8,128)S(1)}, u32[]{:S(2)}) copy-start(f32[8,128]{1,0:T(8,128)S(1)} %get-tuple-element.78.refs_10_) | copy-start | bytes 12292
  90.1 10.0 %all-to-all-start.3 = ((f32[8,8,128]{2,1,0:T(8,128)}), f32[8,8,128]{2,1,0:T(8,128)S(1)}, u32[]{:S(2)}, u32[]{:S(2)}) async-start(f32[8,8,128]{2,1,0:T(8,128)} %get-tuple-element.72), calls=%async_computation.3 | async-start | bytes 65536 | tf_op jit(solution)/shard_map/all_to_all | solution.py:710
  100.1 0.6 copy-start.14
  127.9 18.6 %all-to-all-start.5 = ((bf16[32,64,128]{2,1,0:T(8,128)(2,1)}), bf16[32,64,128]{2,1,0:T(8,128)(2,1)S(1)}, u32[]{:S(2)}, u32[]{:S(2)}) async-start(bf16[32,64,128]{2,1,0:T(8,128)(2,1)} %shard_map.195), calls=%async_computation.5 | async-start | bytes 1048576 | tf_op jit(solution)/shard_map/all_to_all | solution.py:710
  131.1 6.0 %collective-permute-start.3 = (bf16[8,32,128]{2,1,0:T(8,128)(2,1)S(1)}, bf16[8,32,128]{2,1,0:T(8,128)(2,1)S(1)}, u32[]{:S(2)}, u32[]{:S(2)}) collective-permute-start(bf16[8,32,128]{2,1,0:T(8,128)(2,1)S(1)} %get-tuple-element.91), channel_id=1, source_target_pairs={{0,1},{1,2},{2,3},{3,0},{4,5},{5,6},{6,7},{7,4},{8,9},{9,10},{10,1... | collective-permute-start | bytes 196616 | tf_op jit(solution)/shard_map/ppermute | solution.py:705
  131.4 8.6 %collective-permute-start.4 = (bf16[8,32,128]{2,1,0:T(8,128)(2,1)S(1)}, bf16[8,32,128]{2,1,0:T(8,128)(2,1)S(1)}, u32[]{:S(2)}, u32[]{:S(2)}) collective-permute-start(bf16[8,32,128]{2,1,0:T(8,128)(2,1)S(1)} %get-tuple-element.93), channel_id=1, source_target_pairs={{0,2},{1,3},{2,0},{3,1},{4,6},{5,7},{6,4},{7,5},{8,10},{9,11},{10,... | collective-permute-start | bytes 196616 | tf_op jit(solution)/shard_map/ppermute | solution.py:705
  133.0 6.9 %collective-permute-start.5 = (bf16[8,32,128]{2,1,0:T(8,128)(2,1)S(1)}, bf16[8,32,128]{2,1,0:T(8,128)(2,1)S(1)}, u32[]{:S(2)}, u32[]{:S(2)}) collective-permute-start(bf16[8,32,128]{2,1,0:T(8,128)(2,1)S(1)} %get-tuple-element.92), channel_id=1, source_target_pairs={{0,3},{1,0},{2,1},{3,2},{4,7},{5,4},{6,5},{7,6},{8,11},{9,8},{10,9... | collective-permute-start | bytes 196616 | tf_op jit(solution)/shard_map/ppermute | solution.py:705
  146.5 0.8 copy-start.9

commit v4 on v3

--- a/solution.py
+++ b/solution.py
@@ -15,9 +15,6 @@
 
 
 MIB = 1 << 20
-
-
-MEMORY = 60
 
 
 F32 = jnp.float32
@@ -226,6 +223,20 @@
     score_ref[...] = jnp.concatenate(split(folded), axis=-1)
 
 
+def source_of(turn_ref, device, devices):
+    return (device + devices - turn_ref[0]) % devices
+
+
+def upstream_rows(grad_ref, turn_ref, rows, cols):
+    devices = grad_ref.shape[0]
+    piece = cols // devices
+    parts = [
+        grad_ref[source_of(turn_ref, device, devices), : rows * piece].reshape(rows, piece, -1)
+        for device in range(devices)
+    ]
+    return jnp.concatenate(parts, axis=1)
+
+
 def score_kernel(
     dates,
     norm_count,
@@ -237,6 +248,7 @@
     shift_ref,
     grad_ref,
     valid_ref,
+    turn_ref,
     key_ref,
     query_ref,
     feat_ref,
@@ -266,19 +278,25 @@
     linear = block_ref[0].astype(F32) * scale + shift
     features = (linear * sigmoid(linear) + encoding(day_ref[date], width)).astype(BF16)
     feat_ref[0] = features
-    upstream = grad_ref[...]
-    upstream = jnp.stack([upstream[:, row].reshape(cols, width) for row in range(rows)])
+    upstream = upstream_rows(grad_ref, turn_ref, rows, cols)
     parts = split(upstream.astype(F32) * features.astype(F32))
     parts = jnp.concatenate(parts, axis=-1).reshape(rows * cols, 2 * width)
     attn = product(parts, spread_ref[...], 1, 0).reshape(rows, cols, width) * grad_scale
     both = product(features.reshape(rows * cols, width), score_ref[...], 1, 0)
     scores = (both[:, :width] + both[:, width:]).reshape(rows, cols, width)
+    devices = grad_ref.shape[0]
+    valid = jnp.zeros((rows, width), F32)
+    for device in range(devices):
+        piece = valid_ref[
+            source_of(turn_ref, device, devices), pl.ds(pl.multiple_of(date * rows, rows), rows), :
+        ]
+        valid = valid + pltpu.roll(piece, device * (cols // devices), 1)
     diagonal = lax.broadcasted_iota(jnp.int32, (cols, cols), 0) == lax.broadcasted_iota(
         jnp.int32, (cols, cols), 1
     )
     ones = jnp.ones((cols, width), BF16)
     clear = jnp.concatenate(
-        [jnp.where(diagonal, valid_ref[0, row : row + 1], 0.0) for row in range(rows)], axis=0
+        [jnp.where(diagonal, valid[row : row + 1], 0.0) for row in range(rows)], axis=0
     ).astype(BF16)
     clear = product(clear, ones, 1, 0).reshape(rows, cols, width)
     exponent = clear * jnp.exp(scores)
@@ -313,6 +331,7 @@
     shift_ref,
     query_ref,
     grad_ref,
+    turn_ref,
     key_ref,
     grad_out_ref,
     part_ref,
@@ -353,8 +372,7 @@
     lane = lax.broadcasted_iota(jnp.int32, spread_grad.shape, 2) % (width // 16)
     key_grads = jnp.where(lane == 5, rest, spread_grad).astype(BF16).reshape(rows * cols, width)
     key_out_ref[...] += product(features.reshape(rows * cols, width), key_grads, 0, 0)
-    upstream = grad_ref[...]
-    upstream = jnp.stack([upstream[:, row].reshape(cols, width) for row in range(rows)])
+    upstream = upstream_rows(grad_ref, turn_ref, rows, cols)
     feat_grad = rounded * (upstream.astype(F32) * grad_scale) + product(
         key_grads, key_ref[...], 1, 1
     ).reshape(rows, cols, width)
@@ -628,31 +646,38 @@
 
 
 def streamed(kernel, dates, kinds, out_count):
-    count = kinds.count("date")
+    places = [place for place, kind in enumerate(kinds) if kind != "scalar"]
 
     def body(*refs):
         inputs, rest = list(refs[: len(kinds)]), refs[len(kinds) :]
         outputs, scratch = rest[:out_count], rest[out_count:]
+        count = len(places)
         buffers, ready, scratch = scratch[:count], scratch[count], scratch[count + 1 :]
         date = pl.program_id(0)
-        places = [place for place, kind in enumerate(kinds) if kind == "date"]
+        views = list(inputs)
 
         def copy(index, step):
-            return pltpu.make_async_copy(
-                inputs[places[index]].at[step], buffers[index].at[step], ready.at[index, step]
-            )
+            source, target = inputs[places[index]], buffers[index]
+            if kinds[places[index]] == "date":
+                source, target = source.at[step], target.at[step]
+            return pltpu.make_async_copy(source, target, ready.at[index, step])
 
         @pl.when(date == 0)
         def _():
             for step in range(dates):
-                for index in range(count):
-                    copy(index, step).start()
-
-        for index in range(count):
-            copy(index, date).wait()
-        views = list(inputs)
+                for index, place in enumerate(places):
+                    if step == 0 or kinds[place] == "date":
+                        copy(index, step).start()
+            for index, place in enumerate(places):
+                if kinds[place] == "all":
+                    copy(index, 0).wait()
+
         for index, place in enumerate(places):
-            views[place] = buffers[index].at[pl.ds(date, 1)]
+            if kinds[place] == "date":
+                copy(index, date).wait()
+                views[place] = buffers[index].at[pl.ds(date, 1)]
+            else:
+                views[place] = buffers[index]
         kernel(*views, *outputs, *scratch)
 
     return body
@@ -663,28 +688,30 @@
     return pl.BlockSpec(tuple(shape), lambda date: zeros)
 
 
-def call(kernel, dates, inputs, outputs, scratch, flops, memory=MEMORY):
+def call(kernel, dates, inputs, outputs, scratch, flops, stream=False):
     in_specs, arrays, buffers = [], [], []
     for kind, array in inputs:
         arrays.append(array)
         if kind == "scalar":
             in_specs.append(pl.BlockSpec(memory_space=pltpu.SMEM))
-        elif kind == "date":
+        elif stream:
             in_specs.append(pl.BlockSpec(memory_space=pl.ANY))
             buffers.append(pltpu.VMEM(array.shape, array.dtype))
         else:
-            in_specs.append(whole(array.shape))
+            in_specs.append((per_date if kind == "date" else whole)(array.shape))
     out_specs = [(per_date if kind == "date" else whole)(shape) for kind, shape, _ in outputs]
     moved = sum(array.size * array.dtype.itemsize for array in arrays)
-    ready = pltpu.SemaphoreType.DMA((len(buffers), dates))
+    if stream:
+        kernel = streamed(kernel, dates, [kind for kind, _ in inputs], len(outputs))
+        scratch = buffers + [pltpu.SemaphoreType.DMA((len(buffers), dates))] + scratch
     return pl.pallas_call(
-        streamed(kernel, dates, [kind for kind, _ in inputs], len(outputs)),
+        kernel,
         grid=(dates,),
         in_specs=in_specs,
         out_specs=out_specs,
         out_shape=[jax.ShapeDtypeStruct(shape, dtype) for _, shape, dtype in outputs],
-        scratch_shapes=buffers + [ready] + scratch,
-        compiler_params=pltpu.CompilerParams(vmem_limit_bytes=memory * MIB),
+        scratch_shapes=scratch,
+        compiler_params=pltpu.CompilerParams(vmem_limit_bytes=(60 if stream else 24) * MIB),
         cost_estimate=pl.CostEstimate(flops=flops, bytes_accessed=2 * moved, transcendentals=0),
     )(*arrays)
 
@@ -693,6 +720,15 @@
     devices = lax.axis_size("rows")
     pairs = [(i, i + by) for i in range(devices) if 0 <= i + by < devices]
     return lax.ppermute(array, "rows", pairs)
+
+
+def turned(array):
+    devices = lax.axis_size("dates")
+    pieces = [array]
+    for step in range(1, devices):
+        pairs = [((i + step) % devices, i) for i in range(devices)]
+        pieces.append(lax.ppermute(array, "dates", pairs))
+    return jnp.stack(pieces)
 
 
 def sum_of_parts(parts):
@@ -725,7 +761,7 @@
     spread = pl.pallas_call(
         total_kernel,
         out_shape=jax.ShapeDtypeStruct(pieces.shape, BF16),
-        compiler_params=pltpu.CompilerParams(vmem_limit_bytes=MEMORY * MIB),
+        compiler_params=pltpu.CompilerParams(vmem_limit_bytes=16 * MIB),
     )(pieces)
     count, rows, width = pieces.shape
     return exchange(spread, ("rows", "dates")).reshape(count * rows, width)
@@ -785,9 +821,18 @@
         edge_kernel,
         out_shape=[jax.ShapeDtypeStruct(edge_rows, BF16)] * 2,
         scratch_shapes=[pltpu.VMEM((3 * pair_width, 2 * width), BF16)],
-        compiler_params=pltpu.CompilerParams(vmem_limit_bytes=MEMORY * MIB),
+        compiler_params=pltpu.CompilerParams(vmem_limit_bytes=16 * MIB),
     )(high, above, last, below, conv_weight)
+    valid, out_grad, _ = lax.optimization_barrier((valid, out_grad, halo_up))
+    grad_rows = out_grad.size // width
+    valid_rows = valid.astype(BF16).reshape(valid.shape[0] * rows, -1)
+    valid_rows = jnp.pad(valid_rows, ((0, 0), (0, width - valid_rows.shape[1])))
+    packed = jnp.concatenate([out_grad.reshape(grad_rows, width), valid_rows])
+    sources = turned(packed)
+    clear = lax.dynamic_slice_in_dim(sources, grad_rows + date_start * rows, dates * rows, 1)
+    clear = clear.astype(F32)
     days = lax.dynamic_slice_in_dim(day_index, date_start, dates, 0)
+    turn = lax.axis_index("dates").reshape(1)
     place = lax.axis_index("rows").reshape(1)
 
     block_out, hidden, first_norm, sums = call(
@@ -813,16 +858,6 @@
         9 * flops,
     )
     stats = exchange(sums, "rows")
-    sums, valid, out_grad = lax.optimization_barrier((sums, valid, out_grad))
-    grad_rows, valid_rows = out_grad.size // width, valid.size // width
-    packed = jnp.concatenate(
-        [out_grad.reshape(grad_rows, width), valid.astype(BF16).reshape(valid_rows, width)]
-    )
-    packed = gather(packed[None], "dates")
-    grads_here = packed[:, :grad_rows].reshape((date_devs,) + out_grad.shape)
-    clear = packed[:, grad_rows:].reshape((date_devs,) + valid.shape)
-    clear = lax.dynamic_slice_in_dim(clear, date_start, dates, 1)
-    clear = clear.transpose(1, 2, 0, 3).reshape(dates, rows, cols).astype(F32)
     features, exponent, attn, norm, packed, key_wide, query_wide = call(
         functools.partial(score_kernel, dates, norm_count, grad_scale),
         dates,
@@ -832,8 +867,9 @@
             ("all", stats),
             ("all", gn_gain),
             ("all", gn_shift),
-            ("all", grads_here),
-            ("date", clear),
+            ("all", sources),
+            ("all", clear),
+            ("scalar", turn),
             ("all", key_weight.T),
             ("all", queries.T),
         ],
@@ -853,7 +889,6 @@
             pltpu.VMEM((width, 2 * width), BF16),
         ],
         5 * flops,
-        24,
     )
     packed = gather(packed, "dates")
     block_grad, attended, key_part, vectors, sums = call(
@@ -869,7 +904,8 @@
             ("all", gn_gain),
             ("all", gn_shift),
             ("all", query_wide),
-            ("all", grads_here),
+            ("all", sources),
+            ("scalar", turn),
             ("all", key_wide),
         ],
         [
@@ -881,7 +917,6 @@
         ],
         [pltpu.VMEM(frame[1:], F32)] * 3,
         5 * flops,
-        24,
     )
     tails = exchange(sums, "rows")
     pre_grad, linear_grad, first_vectors, sums = call(
@@ -913,6 +948,7 @@
             pltpu.VMEM((rows + 4, cols, width), BF16),
         ],
         9 * flops,
+        True,
     )
     tails = exchange(sums, "rows")
     (block_rows,) = call(
@@ -922,6 +958,7 @@
         [("all", (10 * width, width), BF16)],
         [pltpu.VMEM((3 * width, 3 * width), F32)],
         9 * flops,
+        True,
     )
     tails, block_rows = lax.optimization_barrier((tails, block_rows))
     conv_count = 9 * pair_width // 2 + 32
@@ -945,6 +982,7 @@
         [("all", (padded_count(10 * width + conv_count, devices), width), BF16)],
         [pltpu.VMEM((2 * dates, width), F32), pltpu.VMEM((3 * pair_width, 2 * width), F32)],
         6 * flops,
+        True,
     )
     pieces = scatter(rows_all)
     attended, _ = lax.optimization_barrier((attended, rows_all))
@@ -959,7 +997,7 @@
     conv_total, block_total, key_total, query_total, *totals = pl.pallas_call(
         functools.partial(final_kernel, depth),
         out_shape=[jax.ShapeDtypeStruct(shape, F32) for shape in shapes],
-        compiler_params=pltpu.CompilerParams(vmem_limit_bytes=MEMORY * MIB),
+        compiler_params=pltpu.CompilerParams(vmem_limit_bytes=16 * MIB),
     )(rows_all)
     totals = [total.reshape(width) for total in totals]
     return (

time: 150 us -> 144 us (0.960)
  Pallas kernels: 44.1 us -> 32.8 us
  waiting for transfers between devices: 22.1 us -> 29.4 us
  blocking collectives: 42.4 us -> 35.7 us
  local copies, waits for them, and re-layouts: 9.36 us -> 12.4 us
  starting transfers between devices: 29.7 us -> 31.5 us
    pallas_call x7, Pallas kernels: 37.8 us -> 30.5 us  [call(): pl.pallas_call(kernel, grid=(dates,), in_specs=in_specs, out_specs=out_sp...]
    ppermute x3, waiting for transfers between devices: 0.01 us -> 6.25 us  [shifted(): return lax.ppermute(array, 'rows', pairs)]
    all_gather x2 -> x1, blocking collectives: 13.1 us -> 7.18 us  [gather(): return lax.all_gather(array, axis, axis=0, tiled=True)]
    unnamed x39 -> x54, local copies, waits for them, and re-layouts: 6.95 us -> 9.58 us
    pallas_call x1, Pallas kernels: 2.28 us -> 0.45 us  [local(): pl.pallas_call(edge_kernel, out_shape=[jax.ShapeDtypeStruct(edge_rows, BF...]
    ppermute x0 -> x3, starting transfers between devices: none -> 1.79 us  [turned(): pieces.append(lax.ppermute(array, 'dates', pairs))]
  transfers between devices with their start and end apart: 10 -> 13, of which waited for: 6 -> 7; matrix products, arithmetic and copies ran while one was open for 1% -> 2% of each run, Pallas kernels for 8% -> 8%
where the time goes in v4:
time: 144 us
  blocking collectives  35.7 us (25%)
  Pallas kernels  32.8 us (23%)
  starting transfers between devices  31.5 us (22%)
  waiting for transfers between devices  29.4 us (20%)
  local copies, waits for them, and re-layouts  12.4 us (9%)
    pallas_call x7, Pallas kernels, call(): pl.pallas_call(kernel, grid=(dates,), in_specs=in_specs, out_specs=out_sp...  30.5 us
    all_to_all x2, blocking collectives, exchange(): return lax.all_to_all(pieces, axes, split_axis=0, concat_axis=0, tiled=True)  28.5 us
    all_to_all x4, waiting for transfers between devices, exchange(): return lax.all_to_all(pieces, axes, split_axis=0, concat_axis=0, tiled=True)  17.6 us
    all_to_all x4, starting transfers between devices, exchange(): return lax.all_to_all(pieces, axes, split_axis=0, concat_axis=0, tiled=True)  15.5 us
    ppermute x3, starting transfers between devices, shifted(): return lax.ppermute(array, 'rows', pairs)  10.9 us
    unnamed x54, local copies, waits for them, and re-layouts  9.58 us
    all_gather x1, blocking collectives, gather(): return lax.all_gather(array, axis, axis=0, tiled=True)  7.18 us
    ppermute x3, waiting for transfers between devices, shifted(): return lax.ppermute(array, 'rows', pairs)  6.25 us
  transfers between devices with their start and end apart: 13, of which 7 were waited for; matrix products, arithmetic and copies ran while one was open for 2% of the time, Pallas kernels for 8%

profile of v4, /device:TPU:0, one launch (start us, length us, event | category | flops | bytes accessed | tf_op | source)
XLA Modules:
  0.0 143.5 jit_solution(12754530600733308526)
XLA Ops:
  0.6 1.1 fusion.6
  1.7 4.9 %collective-permute-start.1 = (bf16[4,2,128,128]{3,2,1,0:T(8,128)(2,1)S(1)}, bf16[4,2,128,128]{3,2,1,0:T(8,128)(2,1)S(1)}, u32[]{:S(2)}, u32[]{:S(2)}) collective-permute-start(bf16[4,2,128,128]{3,2,1,0:T(8,128)(2,1)S(1)} %get-tuple-element.90), channel_id=1, source_target_pairs={{0,4},{4,8},{8,12},{12,16},{16,20},{20,24},{24,28},{1,5},{5,9},{9,... | collective-permute-start | bytes 786440 | tf_op jit(solution)/shard_map/ppermute | solution.py:722
  6.6 1.4 collective-permute-start.2
  8.1 1.0 slice_bitcast_fusion.last_ref
  9.0 4.6 %collective-permute-start = (bf16[4,128,128]{2,1,0:T(8,128)(2,1)S(1)}, bf16[4,128,128]{2,1,0:T(8,128)(2,1)S(1)}, u32[]{:S(2)}, u32[]{:S(2)}) collective-permute-start(bf16[4,128,128]{2,1,0:T(8,128)(2,1)S(1)} %slice_bitcast_fusion.last_ref), channel_id=1, source_target_pairs={{0,4},{4,8},{8,12},{12,16},{16,20},{20,24},{24,28},{1,5},{5,9},{9,... | collective-permute-start | bytes 393224 | tf_op jit(solution)/shard_map/ppermute | solution.py:722
  13.6 0.7 dynamic_slice.19.day_ref
  14.3 6.2 %collective-permute-done.above_ref.refs_1_ = bf16[4,128,128]{2,1,0:T(8,128)(2,1)S(1)} collective-permute-done((bf16[4,128,128]{2,1,0:T(8,128)(2,1)S(1)}, bf16[4,128,128]{2,1,0:T(8,128)(2,1)S(1)}, u32[]{:S(2)}, u32[]{:S(2)}) %collective-permute-start) | collective-permute-done | bytes 131104 | tf_op jit(solution)/shard_map/ppermute | solution.py:722
  20.6 1.6 %copy-done = bf16[4,16,128,128]{3,2,1,0:T(8,128)(2,1)S(1)} copy-done((bf16[4,16,128,128]{3,2,1,0:T(8,128)(2,1)S(1)}, bf16[4,16,128,128]{3,2,1,0:T(8,128)(2,1)}, u32[]{:S(2)}) %copy-start) | copy-done | bytes 2097176
  22.2 0.9 copy-done.6
  23.1 2.5 %shard_map.187 = (bf16[4,8,128,128]{3,2,1,0:T(8,128)(2,1)S(1)}, f32[8,8,128]{2,1,0:T(8,128)}) custom-call(bf16[4,8,2,128,128]{4,3,2,1,0:T(8,128)(2,1)S(1)} %bitcast.41, bf16[4,128,128]{2,1,0:T(8,128)(2,1)S(1)} %collective-permute-done.above_ref.refs_1_, bf16[3,3,64,128]{3,2,1,0:T(8,128)(2,1)S(1)} %copy-done.6), custom_call_target="tpu_custom_call" | custom-call | flops 805306368 | bytes 4751360 | tf_op jit(solution)/shard_map/pallas_call | solution.py:707
  25.7 5.8 %all-to-all-start = ((f32[8,8,128]{2,1,0:T(8,128)}), f32[8,8,128]{2,1,0:T(8,128)S(1)}, u32[]{:S(2)}, u32[]{:S(2)}) async-start(f32[8,8,128]{2,1,0:T(8,128)} %get-tuple-element.50), calls=%async_computation | async-start | bytes 65536 | tf_op jit(solution)/shard_map/all_to_all | solution.py:746
  31.5 0.5 shard_map.188
  32.0 0.6 copy-done.15
  32.6 0.6 copy-done.17
  33.3 0.1 collective-permute-start.3
  33.4 1.6 %collective-permute-start.4 = (bf16[384,128]{1,0:T(8,128)(2,1)S(1)}, bf16[384,128]{1,0:T(8,128)(2,1)S(1)}, u32[]{:S(2)}, u32[]{:S(2)}) collective-permute-start(bf16[384,128]{1,0:T(8,128)(2,1)S(1)} %get-tuple-element.95), channel_id=1, source_target_pairs={{2,0},{3,1},{0,2},{1,3},{6,4},{7,5},{4,6},{5,7},{10,8},{11,9},{8,1... | collective-permute-start | bytes 294920 | tf_op jit(solution)/shard_map/ppermute | solution.py:730
  34.9 0.2 collective-permute-start.5
  35.1 3.0 %all-to-all-done.stats_ref = f32[8,8,128]{2,1,0:T(8,128)S(1)} async-done(((f32[8,8,128]{2,1,0:T(8,128)}), f32[8,8,128]{2,1,0:T(8,128)S(1)}, u32[]{:S(2)}, u32[]{:S(2)}) %all-to-all-start) | async-done | bytes 32800 | tf_op jit(solution)/shard_map/all_to_all | solution.py:746
  38.2 0.9 copy-done.16
  39.1 0.9 copy-done.18
  40.0 3.7 %shard_map.189 = (bf16[4,8,128,128]{3,2,1,0:T(8,128)(2,1)S(1)}, bf16[4,10,128,128]{3,2,1,0:T(8,128)(2,1)S(1)}, f32[8,128]{1,0:T(8,128)S(1)}, f32[8,8,128]{2,1,0:T(8,128)}) custom-call(s32[1]{0:T(128)} %bitcast.edge_ref.refs_0_, bf16[4,8,128,128]{3,2,1,0:T(8,128)(2,1)S(1)} %get-tuple-element.49.conv_ref.refs_6_.refs_4_, bf16[4,128,128]{2,1,0:T(8,128)(2,1)S(1)} %copy-done.16, ...), custom_call_target="tpu_custom_call" | custom-call | flops 1207959552 | bytes 3278856 | tf_op jit(solution)/shard_map/pallas_call | solution.py:707
  43.7 0.6 copy-done.8
  44.3 1.1 copy-done.23
  45.3 3.3 %all-to-all-start.1 = ((f32[8,8,128]{2,1,0:T(8,128)}), f32[8,8,128]{2,1,0:T(8,128)S(1)}, u32[]{:S(2)}, u32[]{:S(2)}) async-start(f32[8,8,128]{2,1,0:T(8,128)} %get-tuple-element.57), calls=%async_computation.1 | async-start | bytes 65536 | tf_op jit(solution)/shard_map/all_to_all | solution.py:746
  48.8 6.5 %all-to-all-done.1.stats_ref = f32[8,8,128]{2,1,0:T(8,128)S(1)} async-done(((f32[8,8,128]{2,1,0:T(8,128)}), f32[8,8,128]{2,1,0:T(8,128)S(1)}, u32[]{:S(2)}, u32[]{:S(2)}) %all-to-all-start.1) | async-done | bytes 32800 | tf_op jit(solution)/shard_map/all_to_all | solution.py:746
  55.3 3.8 %shard_map.190 = (bf16[4,8,128,128]{3,2,1,0:T(8,128)(2,1)S(1)}, f32[4,8,128,128]{3,2,1,0:T(8,128)S(1)}, f32[4,8,128,128]{3,2,1,0:T(8,128)S(1)}, f32[8,128]{1,0:T...) custom-call(s32[4]{0:T(128)S(1)} %dynamic_slice.19.day_ref, ...), custom_call_target="tpu_custom_call" | custom-call | flops 671088640 | bytes 3115560 | tf_op jit(solution)/shard_map/pallas_call | solution.py:707
  59.2 7.2 %all_gather.3.packed_ref = f32[4,2,128,128]{3,2,1,0:T(8,128)S(1)} all-gather(f32[1,2,128,128]{3,2,1,0:T(8,128)S(1)} %get-tuple-element.60), channel_id=1, replica_groups=mesh['rows'=8,'dates'=4] {'dates'}, dimensions={0}, use_global_device_ids=true | all-gather | bytes 655360 | tf_op jit(solution)/shard_map/all_gather | solution.py:750
  66.4 3.8 %shard_map.191 = (bf16[4,8,128,128]{3,2,1,0:T(8,128)(2,1)S(1)}, bf16[4,8,32,128]{3,2,1,0:T(8,128)(2,1)S(1)}, f32[128,128]{1,0:T(8,128)S(1)}, f32[8,128]{1,0:T(8,128)S(1)}, f32[8,8,128]{2,1,0:T(8,128)S(1)}) custom-call(f32[4,2,128,128]{3,2,1,0:T(8,128)S(1)} %all_gather.3.packed_ref, bf16[4,8,128,128]{3,2,1,0:T(8,128)(2,1)S(1)} %get-tuple-element.61.feat_ref, ...), custom_call_target="tpu_custom_call" | custom-call | flops 671088640 | bytes 14501896 | tf_op jit(solution)/shard_map/pallas_call | solution.py:707
  70.2 1.0 copy-done.13
  71.2 0.6 copy-done.19
  71.8 9.7 %all_to_all.30.refs_3_ = f32[8,8,128]{2,1,0:T(8,128)} all-to-all(f32[8,8,128]{2,1,0:T(8,128)S(1)} %get-tuple-element.69), channel_id=1, replica_groups=mesh['rows'=8,'dates'=4] {'rows'}, dimensions={0} | all-to-all | bytes 65536 | tf_op jit(solution)/shard_map/all_to_all | solution.py:746
  81.6 7.1 %shard_map.192 = (bf16[4,8,128,128]{3,2,1,0:T(8,128)(2,1)}, bf16[4,10,128,128]{3,2,1,0:T(8,128)(2,1)}, f32[8,128]{1,0:T(8,128)}, f32[8,8,128]{2,1,0:T(8,128)}) custom-call(s32[1]{0:T(128)} %bitcast.edge_ref.refs_0_, bf16[4,8,128,128]{3,2,1,0:T(8,128)(2,1)} %copy-done.13, bf16[4,8,128,128]{3,2,1,0:T(8,128)(2,1)} %copy-done.1, ...), custom_call_target="tpu_custom_call" | custom-call | flops 1207959552 | bytes 7489544 | tf_op jit(solution)/shard_map/pallas_call | solution.py:707
  88.7 3.4 %all-to-all-start.3 = ((f32[8,8,128]{2,1,0:T(8,128)}), f32[8,8,128]{2,1,0:T(8,128)S(1)}, u32[]{:S(2)}, u32[]{:S(2)}) async-start(f32[8,8,128]{2,1,0:T(8,128)} %get-tuple-element.72), calls=%async_computation.3 | async-start | bytes 65536 | tf_op jit(solution)/shard_map/all_to_all | solution.py:746
  92.1 4.5 %shard_map.193.refs_11_ = bf16[1280,128]{1,0:T(8,128)(2,1)} custom-call(bf16[4,10,128,128]{3,2,1,0:T(8,128)(2,1)} %copy-done.23, bf16[4,8,128,128]{3,2,1,0:T(8,128)(2,1)} %get-tuple-element.74.refs_1_, f32[128,128]{1,0:T(8,128)} %copy-done.19), custom_call_target="tpu_custom_call" | custom-call | flops 1207959552 | bytes 4849664 | tf_op jit(solution)/shard_map/pallas_call | solution.py:707
  96.6 2.1 %all-to-all-done.3.refs_6_ = f32[8,8,128]{2,1,0:T(8,128)S(1)} async-done(((f32[8,8,128]{2,1,0:T(8,128)}), f32[8,8,128]{2,1,0:T(8,128)S(1)}, u32[]{:S(2)}, u32[]{:S(2)}) %all-to-all-start.3) | async-done | bytes 32800 | tf_op jit(solution)/shard_map/all_to_all | solution.py:746
  98.7 0.6 copy-done.24
  99.3 4.9 %shard_map.194 = bf16[2048,128]{1,0:T(8,128)(2,1)} custom-call(bf16[4,8,2,128,128]{4,3,2,1,0:T(8,128)(2,1)} %bitcast.40, bf16[4,128,128]{2,1,0:T(8,128)(2,1)} %copy-done.5, bf16[4,2,128,128]{3,2,1,0:T(8,128)(2,1)} %copy-done.3, bf16[4,2,128,128]{3,2,1,0:T(8,128)(2,1)} %copy-done.4, bf16[4,8,128,128]{3,2,1,0:T(8,128)(2,1)} %copy-done.2, ...), custom_call_target="tpu_custom_call" | custom-call | flops 805306368 | bytes 10970112 | tf_op jit(solution)/shard_map/pallas_call | solution.py:707
  104.2 18.8 %all_to_all.31.in_ref = bf16[32,64,128]{2,1,0:T(8,128)(2,1)S(1)} all-to-all(bf16[32,64,128]{2,1,0:T(8,128)(2,1)} %bitcast.54), channel_id=1, replica_groups=mesh['rows'=8,'dates'=4] {'rows','dates'}, dimensions={0} | all-to-all | bytes 1048576 | tf_op jit(solution)/shard_map/all_to_all | solution.py:746
  123.0 0.9 shard_map.195
  123.9 3.1 %all-to-all-start.5 = ((bf16[32,64,128]{2,1,0:T(8,128)(2,1)}), bf16[32,64,128]{2,1,0:T(8,128)(2,1)S(1)}, u32[]{:S(2)}, u32[]{:S(2)}) async-start(bf16[32,64,128]{2,1,0:T(8,128)(2,1)} %shard_map.195), calls=%async_computation.5 | async-start | bytes 1048576 | tf_op jit(solution)/shard_map/all_to_all | solution.py:746
  127.1 0.3 collective-permute-start.6
  127.4 1.7 %collective-permute-start.7 = (bf16[8,32,128]{2,1,0:T(8,128)(2,1)S(1)}, bf16[8,32,128]{2,1,0:T(8,128)(2,1)S(1)}, u32[]{:S(2)}, u32[]{:S(2)}) collective-permute-start(bf16[8,32,128]{2,1,0:T(8,128)(2,1)S(1)} %get-tuple-element.93), channel_id=1, source_target_pairs={{0,2},{1,3},{2,0},{3,1},{4,6},{5,7},{6,4},{7,5},{8,10},{9,11},{10,... | collective-permute-start | bytes 196616 | tf_op jit(solution)/shard_map/ppermute | solution.py:741
  129.0 1.3 collective-permute-start.8
  130.4 2.7 %collective-permute-done.6 = bf16[8,32,128]{2,1,0:T(8,128)(2,1)S(1)} collective-permute-done((bf16[8,32,128]{2,1,0:T(8,128)(2,1)S(1)}, bf16[8,32,128]{2,1,0:T(8,128)(2,1)S(1)}, u32[]{:S(2)}, u32[]{:S(2)}) %collective-permute-start.6) | collective-permute-done | bytes 65568 | tf_op jit(solution)/shard_map/ppermute | solution.py:741
  133.1 2.9 %collective-permute-done.7 = bf16[8,32,128]{2,1,0:T(8,128)(2,1)S(1)} collective-permute-done((bf16[8,32,128]{2,1,0:T(8,128)(2,1)S(1)}, bf16[8,32,128]{2,1,0:T(8,128)(2,1)S(1)}, u32[]{:S(2)}, u32[]{:S(2)}) %collective-permute-start.7) | collective-permute-done | bytes 65568 | tf_op jit(solution)/shard_map/ppermute | solution.py:741
  136.0 0.7 fusion.3
  136.6 5.9 %all-to-all-done.5 = bf16[32,64,128]{2,1,0:T(8,128)(2,1)S(1)} async-done(((bf16[32,64,128]{2,1,0:T(8,128)(2,1)}), bf16[32,64,128]{2,1,0:T(8,128)(2,1)S(1)}, u32[]{:S(2)}, u32[]{:S(2)}) %all-to-all-start.5) | async-done | bytes 524320 | tf_op jit(solution)/shard_map/all_to_all | solution.py:746
  142.5 1.0 shard_map.196
  (54 shorter events, 0.2 us)
Async XLA Ops:
  1.7 29.7 %collective-permute-start.1 = (bf16[4,2,128,128]{3,2,1,0:T(8,128)(2,1)S(1)}, bf16[4,2,128,128]{3,2,1,0:T(8,128)(2,1)S(1)}, u32[]{:S(2)}, u32[]{:S(2)}) collective-permute-start(bf16[4,2,128,128]{3,2,1,0:T(8,128)(2,1)S(1)} %get-tuple-element.90), channel_id=1, source_target_pairs={{0,4},{4,8},{8,12},{12,16},{16,20},{20,24},{24,28},{1,5},{5,9},{9,... | collective-permute-start | bytes 786440 | tf_op jit(solution)/shard_map/ppermute | solution.py:722
  6.6 26.6 %copy-start.25 = (s32[16,8,32]{2,1,0:T(8,128)S(1)}, s32[16,8,32]{2,1,0:T(8,128)}, u32[]{:S(2)}) copy-start(s32[16,8,32]{2,1,0:T(8,128)} %param.14) | copy-start | bytes 49156
  6.6 24.8 %collective-permute-start.2 = (bf16[4,2,128,128]{3,2,1,0:T(8,128)(2,1)S(1)}, bf16[4,2,128,128]{3,2,1,0:T(8,128)(2,1)S(1)}, u32[]{:S(2)}, u32[]{:S(2)}) collective-permute-start(bf16[4,2,128,128]{3,2,1,0:T(8,128)(2,1)S(1)} %get-tuple-element.89), channel_id=1, source_target_pairs={{4,0},{8,4},{12,8},{16,12},{20,16},{24,20},{28,24},{5,1},{9,5},{13... | collective-permute-start | bytes 786440 | tf_op jit(solution)/shard_map/ppermute | solution.py:722
  8.1 25.2 %copy-start.26 = (bf16[8,32,128]{2,1,0:T(8,128)(2,1)S(1)}, bf16[8,32,128]{2,1,0:T(8,128)(2,1)}, u32[]{:S(2)}) copy-start(bf16[8,32,128]{2,1,0:T(8,128)(2,1)} %param.15) | copy-start | bytes 196612
  9.0 11.5 %collective-permute-start = (bf16[4,128,128]{2,1,0:T(8,128)(2,1)S(1)}, bf16[4,128,128]{2,1,0:T(8,128)(2,1)S(1)}, u32[]{:S(2)}, u32[]{:S(2)}) collective-permute-start(bf16[4,128,128]{2,1,0:T(8,128)(2,1)S(1)} %slice_bitcast_fusion.last_ref), channel_id=1, source_target_pairs={{0,4},{4,8},{8,12},{12,16},{16,20},{20,24},{24,28},{1,5},{5,9},{9,... | collective-permute-start | bytes 393224 | tf_op jit(solution)/shard_map/ppermute | solution.py:722
  20.6 12.7 %copy-start.5 = (bf16[4,128,128]{2,1,0:T(8,128)(2,1)}, bf16[4,128,128]{2,1,0:T(8,128)(2,1)S(1)}, u32[]{:S(2)}) copy-start(bf16[4,128,128]{2,1,0:T(8,128)(2,1)S(1)} %collective-permute-done.above_ref.refs_1_) | copy-start | bytes 393220
  20.6 1.6 %copy-start = (bf16[4,16,128,128]{3,2,1,0:T(8,128)(2,1)S(1)}, bf16[4,16,128,128]{3,2,1,0:T(8,128)(2,1)}, u32[]{:S(2)}) copy-start(bf16[4,16,128,128]{3,2,1,0:T(8,128)(2,1)} %param.12) | copy-start | bytes 6291460
  22.2 0.9 copy-start.6
  23.1 15.0 %copy-start.12 = (f32[128]{0:T(128)S(1)}, f32[128]{0:T(128)}, u32[]{:S(2)}) copy-start(f32[128]{0:T(128)} %param.17) | copy-start | bytes 1540
  23.1 15.0 %copy-start.14 = (bf16[3,3,128,128]{3,2,1,0:T(8,128)(2,1)S(1)}, bf16[3,3,128,128]{3,2,1,0:T(8,128)(2,1)}, u32[]{:S(2)}) copy-start(bf16[3,3,128,128]{3,2,1,0:T(8,128)(2,1)} %refs_5_.1) | copy-start | bytes 884740
  23.1 15.0 %copy-start.22 = (f32[128]{0:T(128)S(1)}, f32[128]{0:T(128)}, u32[]{:S(2)}) copy-start(f32[128]{0:T(128)} %param.18) | copy-start | bytes 1540
  25.7 18.0 %copy-start.2 = (bf16[4,8,128,128]{3,2,1,0:T(8,128)(2,1)}, bf16[4,8,128,128]{3,2,1,0:T(8,128)(2,1)S(1)}, u32[]{:S(2)}) copy-start(bf16[4,8,128,128]{3,2,1,0:T(8,128)(2,1)S(1)} %get-tuple-element.49.conv_ref.refs_6_.refs_4_) | copy-start | bytes 3145732
  25.7 12.5 %all-to-all-start = ((f32[8,8,128]{2,1,0:T(8,128)}), f32[8,8,128]{2,1,0:T(8,128)S(1)}, u32[]{:S(2)}, u32[]{:S(2)}) async-start(f32[8,8,128]{2,1,0:T(8,128)} %get-tuple-element.50), calls=%async_computation | async-start | bytes 65536 | tf_op jit(solution)/shard_map/all_to_all | solution.py:746
  31.5 12.2 %copy-start.3 = (bf16[4,2,128,128]{3,2,1,0:T(8,128)(2,1)}, bf16[4,2,128,128]{3,2,1,0:T(8,128)(2,1)S(1)}, u32[]{:S(2)}) copy-start(bf16[4,2,128,128]{3,2,1,0:T(8,128)(2,1)S(1)} %collective-permute-done.1.high_ref.refs_2_) | copy-start | bytes 786436
  31.5 12.2 %copy-start.4 = (bf16[4,2,128,128]{3,2,1,0:T(8,128)(2,1)}, bf16[4,2,128,128]{3,2,1,0:T(8,128)(2,1)S(1)}, u32[]{:S(2)}) copy-start(bf16[4,2,128,128]{3,2,1,0:T(8,128)(2,1)S(1)} %collective-permute-done.2.below_ref.refs_3_) | copy-start | bytes 786436
  31.9 0.7 copy-start.15
  32.6 0.7 copy-start.17
  33.3 15.4 %collective-permute-start.3 = (bf16[384,128]{1,0:T(8,128)(2,1)S(1)}, bf16[384,128]{1,0:T(8,128)(2,1)S(1)}, u32[]{:S(2)}, u32[]{:S(2)}) collective-permute-start(bf16[384,128]{1,0:T(8,128)(2,1)S(1)} %get-tuple-element.95), channel_id=1, source_target_pairs={{1,0},{2,1},{3,2},{0,3},{5,4},{6,5},{7,6},{4,7},{9,8},{10,9},{11,1... | collective-permute-start | bytes 294920 | tf_op jit(solution)/shard_map/ppermute | solution.py:730
  33.4 15.3 %collective-permute-start.4 = (bf16[384,128]{1,0:T(8,128)(2,1)S(1)}, bf16[384,128]{1,0:T(8,128)(2,1)S(1)}, u32[]{:S(2)}, u32[]{:S(2)}) collective-permute-start(bf16[384,128]{1,0:T(8,128)(2,1)S(1)} %get-tuple-element.95), channel_id=1, source_target_pairs={{2,0},{3,1},{0,2},{1,3},{6,4},{7,5},{4,6},{5,7},{10,8},{11,9},{8,1... | collective-permute-start | bytes 294920 | tf_op jit(solution)/shard_map/ppermute | solution.py:730
  34.9 13.8 %collective-permute-start.5 = (bf16[384,128]{1,0:T(8,128)(2,1)S(1)}, bf16[384,128]{1,0:T(8,128)(2,1)S(1)}, u32[]{:S(2)}, u32[]{:S(2)}) collective-permute-start(bf16[384,128]{1,0:T(8,128)(2,1)S(1)} %get-tuple-element.95), channel_id=1, source_target_pairs={{3,0},{0,1},{1,2},{2,3},{7,4},{4,5},{5,6},{6,7},{11,8},{8,9},{9,10... | collective-permute-start | bytes 294920 | tf_op jit(solution)/shard_map/ppermute | solution.py:730
  38.1 0.9 copy-start.16
  39.1 0.9 copy-start.18
  40.0 15.4 %copy-start.10 = (f32[128]{0:T(128)S(1)}, f32[128]{0:T(128)}, u32[]{:S(2)}) copy-start(f32[128]{0:T(128)} %param.20) | copy-start | bytes 1540
  40.0 15.4 %copy-start.11 = (f32[128]{0:T(128)S(1)}, f32[128]{0:T(128)}, u32[]{:S(2)}) copy-start(f32[128]{0:T(128)} %param.21) | copy-start | bytes 1540
  40.0 15.4 %copy-start.20 = (bf16[128,64]{0,1:T(8,128)(2,1)S(1)}, bf16[128,64]{0,1:T(8,128)(2,1)}, u32[]{:S(2)}) copy-start(bf16[128,64]{0,1:T(8,128)(2,1)} %param.22) | copy-start | bytes 49156
  40.0 15.4 %copy-start.21 = (f32[16,4]{0,1:T(4,128)S(1)}, f32[16,4]{0,1:T(4,128)}, u32[]{:S(2)}) copy-start(f32[16,4]{0,1:T(4,128)} %param.23) | copy-start | bytes 772
  43.7 0.6 copy-start.8
  44.3 1.1 copy-start.23
  45.3 24.8 %copy-start.1 = (bf16[4,8,128,128]{3,2,1,0:T(8,128)(2,1)}, bf16[4,8,128,128]{3,2,1,0:T(8,128)(2,1)S(1)}, u32[]{:S(2)}) copy-start(bf16[4,8,128,128]{3,2,1,0:T(8,128)(2,1)S(1)} %get-tuple-element.56.block_ref.refs_2_) | copy-start | bytes 3145732
  45.3 10.0 %all-to-all-start.1 = ((f32[8,8,128]{2,1,0:T(8,128)}), f32[8,8,128]{2,1,0:T(8,128)S(1)}, u32[]{:S(2)}, u32[]{:S(2)}) async-start(f32[8,8,128]{2,1,0:T(8,128)} %get-tuple-element.57), calls=%async_computation.1 | async-start | bytes 65536 | tf_op jit(solution)/shard_map/all_to_all | solution.py:746
  59.2 11.0 %copy-start.7 = (f32[8,128]{1,0:T(8,128)}, f32[8,128]{1,0:T(8,128)S(1)}, u32[]{:S(2)}) copy-start(f32[8,128]{1,0:T(8,128)S(1)} %get-tuple-element.64.norm_ref.refs_4_) | copy-start | bytes 12292
  70.2 1.0 copy-start.13
  71.2 0.6 copy-start.19
  71.8 9.7 %copy-start.9 = (f32[8,128]{1,0:T(8,128)}, f32[8,128]{1,0:T(8,128)S(1)}, u32[]{:S(2)}) copy-start(f32[8,128]{1,0:T(8,128)S(1)} %get-tuple-element.78.refs_10_) | copy-start | bytes 12292
  88.7 10.0 %all-to-all-start.3 = ((f32[8,8,128]{2,1,0:T(8,128)}), f32[8,8,128]{2,1,0:T(8,128)S(1)}, u32[]{:S(2)}, u32[]{:S(2)}) async-start(f32[8,8,128]{2,1,0:T(8,128)} %get-tuple-element.72), calls=%async_computation.3 | async-start | bytes 65536 | tf_op jit(solution)/shard_map/all_to_all | solution.py:746
  98.7 0.6 copy-start.24
  123.9 18.6 %all-to-all-start.5 = ((bf16[32,64,128]{2,1,0:T(8,128)(2,1)}), bf16[32,64,128]{2,1,0:T(8,128)(2,1)S(1)}, u32[]{:S(2)}, u32[]{:S(2)}) async-start(bf16[32,64,128]{2,1,0:T(8,128)(2,1)} %shard_map.195), calls=%async_computation.5 | async-start | bytes 1048576 | tf_op jit(solution)/shard_map/all_to_all | solution.py:746
  127.1 6.0 %collective-permute-start.6 = (bf16[8,32,128]{2,1,0:T(8,128)(2,1)S(1)}, bf16[8,32,128]{2,1,0:T(8,128)(2,1)S(1)}, u32[]{:S(2)}, u32[]{:S(2)}) collective-permute-start(bf16[8,32,128]{2,1,0:T(8,128)(2,1)S(1)} %get-tuple-element.91), channel_id=1, source_target_pairs={{0,1},{1,2},{2,3},{3,0},{4,5},{5,6},{6,7},{7,4},{8,9},{9,10},{10,1... | collective-permute-start | bytes 196616 | tf_op jit(solution)/shard_map/ppermute | solution.py:741
  127.4 8.6 %collective-permute-start.7 = (bf16[8,32,128]{2,1,0:T(8,128)(2,1)S(1)}, bf16[8,32,128]{2,1,0:T(8,128)(2,1)S(1)}, u32[]{:S(2)}, u32[]{:S(2)}) collective-permute-start(bf16[8,32,128]{2,1,0:T(8,128)(2,1)S(1)} %get-tuple-element.93), channel_id=1, source_target_pairs={{0,2},{1,3},{2,0},{3,1},{4,6},{5,7},{6,4},{7,5},{8,10},{9,11},{10,... | collective-permute-start | bytes 196616 | tf_op jit(solution)/shard_map/ppermute | solution.py:741
  129.0 6.9 %collective-permute-start.8 = (bf16[8,32,128]{2,1,0:T(8,128)(2,1)S(1)}, bf16[8,32,128]{2,1,0:T(8,128)(2,1)S(1)}, u32[]{:S(2)}, u32[]{:S(2)}) collective-permute-start(bf16[8,32,128]{2,1,0:T(8,128)(2,1)S(1)} %get-tuple-element.92), channel_id=1, source_target_pairs={{0,3},{1,0},{2,1},{3,2},{4,7},{5,4},{6,5},{7,6},{8,11},{9,8},{10,9... | collective-permute-start | bytes 196616 | tf_op jit(solution)/shard_map/ppermute | solution.py:741

commit v5 on v4

--- a/solution.py
+++ b/solution.py
@@ -542,9 +542,12 @@
     vector_ref,
     other_ref,
     block_rows_ref,
-    out_ref,
+    turn_ref,
+    keep_ref,
+    give_ref,
     factors,
     total,
+    out_ref,
 ):
     date = pl.program_id(0)
     rows, cols, width = conv_ref.shape[1:]
@@ -598,6 +601,12 @@
             start += 16
         if out_ref.shape[0] > start:
             out_ref[start:] = jnp.zeros_like(out_ref[start:])
+        half_rows = keep_ref.shape[0]
+        core = turn_ref[0] % 2
+        start = pl.multiple_of(core * half_rows, half_rows)
+        keep_ref[...] = out_ref[pl.ds(start, half_rows), :]
+        start = pl.multiple_of((1 - core) * half_rows, half_rows)
+        give_ref[...] = out_ref[pl.ds(start, half_rows), :]
 
 
 def total_kernel(in_ref, out_ref):
@@ -606,7 +615,23 @@
         out_ref[copy] = total
 
 
-def final_kernel(depth, rows_ref, conv_ref, block_ref, key_ref, query_ref, *vector_refs):
+def final_kernel(
+    depth,
+    turn_ref,
+    own_ref,
+    other_ref,
+    conv_ref,
+    block_ref,
+    key_ref,
+    query_ref,
+    *refs,
+):
+    vector_refs, rows_ref = refs[:-1], refs[-1]
+    half_rows = own_ref.shape[0]
+    core = turn_ref[0] % 2
+    rows_ref[pl.ds(pl.multiple_of(core * half_rows, half_rows), half_rows), :] = own_ref[...]
+    start = pl.multiple_of((1 - core) * half_rows, half_rows)
+    rows_ref[pl.ds(start, half_rows), :] = other_ref[...]
     conv_end, block_end, width = conv_ref.shape[0], block_ref.shape[0], block_ref.shape[1]
     block_ref[...] = rows_ref[:block_end].astype(F32)
     wide = key_ref.shape[0]
@@ -645,40 +670,56 @@
     return pl.BlockSpec((1,) + tuple(shape[1:]), lambda date: (date,) + zeros)
 
 
-def streamed(kernel, dates, kinds, out_count):
-    places = [place for place, kind in enumerate(kinds) if kind != "scalar"]
+def streamed(kernel, dates, kinds, out_kinds, stream):
+    loads = [place for place, kind in enumerate(kinds) if stream and kind != "scalar"]
+    stores = [place for place, kind in enumerate(out_kinds) if kind == "direct"]
 
     def body(*refs):
         inputs, rest = list(refs[: len(kinds)]), refs[len(kinds) :]
-        outputs, scratch = rest[:out_count], rest[out_count:]
-        count = len(places)
-        buffers, ready, scratch = scratch[:count], scratch[count], scratch[count + 1 :]
+        outputs, scratch = list(rest[: len(out_kinds)]), rest[len(out_kinds) :]
+        loaded, scratch = scratch[: len(loads)], scratch[len(loads) :]
+        stored, scratch = scratch[: len(stores)], scratch[len(stores) :]
+        ready, done, scratch = scratch[0], scratch[1], scratch[2:]
         date = pl.program_id(0)
-        views = list(inputs)
-
-        def copy(index, step):
-            source, target = inputs[places[index]], buffers[index]
-            if kinds[places[index]] == "date":
+        views, results = list(inputs), list(outputs)
+
+        def load(index, step):
+            source, target = inputs[loads[index]], loaded[index]
+            if kinds[loads[index]] == "date":
                 source, target = source.at[step], target.at[step]
             return pltpu.make_async_copy(source, target, ready.at[index, step])
+
+        def store(index, step):
+            source, target = stored[index].at[step], outputs[stores[index]].at[step]
+            return pltpu.make_async_copy(source, target, done.at[index, step])
 
         @pl.when(date == 0)
         def _():
             for step in range(dates):
-                for index, place in enumerate(places):
+                for index, place in enumerate(loads):
                     if step == 0 or kinds[place] == "date":
-                        copy(index, step).start()
-            for index, place in enumerate(places):
-                if kinds[place] == "all":
-                    copy(index, 0).wait()
-
-        for index, place in enumerate(places):
+                        load(index, step).start()
+            for index, place in enumerate(loads):
+                if kinds[place] != "date":
+                    load(index, 0).wait()
+
+        for index, place in enumerate(loads):
             if kinds[place] == "date":
-                copy(index, date).wait()
-                views[place] = buffers[index].at[pl.ds(date, 1)]
+                load(index, date).wait()
+                views[place] = loaded[index].at[pl.ds(date, 1)]
             else:
-                views[place] = buffers[index]
-        kernel(*views, *outputs, *scratch)
+                views[place] = loaded[index]
+        for index, place in enumerate(stores):
+            results[place] = stored[index].at[pl.ds(date, 1)]
+        kernel(*views, *results, *scratch)
+        for index in range(len(stores)):
+            store(index, date).start()
+
+        @pl.when(date == dates - 1)
+        def _():
+            for step in range(dates):
+                for index in range(len(stores)):
+                    store(index, step).wait()
 
     return body
 
@@ -691,6 +732,9 @@
 def call(kernel, dates, inputs, outputs, scratch, flops, stream=False):
     in_specs, arrays, buffers = [], [], []
     for kind, array in inputs:
+        large = array.size * array.dtype.itemsize >= MIB // 2
+        if kind in ("far", "still") or (stream and kind == "date" and large):
+            array = pltpu.with_memory_space_constraint(array, pltpu.HBM)
         arrays.append(array)
         if kind == "scalar":
             in_specs.append(pl.BlockSpec(memory_space=pltpu.SMEM))
@@ -698,20 +742,30 @@
             in_specs.append(pl.BlockSpec(memory_space=pl.ANY))
             buffers.append(pltpu.VMEM(array.shape, array.dtype))
         else:
-            in_specs.append((per_date if kind == "date" else whole)(array.shape))
-    out_specs = [(per_date if kind == "date" else whole)(shape) for kind, shape, _ in outputs]
-    moved = sum(array.size * array.dtype.itemsize for array in arrays)
-    if stream:
-        kernel = streamed(kernel, dates, [kind for kind, _ in inputs], len(outputs))
-        scratch = buffers + [pltpu.SemaphoreType.DMA((len(buffers), dates))] + scratch
+            in_specs.append((per_date if kind in ("date", "far") else whole)(array.shape))
+    out_specs, out_shape = [], []
+    for kind, shape, dtype in outputs:
+        if kind == "direct":
+            out_specs.append(pl.BlockSpec(memory_space=pltpu.HBM))
+            buffers.append(pltpu.VMEM(shape, dtype))
+        else:
+            out_specs.append((per_date if kind == "date" else whole)(shape))
+        pinned = kind == "direct" or (stream and kind == "date")
+        out_shape.append((pltpu.HBM if pinned else jax.ShapeDtypeStruct)(shape, dtype))
+    moved = sum(array.size * array.dtype.itemsize for _, array in inputs)
+    if buffers:
+        kinds, out_kinds = [kind for kind, _ in inputs], [kind for kind, _, _ in outputs]
+        kernel = streamed(kernel, dates, kinds, out_kinds, stream)
+        ready = pltpu.SemaphoreType.DMA((max(len(inputs), len(outputs)), dates))
+        scratch = buffers + [ready, ready] + scratch
     return pl.pallas_call(
         kernel,
         grid=(dates,),
         in_specs=in_specs,
         out_specs=out_specs,
-        out_shape=[jax.ShapeDtypeStruct(shape, dtype) for _, shape, dtype in outputs],
+        out_shape=out_shape,
         scratch_shapes=scratch,
-        compiler_params=pltpu.CompilerParams(vmem_limit_bytes=(60 if stream else 24) * MIB),
+        compiler_params=pltpu.CompilerParams(vmem_limit_bytes=(40 if stream else 24) * MIB),
         cost_estimate=pl.CostEstimate(flops=flops, bytes_accessed=2 * moved, transcendentals=0),
     )(*arrays)
 
@@ -750,11 +804,24 @@
     return lax.all_gather(array, axis, axis=0, tiled=True)
 
 
-def scatter(rows_array):
+def other_core(array):
+    devices = lax.axis_size("dates")
+    return lax.ppermute(array, "dates", [(i, i + 1 - 2 * (i % 2)) for i in range(devices)])
+
+
+def exchange_cores(pieces):
     axes = ("rows", "dates")
     devices = lax.axis_size(axes)
+    groups = [list(range(core, devices, 2)) for core in range(2)]
+    return lax.all_to_all(
+        pieces, axes, split_axis=0, concat_axis=0, axis_index_groups=groups, tiled=True
+    )
+
+
+def scatter(rows_array):
+    devices = lax.axis_size(("rows", "dates")) // 2
     count, width = rows_array.shape
-    return exchange(rows_array.reshape(devices, count // devices, width), axes)
+    return exchange_cores(rows_array.reshape(devices, count // devices, width))
 
 
 def collect(pieces):
@@ -764,7 +831,7 @@
         compiler_params=pltpu.CompilerParams(vmem_limit_bytes=16 * MIB),
     )(pieces)
     count, rows, width = pieces.shape
-    return exchange(spread, ("rows", "dates")).reshape(count * rows, width)
+    return exchange_cores(spread).reshape(count * rows, width)
 
 
 def padded_count(count, devices):
@@ -804,16 +871,17 @@
     gn_gain, gn_shift = rows_of(gn_gain), rows_of(gn_shift)
     last = images[:, -1]
     above = shifted(last, 1)
-    high = shifted(images[:, -3:-1], 1)
-    below = shifted(images[:, :2], -1)
+    high, below, above = lax.optimization_barrier((images[:, -3:-1], images[:, :2], above))
+    high, below = shifted(high, 1), shifted(below, -1)
     paired = images.reshape(dates, rows, 2, cols, pair_width)
     conv_out, sums = call(
         functools.partial(down_kernel, dates),
         dates,
-        [("date", paired), ("date", above), ("all", conv_weight)],
+        [("date", paired), ("date", above), ("still", conv_weight)],
         [("date", frame, BF16), ("all", (row_devs, 2 * dates, width), F32)],
         [pltpu.VMEM((3 * pair_width, 2 * width), BF16)],
         6 * flops,
+        True,
     )
     stats = exchange(sums, "rows")
     high, below, last, _ = lax.optimization_barrier((high, below, last, sums))
@@ -846,7 +914,7 @@
             ("all", stats),
             ("all", first_gain),
             ("all", first_shift),
-            ("all", block_weight),
+            ("still", block_weight),
         ],
         [
             ("date", frame, BF16),
@@ -856,6 +924,7 @@
         ],
         [pltpu.VMEM((3 * width, 3 * width), BF16)],
         9 * flops,
+        True,
     )
     stats = exchange(sums, "rows")
     features, exponent, attn, norm, packed, key_wide, query_wide = call(
@@ -863,7 +932,7 @@
         dates,
         [
             ("scalar", days),
-            ("date", block_out),
+            ("far", block_out),
             ("all", stats),
             ("all", gn_gain),
             ("all", gn_shift),
@@ -895,7 +964,7 @@
         functools.partial(attend_kernel, dates, grad_scale),
         dates,
         [
-            ("all", packed),
+            ("still", packed),
             ("date", features),
             ("date", exponent),
             ("date", attn),
@@ -909,7 +978,7 @@
             ("all", key_wide),
         ],
         [
-            ("date", frame, BF16),
+            ("direct", frame, BF16),
             ("all", (date_devs, rows, cols // date_devs, width), BF16),
             ("all", (width, width), F32),
             ("all", (8, width), F32),
@@ -928,7 +997,7 @@
             ("date", block_out),
             ("all", tails),
             ("all", norm),
-            ("all", block_weight),
+            ("still", block_weight),
             ("date", conv_out),
             ("date", halo_up),
             ("date", halo_down),
@@ -962,7 +1031,8 @@
     )
     tails, block_rows = lax.optimization_barrier((tails, block_rows))
     conv_count = 9 * pair_width // 2 + 32
-    (rows_all,) = call(
+    half_rows = padded_count(10 * width + conv_count, devices) // 2
+    keep, give = call(
         functools.partial(conv_grad_kernel, dates, norm_count),
         dates,
         [
@@ -978,16 +1048,23 @@
             ("all", first_vectors),
             ("all", vectors),
             ("all", block_rows),
-        ],
-        [("all", (padded_count(10 * width + conv_count, devices), width), BF16)],
-        [pltpu.VMEM((2 * dates, width), F32), pltpu.VMEM((3 * pair_width, 2 * width), F32)],
+            ("scalar", turn),
+        ],
+        [("all", (half_rows, width), BF16)] * 2,
+        [
+            pltpu.VMEM((2 * dates, width), F32),
+            pltpu.VMEM((3 * pair_width, 2 * width), F32),
+            pltpu.VMEM((2 * half_rows, width), BF16),
+        ],
         6 * flops,
         True,
     )
-    pieces = scatter(rows_all)
-    attended, _ = lax.optimization_barrier((attended, rows_all))
+    rows_half = (keep.astype(F32) + other_core(give).astype(F32)).astype(BF16)
+    pieces = scatter(rows_half)
+    attended, _ = lax.optimization_barrier((attended, rows_half))
     attended = sum_of_parts(attended)
-    rows_all = collect(pieces)
+    rows_half = collect(pieces)
+    rows_other = other_core(rows_half)
     shapes = [
         (9 * pair_width // 2, width),
         (9 * width, width),
@@ -996,9 +1073,15 @@
     ] + [(1, width)] * 4
     conv_total, block_total, key_total, query_total, *totals = pl.pallas_call(
         functools.partial(final_kernel, depth),
+        in_specs=[
+            pl.BlockSpec(memory_space=pltpu.SMEM),
+            pl.BlockSpec(memory_space=pltpu.VMEM),
+            pl.BlockSpec(memory_space=pltpu.VMEM),
+        ],
         out_shape=[jax.ShapeDtypeStruct(shape, F32) for shape in shapes],
+        scratch_shapes=[pltpu.VMEM((2 * half_rows, width), BF16)],
         compiler_params=pltpu.CompilerParams(vmem_limit_bytes=16 * MIB),
-    )(rows_all)
+    )(turn, rows_half, rows_other)
     totals = [total.reshape(width) for total in totals]
     return (
         attended,

time: 144 us -> 132 us (0.917)
  local copies, waits for them, and re-layouts: 12.4 us -> 2.8 us
  Pallas kernels: 32.8 us -> 38.6 us
  waiting for transfers between devices: 29.4 us -> 23.6 us
  blocking collectives: 35.7 us -> 30.3 us
  starting transfers between devices: 31.5 us -> 34.1 us
    all_to_all x2 -> x1, blocking collectives: 28.5 us -> 9.06 us  [exchange(): return lax.all_to_all(pieces, axes, split_axis=0, concat_axis=0, tiled=True)]
    all_to_all x0 -> x1, blocking collectives: none -> 13.6 us  [exchange_cores(): lax.all_to_all(pieces, axes, split_axis=0, concat_axis=0, axis_index_grou...]
    unnamed x54 -> x20, local copies, waits for them, and re-layouts: 9.58 us -> 0.05 us
    all_to_all x0 -> x1, waiting for transfers between devices: none -> 5.96 us  [exchange_cores(): lax.all_to_all(pieces, axes, split_axis=0, concat_axis=0, axis_index_grou...]
    pallas_call x7, Pallas kernels: 30.5 us -> 36.4 us  [call(): pl.pallas_call(kernel, grid=(dates,), in_specs=in_specs, out_specs=out_sp...]
    ppermute x3, waiting for transfers between devices: 5.59 us -> 0.01 us  [sum_of_parts(): total = total + lax.ppermute(piece, 'dates', pairs).astype(F32)]
    ppermute x3, waiting for transfers between devices: 6.25 us -> 1.63 us  [shifted(): return lax.ppermute(array, 'rows', pairs)]
    all_to_all x4 -> x3, waiting for transfers between devices: 17.6 us -> 13.6 us  [exchange(): return lax.all_to_all(pieces, axes, split_axis=0, concat_axis=0, tiled=True)]
  transfers between devices with their start and end apart: 13 -> 15, of which waited for: 7 -> 7; matrix products, arithmetic and copies ran while one was open for 2% -> 2% of each run, Pallas kernels for 8% -> 11%
where the time goes in v5:
time: 132 us; the launch traced here: 131 us
  Pallas kernels  38.6 us (29%)
  starting transfers between devices  34.1 us (26%)
  blocking collectives  30.3 us (23%)
  waiting for transfers between devices  23.6 us (18%)
  local copies, waits for them, and re-layouts  2.8 us (2%)
    pallas_call x7, Pallas kernels, call(): pl.pallas_call(kernel, grid=(dates,), in_specs=in_specs, out_specs=out_sp...  36.4 us
    all_to_all x3, starting transfers between devices, exchange(): return lax.all_to_all(pieces, axes, split_axis=0, concat_axis=0, tiled=True)  14.6 us
    all_to_all x3, waiting for transfers between devices, exchange(): return lax.all_to_all(pieces, axes, split_axis=0, concat_axis=0, tiled=True)  13.6 us
    all_to_all x1, blocking collectives, exchange_cores(): lax.all_to_all(pieces, axes, split_axis=0, concat_axis=0, axis_index_grou...  13.6 us
    ppermute x3, starting transfers between devices, shifted(): return lax.ppermute(array, 'rows', pairs)  10.7 us
    all_to_all x1, blocking collectives, exchange(): return lax.all_to_all(pieces, axes, split_axis=0, concat_axis=0, tiled=True)  9.06 us
    all_gather x1, blocking collectives, gather(): return lax.all_gather(array, axis, axis=0, tiled=True)  7.62 us
    all_to_all x1, waiting for transfers between devices, exchange_cores(): lax.all_to_all(pieces, axes, split_axis=0, concat_axis=0, axis_index_grou...  5.96 us
  transfers between devices with their start and end apart: 15, of which 7 were waited for; matrix products, arithmetic and copies ran while one was open for 2% of the time, Pallas kernels for 11%

profile of v5, /device:TPU:0, one launch (start us, length us, event | category | flops | bytes accessed | tf_op | source)
XLA Modules:
  0.0 131.3 jit_solution(14405806136559054364)
XLA Ops:
  0.6 0.9 slice_bitcast_fusion.last_ref
  1.6 0.0 copy-start.1
  1.6 5.0 %collective-permute-start = (bf16[4,128,128]{2,1,0:T(8,128)(2,1)S(1)}, bf16[4,128,128]{2,1,0:T(8,128)(2,1)S(1)}, u32[]{:S(2)}, u32[]{:S(2)}) collective-permute-start(bf16[4,128,128]{2,1,0:T(8,128)(2,1)S(1)} %slice_bitcast_fusion.last_ref), channel_id=1, source_target_pairs={{0,4},{4,8},{8,12},{12,16},{16,20},{20,24},{24,28},{1,5},{5,9},{9,... | collective-permute-start | bytes 393224 | tf_op jit(solution)/shard_map/ppermute | solution.py:776
  6.6 1.1 fusion.6
  7.7 0.0 copy-start.8
  7.7 0.0 copy-start.9
  7.7 1.6 %collective-permute-done.refs_1_.above_ref = bf16[4,128,128]{2,1,0:T(8,128)(2,1)S(1)} collective-permute-done((bf16[4,128,128]{2,1,0:T(8,128)(2,1)S(1)}, bf16[4,128,128]{2,1,0:T(8,128)(2,1)S(1)}, u32[]{:S(2)}, u32[]{:S(2)}) %collective-permute-start) | collective-permute-done | bytes 131104 | tf_op jit(solution)/shard_map/ppermute | solution.py:776
  9.3 4.4 %collective-permute-start.1 = (bf16[4,2,128,128]{3,2,1,0:T(8,128)(2,1)S(1)}, bf16[4,2,128,128]{3,2,1,0:T(8,128)(2,1)S(1)}, u32[]{:S(2)}, u32[]{:S(2)}) collective-permute-start(bf16[4,2,128,128]{3,2,1,0:T(8,128)(2,1)S(1)} %get-tuple-element.56), channel_id=1, source_target_pairs={{0,4},{4,8},{8,12},{12,16},{16,20},{20,24},{24,28},{1,5},{5,9},{9,... | collective-permute-start | bytes 786440 | tf_op jit(solution)/shard_map/ppermute | solution.py:776
  13.7 1.3 collective-permute-start.2
  15.0 0.7 dynamic_slice.19.day_ref
  15.8 4.1 %shard_map.187 = (bf16[4,8,128,128]{3,2,1,0:T(8,128)(2,1)}, f32[8,8,128]{2,1,0:T(8,128)}) custom-call(bf16[4,8,2,128,128]{4,3,2,1,0:T(8,128)(2,1)} %bitcast.53, bf16[4,128,128]{2,1,0:T(8,128)(2,1)S(1)} %collective-permute-done.refs_1_.above_ref, bf16[3,3,64,128]{3,2,1,0:T(8,128)(2,1)} %weight_ref.1), custom_call_target="tpu_custom_call" | custom-call | flops 805306368 | bytes 4751360 | tf_op jit(solution)/shard_map/pallas_call | solution.py:761
  19.9 7.8 %all-to-all-start = ((f32[8,8,128]{2,1,0:T(8,128)}), f32[8,8,128]{2,1,0:T(8,128)S(1)}, u32[]{:S(2)}, u32[]{:S(2)}) async-start(f32[8,8,128]{2,1,0:T(8,128)} %get-tuple-element.58), calls=%async_computation | async-start | bytes 65536 | tf_op jit(solution)/shard_map/all_to_all | solution.py:800
  27.7 0.0 collective-permute-done.2.below_ref.refs_3_
  27.7 0.4 shard_map.188
  28.2 0.1 collective-permute-start.3
  28.3 1.6 %collective-permute-start.4 = (bf16[384,128]{1,0:T(8,128)(2,1)S(1)}, bf16[384,128]{1,0:T(8,128)(2,1)S(1)}, u32[]{:S(2)}, u32[]{:S(2)}) collective-permute-start(bf16[384,128]{1,0:T(8,128)(2,1)S(1)} %get-tuple-element.105), channel_id=1, source_target_pairs={{2,0},{3,1},{0,2},{1,3},{6,4},{7,5},{4,6},{5,7},{10,8},{11,9},{8,1... | collective-permute-start | bytes 294920 | tf_op jit(solution)/shard_map/ppermute | solution.py:784
  29.8 0.2 collective-permute-start.5
  30.0 4.4 %all-to-all-done.refs_4_ = f32[8,8,128]{2,1,0:T(8,128)S(1)} async-done(((f32[8,8,128]{2,1,0:T(8,128)}), f32[8,8,128]{2,1,0:T(8,128)S(1)}, u32[]{:S(2)}, u32[]{:S(2)}) %all-to-all-start) | async-done | bytes 32800 | tf_op jit(solution)/shard_map/all_to_all | solution.py:800
  34.4 0.0 copy-start.5
  34.4 0.0 copy-start.6
  34.4 5.5 %shard_map.189 = (bf16[4,8,128,128]{3,2,1,0:T(8,128)(2,1)}, bf16[4,10,128,128]{3,2,1,0:T(8,128)(2,1)}, f32[8,128]{1,0:T(8,128)S(1)}, f32[8,8,128]{2,1,0:T(8,128)}) custom-call(s32[1]{0:T(128)} %bitcast.refs_0_, bf16[4,8,128,128]{3,2,1,0:T(8,128)(2,1)} %get-tuple-element.55.refs_1_.refs_6_.refs_4_, ...), custom_call_target="tpu_custom_call" | custom-call | flops 1207959552 | bytes 3278856 | tf_op jit(solution)/shard_map/pallas_call | solution.py:761
  40.0 3.5 %all-to-all-start.1 = ((f32[8,8,128]{2,1,0:T(8,128)}), f32[8,8,128]{2,1,0:T(8,128)S(1)}, u32[]{:S(2)}, u32[]{:S(2)}) async-start(f32[8,8,128]{2,1,0:T(8,128)} %get-tuple-element.65), calls=%async_computation.1 | async-start | bytes 65536 | tf_op jit(solution)/shard_map/all_to_all | solution.py:800
  43.5 0.0 collective-permute-done.4
  43.5 0.0 collective-permute-done.5
  43.5 0.1 pad_maximum_fusion.grad_ref.refs_9_
  43.6 6.5 %all-to-all-done.1.stats_ref = f32[8,8,128]{2,1,0:T(8,128)S(1)} async-done(((f32[8,8,128]{2,1,0:T(8,128)}), f32[8,8,128]{2,1,0:T(8,128)S(1)}, u32[]{:S(2)}, u32[]{:S(2)}) %all-to-all-start.1) | async-done | bytes 32800 | tf_op jit(solution)/shard_map/all_to_all | solution.py:800
  50.1 4.5 %shard_map.190 = (bf16[4,8,128,128]{3,2,1,0:T(8,128)(2,1)S(1)}, f32[4,8,128,128]{3,2,1,0:T(8,128)S(1)}, f32[4,8,128,128]{3,2,1,0:T(8,128)S(1)}, f32[8,128]{1,0:T...) custom-call(s32[4]{0:T(128)S(1)} %dynamic_slice.19.day_ref, ...), custom_call_target="tpu_custom_call" | custom-call | flops 671088640 | bytes 3115560 | tf_op jit(solution)/shard_map/pallas_call | solution.py:761
  54.7 7.6 %all_gather.3.refs_0_ = f32[4,2,128,128]{3,2,1,0:T(8,128)} all-gather(f32[1,2,128,128]{3,2,1,0:T(8,128)S(1)} %get-tuple-element.68), channel_id=1, replica_groups=mesh['rows'=8,'dates'=4] {'dates'}, dimensions={0}, use_global_device_ids=true | all-gather | bytes 655360 | tf_op jit(solution)/shard_map/all_gather | solution.py:804
  62.3 6.4 %shard_map.191 = (bf16[4,8,128,128]{3,2,1,0:T(8,128)(2,1)}, bf16[4,8,32,128]{3,2,1,0:T(8,128)(2,1)S(1)}, f32[128,128]{1,0:T(8,128)S(1)}, f32[8,128]{1,0:T(8,128)S(1)}, f32[8,8,128]{2,1,0:T(8,128)S(1)}) custom-call(f32[4,2,128,128]{3,2,1,0:T(8,128)} %all_gather.3.refs_0_, bf16[4,8,128,128]{3,2,1,0:T(8,128)(2,1)S(1)} %get-tuple-element.69.refs_1_, ...), custom_call_target="tpu_custom_call" | custom-call | flops 671088640 | bytes 14501896 | tf_op jit(solution)/shard_map/pallas_call | solution.py:761
  68.7 9.1 %all_to_all.30.refs_3_ = f32[8,8,128]{2,1,0:T(8,128)S(1)} all-to-all(f32[8,8,128]{2,1,0:T(8,128)S(1)} %get-tuple-element.77), channel_id=1, replica_groups=mesh['rows'=8,'dates'=4] {'rows'}, dimensions={0} | all-to-all | bytes 65536 | tf_op jit(solution)/shard_map/all_to_all | solution.py:800
  77.8 7.5 %shard_map.192 = (bf16[4,8,128,128]{3,2,1,0:T(8,128)(2,1)}, bf16[4,10,128,128]{3,2,1,0:T(8,128)(2,1)}, f32[8,128]{1,0:T(8,128)S(1)}, f32[8,8,128]{2,1,0:T(8,128)}) custom-call(s32[1]{0:T(128)} %bitcast.refs_0_, bf16[4,8,128,128]{3,2,1,0:T(8,128)(2,1)} %get-tuple-element.76.refs_1_, bf16[4,8,128,128]{3,2,1,0:T(8,128)(2,1)} %get-tuple-element.64.block_ref.refs_4_.refs_2_, ...), custom_call_target="tpu_custom_call" | custom-call | flops 1207959552 | bytes 7489544 | tf_op jit(solution)/shard_map/pallas_call | solution.py:761
  85.3 3.4 %all-to-all-start.3 = ((f32[8,8,128]{2,1,0:T(8,128)}), f32[8,8,128]{2,1,0:T(8,128)S(1)}, u32[]{:S(2)}, u32[]{:S(2)}) async-start(f32[8,8,128]{2,1,0:T(8,128)} %get-tuple-element.80), calls=%async_computation.3 | async-start | bytes 65536 | tf_op jit(solution)/shard_map/all_to_all | solution.py:800
  88.6 3.8 %shard_map.193.refs_11_ = bf16[1280,128]{1,0:T(8,128)(2,1)S(1)} custom-call(bf16[4,10,128,128]{3,2,1,0:T(8,128)(2,1)} %get-tuple-element.81.refs_0_, bf16[4,8,128,128]{3,2,1,0:T(8,128)(2,1)} %get-tuple-element.82.refs_1_, f32[128,128]{1,0:T(8,128)S(1)} %get-tuple-element.83.refs_2_), custom_call_target="tpu_custom_call" | custom-call | flops 1207959552 | bytes 4849664 | tf_op jit(solution)/shard_map/pallas_call | solution.py:761
  92.5 2.8 %all-to-all-done.3.refs_6_ = f32[8,8,128]{2,1,0:T(8,128)S(1)} async-done(((f32[8,8,128]{2,1,0:T(8,128)}), f32[8,8,128]{2,1,0:T(8,128)S(1)}, u32[]{:S(2)}, u32[]{:S(2)}) %all-to-all-start.3) | async-done | bytes 32800 | tf_op jit(solution)/shard_map/all_to_all | solution.py:800
  95.3 4.4 %shard_map.194 = (bf16[1024,128]{1,0:T(8,128)(2,1)S(1)}, bf16[1024,128]{1,0:T(8,128)(2,1)S(1)}) custom-call(bf16[4,8,2,128,128]{4,3,2,1,0:T(8,128)(2,1)} %bitcast.54, bf16[4,128,128]{2,1,0:T(8,128)(2,1)S(1)} %collective-permute-done.refs_1_.above_ref, bf16[4,2,128,128]{3,2,1,0:T(8,128)(2,1)S(1)} %collective-permute-done.1.high_ref.refs_2_, ...), custom_call_target="tpu_custom_call" | custom-call | flops 805306368 | bytes 10970120 | tf_op jit(solution)/shard_map/pallas_call | solution.py:761
  99.7 0.1 collective-permute-start.6
  99.8 1.5 %collective-permute-done.6 = bf16[1024,128]{1,0:T(8,128)(2,1)S(1)} collective-permute-done((bf16[1024,128]{1,0:T(8,128)(2,1)S(1)}, bf16[1024,128]{1,0:T(8,128)(2,1)S(1)}, u32[]{:S(2)}, u32[]{:S(2)}) %collective-permute-start.6) | collective-permute-done | bytes 262176 | tf_op jit(solution)/shard_map/ppermute | solution.py:809
  101.3 0.1 add_convert_fusion
  101.4 13.6 %all_to_all.31.in_ref = bf16[16,64,128]{2,1,0:T(8,128)(2,1)S(1)} all-to-all(bf16[16,64,128]{2,1,0:T(8,128)(2,1)S(1)} %bitcast.55), channel_id=1, replica_groups={{0,2,4,6,8,10,12,14,16,18,20,22,24,26,28,30},{1,3,5,7,9,11,13,15,17,19,..., dimensions={0} | all-to-all | bytes 524288 | tf_op jit(solution)/shard_map/all_to_all | solution.py:816
  115.0 0.8 shard_map.195
  115.7 3.5 %all-to-all-start.5 = ((bf16[16,64,128]{2,1,0:T(8,128)(2,1)}), bf16[16,64,128]{2,1,0:T(8,128)(2,1)S(1)}, u32[]{:S(2)}, u32[]{:S(2)}) async-start(bf16[16,64,128]{2,1,0:T(8,128)(2,1)} %shard_map.195), calls=%async_computation.5 | async-start | bytes 524288 | tf_op jit(solution)/shard_map/all_to_all | solution.py:816
  119.3 0.1 collective-permute-start.7
  119.4 1.9 %collective-permute-start.8 = (bf16[8,32,128]{2,1,0:T(8,128)(2,1)S(1)}, bf16[8,32,128]{2,1,0:T(8,128)(2,1)S(1)}, u32[]{:S(2)}, u32[]{:S(2)}) collective-permute-start(bf16[8,32,128]{2,1,0:T(8,128)(2,1)S(1)} %get-tuple-element.103), channel_id=1, source_target_pairs={{0,2},{1,3},{2,0},{3,1},{4,6},{5,7},{6,4},{7,5},{8,10},{9,11},{10,... | collective-permute-start | bytes 196616 | tf_op jit(solution)/shard_map/ppermute | solution.py:795
  121.3 1.4 %collective-permute-start.9 = (bf16[8,32,128]{2,1,0:T(8,128)(2,1)S(1)}, bf16[8,32,128]{2,1,0:T(8,128)(2,1)S(1)}, u32[]{:S(2)}, u32[]{:S(2)}) collective-permute-start(bf16[8,32,128]{2,1,0:T(8,128)(2,1)S(1)} %get-tuple-element.102), channel_id=1, source_target_pairs={{0,3},{1,0},{2,1},{3,2},{4,7},{5,4},{6,5},{7,6},{8,11},{9,8},{10,9... | collective-permute-start | bytes 196616 | tf_op jit(solution)/shard_map/ppermute | solution.py:795
  122.7 6.0 %all-to-all-done.5 = bf16[16,64,128]{2,1,0:T(8,128)(2,1)S(1)} async-done(((bf16[16,64,128]{2,1,0:T(8,128)(2,1)}), bf16[16,64,128]{2,1,0:T(8,128)(2,1)S(1)}, u32[]{:S(2)}, u32[]{:S(2)}) %all-to-all-start.5) | async-done | bytes 262176 | tf_op jit(solution)/shard_map/all_to_all | solution.py:816
  128.7 0.7 fusion.3
  129.4 0.8 collective-permute-done.10.other_ref
  130.2 1.0 shard_map.196
  (25 shorter events, 0.1 us)
Async XLA Ops:
  1.6 26.1 %copy-start.1 = (bf16[3,3,64,128]{3,2,1,0:T(8,128)(2,1)S(1)}, bf16[3,3,64,128]{3,2,1,0:T(8,128)(2,1)}, u32[]{:S(2)}) copy-start(bf16[3,3,64,128]{3,2,1,0:T(8,128)(2,1)} %weight_ref.1) | copy-start | bytes 442372
  1.6 7.7 %collective-permute-start = (bf16[4,128,128]{2,1,0:T(8,128)(2,1)S(1)}, bf16[4,128,128]{2,1,0:T(8,128)(2,1)S(1)}, u32[]{:S(2)}, u32[]{:S(2)}) collective-permute-start(bf16[4,128,128]{2,1,0:T(8,128)(2,1)S(1)} %slice_bitcast_fusion.last_ref), channel_id=1, source_target_pairs={{0,4},{4,8},{8,12},{12,16},{16,20},{20,24},{24,28},{1,5},{5,9},{9,... | collective-permute-start | bytes 393224 | tf_op jit(solution)/shard_map/ppermute | solution.py:776
  7.7 20.5 %copy-start.8 = (s32[16,8,32]{2,1,0:T(8,128)S(1)}, s32[16,8,32]{2,1,0:T(8,128)}, u32[]{:S(2)}) copy-start(s32[16,8,32]{2,1,0:T(8,128)} %param.14) | copy-start | bytes 49156
  7.7 20.5 %copy-start.9 = (bf16[8,32,128]{2,1,0:T(8,128)(2,1)S(1)}, bf16[8,32,128]{2,1,0:T(8,128)(2,1)}, u32[]{:S(2)}) copy-start(bf16[8,32,128]{2,1,0:T(8,128)(2,1)} %param.15) | copy-start | bytes 196612
  9.3 18.3 %collective-permute-start.1 = (bf16[4,2,128,128]{3,2,1,0:T(8,128)(2,1)S(1)}, bf16[4,2,128,128]{3,2,1,0:T(8,128)(2,1)S(1)}, u32[]{:S(2)}, u32[]{:S(2)}) collective-permute-start(bf16[4,2,128,128]{3,2,1,0:T(8,128)(2,1)S(1)} %get-tuple-element.56), channel_id=1, source_target_pairs={{0,4},{4,8},{8,12},{12,16},{16,20},{20,24},{24,28},{1,5},{5,9},{9,... | collective-permute-start | bytes 786440 | tf_op jit(solution)/shard_map/ppermute | solution.py:776
  13.7 14.0 %collective-permute-start.2 = (bf16[4,2,128,128]{3,2,1,0:T(8,128)(2,1)S(1)}, bf16[4,2,128,128]{3,2,1,0:T(8,128)(2,1)S(1)}, u32[]{:S(2)}, u32[]{:S(2)}) collective-permute-start(bf16[4,2,128,128]{3,2,1,0:T(8,128)(2,1)S(1)} %get-tuple-element.57), channel_id=1, source_target_pairs={{4,0},{8,4},{12,8},{16,12},{20,16},{24,20},{28,24},{5,1},{9,5},{13... | collective-permute-start | bytes 786440 | tf_op jit(solution)/shard_map/ppermute | solution.py:776
  15.8 18.6 %copy-start.4 = (f32[128]{0:T(128)S(1)}, f32[128]{0:T(128)}, u32[]{:S(2)}) copy-start(f32[128]{0:T(128)} %param.17) | copy-start | bytes 1540
  15.8 18.6 %copy-start.7 = (f32[128]{0:T(128)S(1)}, f32[128]{0:T(128)}, u32[]{:S(2)}) copy-start(f32[128]{0:T(128)} %param.18) | copy-start | bytes 1540
  19.9 14.5 %all-to-all-start = ((f32[8,8,128]{2,1,0:T(8,128)}), f32[8,8,128]{2,1,0:T(8,128)S(1)}, u32[]{:S(2)}, u32[]{:S(2)}) async-start(f32[8,8,128]{2,1,0:T(8,128)} %get-tuple-element.58), calls=%async_computation | async-start | bytes 65536 | tf_op jit(solution)/shard_map/all_to_all | solution.py:800
  28.2 15.2 %collective-permute-start.3 = (bf16[384,128]{1,0:T(8,128)(2,1)S(1)}, bf16[384,128]{1,0:T(8,128)(2,1)S(1)}, u32[]{:S(2)}, u32[]{:S(2)}) collective-permute-start(bf16[384,128]{1,0:T(8,128)(2,1)S(1)} %get-tuple-element.105), channel_id=1, source_target_pairs={{1,0},{2,1},{3,2},{0,3},{5,4},{6,5},{7,6},{4,7},{9,8},{10,9},{11,1... | collective-permute-start | bytes 294920 | tf_op jit(solution)/shard_map/ppermute | solution.py:784
  28.3 15.2 %collective-permute-start.4 = (bf16[384,128]{1,0:T(8,128)(2,1)S(1)}, bf16[384,128]{1,0:T(8,128)(2,1)S(1)}, u32[]{:S(2)}, u32[]{:S(2)}) collective-permute-start(bf16[384,128]{1,0:T(8,128)(2,1)S(1)} %get-tuple-element.105), channel_id=1, source_target_pairs={{2,0},{3,1},{0,2},{1,3},{6,4},{7,5},{4,6},{5,7},{10,8},{11,9},{8,1... | collective-permute-start | bytes 294920 | tf_op jit(solution)/shard_map/ppermute | solution.py:784
  29.8 13.6 %collective-permute-start.5 = (bf16[384,128]{1,0:T(8,128)(2,1)S(1)}, bf16[384,128]{1,0:T(8,128)(2,1)S(1)}, u32[]{:S(2)}, u32[]{:S(2)}) collective-permute-start(bf16[384,128]{1,0:T(8,128)(2,1)S(1)} %get-tuple-element.105), channel_id=1, source_target_pairs={{3,0},{0,1},{1,2},{2,3},{7,4},{4,5},{5,6},{6,7},{11,8},{8,9},{9,10... | collective-permute-start | bytes 294920 | tf_op jit(solution)/shard_map/ppermute | solution.py:784
  34.4 15.7 %copy-start.2 = (f32[128]{0:T(128)S(1)}, f32[128]{0:T(128)}, u32[]{:S(2)}) copy-start(f32[128]{0:T(128)} %param.20) | copy-start | bytes 1540
  34.4 15.7 %copy-start.3 = (f32[128]{0:T(128)S(1)}, f32[128]{0:T(128)}, u32[]{:S(2)}) copy-start(f32[128]{0:T(128)} %param.21) | copy-start | bytes 1540
  34.4 15.7 %copy-start.5 = (bf16[128,64]{0,1:T(8,128)(2,1)S(1)}, bf16[128,64]{0,1:T(8,128)(2,1)}, u32[]{:S(2)}) copy-start(bf16[128,64]{0,1:T(8,128)(2,1)} %param.22) | copy-start | bytes 49156
  34.4 15.7 %copy-start.6 = (f32[16,4]{0,1:T(4,128)S(1)}, f32[16,4]{0,1:T(4,128)}, u32[]{:S(2)}) copy-start(f32[16,4]{0,1:T(4,128)} %param.23) | copy-start | bytes 772
  40.0 22.3 %copy-start = (bf16[4,8,128,128]{3,2,1,0:T(8,128)(2,1)S(1)}, bf16[4,8,128,128]{3,2,1,0:T(8,128)(2,1)}, u32[]{:S(2)}) copy-start(bf16[4,8,128,128]{3,2,1,0:T(8,128)(2,1)} %get-tuple-element.64.block_ref.refs_4_.refs_2_) | copy-start | bytes 3145732
  40.0 10.1 %all-to-all-start.1 = ((f32[8,8,128]{2,1,0:T(8,128)}), f32[8,8,128]{2,1,0:T(8,128)S(1)}, u32[]{:S(2)}, u32[]{:S(2)}) async-start(f32[8,8,128]{2,1,0:T(8,128)} %get-tuple-element.65), calls=%async_computation.1 | async-start | bytes 65536 | tf_op jit(solution)/shard_map/all_to_all | solution.py:800
  85.3 10.0 %all-to-all-start.3 = ((f32[8,8,128]{2,1,0:T(8,128)}), f32[8,8,128]{2,1,0:T(8,128)S(1)}, u32[]{:S(2)}, u32[]{:S(2)}) async-start(f32[8,8,128]{2,1,0:T(8,128)} %get-tuple-element.80), calls=%async_computation.3 | async-start | bytes 65536 | tf_op jit(solution)/shard_map/all_to_all | solution.py:800
  99.7 1.6 %collective-permute-start.6 = (bf16[1024,128]{1,0:T(8,128)(2,1)S(1)}, bf16[1024,128]{1,0:T(8,128)(2,1)S(1)}, u32[]{:S(2)}, u32[]{:S(2)}) collective-permute-start(bf16[1024,128]{1,0:T(8,128)(2,1)S(1)} %get-tuple-element.89), channel_id=1, source_target_pairs={{0,1},{1,0},{2,3},{3,2},{4,5},{5,4},{6,7},{7,6},{8,9},{9,8},{10,11... | collective-permute-start | bytes 786440 | tf_op jit(solution)/shard_map/ppermute | solution.py:809
  115.7 13.0 %all-to-all-start.5 = ((bf16[16,64,128]{2,1,0:T(8,128)(2,1)}), bf16[16,64,128]{2,1,0:T(8,128)(2,1)S(1)}, u32[]{:S(2)}, u32[]{:S(2)}) async-start(bf16[16,64,128]{2,1,0:T(8,128)(2,1)} %shard_map.195), calls=%async_computation.5 | async-start | bytes 524288 | tf_op jit(solution)/shard_map/all_to_all | solution.py:816
  119.3 9.4 %collective-permute-start.7 = (bf16[8,32,128]{2,1,0:T(8,128)(2,1)S(1)}, bf16[8,32,128]{2,1,0:T(8,128)(2,1)S(1)}, u32[]{:S(2)}, u32[]{:S(2)}) collective-permute-start(bf16[8,32,128]{2,1,0:T(8,128)(2,1)S(1)} %get-tuple-element.101), channel_id=1, source_target_pairs={{0,1},{1,2},{2,3},{3,0},{4,5},{5,6},{6,7},{7,4},{8,9},{9,10},{10,1... | collective-permute-start | bytes 196616 | tf_op jit(solution)/shard_map/ppermute | solution.py:795
  119.4 9.3 %collective-permute-start.8 = (bf16[8,32,128]{2,1,0:T(8,128)(2,1)S(1)}, bf16[8,32,128]{2,1,0:T(8,128)(2,1)S(1)}, u32[]{:S(2)}, u32[]{:S(2)}) collective-permute-start(bf16[8,32,128]{2,1,0:T(8,128)(2,1)S(1)} %get-tuple-element.103), channel_id=1, source_target_pairs={{0,2},{1,3},{2,0},{3,1},{4,6},{5,7},{6,4},{7,5},{8,10},{9,11},{10,... | collective-permute-start | bytes 196616 | tf_op jit(solution)/shard_map/ppermute | solution.py:795
  121.3 7.4 %collective-permute-start.9 = (bf16[8,32,128]{2,1,0:T(8,128)(2,1)S(1)}, bf16[8,32,128]{2,1,0:T(8,128)(2,1)S(1)}, u32[]{:S(2)}, u32[]{:S(2)}) collective-permute-start(bf16[8,32,128]{2,1,0:T(8,128)(2,1)S(1)} %get-tuple-element.102), channel_id=1, source_target_pairs={{0,3},{1,0},{2,1},{3,2},{4,7},{5,4},{6,5},{7,6},{8,11},{9,8},{10,9... | collective-permute-start | bytes 196616 | tf_op jit(solution)/shard_map/ppermute | solution.py:795
  128.7 1.5 %collective-permute-start.10 = (bf16[1024,128]{1,0:T(8,128)(2,1)S(1)}, bf16[1024,128]{1,0:T(8,128)(2,1)S(1)}, u32[]{:S(2)}, u32[]{:S(2)}) collective-permute-start(bf16[1024,128]{1,0:T(8,128)(2,1)S(1)} %bitcast.40), channel_id=1, source_target_pairs={{0,1},{1,0},{2,3},{3,2},{4,5},{5,4},{6,7},{7,6},{8,9},{9,8},{10,11... | collective-permute-start | bytes 786440 | tf_op jit(solution)/shard_map/ppermute | solution.py:809

commit v6 on v5

--- a/solution.py
+++ b/solution.py
@@ -105,11 +105,11 @@
     return (both[..., :width] + from_left(both[..., width:])).astype(BF16)
 
 
-def down_kernel(dates, img_ref, above_ref, weight_ref, out_ref, sums_ref, table):
-    date = pl.program_id(0)
-
-    @pl.when(date == 0)
-    def _():
+def down_kernel(
+    date, dates, img_ref, above_ref, weight_ref, out_ref, sums_ref, table
+):
+
+    if date == 0:
         down_table(weight_ref, table)
 
     even, odd = img_ref[0, :, 0], img_ref[0, :, 1]
@@ -120,7 +120,9 @@
     store_sums(sums_ref, date, dates, column_sum(values), column_sum(values * values))
 
 
-def edge_kernel(high_ref, above_ref, last_ref, below_ref, weight_ref, up_ref, down_ref, table):
+def edge_kernel(
+    step, steps, high_ref, above_ref, last_ref, below_ref, weight_ref, up_ref, down_ref, table
+):
     dates = above_ref.shape[0]
     down_table(weight_ref, table)
     taps = [
@@ -134,9 +136,8 @@
 
 
 def block_kernel(
+    date,
     dates,
-    norm_count,
-    row_devs,
     edge_ref,
     conv_ref,
     up_ref,
@@ -150,12 +151,13 @@
     norm_ref,
     sums_ref,
     table,
+    *,
+    norm_count,
+    row_devs,
 ):
-    date = pl.program_id(0)
     width = conv_ref.shape[-1]
 
-    @pl.when(date == 0)
-    def _():
+    if date == 0:
         norm_table(stats_ref, norm_ref, dates, norm_count)
         for row_tap in range(3):
             for col_tap in range(3):
@@ -238,9 +240,8 @@
 
 
 def score_kernel(
+    date,
     dates,
-    norm_count,
-    grad_scale,
     day_ref,
     block_ref,
     stats_ref,
@@ -262,12 +263,13 @@
     mean,
     spread_ref,
     score_ref,
+    *,
+    norm_count,
+    grad_scale,
 ):
-    date = pl.program_id(0)
     rows, cols, width = block_ref.shape[1:]
 
-    @pl.when(date == 0)
-    def _():
+    if date == 0:
         norm_table(stats_ref, norm_ref, dates, norm_count)
         fold_keys(key_ref, query_ref, wide_ref, vector_ref, spread_ref, score_ref)
         total[...] = jnp.zeros_like(total)
@@ -276,7 +278,7 @@
     scale = norm_ref[pl.ds(dates + date, 1), :] * gain_ref[...]
     shift = shift_ref[...] - norm_ref[pl.ds(date, 1), :] * scale
     linear = block_ref[0].astype(F32) * scale + shift
-    features = (linear * sigmoid(linear) + encoding(day_ref[date], width)).astype(BF16)
+    features = (linear * sigmoid(linear) + encoding(day_ref[turn_ref[0] * dates + date], width)).astype(BF16)
     feat_ref[0] = features
     upstream = upstream_rows(grad_ref, turn_ref, rows, cols)
     parts = split(upstream.astype(F32) * features.astype(F32))
@@ -288,7 +290,7 @@
     valid = jnp.zeros((rows, width), F32)
     for device in range(devices):
         piece = valid_ref[
-            source_of(turn_ref, device, devices), pl.ds(pl.multiple_of(date * rows, rows), rows), :
+            source_of(turn_ref, device, devices), pl.ds(date * rows, rows), :
         ]
         valid = valid + pltpu.roll(piece, device * (cols // devices), 1)
     diagonal = lax.broadcasted_iota(jnp.int32, (cols, cols), 0) == lax.broadcasted_iota(
@@ -307,8 +309,7 @@
     exp_ref[0] = exponent
     attn_ref[0] = attn
 
-    @pl.when(date == dates - 1)
-    def _():
+    if date == dates - 1:
         place = lax.broadcasted_iota(jnp.int32, (cols, width), 1) % rows
         for index, source in enumerate((total, mean)):
             dense = jnp.zeros((cols, width), F32)
@@ -319,8 +320,8 @@
 
 
 def attend_kernel(
+    date,
     dates,
-    grad_scale,
     packed_ref,
     feat_ref,
     exp_ref,
@@ -341,12 +342,12 @@
     inverse,
     average,
     attended,
+    *,
+    grad_scale,
 ):
-    date = pl.program_id(0)
     rows, cols, width = block_ref.shape[1:]
 
-    @pl.when(date == 0)
-    def _():
+    if date == 0:
         denominator = jnp.sum(packed_ref[:, 0], axis=0)
         reciprocal = 1.0 / denominator
         mean = jnp.sum(packed_ref[:, 0] * reciprocal * packed_ref[:, 1], axis=0)
@@ -390,8 +391,7 @@
     store_sums(sums_ref, date, dates, first * gain, second * gain)
     grad_out_ref[0] = (linear_grad * gain).astype(BF16)
 
-    @pl.when(date == dates - 1)
-    def _():
+    if date == dates - 1:
         devices, piece = part_ref.shape[0], part_ref.shape[2]
         for device in range(devices):
             part_ref[device] = attended[:, device * piece : (device + 1) * piece].astype(BF16)
@@ -405,9 +405,8 @@
 
 
 def hidden_kernel(
+    date,
     dates,
-    norm_count,
-    row_devs,
     edge_ref,
     grad_ref,
     block_ref,
@@ -427,12 +426,13 @@
     table,
     factors,
     padded,
+    *,
+    norm_count,
+    row_devs,
 ):
-    date = pl.program_id(0)
     rows, cols, width = block_ref.shape[1:]
 
-    @pl.when(date == 0)
-    def _():
+    if date == 0:
         tails = group_sum(jnp.sum(tails_ref[...], axis=0)) / norm_count
         mean, inverse = norm_ref[:dates], norm_ref[dates:]
         slope = -inverse * inverse * tails[dates:]
@@ -491,12 +491,12 @@
     store_sums(sums_ref, date, dates, first * gain, second * gain)
 
 
-def block_grad_kernel(dates, hidden_ref, pre_ref, key_ref, out_ref, total):
-    date = pl.program_id(0)
+def block_grad_kernel(
+    date, dates, hidden_ref, pre_ref, key_ref, out_ref, total
+):
     rows, cols, width = pre_ref.shape[1:]
 
-    @pl.when(date == 0)
-    def _():
+    if date == 0:
         total[...] = jnp.zeros_like(total)
 
     grads = pre_ref[0].astype(F32)
@@ -508,8 +508,7 @@
     ).reshape(rows * cols, 3 * width)
     total[...] += product(taps, grads, 0, 0)
 
-    @pl.when(date == dates - 1)
-    def _():
+    if date == dates - 1:
         for row_tap in range(3):
             for col_tap in range(3):
                 base = (row_tap * 3 + col_tap) * width
@@ -528,8 +527,8 @@
 
 
 def conv_grad_kernel(
+    date,
     dates,
-    norm_count,
     img_ref,
     above_ref,
     high_ref,
@@ -548,13 +547,13 @@
     factors,
     total,
     out_ref,
+    *,
+    norm_count,
 ):
-    date = pl.program_id(0)
     rows, cols, width = conv_ref.shape[1:]
     half = width // 2
 
-    @pl.when(date == 0)
-    def _():
+    if date == 0:
         tails = group_sum(jnp.sum(tails_ref[...], axis=0)) / norm_count
         mean, inverse = norm_ref[:dates], norm_ref[dates:]
         slope = -inverse * inverse * tails[dates:]
@@ -583,8 +582,7 @@
     taps = jnp.concatenate(taps, axis=-1).reshape(reach * cols, 3 * width)
     total[...] += product(taps, grads, 0, 0)
 
-    @pl.when(date == dates - 1)
-    def _():
+    if date == dates - 1:
         begin = block_rows_ref.shape[0]
         out_ref[:begin] = block_rows_ref[...]
         for tap in range(3):
@@ -665,107 +663,75 @@
     query_ref[...] = query[:depth]
 
 
-def per_date(shape):
-    zeros = (0,) * (len(shape) - 1)
-    return pl.BlockSpec((1,) + tuple(shape[1:]), lambda date: (date,) + zeros)
-
-
-def streamed(kernel, dates, kinds, out_kinds, stream):
-    loads = [place for place, kind in enumerate(kinds) if stream and kind != "scalar"]
-    stores = [place for place, kind in enumerate(out_kinds) if kind == "direct"]
-
-    def body(*refs):
-        inputs, rest = list(refs[: len(kinds)]), refs[len(kinds) :]
-        outputs, scratch = list(rest[: len(out_kinds)]), rest[len(out_kinds) :]
-        loaded, scratch = scratch[: len(loads)], scratch[len(loads) :]
-        stored, scratch = scratch[: len(stores)], scratch[len(stores) :]
-        ready, done, scratch = scratch[0], scratch[1], scratch[2:]
-        date = pl.program_id(0)
-        views, results = list(inputs), list(outputs)
-
-        def load(index, step):
-            source, target = inputs[loads[index]], loaded[index]
-            if kinds[loads[index]] == "date":
-                source, target = source.at[step], target.at[step]
-            return pltpu.make_async_copy(source, target, ready.at[index, step])
-
-        def store(index, step):
-            source, target = stored[index].at[step], outputs[stores[index]].at[step]
-            return pltpu.make_async_copy(source, target, done.at[index, step])
-
-        @pl.when(date == 0)
-        def _():
-            for step in range(dates):
-                for index, place in enumerate(loads):
-                    if step == 0 or kinds[place] == "date":
-                        load(index, step).start()
-            for index, place in enumerate(loads):
-                if kinds[place] != "date":
-                    load(index, 0).wait()
-
-        for index, place in enumerate(loads):
-            if kinds[place] == "date":
-                load(index, date).wait()
-                views[place] = loaded[index].at[pl.ds(date, 1)]
-            else:
-                views[place] = loaded[index]
-        for index, place in enumerate(stores):
-            results[place] = stored[index].at[pl.ds(date, 1)]
-        kernel(*views, *results, *scratch)
-        for index in range(len(stores)):
-            store(index, date).start()
-
-        @pl.when(date == dates - 1)
-        def _():
-            for step in range(dates):
-                for index in range(len(stores)):
-                    store(index, step).wait()
-
-    return body
-
-
-def whole(shape):
-    zeros = (0,) * len(shape)
-    return pl.BlockSpec(tuple(shape), lambda date: zeros)
-
-
-def call(kernel, dates, inputs, outputs, scratch, flops, stream=False):
-    in_specs, arrays, buffers = [], [], []
-    for kind, array in inputs:
-        large = array.size * array.dtype.itemsize >= MIB // 2
-        if kind in ("far", "still") or (stream and kind == "date" and large):
-            array = pltpu.with_memory_space_constraint(array, pltpu.HBM)
-        arrays.append(array)
+def call(kernel, dates, inputs, outputs, scratch, flops):
+    in_specs, out_specs, arrays, out_shape, buffers = [], [], [], [], []
+    in_vmem, in_hbm = pl.BlockSpec(memory_space=pltpu.VMEM), pl.BlockSpec(memory_space=pltpu.HBM)
+    loads, stores = [], []
+    for place, (kind, array) in enumerate(inputs):
         if kind == "scalar":
             in_specs.append(pl.BlockSpec(memory_space=pltpu.SMEM))
-        elif stream:
-            in_specs.append(pl.BlockSpec(memory_space=pl.ANY))
+        elif "far" in kind:
+            array = pltpu.with_memory_space_constraint(array, pltpu.HBM)
+            in_specs.append(in_hbm)
+            loads.append(place)
             buffers.append(pltpu.VMEM(array.shape, array.dtype))
         else:
-            in_specs.append((per_date if kind in ("date", "far") else whole)(array.shape))
-    out_specs, out_shape = [], []
-    for kind, shape, dtype in outputs:
-        if kind == "direct":
-            out_specs.append(pl.BlockSpec(memory_space=pltpu.HBM))
+            in_specs.append(in_vmem)
+        arrays.append(array)
+    for place, (kind, shape, dtype) in enumerate(outputs):
+        if "far" in kind:
+            out_shape.append(pltpu.HBM(shape, dtype))
+            out_specs.append(in_hbm)
+            stores.append(place)
             buffers.append(pltpu.VMEM(shape, dtype))
         else:
-            out_specs.append((per_date if kind == "date" else whole)(shape))
-        pinned = kind == "direct" or (stream and kind == "date")
-        out_shape.append((pltpu.HBM if pinned else jax.ShapeDtypeStruct)(shape, dtype))
+            out_shape.append(jax.ShapeDtypeStruct(shape, dtype))
+            out_specs.append(in_vmem)
+    copies = len(loads) + len(stores)
+
+    def body(*refs):
+        views, rest = list(refs[: len(inputs)]), refs[len(inputs) :]
+        results, rest = list(rest[: len(outputs)]), rest[len(outputs) :]
+        buffer_refs, rest = rest[:copies], rest[copies:]
+        started = []
+        for index, place in enumerate(loads):
+            started.append(
+                pltpu.make_async_copy(views[place], buffer_refs[index], rest[0].at[index])
+            )
+            started[-1].start()
+            views[place] = buffer_refs[index]
+        sent = []
+        for index, place in enumerate(stores):
+            buffer = buffer_refs[len(loads) + index]
+            sent.append(
+                pltpu.make_async_copy(buffer, results[place], rest[0].at[len(loads) + index])
+            )
+            results[place] = buffer
+        for copy in started:
+            copy.wait()
+        for date in range(dates):
+            ins = [
+                view.at[pl.ds(date, 1)] if "date" in kind else view
+                for view, (kind, _) in zip(views, inputs)
+            ]
+            outs = [
+                result.at[pl.ds(date, 1)] if "date" in kind else result
+                for result, (kind, _, _) in zip(results, outputs)
+            ]
+            kernel(date, dates, *ins, *outs, *rest[1:])
+        for copy in sent:
+            copy.start()
+        for copy in sent:
+            copy.wait()
+
     moved = sum(array.size * array.dtype.itemsize for _, array in inputs)
-    if buffers:
-        kinds, out_kinds = [kind for kind, _ in inputs], [kind for kind, _, _ in outputs]
-        kernel = streamed(kernel, dates, kinds, out_kinds, stream)
-        ready = pltpu.SemaphoreType.DMA((max(len(inputs), len(outputs)), dates))
-        scratch = buffers + [ready, ready] + scratch
     return pl.pallas_call(
-        kernel,
-        grid=(dates,),
+        body,
         in_specs=in_specs,
         out_specs=out_specs,
         out_shape=out_shape,
-        scratch_shapes=scratch,
-        compiler_params=pltpu.CompilerParams(vmem_limit_bytes=(40 if stream else 24) * MIB),
+        scratch_shapes=buffers + [pltpu.SemaphoreType.DMA((max(copies, 1),))] + scratch,
+        compiler_params=pltpu.CompilerParams(vmem_limit_bytes=40 * MIB),
         cost_estimate=pl.CostEstimate(flops=flops, bytes_accessed=2 * moved, transcendentals=0),
     )(*arrays)
 
@@ -783,6 +749,16 @@
         pairs = [((i + step) % devices, i) for i in range(devices)]
         pieces.append(lax.ppermute(array, "dates", pairs))
     return jnp.stack(pieces)
+
+
+def row_totals(sums):
+    devices = lax.axis_size("rows")
+    step = 1
+    while step < devices:
+        pairs = [(i, i ^ step) for i in range(devices)]
+        sums = sums + lax.ppermute(sums, "rows", pairs)
+        step *= 2
+    return sums
 
 
 def sum_of_parts(parts):
@@ -871,68 +847,69 @@
     gn_gain, gn_shift = rows_of(gn_gain), rows_of(gn_shift)
     last = images[:, -1]
     above = shifted(last, 1)
-    high, below, above = lax.optimization_barrier((images[:, -3:-1], images[:, :2], above))
-    high, below = shifted(high, 1), shifted(below, -1)
-    paired = images.reshape(dates, rows, 2, cols, pair_width)
-    conv_out, sums = call(
-        functools.partial(down_kernel, dates),
-        dates,
-        [("date", paired), ("date", above), ("still", conv_weight)],
-        [("date", frame, BF16), ("all", (row_devs, 2 * dates, width), F32)],
-        [pltpu.VMEM((3 * pair_width, 2 * width), BF16)],
-        6 * flops,
-        True,
-    )
-    stats = exchange(sums, "rows")
-    high, below, last, _ = lax.optimization_barrier((high, below, last, sums))
-    halo_up, halo_down = pl.pallas_call(
-        edge_kernel,
-        out_shape=[jax.ShapeDtypeStruct(edge_rows, BF16)] * 2,
-        scratch_shapes=[pltpu.VMEM((3 * pair_width, 2 * width), BF16)],
-        compiler_params=pltpu.CompilerParams(vmem_limit_bytes=16 * MIB),
-    )(high, above, last, below, conv_weight)
-    valid, out_grad, _ = lax.optimization_barrier((valid, out_grad, halo_up))
     grad_rows = out_grad.size // width
     valid_rows = valid.astype(BF16).reshape(valid.shape[0] * rows, -1)
     valid_rows = jnp.pad(valid_rows, ((0, 0), (0, width - valid_rows.shape[1])))
     packed = jnp.concatenate([out_grad.reshape(grad_rows, width), valid_rows])
+    high, below, above, packed = lax.optimization_barrier(
+        (images[:, -3:-1], images[:, :2], above, packed)
+    )
+    high, below = shifted(high, 1), shifted(below, -1)
+    paired = images.reshape(dates, rows, 2, cols, pair_width)
+    conv_out, sums = call(
+        down_kernel,
+        dates,
+        [("date far", paired), ("date", above), ("all far", conv_weight)],
+        [("date far", frame, BF16), ("all", (row_devs, 2 * dates, width), F32)],
+        [pltpu.VMEM((3 * pair_width, 2 * width), BF16)],
+        6 * flops,
+    )
+    stats = exchange(sums, "rows")
+    high, below, last, _ = lax.optimization_barrier((high, below, last, sums))
+    halo_up, halo_down = call(
+        edge_kernel,
+        1,
+        [("all", high), ("all", above), ("all", last), ("all", below), ("all far", conv_weight)],
+        [("all far", edge_rows, BF16)] * 2,
+        [pltpu.VMEM((3 * pair_width, 2 * width), BF16)],
+        6 * flops // rows,
+    )
+    packed, _ = lax.optimization_barrier((packed, halo_up))
     sources = turned(packed)
     clear = lax.dynamic_slice_in_dim(sources, grad_rows + date_start * rows, dates * rows, 1)
     clear = clear.astype(F32)
-    days = lax.dynamic_slice_in_dim(day_index, date_start, dates, 0)
     turn = lax.axis_index("dates").reshape(1)
     place = lax.axis_index("rows").reshape(1)
 
     block_out, hidden, first_norm, sums = call(
-        functools.partial(block_kernel, dates, norm_count, row_devs),
+        functools.partial(block_kernel, norm_count=norm_count, row_devs=row_devs),
         dates,
         [
             ("scalar", place),
-            ("date", conv_out),
-            ("date", halo_up),
-            ("date", halo_down),
+            ("date far", conv_out),
+            ("date far", halo_up),
+            ("date far", halo_down),
             ("all", stats),
             ("all", first_gain),
             ("all", first_shift),
-            ("still", block_weight),
-        ],
-        [
-            ("date", frame, BF16),
-            ("date", (dates, rows + 2, cols, width), BF16),
+            ("all far", block_weight),
+        ],
+        [
+            ("date far", frame, BF16),
+            ("date far", (dates, rows + 2, cols, width), BF16),
             ("all", (2 * dates, width), F32),
             ("all", (row_devs, 2 * dates, width), F32),
         ],
         [pltpu.VMEM((3 * width, 3 * width), BF16)],
         9 * flops,
-        True,
     )
     stats = exchange(sums, "rows")
     features, exponent, attn, norm, packed, key_wide, query_wide = call(
-        functools.partial(score_kernel, dates, norm_count, grad_scale),
+        functools.partial(score_kernel, norm_count=norm_count, grad_scale=grad_scale),
         dates,
         [
-            ("scalar", days),
-            ("far", block_out),
+            ("scalar", day_index),
+            ("date far", block_out),
             ("all", stats),
             ("all", gn_gain),
             ("all", gn_shift),
@@ -961,10 +938,10 @@
     )
     packed = gather(packed, "dates")
     block_grad, attended, key_part, vectors, sums = call(
-        functools.partial(attend_kernel, dates, grad_scale),
+        functools.partial(attend_kernel, grad_scale=grad_scale),
         dates,
         [
-            ("still", packed),
+            ("all", packed),
             ("date", features),
             ("date", exponent),
             ("date", attn),
@@ -978,36 +955,36 @@
             ("all", key_wide),
         ],
         [
-            ("direct", frame, BF16),
-            ("all", (date_devs, rows, cols // date_devs, width), BF16),
-            ("all", (width, width), F32),
+            ("date far", frame, BF16),
+            ("all far", (date_devs, rows, cols // date_devs, width), BF16),
+            ("all far", (width, width), F32),
             ("all", (8, width), F32),
-            ("all", (row_devs, 2 * dates, width), F32),
+            ("all", (1, 2 * dates, width), F32),
         ],
         [pltpu.VMEM(frame[1:], F32)] * 3,
         5 * flops,
     )
-    tails = exchange(sums, "rows")
+    tails = row_totals(sums)
     pre_grad, linear_grad, first_vectors, sums = call(
-        functools.partial(hidden_kernel, dates, norm_count, row_devs),
+        functools.partial(hidden_kernel, norm_count=norm_count, row_devs=row_devs),
         dates,
         [
             ("scalar", place),
-            ("date", block_grad),
-            ("date", block_out),
+            ("date far", block_grad),
+            ("date far", block_out),
             ("all", tails),
             ("all", norm),
-            ("still", block_weight),
-            ("date", conv_out),
-            ("date", halo_up),
-            ("date", halo_down),
+            ("all far", block_weight),
+            ("date far", conv_out),
+            ("date far", halo_up),
+            ("date far", halo_down),
             ("all", first_norm),
             ("all", first_gain),
             ("all", first_shift),
         ],
         [
-            ("date", frame, BF16),
-            ("date", (dates, rows + 2, cols, width), BF16),
+            ("date far", frame, BF16),
+            ("date far", (dates, rows + 2, cols, width), BF16),
             ("all", (8, width), F32),
             ("all", (row_devs, 2 * dates, width), F32),
         ],
@@ -1017,37 +994,35 @@
             pltpu.VMEM((rows + 4, cols, width), BF16),
         ],
         9 * flops,
-        True,
     )
     tails = exchange(sums, "rows")
     (block_rows,) = call(
-        functools.partial(block_grad_kernel, dates),
+        block_grad_kernel,
         dates,
-        [("date", hidden), ("date", pre_grad), ("all", key_part)],
-        [("all", (10 * width, width), BF16)],
+        [("date far", hidden), ("date far", pre_grad), ("all far", key_part)],
+        [("all far", (10 * width, width), BF16)],
         [pltpu.VMEM((3 * width, 3 * width), F32)],
         9 * flops,
-        True,
     )
     tails, block_rows = lax.optimization_barrier((tails, block_rows))
     conv_count = 9 * pair_width // 2 + 32
     half_rows = padded_count(10 * width + conv_count, devices) // 2
     keep, give = call(
-        functools.partial(conv_grad_kernel, dates, norm_count),
+        functools.partial(conv_grad_kernel, norm_count=norm_count),
         dates,
         [
-            ("date", paired),
+            ("date far", paired),
             ("date", above),
             ("date", high),
             ("date", below),
-            ("date", conv_out),
-            ("date", linear_grad),
+            ("date far", conv_out),
+            ("date far", linear_grad),
             ("all", tails),
             ("all", first_norm),
             ("all", first_gain),
             ("all", first_vectors),
             ("all", vectors),
-            ("all", block_rows),
+            ("all far", block_rows),
             ("scalar", turn),
         ],
         [("all", (half_rows, width), BF16)] * 2,
@@ -1057,7 +1032,6 @@
             pltpu.VMEM((2 * half_rows, width), BF16),
         ],
         6 * flops,
-        True,
     )
     rows_half = (keep.astype(F32) + other_core(give).astype(F32)).astype(BF16)
     pieces = scatter(rows_half)

time: 132 us -> 131 us (level)
  blocking collectives: 30.3 us -> 21.2 us
  waiting for transfers between devices: 23.6 us -> 30.4 us
  other arithmetic: 0.84 us -> 2.55 us
    ppermute x0 -> x3, waiting for transfers between devices: none -> 10.3 us  [row_totals(): sums = sums + lax.ppermute(sums, 'rows', pairs)]
    all_to_all x1 -> x0, blocking collectives: 9.06 us -> none  [exchange(): return lax.all_to_all(pieces, axes, split_axis=0, concat_axis=0, tiled=True)]
    all_to_all x3, waiting for transfers between devices: 13.6 us -> 11.8 us  [exchange(): return lax.all_to_all(pieces, axes, split_axis=0, concat_axis=0, tiled=True)]
    ppermute x3, waiting for transfers between devices: 1.63 us -> 0.01 us  [shifted(): return lax.ppermute(array, 'rows', pairs)]
    ppermute x0 -> x3, starting transfers between devices: none -> 1.45 us  [row_totals(): sums = sums + lax.ppermute(sums, 'rows', pairs)]
  transfers between devices with their start and end apart: 15 -> 18, of which waited for: 7 -> 9; matrix products, arithmetic and copies ran while one was open for 2% -> 3% of each run, Pallas kernels for 11% -> 13%
where the time goes in v6:
time: 131 us; the launch traced here: 130 us
  Pallas kernels  37.7 us (29%)
  starting transfers between devices  35.3 us (27%)
  waiting for transfers between devices  30.4 us (23%)
  blocking collectives  21.2 us (16%)
  other arithmetic  2.55 us (2%)
  local copies, waits for them, and re-layouts  2.06 us (2%)
    pallas_call x8, Pallas kernels, call(): pl.pallas_call(body, in_specs=in_specs, out_specs=out_specs, out_shape=ou...  35.9 us
    all_to_all x3, starting transfers between devices, exchange(): return lax.all_to_all(pieces, axes, split_axis=0, concat_axis=0, tiled=True)  14.6 us
    all_to_all x1, blocking collectives, exchange_cores(): lax.all_to_all(pieces, axes, split_axis=0, concat_axis=0, axis_index_grou...  13.9 us
    all_to_all x3, waiting for transfers between devices, exchange(): return lax.all_to_all(pieces, axes, split_axis=0, concat_axis=0, tiled=True)  11.8 us
    ppermute x3, starting transfers between devices, shifted(): return lax.ppermute(array, 'rows', pairs)  10.5 us
    ppermute x3, waiting for transfers between devices, row_totals(): sums = sums + lax.ppermute(sums, 'rows', pairs)  10.3 us
    all_gather x1, blocking collectives, gather(): return lax.all_gather(array, axis, axis=0, tiled=True)  7.35 us
    all_to_all x1, waiting for transfers between devices, exchange_cores(): lax.all_to_all(pieces, axes, split_axis=0, concat_axis=0, axis_index_grou...  5.95 us
  transfers between devices with their start and end apart: 18, of which 9 were waited for; matrix products, arithmetic and copies ran while one was open for 3% of the time, Pallas kernels for 13%

profile of v6, /device:TPU:0, one launch (start us, length us, event | category | flops | bytes accessed | tf_op | source)
XLA Modules:
  0.0 130.3 jit_solution(3765760648805784117)
XLA Ops:
  0.6 0.9 slice_bitcast_fusion.refs_2_
  1.6 4.9 %collective-permute-start = (bf16[4,128,128]{2,1,0:T(8,128)(2,1)S(1)}, bf16[4,128,128]{2,1,0:T(8,128)(2,1)S(1)}, u32[]{:S(2)}, u32[]{:S(2)}) collective-permute-start(bf16[4,128,128]{2,1,0:T(8,128)(2,1)S(1)} %slice_bitcast_fusion.refs_2_), channel_id=1, source_target_pairs={{0,4},{4,8},{8,12},{12,16},{16,20},{20,24},{24,28},{1,5},{5,9},{9,... | collective-permute-start | bytes 393224 | tf_op jit(solution)/shard_map/ppermute | solution.py:742
  6.5 1.1 fusion.5
  7.5 0.8 convert_bitcast_fusion
  8.4 0.9 fusion.4
  9.3 4.3 %collective-permute-start.1 = (bf16[4,2,128,128]{3,2,1,0:T(8,128)(2,1)S(1)}, bf16[4,2,128,128]{3,2,1,0:T(8,128)(2,1)S(1)}, u32[]{:S(2)}, u32[]{:S(2)}) collective-permute-start(bf16[4,2,128,128]{3,2,1,0:T(8,128)(2,1)S(1)} %get-tuple-element.56), channel_id=1, source_target_pairs={{0,4},{4,8},{8,12},{12,16},{16,20},{20,24},{24,28},{1,5},{5,9},{9,... | collective-permute-start | bytes 786440 | tf_op jit(solution)/shard_map/ppermute | solution.py:742
  13.6 1.3 collective-permute-start.2
  14.9 4.5 %shard_map.187 = (bf16[4,8,128,128]{3,2,1,0:T(8,128)(2,1)}, f32[8,8,128]{2,1,0:T(8,128)}) custom-call(bf16[4,8,2,128,128]{4,3,2,1,0:T(8,128)(2,1)} %bitcast.52, bf16[4,128,128]{2,1,0:T(8,128)(2,1)S(1)} %collective-permute-done.refs_1_, bf16[3,3,64,128]{3,2,1,0:T(8,128)(2,1)} %refs_4_.1), custom_call_target="tpu_custom_call" | custom-call | flops 805306368 | bytes 4751360 | tf_op jit(solution)/shard_map/pallas_call | solution.py:728
  19.4 7.8 %all-to-all-start = ((f32[8,8,128]{2,1,0:T(8,128)}), f32[8,8,128]{2,1,0:T(8,128)S(1)}, u32[]{:S(2)}, u32[]{:S(2)}) async-start(f32[8,8,128]{2,1,0:T(8,128)} %get-tuple-element.58), calls=%async_computation | async-start | bytes 65536 | tf_op jit(solution)/shard_map/all_to_all | solution.py:776
  27.2 2.0 %shard_map.188 = (bf16[4,128,128]{2,1,0:T(8,128)(2,1)}, bf16[4,128,128]{2,1,0:T(8,128)(2,1)}) custom-call(bf16[4,2,128,128]{3,2,1,0:T(8,128)(2,1)S(1)} %collective-permute-done.1.refs_0_.refs_2_, bf16[4,128,128]{2,1,0:T(8,128)(2,1)S(1)} %collective-permute-done.refs_1_, bf16[4,128,128]{2,1,0:T(8,128)(2,1)S(1)} %slice_bitcast_fusion.refs_2_, ...), custom_call_target="tpu_custom_call" | custom-call | flops 100663296 | bytes 1867776 | tf_op jit(solution)/shard_map/pallas_call | solution.py:728
  29.3 0.1 collective-permute-start.3
  29.3 1.6 %collective-permute-start.4 = (bf16[384,128]{1,0:T(8,128)(2,1)S(1)}, bf16[384,128]{1,0:T(8,128)(2,1)S(1)}, u32[]{:S(2)}, u32[]{:S(2)}) collective-permute-start(bf16[384,128]{1,0:T(8,128)(2,1)S(1)} %fusion.4), channel_id=1, source_target_pairs={{2,0},{3,1},{0,2},{1,3},{6,4},{7,5},{4,6},{5,7},{10,8},{11,9},{8,1... | collective-permute-start | bytes 294920 | tf_op jit(solution)/shard_map/ppermute | solution.py:750
  30.9 0.2 collective-permute-start.5
  31.1 2.8 %all-to-all-done.refs_4_ = f32[8,8,128]{2,1,0:T(8,128)S(1)} async-done(((f32[8,8,128]{2,1,0:T(8,128)}), f32[8,8,128]{2,1,0:T(8,128)S(1)}, u32[]{:S(2)}, u32[]{:S(2)}) %all-to-all-start) | async-done | bytes 32800 | tf_op jit(solution)/shard_map/all_to_all | solution.py:776
  33.9 0.0 copy-start.4
  33.9 0.0 copy-start.5
  33.9 5.7 %shard_map.189 = (bf16[4,8,128,128]{3,2,1,0:T(8,128)(2,1)}, bf16[4,10,128,128]{3,2,1,0:T(8,128)(2,1)}, f32[8,128]{1,0:T(8,128)S(1)}, f32[8,8,128]{2,1,0:T(8,128)}) custom-call(s32[1]{0:T(128)} %bitcast.refs_0_, bf16[4,8,128,128]{3,2,1,0:T(8,128)(2,1)} %get-tuple-element.55.refs_1_.refs_6_.refs_4_, bf16[4,128,128]{2,1,0:T(8,128)(2,1)} %get-tuple-element.62.refs_2_.refs_7_, ...), custom_call_target="tpu_custom_call" | custom-call | flops 1207959552 | bytes 3278856 | tf_op jit(solution)/shard_map/pallas_call | solution.py:728
  39.7 3.5 %all-to-all-start.1 = ((f32[8,8,128]{2,1,0:T(8,128)}), f32[8,8,128]{2,1,0:T(8,128)S(1)}, u32[]{:S(2)}, u32[]{:S(2)}) async-start(f32[8,8,128]{2,1,0:T(8,128)} %get-tuple-element.65), calls=%async_computation.1 | async-start | bytes 65536 | tf_op jit(solution)/shard_map/all_to_all | solution.py:776
  43.2 0.1 pad_maximum_fusion.refs_5_.refs_9_
  43.3 6.5 %all-to-all-done.1.refs_2_ = f32[8,8,128]{2,1,0:T(8,128)S(1)} async-done(((f32[8,8,128]{2,1,0:T(8,128)}), f32[8,8,128]{2,1,0:T(8,128)S(1)}, u32[]{:S(2)}, u32[]{:S(2)}) %all-to-all-start.1) | async-done | bytes 32800 | tf_op jit(solution)/shard_map/all_to_all | solution.py:776
  49.8 4.1 %shard_map.190 = (bf16[4,8,128,128]{3,2,1,0:T(8,128)(2,1)S(1)}, f32[4,8,128,128]{3,2,1,0:T(8,128)S(1)}, f32[4,8,128,128]{3,2,1,0:T(8,128)S(1)}, f32[8,128]{1,0:T...) custom-call(s32[16]{0:T(128)S(1)} %copy-done.6, ...), custom_call_target="tpu_custom_call" | custom-call | flops 671088640 | bytes 3115656 | tf_op jit(solution)/shard_map/pallas_call | solution.py:728
  53.9 7.4 %all_gather.3.refs_0_ = f32[4,2,128,128]{3,2,1,0:T(8,128)S(1)} all-gather(f32[1,2,128,128]{3,2,1,0:T(8,128)S(1)} %get-tuple-element.68), channel_id=1, replica_groups=mesh['rows'=8,'dates'=4] {'dates'}, dimensions={0}, use_global_device_ids=true | all-gather | bytes 655360 | tf_op jit(solution)/shard_map/all_gather | solution.py:780
  61.3 4.1 %shard_map.191 = (bf16[4,8,128,128]{3,2,1,0:T(8,128)(2,1)}, bf16[4,8,32,128]{3,2,1,0:T(8,128)(2,1)}, f32[128,128]{1,0:T(8,128)}, f32[8,128]{1,0:T(8,128)S(1)}, f32[1,8,128]{2,1,0:T(8,128)S(1)}) custom-call(f32[4,2,128,128]{3,2,1,0:T(8,128)S(1)} %all_gather.3.refs_0_, bf16[4,8,128,128]{3,2,1,0:T(8,128)(2,1)S(1)} %get-tuple-element.69.refs_1_, ...), custom_call_target="tpu_custom_call" | custom-call | flops 671088640 | bytes 14501896 | tf_op jit(solution)/shard_map/pallas_call | solution.py:728
  65.4 0.5 collective-permute-start.6
  65.9 3.1 %collective-permute-done.6 = f32[1,8,128]{2,1,0:T(8,128)S(1)} collective-permute-done((f32[1,8,128]{2,1,0:T(8,128)S(1)}, f32[1,8,128]{2,1,0:T(8,128)S(1)}, u32[]{:S(2)}, u32[]{:S(2)}) %collective-permute-start.6) | collective-permute-done | bytes 4128 | tf_op jit(solution)/shard_map/ppermute | solution.py:759
  69.1 0.4 collective-permute-start.7
  69.4 3.2 %collective-permute-done.7 = f32[1,8,128]{2,1,0:T(8,128)S(1)} collective-permute-done((f32[1,8,128]{2,1,0:T(8,128)S(1)}, f32[1,8,128]{2,1,0:T(8,128)S(1)}, u32[]{:S(2)}, u32[]{:S(2)}) %collective-permute-start.7) | collective-permute-done | bytes 4128 | tf_op jit(solution)/shard_map/ppermute | solution.py:759
  72.7 0.5 collective-permute-start.8
  73.2 4.0 %collective-permute-done.8 = f32[1,8,128]{2,1,0:T(8,128)S(1)} collective-permute-done((f32[1,8,128]{2,1,0:T(8,128)S(1)}, f32[1,8,128]{2,1,0:T(8,128)S(1)}, u32[]{:S(2)}, u32[]{:S(2)}) %collective-permute-start.8) | collective-permute-done | bytes 4128 | tf_op jit(solution)/shard_map/ppermute | solution.py:759
  77.2 7.4 %shard_map.192 = (bf16[4,8,128,128]{3,2,1,0:T(8,128)(2,1)}, bf16[4,10,128,128]{3,2,1,0:T(8,128)(2,1)}, f32[8,128]{1,0:T(8,128)S(1)}, f32[8,8,128]{2,1,0:T(8,128)}) custom-call(s32[1]{0:T(128)} %bitcast.refs_0_, bf16[4,8,128,128]{3,2,1,0:T(8,128)(2,1)} %get-tuple-element.76.refs_1_, bf16[4,8,128,128]{3,2,1,0:T(8,128)(2,1)} %get-tuple-element.64.refs_1_.refs_4_.refs_2_, ...), custom_call_target="tpu_custom_call" | custom-call | flops 1207959552 | bytes 7432200 | tf_op jit(solution)/shard_map/pallas_call | solution.py:728
  84.6 3.4 %all-to-all-start.2 = ((f32[8,8,128]{2,1,0:T(8,128)}), f32[8,8,128]{2,1,0:T(8,128)S(1)}, u32[]{:S(2)}, u32[]{:S(2)}) async-start(f32[8,8,128]{2,1,0:T(8,128)} %get-tuple-element.80), calls=%async_computation.2 | async-start | bytes 65536 | tf_op jit(solution)/shard_map/all_to_all | solution.py:776
  88.0 4.2 %shard_map.193.refs_11_ = bf16[1280,128]{1,0:T(8,128)(2,1)} custom-call(bf16[4,10,128,128]{3,2,1,0:T(8,128)(2,1)} %get-tuple-element.81.refs_0_, bf16[4,8,128,128]{3,2,1,0:T(8,128)(2,1)} %get-tuple-element.82.refs_1_, f32[128,128]{1,0:T(8,128)} %get-tuple-element.83.refs_2_), custom_call_target="tpu_custom_call" | custom-call | flops 1207959552 | bytes 4849664 | tf_op jit(solution)/shard_map/pallas_call | solution.py:728
  92.2 2.4 %all-to-all-done.2.refs_6_ = f32[8,8,128]{2,1,0:T(8,128)S(1)} async-done(((f32[8,8,128]{2,1,0:T(8,128)}), f32[8,8,128]{2,1,0:T(8,128)S(1)}, u32[]{:S(2)}, u32[]{:S(2)}) %all-to-all-start.2) | async-done | bytes 32800 | tf_op jit(solution)/shard_map/all_to_all | solution.py:776
  94.6 3.8 %shard_map.194 = (bf16[1024,128]{1,0:T(8,128)(2,1)S(1)}, bf16[1024,128]{1,0:T(8,128)(2,1)S(1)}) custom-call(bf16[4,8,2,128,128]{4,3,2,1,0:T(8,128)(2,1)} %bitcast.53, bf16[4,128,128]{2,1,0:T(8,128)(2,1)S(1)} %collective-permute-done.refs_1_, bf16[4,2,128,128]{3,2,1,0:T(8,128)(2,1)S(1)} %collective-permute-done.1.refs_0_.refs_2_, ...), custom_call_target="tpu_custom_call" | custom-call | flops 805306368 | bytes 10970120 | tf_op jit(solution)/shard_map/pallas_call | solution.py:728
  98.4 0.0 copy-start.8
  98.4 0.1 collective-permute-start.9
  98.5 1.5 %collective-permute-done.9 = bf16[1024,128]{1,0:T(8,128)(2,1)S(1)} collective-permute-done((bf16[1024,128]{1,0:T(8,128)(2,1)S(1)}, bf16[1024,128]{1,0:T(8,128)(2,1)S(1)}, u32[]{:S(2)}, u32[]{:S(2)}) %collective-permute-start.9) | collective-permute-done | bytes 262176 | tf_op jit(solution)/shard_map/ppermute | solution.py:785
  100.0 0.1 add_convert_fusion
  100.1 13.9 %all_to_all.25.in_ref = bf16[16,64,128]{2,1,0:T(8,128)(2,1)S(1)} all-to-all(bf16[16,64,128]{2,1,0:T(8,128)(2,1)S(1)} %bitcast.54), channel_id=1, replica_groups={{0,2,4,6,8,10,12,14,16,18,20,22,24,26,28,30},{1,3,5,7,9,11,13,15,17,19,..., dimensions={0} | all-to-all | bytes 524288 | tf_op jit(solution)/shard_map/all_to_all | solution.py:792
  114.0 0.8 shard_map.195
  114.7 3.5 %all-to-all-start.4 = ((bf16[16,64,128]{2,1,0:T(8,128)(2,1)}), bf16[16,64,128]{2,1,0:T(8,128)(2,1)S(1)}, u32[]{:S(2)}, u32[]{:S(2)}) async-start(bf16[16,64,128]{2,1,0:T(8,128)(2,1)} %shard_map.195), calls=%async_computation.4 | async-start | bytes 524288 | tf_op jit(solution)/shard_map/all_to_all | solution.py:792
  118.4 0.1 collective-permute-start.10
  118.4 1.9 %collective-permute-start.11 = (bf16[8,32,128]{2,1,0:T(8,128)(2,1)S(1)}, bf16[8,32,128]{2,1,0:T(8,128)(2,1)S(1)}, u32[]{:S(2)}, u32[]{:S(2)}) collective-permute-start(bf16[8,32,128]{2,1,0:T(8,128)(2,1)S(1)} %get-tuple-element.103), channel_id=1, source_target_pairs={{0,2},{1,3},{2,0},{3,1},{4,6},{5,7},{6,4},{7,5},{8,10},{9,11},{10,... | collective-permute-start | bytes 196616 | tf_op jit(solution)/shard_map/ppermute | solution.py:771
  120.4 1.4 %collective-permute-start.12 = (bf16[8,32,128]{2,1,0:T(8,128)(2,1)S(1)}, bf16[8,32,128]{2,1,0:T(8,128)(2,1)S(1)}, u32[]{:S(2)}, u32[]{:S(2)}) collective-permute-start(bf16[8,32,128]{2,1,0:T(8,128)(2,1)S(1)} %get-tuple-element.102), channel_id=1, source_target_pairs={{0,3},{1,0},{2,1},{3,2},{4,7},{5,4},{6,5},{7,6},{8,11},{9,8},{10,9... | collective-permute-start | bytes 196616 | tf_op jit(solution)/shard_map/ppermute | solution.py:771
  121.8 5.9 %all-to-all-done.4 = bf16[16,64,128]{2,1,0:T(8,128)(2,1)S(1)} async-done(((bf16[16,64,128]{2,1,0:T(8,128)(2,1)}), bf16[16,64,128]{2,1,0:T(8,128)(2,1)S(1)}, u32[]{:S(2)}, u32[]{:S(2)}) %all-to-all-start.4) | async-done | bytes 262176 | tf_op jit(solution)/shard_map/all_to_all | solution.py:792
  127.7 0.7 fusion.3
  128.4 0.8 collective-permute-done.13.other_ref
  129.2 1.0 shard_map.196
  (30 shorter events, 0.1 us)
Async XLA Ops:
  1.6 7.7 %collective-permute-start = (bf16[4,128,128]{2,1,0:T(8,128)(2,1)S(1)}, bf16[4,128,128]{2,1,0:T(8,128)(2,1)S(1)}, u32[]{:S(2)}, u32[]{:S(2)}) collective-permute-start(bf16[4,128,128]{2,1,0:T(8,128)(2,1)S(1)} %slice_bitcast_fusion.refs_2_), channel_id=1, source_target_pairs={{0,4},{4,8},{8,12},{12,16},{16,20},{20,24},{24,28},{1,5},{5,9},{9,... | collective-permute-start | bytes 393224 | tf_op jit(solution)/shard_map/ppermute | solution.py:742
  8.4 25.5 %copy-start.3 = (f32[128]{0:T(128)S(1)}, f32[128]{0:T(128)}, u32[]{:S(2)}) copy-start(f32[128]{0:T(128)} %param.17) | copy-start | bytes 1540
  8.4 25.5 %copy-start.7 = (f32[128]{0:T(128)S(1)}, f32[128]{0:T(128)}, u32[]{:S(2)}) copy-start(f32[128]{0:T(128)} %param.18) | copy-start | bytes 1540
  9.3 17.9 %collective-permute-start.1 = (bf16[4,2,128,128]{3,2,1,0:T(8,128)(2,1)S(1)}, bf16[4,2,128,128]{3,2,1,0:T(8,128)(2,1)S(1)}, u32[]{:S(2)}, u32[]{:S(2)}) collective-permute-start(bf16[4,2,128,128]{3,2,1,0:T(8,128)(2,1)S(1)} %get-tuple-element.56), channel_id=1, source_target_pairs={{0,4},{4,8},{8,12},{12,16},{16,20},{20,24},{24,28},{1,5},{5,9},{9,... | collective-permute-start | bytes 786440 | tf_op jit(solution)/shard_map/ppermute | solution.py:742
  13.6 13.6 %collective-permute-start.2 = (bf16[4,2,128,128]{3,2,1,0:T(8,128)(2,1)S(1)}, bf16[4,2,128,128]{3,2,1,0:T(8,128)(2,1)S(1)}, u32[]{:S(2)}, u32[]{:S(2)}) collective-permute-start(bf16[4,2,128,128]{3,2,1,0:T(8,128)(2,1)S(1)} %get-tuple-element.57), channel_id=1, source_target_pairs={{4,0},{8,4},{12,8},{16,12},{20,16},{24,20},{28,24},{5,1},{9,5},{13... | collective-permute-start | bytes 786440 | tf_op jit(solution)/shard_map/ppermute | solution.py:742
  19.4 14.5 %all-to-all-start = ((f32[8,8,128]{2,1,0:T(8,128)}), f32[8,8,128]{2,1,0:T(8,128)S(1)}, u32[]{:S(2)}, u32[]{:S(2)}) async-start(f32[8,8,128]{2,1,0:T(8,128)} %get-tuple-element.58), calls=%async_computation | async-start | bytes 65536 | tf_op jit(solution)/shard_map/all_to_all | solution.py:776
  29.3 13.9 %collective-permute-start.3 = (bf16[384,128]{1,0:T(8,128)(2,1)S(1)}, bf16[384,128]{1,0:T(8,128)(2,1)S(1)}, u32[]{:S(2)}, u32[]{:S(2)}) collective-permute-start(bf16[384,128]{1,0:T(8,128)(2,1)S(1)} %fusion.4), channel_id=1, source_target_pairs={{1,0},{2,1},{3,2},{0,3},{5,4},{6,5},{7,6},{4,7},{9,8},{10,9},{11,1... | collective-permute-start | bytes 294920 | tf_op jit(solution)/shard_map/ppermute | solution.py:750
  29.3 13.8 %collective-permute-start.4 = (bf16[384,128]{1,0:T(8,128)(2,1)S(1)}, bf16[384,128]{1,0:T(8,128)(2,1)S(1)}, u32[]{:S(2)}, u32[]{:S(2)}) collective-permute-start(bf16[384,128]{1,0:T(8,128)(2,1)S(1)} %fusion.4), channel_id=1, source_target_pairs={{2,0},{3,1},{0,2},{1,3},{6,4},{7,5},{4,6},{5,7},{10,8},{11,9},{8,1... | collective-permute-start | bytes 294920 | tf_op jit(solution)/shard_map/ppermute | solution.py:750
  30.9 12.3 %collective-permute-start.5 = (bf16[384,128]{1,0:T(8,128)(2,1)S(1)}, bf16[384,128]{1,0:T(8,128)(2,1)S(1)}, u32[]{:S(2)}, u32[]{:S(2)}) collective-permute-start(bf16[384,128]{1,0:T(8,128)(2,1)S(1)} %fusion.4), channel_id=1, source_target_pairs={{3,0},{0,1},{1,2},{2,3},{7,4},{4,5},{5,6},{6,7},{11,8},{8,9},{9,10... | collective-permute-start | bytes 294920 | tf_op jit(solution)/shard_map/ppermute | solution.py:750
  33.9 15.9 %copy-start.1 = (f32[128]{0:T(128)S(1)}, f32[128]{0:T(128)}, u32[]{:S(2)}) copy-start(f32[128]{0:T(128)} %param.20) | copy-start | bytes 1540
  33.9 15.9 %copy-start.2 = (f32[128]{0:T(128)S(1)}, f32[128]{0:T(128)}, u32[]{:S(2)}) copy-start(f32[128]{0:T(128)} %param.21) | copy-start | bytes 1540
  33.9 15.9 %copy-start.4 = (bf16[128,64]{0,1:T(8,128)(2,1)S(1)}, bf16[128,64]{0,1:T(8,128)(2,1)}, u32[]{:S(2)}) copy-start(bf16[128,64]{0,1:T(8,128)(2,1)} %param.22) | copy-start | bytes 49156
  33.9 15.9 %copy-start.5 = (f32[16,4]{0,1:T(4,128)S(1)}, f32[16,4]{0,1:T(4,128)}, u32[]{:S(2)}) copy-start(f32[16,4]{0,1:T(4,128)} %param.23) | copy-start | bytes 772
  33.9 15.9 %copy-start.6 = (s32[16]{0:T(128)S(1)}, s32[16]{0:T(128)}, u32[]{:S(2)}) copy-start(s32[16]{0:T(128)} %refs_0_.1) | copy-start | bytes 196
  39.6 21.6 %copy-start = (bf16[4,8,128,128]{3,2,1,0:T(8,128)(2,1)S(1)}, bf16[4,8,128,128]{3,2,1,0:T(8,128)(2,1)}, u32[]{:S(2)}) copy-start(bf16[4,8,128,128]{3,2,1,0:T(8,128)(2,1)} %get-tuple-element.64.refs_1_.refs_4_.refs_2_) | copy-start | bytes 3145732
  39.7 10.1 %all-to-all-start.1 = ((f32[8,8,128]{2,1,0:T(8,128)}), f32[8,8,128]{2,1,0:T(8,128)S(1)}, u32[]{:S(2)}, u32[]{:S(2)}) async-start(f32[8,8,128]{2,1,0:T(8,128)} %get-tuple-element.65), calls=%async_computation.1 | async-start | bytes 65536 | tf_op jit(solution)/shard_map/all_to_all | solution.py:776
  65.4 3.7 %collective-permute-start.6 = (f32[1,8,128]{2,1,0:T(8,128)S(1)}, f32[1,8,128]{2,1,0:T(8,128)S(1)}, u32[]{:S(2)}, u32[]{:S(2)}) collective-permute-start(f32[1,8,128]{2,1,0:T(8,128)S(1)} %get-tuple-element.77), channel_id=1, source_target_pairs={{0,4},{4,0},{8,12},{12,8},{16,20},{20,16},{24,28},{28,24},{1,5},{5... | collective-permute-start | bytes 12296 | tf_op jit(solution)/shard_map/ppermute | solution.py:759
  69.1 3.6 %collective-permute-start.7 = (f32[1,8,128]{2,1,0:T(8,128)S(1)}, f32[1,8,128]{2,1,0:T(8,128)S(1)}, u32[]{:S(2)}, u32[]{:S(2)}) collective-permute-start(f32[1,8,128]{2,1,0:T(8,128)S(1)} %add.61), channel_id=1, source_target_pairs={{0,8},{4,12},{8,0},{12,4},{16,24},{20,28},{24,16},{28,20},{1,9},{5... | collective-permute-start | bytes 12296 | tf_op jit(solution)/shard_map/ppermute | solution.py:759
  72.7 4.5 %collective-permute-start.8 = (f32[1,8,128]{2,1,0:T(8,128)S(1)}, f32[1,8,128]{2,1,0:T(8,128)S(1)}, u32[]{:S(2)}, u32[]{:S(2)}) collective-permute-start(f32[1,8,128]{2,1,0:T(8,128)S(1)} %add.62), channel_id=1, source_target_pairs={{0,16},{4,20},{8,24},{12,28},{16,0},{20,4},{24,8},{28,12},{1,17},{... | collective-permute-start | bytes 12296 | tf_op jit(solution)/shard_map/ppermute | solution.py:759
  84.6 10.0 %all-to-all-start.2 = ((f32[8,8,128]{2,1,0:T(8,128)}), f32[8,8,128]{2,1,0:T(8,128)S(1)}, u32[]{:S(2)}, u32[]{:S(2)}) async-start(f32[8,8,128]{2,1,0:T(8,128)} %get-tuple-element.80), calls=%async_computation.2 | async-start | bytes 65536 | tf_op jit(solution)/shard_map/all_to_all | solution.py:776
  98.4 19.9 %copy-start.8 = (bf16[4,8,32,128]{3,2,1,0:T(8,128)(2,1)S(1)}, bf16[4,8,32,128]{3,2,1,0:T(8,128)(2,1)}, u32[]{:S(2)}) copy-start(bf16[4,8,32,128]{3,2,1,0:T(8,128)(2,1)} %get-tuple-element.90) | copy-start | bytes 786436
  98.4 1.6 %collective-permute-start.9 = (bf16[1024,128]{1,0:T(8,128)(2,1)S(1)}, bf16[1024,128]{1,0:T(8,128)(2,1)S(1)}, u32[]{:S(2)}, u32[]{:S(2)}) collective-permute-start(bf16[1024,128]{1,0:T(8,128)(2,1)S(1)} %get-tuple-element.89), channel_id=1, source_target_pairs={{0,1},{1,0},{2,3},{3,2},{4,5},{5,4},{6,7},{7,6},{8,9},{9,8},{10,11... | collective-permute-start | bytes 786440 | tf_op jit(solution)/shard_map/ppermute | solution.py:785
  114.7 13.0 %all-to-all-start.4 = ((bf16[16,64,128]{2,1,0:T(8,128)(2,1)}), bf16[16,64,128]{2,1,0:T(8,128)(2,1)S(1)}, u32[]{:S(2)}, u32[]{:S(2)}) async-start(bf16[16,64,128]{2,1,0:T(8,128)(2,1)} %shard_map.195), calls=%async_computation.4 | async-start | bytes 524288 | tf_op jit(solution)/shard_map/all_to_all | solution.py:792
  118.4 9.3 %collective-permute-start.10 = (bf16[8,32,128]{2,1,0:T(8,128)(2,1)S(1)}, bf16[8,32,128]{2,1,0:T(8,128)(2,1)S(1)}, u32[]{:S(2)}, u32[]{:S(2)}) collective-permute-start(bf16[8,32,128]{2,1,0:T(8,128)(2,1)S(1)} %get-tuple-element.101), channel_id=1, source_target_pairs={{0,1},{1,2},{2,3},{3,0},{4,5},{5,6},{6,7},{7,4},{8,9},{9,10},{10,1... | collective-permute-start | bytes 196616 | tf_op jit(solution)/shard_map/ppermute | solution.py:771
  118.4 9.3 %collective-permute-start.11 = (bf16[8,32,128]{2,1,0:T(8,128)(2,1)S(1)}, bf16[8,32,128]{2,1,0:T(8,128)(2,1)S(1)}, u32[]{:S(2)}, u32[]{:S(2)}) collective-permute-start(bf16[8,32,128]{2,1,0:T(8,128)(2,1)S(1)} %get-tuple-element.103), channel_id=1, source_target_pairs={{0,2},{1,3},{2,0},{3,1},{4,6},{5,7},{6,4},{7,5},{8,10},{9,11},{10,... | collective-permute-start | bytes 196616 | tf_op jit(solution)/shard_map/ppermute | solution.py:771
  120.4 7.4 %collective-permute-start.12 = (bf16[8,32,128]{2,1,0:T(8,128)(2,1)S(1)}, bf16[8,32,128]{2,1,0:T(8,128)(2,1)S(1)}, u32[]{:S(2)}, u32[]{:S(2)}) collective-permute-start(bf16[8,32,128]{2,1,0:T(8,128)(2,1)S(1)} %get-tuple-element.102), channel_id=1, source_target_pairs={{0,3},{1,0},{2,1},{3,2},{4,7},{5,4},{6,5},{7,6},{8,11},{9,8},{10,9... | collective-permute-start | bytes 196616 | tf_op jit(solution)/shard_map/ppermute | solution.py:771
  127.7 1.5 %collective-permute-start.13 = (bf16[1024,128]{1,0:T(8,128)(2,1)S(1)}, bf16[1024,128]{1,0:T(8,128)(2,1)S(1)}, u32[]{:S(2)}, u32[]{:S(2)}) collective-permute-start(bf16[1024,128]{1,0:T(8,128)(2,1)S(1)} %bitcast.39), channel_id=1, source_target_pairs={{0,1},{1,0},{2,3},{3,2},{4,5},{5,4},{6,7},{7,6},{8,9},{9,8},{10,11... | collective-permute-start | bytes 786440 | tf_op jit(solution)/shard_map/ppermute | solution.py:785

commit v7 on v6

--- a/solution.py
+++ b/solution.py
@@ -120,10 +120,37 @@
     store_sums(sums_ref, date, dates, column_sum(values), column_sum(values * values))
 
 
+def sort_halos(place_ref, inner_ref, outer_ref, high_ref, below_ref):
+    odd = place_ref[0] % 2 == 1
+
+    @pl.when(odd)
+    def _():
+        high_ref[...] = inner_ref[...]
+        below_ref[...] = outer_ref[...]
+
+    @pl.when(jnp.logical_not(odd))
+    def _():
+        high_ref[...] = outer_ref[...]
+        below_ref[...] = inner_ref[...]
+
+
 def edge_kernel(
-    step, steps, high_ref, above_ref, last_ref, below_ref, weight_ref, up_ref, down_ref, table
+    step,
+    steps,
+    place_ref,
+    inner_ref,
+    outer_ref,
+    above_ref,
+    last_ref,
+    weight_ref,
+    up_ref,
+    down_ref,
+    table,
+    high_ref,
+    below_ref,
 ):
     dates = above_ref.shape[0]
+    sort_halos(place_ref, inner_ref, outer_ref, high_ref, below_ref)
     down_table(weight_ref, table)
     taps = [
         jnp.concatenate([high_ref[:, 0], last_ref[...]], axis=0),
@@ -226,7 +253,9 @@
 
 
 def source_of(turn_ref, device, devices):
-    return (device + devices - turn_ref[0]) % devices
+    half = devices // 2
+    core = (device + turn_ref[0]) % 2
+    return core * half + (device // 2 + half - turn_ref[0] // 2) % half
 
 
 def upstream_rows(grad_ref, turn_ref, rows, cols):
@@ -257,6 +286,7 @@
     attn_ref,
     norm_ref,
     packed_ref,
+    own_ref,
     wide_ref,
     vector_ref,
     total,
@@ -315,14 +345,18 @@
             dense = jnp.zeros((cols, width), F32)
             for row in range(rows):
                 dense = dense + jnp.where(place == row, source[row], 0.0)
-            for copy in range(packed_ref.shape[0]):
-                packed_ref[copy, index] = dense
+            if index == 0:
+                packed_ref[0, 0] = dense.astype(BF16)
+                own_ref[...] = dense
+            else:
+                packed_ref[0, 1], packed_ref[0, 2] = split(dense)
 
 
 def attend_kernel(
     date,
     dates,
     packed_ref,
+    own_ref,
     feat_ref,
     exp_ref,
     attn_ref,
@@ -348,9 +382,13 @@
     rows, cols, width = block_ref.shape[1:]
 
     if date == 0:
-        denominator = jnp.sum(packed_ref[:, 0], axis=0)
-        reciprocal = 1.0 / denominator
-        mean = jnp.sum(packed_ref[:, 0] * reciprocal * packed_ref[:, 1], axis=0)
+        totals = packed_ref[:, 0].astype(F32)
+        reciprocal = 1.0 / jnp.sum(totals, axis=0)
+        means = packed_ref[:, 1].astype(F32) + packed_ref[:, 2].astype(F32)
+        mean = jnp.sum(totals * reciprocal * means, axis=0)
+        own = own_ref[...]
+        sent = own.astype(BF16).astype(F32)
+        reciprocal = reciprocal * jnp.where(own > 0.0, sent / own, 0.0)
         place = lax.broadcasted_iota(jnp.int32, (cols, width), 1) % rows
         for values, target in ((reciprocal, inverse), (mean, average)):
             parts = jnp.concatenate(split(values), axis=-1)
@@ -531,8 +569,9 @@
     dates,
     img_ref,
     above_ref,
-    high_ref,
-    below_ref,
+    inner_ref,
+    outer_ref,
+    place_ref,
     conv_ref,
     grad_ref,
     tails_ref,
@@ -547,6 +586,8 @@
     factors,
     total,
     out_ref,
+    high_ref,
+    below_ref,
     *,
     norm_count,
 ):
@@ -554,6 +595,7 @@
     half = width // 2
 
     if date == 0:
+        sort_halos(place_ref, inner_ref, outer_ref, high_ref, below_ref)
         tails = group_sum(jnp.sum(tails_ref[...], axis=0)) / norm_count
         mean, inverse = norm_ref[:dates], norm_ref[dates:]
         slope = -inverse * inverse * tails[dates:]
@@ -575,9 +617,9 @@
     even, odd = img_ref[0, :, 0], img_ref[0, :, 1]
     above = above_ref[0][None]
     taps = [
-        jnp.concatenate([high_ref[0, :1], above, odd], axis=0),
-        jnp.concatenate([high_ref[0, 1:], even, below_ref[0, :1]], axis=0),
-        jnp.concatenate([above, odd, below_ref[0, 1:]], axis=0),
+        jnp.concatenate([high_ref[date, :1], above, odd], axis=0),
+        jnp.concatenate([high_ref[date, 1:], even, below_ref[date, :1]], axis=0),
+        jnp.concatenate([above, odd, below_ref[date, 1:]], axis=0),
     ]
     taps = jnp.concatenate(taps, axis=-1).reshape(reach * cols, 3 * width)
     total[...] += product(taps, grads, 0, 0)
@@ -688,41 +730,52 @@
             out_shape.append(jax.ShapeDtypeStruct(shape, dtype))
             out_specs.append(in_vmem)
     copies = len(loads) + len(stores)
+    kinds = [kind for kind, _ in inputs] + [kind for kind, _, _ in outputs]
 
     def body(*refs):
-        views, rest = list(refs[: len(inputs)]), refs[len(inputs) :]
-        results, rest = list(rest[: len(outputs)]), rest[len(outputs) :]
-        buffer_refs, rest = rest[:copies], rest[copies:]
-        started = []
+        views, rest = list(refs[: len(kinds)]), refs[len(kinds) :]
+        buffer_refs, ready, rest = rest[:copies], rest[copies], rest[copies + 1 :]
+
+        def copies_of(place, index, inward):
+            outside, inside = views[place], buffer_refs[index]
+            made = []
+            for date in range(dates if "date" in kinds[place] else 1):
+                here = pl.ds(date, 1) if "date" in kinds[place] else slice(None)
+                pair = (outside.at[here], inside.at[here])
+                source, target = pair if inward else pair[::-1]
+                made.append(pltpu.make_async_copy(source, target, ready.at[index, date]))
+            return made
+
+        incoming = [copies_of(place, index, True) for index, place in enumerate(loads)]
+        outgoing = [
+            copies_of(len(inputs) + place, len(loads) + index, False)
+            for index, place in enumerate(stores)
+        ]
+        for date in range(dates):
+            for moves in incoming:
+                if date < len(moves):
+                    moves[date].start()
         for index, place in enumerate(loads):
-            started.append(
-                pltpu.make_async_copy(views[place], buffer_refs[index], rest[0].at[index])
-            )
-            started[-1].start()
             views[place] = buffer_refs[index]
-        sent = []
         for index, place in enumerate(stores):
-            buffer = buffer_refs[len(loads) + index]
-            sent.append(
-                pltpu.make_async_copy(buffer, results[place], rest[0].at[len(loads) + index])
-            )
-            results[place] = buffer
-        for copy in started:
-            copy.wait()
+            views[len(inputs) + place] = buffer_refs[len(loads) + index]
         for date in range(dates):
-            ins = [
+            for moves in incoming:
+                if date < len(moves):
+                    moves[date].wait()
+            here = [
                 view.at[pl.ds(date, 1)] if "date" in kind else view
-                for view, (kind, _) in zip(views, inputs)
+                for view, kind in zip(views, kinds)
             ]
-            outs = [
-                result.at[pl.ds(date, 1)] if "date" in kind else result
-                for result, (kind, _, _) in zip(results, outputs)
-            ]
-            kernel(date, dates, *ins, *outs, *rest[1:])
-        for copy in sent:
-            copy.start()
-        for copy in sent:
-            copy.wait()
+            kernel(date, dates, *here, *rest)
+            for moves in outgoing:
+                if len(moves) == dates:
+                    moves[date].start()
+                elif date == dates - 1:
+                    moves[0].start()
+        for moves in outgoing:
+            for move in moves:
+                move.wait()
 
     moved = sum(array.size * array.dtype.itemsize for _, array in inputs)
     return pl.pallas_call(
@@ -730,7 +783,7 @@
         in_specs=in_specs,
         out_specs=out_specs,
         out_shape=out_shape,
-        scratch_shapes=buffers + [pltpu.SemaphoreType.DMA((max(copies, 1),))] + scratch,
+        scratch_shapes=buffers + [pltpu.SemaphoreType.DMA((max(copies, 1), dates))] + scratch,
         compiler_params=pltpu.CompilerParams(vmem_limit_bytes=40 * MIB),
         cost_estimate=pl.CostEstimate(flops=flops, bytes_accessed=2 * moved, transcendentals=0),
     )(*arrays)
@@ -745,20 +798,10 @@
 def turned(array):
     devices = lax.axis_size("dates")
     pieces = [array]
-    for step in range(1, devices):
+    for step in range(2, devices, 2):
         pairs = [((i + step) % devices, i) for i in range(devices)]
         pieces.append(lax.ppermute(array, "dates", pairs))
-    return jnp.stack(pieces)
-
-
-def row_totals(sums):
-    devices = lax.axis_size("rows")
-    step = 1
-    while step < devices:
-        pairs = [(i, i ^ step) for i in range(devices)]
-        sums = sums + lax.ppermute(sums, "rows", pairs)
-        step *= 2
-    return sums
+    return jnp.stack(pieces + [other_core(piece) for piece in pieces])
 
 
 def sum_of_parts(parts):
@@ -851,10 +894,14 @@
     valid_rows = valid.astype(BF16).reshape(valid.shape[0] * rows, -1)
     valid_rows = jnp.pad(valid_rows, ((0, 0), (0, width - valid_rows.shape[1])))
     packed = jnp.concatenate([out_grad.reshape(grad_rows, width), valid_rows])
-    high, below, above, packed = lax.optimization_barrier(
-        (images[:, -3:-1], images[:, :2], above, packed)
-    )
-    high, below = shifted(high, 1), shifted(below, -1)
+    row_place = lax.axis_index("rows")
+    odd = row_place % 2 == 1
+    inner = jnp.where(odd, images[:, :2], images[:, -3:-1])
+    outer = jnp.where(odd, images[:, -3:-1], images[:, :2])
+    inner, outer, above, packed = lax.optimization_barrier((inner, outer, above, packed))
+    inner = lax.ppermute(inner, "rows", [(i, i ^ 1) for i in range(row_devs)])
+    pairs = [(i, i + 1) for i in range(1, row_devs - 1, 2)]
+    outer = lax.ppermute(outer, "rows", pairs + [(j, i) for i, j in pairs])
     paired = images.reshape(dates, rows, 2, cols, pair_width)
     conv_out, sums = call(
         down_kernel,
@@ -865,13 +912,25 @@
         6 * flops,
     )
     stats = exchange(sums, "rows")
-    high, below, last, _ = lax.optimization_barrier((high, below, last, sums))
+    inner, outer, last, _ = lax.optimization_barrier((inner, outer, last, sums))
+    place = row_place.reshape(1)
     halo_up, halo_down = call(
         edge_kernel,
         1,
-        [("all", high), ("all", above), ("all", last), ("all", below), ("all far", conv_weight)],
-        [("all far", edge_rows, BF16)] * 2,
-        [pltpu.VMEM((3 * pair_width, 2 * width), BF16)],
+        [
+            ("scalar", place),
+            ("all", inner),
+            ("all", outer),
+            ("all", above),
+            ("all", last),
+            ("all", conv_weight),
+        ],
+        [("all", edge_rows, BF16)] * 2,
+        [
+            pltpu.VMEM((3 * pair_width, 2 * width), BF16),
+            pltpu.VMEM(inner.shape, BF16),
+            pltpu.VMEM(inner.shape, BF16),
+        ],
         6 * flops // rows,
     )
     packed, _ = lax.optimization_barrier((packed, halo_up))
@@ -879,16 +938,14 @@
     clear = lax.dynamic_slice_in_dim(sources, grad_rows + date_start * rows, dates * rows, 1)
     clear = clear.astype(F32)
     turn = lax.axis_index("dates").reshape(1)
-    place = lax.axis_index("rows").reshape(1)
-
     block_out, hidden, first_norm, sums = call(
         functools.partial(block_kernel, norm_count=norm_count, row_devs=row_devs),
         dates,
         [
             ("scalar", place),
             ("date far", conv_out),
-            ("date far", halo_up),
-            ("date far", halo_down),
+            ("date", halo_up),
+            ("date", halo_down),
             ("all", stats),
             ("all", first_gain),
             ("all", first_shift),
@@ -904,7 +961,7 @@
         9 * flops,
     )
     stats = exchange(sums, "rows")
-    features, exponent, attn, norm, packed, key_wide, query_wide = call(
+    features, exponent, attn, norm, packed, own_total, key_wide, query_wide = call(
         functools.partial(score_kernel, norm_count=norm_count, grad_scale=grad_scale),
         dates,
         [
@@ -924,7 +981,8 @@
             ("date", frame, F32),
             ("date", frame, F32),
             ("all", (2 * dates, width), F32),
-            ("all", (1, 2, cols, width), F32),
+            ("all", (1, 3, cols, width), BF16),
+            ("all", (cols, width), F32),
             ("all", (width, width), BF16),
             ("all", (8, width), F32),
         ],
@@ -942,6 +1000,7 @@
         dates,
         [
             ("all", packed),
+            ("all", own_total),
             ("date", features),
             ("date", exponent),
             ("date", attn),
@@ -959,12 +1018,12 @@
             ("all far", (date_devs, rows, cols // date_devs, width), BF16),
             ("all far", (width, width), F32),
             ("all", (8, width), F32),
-            ("all", (1, 2 * dates, width), F32),
+            ("all", (row_devs, 2 * dates, width), F32),
         ],
         [pltpu.VMEM(frame[1:], F32)] * 3,
         5 * flops,
     )
-    tails = row_totals(sums)
+    tails = exchange(sums, "rows")
     pre_grad, linear_grad, first_vectors, sums = call(
         functools.partial(hidden_kernel, norm_count=norm_count, row_devs=row_devs),
         dates,
@@ -976,8 +1035,8 @@
             ("all", norm),
             ("all far", block_weight),
             ("date far", conv_out),
-            ("date far", halo_up),
-            ("date far", halo_down),
+            ("date", halo_up),
+            ("date", halo_down),
             ("all", first_norm),
             ("all", first_gain),
             ("all", first_shift),
@@ -1013,8 +1072,9 @@
         [
             ("date far", paired),
             ("date", above),
-            ("date", high),
-            ("date", below),
+            ("all", inner),
+            ("all", outer),
+            ("scalar", place),
             ("date far", conv_out),
             ("date far", linear_grad),
             ("all", tails),
@@ -1030,6 +1090,8 @@
             pltpu.VMEM((2 * dates, width), F32),
             pltpu.VMEM((3 * pair_width, 2 * width), F32),
             pltpu.VMEM((2 * half_rows, width), BF16),
+            pltpu.VMEM(inner.shape, BF16),
+            pltpu.VMEM(inner.shape, BF16),
         ],
         6 * flops,
     )

time: 131 us -> 131 us (level)
  blocking collectives: 21.2 us -> 29.1 us
  starting transfers between devices: 35.3 us -> 30.5 us
  waiting for transfers between devices: 30.4 us -> 27.9 us
    all_to_all x0 -> x1, blocking collectives: none -> 9.06 us  [exchange(): return lax.all_to_all(pieces, axes, split_axis=0, concat_axis=0, tiled=True)]
    ppermute x3 -> x2, waiting for transfers between devices: 10.3 us -> 4.26 us  [the longest x1 4.26 us: local(): inner = lax.ppermute(inner, 'rows', [(i, i ^ 1) for i in range(row_devs)])]
    ppermute x3 -> x1, starting transfers between devices: 10.5 us -> 4.88 us  [shifted(): return lax.ppermute(array, 'rows', pairs)]
    all_to_all x3, waiting for transfers between devices: 11.8 us -> 15.3 us  [exchange(): return lax.all_to_all(pieces, axes, split_axis=0, concat_axis=0, tiled=True)]
    ppermute x3 -> x2, starting transfers between devices: 1.45 us -> 2.99 us  [the longest x1 2.33 us: local(): inner = lax.ppermute(inner, 'rows', [(i, i ^ 1) for i in range(row_devs)])]
  transfers between devices with their start and end apart: 18 -> 15, of which waited for: 9 -> 7; matrix products, arithmetic and copies ran while one was open for 3% -> 3% of each run, Pallas kernels for 13% -> 12%
where the time goes in v7:
time: 131 us; the launch traced here: 130 us
  Pallas kernels  36.9 us (28%)
  starting transfers between devices  30.5 us (23%)
  blocking collectives  29.1 us (22%)
  waiting for transfers between devices  27.9 us (21%)
  other arithmetic  3.65 us (3%)
    pallas_call x8, Pallas kernels, call(): pl.pallas_call(body, in_specs=in_specs, out_specs=out_specs, out_shape=ou...  35.1 us
    all_to_all x3, waiting for transfers between devices, exchange(): return lax.all_to_all(pieces, axes, split_axis=0, concat_axis=0, tiled=True)  15.3 us
    all_to_all x1, blocking collectives, exchange_cores(): lax.all_to_all(pieces, axes, split_axis=0, concat_axis=0, axis_index_grou...  13.7 us
    all_to_all x3, starting transfers between devices, exchange(): return lax.all_to_all(pieces, axes, split_axis=0, concat_axis=0, tiled=True)  13.6 us
    all_to_all x1, blocking collectives, exchange(): return lax.all_to_all(pieces, axes, split_axis=0, concat_axis=0, tiled=True)  9.06 us
    all_gather x1, blocking collectives, gather(): return lax.all_gather(array, axis, axis=0, tiled=True)  6.33 us
    all_to_all x1, waiting for transfers between devices, exchange_cores(): lax.all_to_all(pieces, axes, split_axis=0, concat_axis=0, axis_index_grou...  5.95 us
    ppermute x1, starting transfers between devices, shifted(): return lax.ppermute(array, 'rows', pairs)  4.88 us
  transfers between devices with their start and end apart: 15, of which 7 were waited for; matrix products, arithmetic and copies ran while one was open for 3% of the time, Pallas kernels for 12%

profile of v7, /device:TPU:0, one launch (start us, length us, event | category | flops | bytes accessed | tf_op | source)
XLA Modules:
  0.0 130.1 jit_solution(12678171673610714003)
XLA Ops:
  0.6 0.9 slice_bitcast_fusion.refs_4_
  1.6 4.9 %collective-permute-start = (bf16[4,128,128]{2,1,0:T(8,128)(2,1)S(1)}, bf16[4,128,128]{2,1,0:T(8,128)(2,1)S(1)}, u32[]{:S(2)}, u32[]{:S(2)}) collective-permute-start(bf16[4,128,128]{2,1,0:T(8,128)(2,1)S(1)} %slice_bitcast_fusion.refs_4_), channel_id=1, source_target_pairs={{0,4},{4,8},{8,12},{12,16},{16,20},{20,24},{24,28},{1,5},{5,9},{9,... | collective-permute-start | bytes 393224 | tf_op jit(solution)/shard_map/ppermute | solution.py:795
  6.5 0.0 copy-start.1
  6.5 1.1 broadcast_select_fusion
  7.6 0.8 convert_bitcast_fusion
  8.4 0.9 fusion.4
  9.3 0.0 collective-permute-done.refs_1_.refs_3_
  9.3 2.3 %collective-permute-start.1 = (bf16[4,2,128,128]{3,2,1,0:T(8,128)(2,1)S(1)}, bf16[4,2,128,128]{3,2,1,0:T(8,128)(2,1)S(1)}, u32[]{:S(2)}, u32[]{:S(2)}) collective-permute-start(bf16[4,2,128,128]{3,2,1,0:T(8,128)(2,1)S(1)} %get-tuple-element.57), channel_id=1, source_target_pairs={{0,4},{4,0},{8,12},{12,8},{16,20},{20,16},{24,28},{28,24},{1,5},{5... | collective-permute-start | bytes 786440 | tf_op jit(solution)/shard_map/ppermute | solution.py:902
  11.7 0.7 collective-permute-start.2
  12.3 5.4 %shard_map.187 = (bf16[4,8,128,128]{3,2,1,0:T(8,128)(2,1)}, f32[8,8,128]{2,1,0:T(8,128)}) custom-call(bf16[4,8,2,128,128]{4,3,2,1,0:T(8,128)(2,1)} %bitcast.52, bf16[4,128,128]{2,1,0:T(8,128)(2,1)S(1)} %collective-permute-done.refs_1_.refs_3_, bf16[3,3,64,128]{3,2,1,0:T(8,128)(2,1)} %refs_5_.2), custom_call_target="tpu_custom_call" | custom-call | flops 805306368 | bytes 4751360 | tf_op jit(solution)/shard_map/pallas_call | solution.py:781
  17.7 4.3 %collective-permute-done.1.refs_1_.refs_2_ = bf16[4,2,128,128]{3,2,1,0:T(8,128)(2,1)S(1)} collective-permute-done((bf16[4,2,128,128]{3,2,1,0:T(8,128)(2,1)S(1)}, bf16[4,2,128,128]{3,2,1,0:T(8,128)(2,1)S(1)}, u32[]{:S(2)}, u32[]{:S(2)}) %collective-permute-start.1) | collective-permute-done | bytes 262176 | tf_op jit(solution)/shard_map/ppermute | solution.py:902
  22.0 0.5 shard_map.188
  22.5 1.6 %collective-permute-start.3 = (bf16[384,128]{1,0:T(8,128)(2,1)S(1)}, bf16[384,128]{1,0:T(8,128)(2,1)S(1)}, u32[]{:S(2)}, u32[]{:S(2)}) collective-permute-start(bf16[384,128]{1,0:T(8,128)(2,1)S(1)} %fusion.4), channel_id=1, source_target_pairs={{2,0},{3,1},{0,2},{1,3},{6,4},{7,5},{4,6},{5,7},{10,8},{11,9},{8,1... | collective-permute-start | bytes 294920 | tf_op jit(solution)/shard_map/ppermute | solution.py:803
  24.0 6.7 %all-to-all-start = ((f32[8,8,128]{2,1,0:T(8,128)}), f32[8,8,128]{2,1,0:T(8,128)S(1)}, u32[]{:S(2)}, u32[]{:S(2)}) async-start(f32[8,8,128]{2,1,0:T(8,128)} %get-tuple-element.59), calls=%async_computation | async-start | bytes 65536 | tf_op jit(solution)/shard_map/all_to_all | solution.py:819
  30.8 0.0 collective-permute-start.4
  30.8 0.5 collective-permute-start.5
  31.3 6.2 %all-to-all-done.refs_4_ = f32[8,8,128]{2,1,0:T(8,128)S(1)} async-done(((f32[8,8,128]{2,1,0:T(8,128)}), f32[8,8,128]{2,1,0:T(8,128)S(1)}, u32[]{:S(2)}, u32[]{:S(2)}) %all-to-all-start) | async-done | bytes 32800 | tf_op jit(solution)/shard_map/all_to_all | solution.py:819
  37.5 0.0 copy-start.5
  37.5 0.0 copy-start.6
  37.5 0.0 copy-start.7
  37.5 5.8 %shard_map.189 = (bf16[4,8,128,128]{3,2,1,0:T(8,128)(2,1)}, bf16[4,10,128,128]{3,2,1,0:T(8,128)(2,1)}, f32[8,128]{1,0:T(8,128)S(1)}, f32[8,8,128]{2,1,0:T(8,128)}) custom-call(s32[1]{0:T(128)} %bitcast.refs_0_.refs_4_, bf16[4,8,128,128]{3,2,1,0:T(8,128)(2,1)} %get-tuple-element.56.refs_1_.refs_6_.refs_5_, ...), custom_call_target="tpu_custom_call" | custom-call | flops 1207959552 | bytes 3278856 | tf_op jit(solution)/shard_map/pallas_call | solution.py:781
  43.4 3.5 %all-to-all-start.1 = ((f32[8,8,128]{2,1,0:T(8,128)}), f32[8,8,128]{2,1,0:T(8,128)S(1)}, u32[]{:S(2)}, u32[]{:S(2)}) async-start(f32[8,8,128]{2,1,0:T(8,128)} %get-tuple-element.66), calls=%async_computation.1 | async-start | bytes 65536 | tf_op jit(solution)/shard_map/all_to_all | solution.py:819
  46.9 0.0 collective-permute-done.5
  46.9 0.1 pad_maximum_fusion.refs_5_.refs_10_
  47.0 6.5 %all-to-all-done.1.refs_2_ = f32[8,8,128]{2,1,0:T(8,128)S(1)} async-done(((f32[8,8,128]{2,1,0:T(8,128)}), f32[8,8,128]{2,1,0:T(8,128)S(1)}, u32[]{:S(2)}, u32[]{:S(2)}) %all-to-all-start.1) | async-done | bytes 32800 | tf_op jit(solution)/shard_map/all_to_all | solution.py:819
  53.5 4.4 %shard_map.190 = (bf16[4,8,128,128]{3,2,1,0:T(8,128)(2,1)S(1)}, f32[4,8,128,128]{3,2,1,0:T(8,128)S(1)}, f32[4,8,128,128]{3,2,1,0:T(8,128)S(1)}, f32[8,128]{1,0:T...) custom-call(s32[16]{0:T(128)S(1)} %copy-done.7, ...), custom_call_target="tpu_custom_call" | custom-call | flops 671088640 | bytes 3115656 | tf_op jit(solution)/shard_map/pallas_call | solution.py:781
  57.9 6.3 %all_gather.3.refs_0_ = bf16[4,3,128,128]{3,2,1,0:T(8,128)(2,1)S(1)} all-gather(bf16[1,3,128,128]{3,2,1,0:T(8,128)(2,1)S(1)} %get-tuple-element.69), channel_id=1, replica_groups=mesh['rows'=8,'dates'=4] {'dates'}, dimensions={0}, use_global_device_ids=true | all-gather | bytes 491520 | tf_op jit(solution)/shard_map/all_gather | solution.py:823
  64.2 3.9 %shard_map.191 = (bf16[4,8,128,128]{3,2,1,0:T(8,128)(2,1)}, bf16[4,8,32,128]{3,2,1,0:T(8,128)(2,1)}, f32[128,128]{1,0:T(8,128)}, f32[8,128]{1,0:T(8,128)S(1)}, f32[8,8,128]{2,1,0:T(8,128)S(1)}) custom-call(bf16[4,3,128,128]{3,2,1,0:T(8,128)(2,1)S(1)} %all_gather.3.refs_0_, f32[128,128]{1,0:T(8,128)S(1)} %get-tuple-element.70.refs_1_, ...), custom_call_target="tpu_custom_call" | custom-call | flops 671088640 | bytes 14370824 | tf_op jit(solution)/shard_map/pallas_call | solution.py:781
  68.2 9.1 %all_to_all.30.refs_3_ = f32[8,8,128]{2,1,0:T(8,128)S(1)} all-to-all(f32[8,8,128]{2,1,0:T(8,128)S(1)} %get-tuple-element.79), channel_id=1, replica_groups=mesh['rows'=8,'dates'=4] {'rows'}, dimensions={0} | all-to-all | bytes 65536 | tf_op jit(solution)/shard_map/all_to_all | solution.py:819
  77.2 7.0 %shard_map.192 = (bf16[4,8,128,128]{3,2,1,0:T(8,128)(2,1)}, bf16[4,10,128,128]{3,2,1,0:T(8,128)(2,1)}, f32[8,128]{1,0:T(8,128)S(1)}, f32[8,8,128]{2,1,0:T(8,128)}) custom-call(s32[1]{0:T(128)} %bitcast.refs_0_.refs_4_, bf16[4,8,128,128]{3,2,1,0:T(8,128)(2,1)} %get-tuple-element.78.refs_1_, ...), custom_call_target="tpu_custom_call" | custom-call | flops 1207959552 | bytes 7489544 | tf_op jit(solution)/shard_map/pallas_call | solution.py:781
  84.2 3.4 %all-to-all-start.3 = ((f32[8,8,128]{2,1,0:T(8,128)}), f32[8,8,128]{2,1,0:T(8,128)S(1)}, u32[]{:S(2)}, u32[]{:S(2)}) async-start(f32[8,8,128]{2,1,0:T(8,128)} %get-tuple-element.82), calls=%async_computation.3 | async-start | bytes 65536 | tf_op jit(solution)/shard_map/all_to_all | solution.py:819
  87.6 4.0 %shard_map.193.refs_12_ = bf16[1280,128]{1,0:T(8,128)(2,1)} custom-call(bf16[4,10,128,128]{3,2,1,0:T(8,128)(2,1)} %get-tuple-element.83.refs_0_, bf16[4,8,128,128]{3,2,1,0:T(8,128)(2,1)} %get-tuple-element.84.refs_1_, f32[128,128]{1,0:T(8,128)} %get-tuple-element.85.refs_2_), custom_call_target="tpu_custom_call" | custom-call | flops 1207959552 | bytes 4849664 | tf_op jit(solution)/shard_map/pallas_call | solution.py:781
  91.6 2.6 %all-to-all-done.3.refs_7_ = f32[8,8,128]{2,1,0:T(8,128)S(1)} async-done(((f32[8,8,128]{2,1,0:T(8,128)}), f32[8,8,128]{2,1,0:T(8,128)S(1)}, u32[]{:S(2)}, u32[]{:S(2)}) %all-to-all-start.3) | async-done | bytes 32800 | tf_op jit(solution)/shard_map/all_to_all | solution.py:819
  94.2 4.1 %shard_map.194 = (bf16[1024,128]{1,0:T(8,128)(2,1)S(1)}, bf16[1024,128]{1,0:T(8,128)(2,1)S(1)}) custom-call(bf16[4,8,2,128,128]{4,3,2,1,0:T(8,128)(2,1)} %bitcast.53, bf16[4,128,128]{2,1,0:T(8,128)(2,1)S(1)} %collective-permute-done.refs_1_.refs_3_, bf16[4,2,128,128]{3,2,1,0:T(8,128)(2,1)S(1)} %collective-permute-done.1.refs_1_.refs_2_, ...), custom_call_target="tpu_custom_call" | custom-call | flops 805306368 | bytes 10970128 | tf_op jit(solution)/shard_map/pallas_call | solution.py:781
  98.4 0.0 copy-start.9
  98.4 0.1 collective-permute-start.6
  98.5 1.5 %collective-permute-done.6 = bf16[1024,128]{1,0:T(8,128)(2,1)S(1)} collective-permute-done((bf16[1024,128]{1,0:T(8,128)(2,1)S(1)}, bf16[1024,128]{1,0:T(8,128)(2,1)S(1)}, u32[]{:S(2)}, u32[]{:S(2)}) %collective-permute-start.6) | collective-permute-done | bytes 262176 | tf_op jit(solution)/shard_map/ppermute | solution.py:828
  100.0 0.1 add_convert_fusion
  100.1 13.7 %all_to_all.31.in_ref = bf16[16,64,128]{2,1,0:T(8,128)(2,1)S(1)} all-to-all(bf16[16,64,128]{2,1,0:T(8,128)(2,1)S(1)} %bitcast.54), channel_id=1, replica_groups={{0,2,4,6,8,10,12,14,16,18,20,22,24,26,28,30},{1,3,5,7,9,11,13,15,17,19,..., dimensions={0} | all-to-all | bytes 524288 | tf_op jit(solution)/shard_map/all_to_all | solution.py:835
  113.7 0.8 shard_map.195
  114.5 3.5 %all-to-all-start.5 = ((bf16[16,64,128]{2,1,0:T(8,128)(2,1)}), bf16[16,64,128]{2,1,0:T(8,128)(2,1)S(1)}, u32[]{:S(2)}, u32[]{:S(2)}) async-start(bf16[16,64,128]{2,1,0:T(8,128)(2,1)} %shard_map.195), calls=%async_computation.5 | async-start | bytes 524288 | tf_op jit(solution)/shard_map/all_to_all | solution.py:835
  118.1 0.1 collective-permute-start.7
  118.2 1.9 %collective-permute-start.8 = (bf16[8,32,128]{2,1,0:T(8,128)(2,1)S(1)}, bf16[8,32,128]{2,1,0:T(8,128)(2,1)S(1)}, u32[]{:S(2)}, u32[]{:S(2)}) collective-permute-start(bf16[8,32,128]{2,1,0:T(8,128)(2,1)S(1)} %get-tuple-element.105), channel_id=1, source_target_pairs={{0,2},{1,3},{2,0},{3,1},{4,6},{5,7},{6,4},{7,5},{8,10},{9,11},{10,... | collective-permute-start | bytes 196616 | tf_op jit(solution)/shard_map/ppermute | solution.py:814
  120.1 1.4 %collective-permute-start.9 = (bf16[8,32,128]{2,1,0:T(8,128)(2,1)S(1)}, bf16[8,32,128]{2,1,0:T(8,128)(2,1)S(1)}, u32[]{:S(2)}, u32[]{:S(2)}) collective-permute-start(bf16[8,32,128]{2,1,0:T(8,128)(2,1)S(1)} %get-tuple-element.104), channel_id=1, source_target_pairs={{0,3},{1,0},{2,1},{3,2},{4,7},{5,4},{6,5},{7,6},{8,11},{9,8},{10,9... | collective-permute-start | bytes 196616 | tf_op jit(solution)/shard_map/ppermute | solution.py:814
  121.5 5.9 %all-to-all-done.5 = bf16[16,64,128]{2,1,0:T(8,128)(2,1)S(1)} async-done(((bf16[16,64,128]{2,1,0:T(8,128)(2,1)}), bf16[16,64,128]{2,1,0:T(8,128)(2,1)S(1)}, u32[]{:S(2)}, u32[]{:S(2)}) %all-to-all-start.5) | async-done | bytes 262176 | tf_op jit(solution)/shard_map/all_to_all | solution.py:835
  127.5 0.7 fusion.3
  128.2 0.8 collective-permute-done.10.other_ref
  129.0 1.0 shard_map.196
  (24 shorter events, 0.1 us)
Async XLA Ops:
  1.6 7.8 %collective-permute-start = (bf16[4,128,128]{2,1,0:T(8,128)(2,1)S(1)}, bf16[4,128,128]{2,1,0:T(8,128)(2,1)S(1)}, u32[]{:S(2)}, u32[]{:S(2)}) collective-permute-start(bf16[4,128,128]{2,1,0:T(8,128)(2,1)S(1)} %slice_bitcast_fusion.refs_4_), channel_id=1, source_target_pairs={{0,4},{4,8},{8,12},{12,16},{16,20},{20,24},{24,28},{1,5},{5,9},{9,... | collective-permute-start | bytes 393224 | tf_op jit(solution)/shard_map/ppermute | solution.py:795
  6.5 15.5 %copy-start.1 = (bf16[3,3,64,128]{3,2,1,0:T(8,128)(2,1)S(1)}, bf16[3,3,64,128]{3,2,1,0:T(8,128)(2,1)}, u32[]{:S(2)}) copy-start(bf16[3,3,64,128]{3,2,1,0:T(8,128)(2,1)} %refs_5_.2) | copy-start | bytes 442372
  8.4 29.0 %copy-start.4 = (f32[128]{0:T(128)S(1)}, f32[128]{0:T(128)}, u32[]{:S(2)}) copy-start(f32[128]{0:T(128)} %param.17) | copy-start | bytes 1540
  8.4 29.0 %copy-start.8 = (f32[128]{0:T(128)S(1)}, f32[128]{0:T(128)}, u32[]{:S(2)}) copy-start(f32[128]{0:T(128)} %param.18) | copy-start | bytes 1540
  9.3 12.6 %collective-permute-start.1 = (bf16[4,2,128,128]{3,2,1,0:T(8,128)(2,1)S(1)}, bf16[4,2,128,128]{3,2,1,0:T(8,128)(2,1)S(1)}, u32[]{:S(2)}, u32[]{:S(2)}) collective-permute-start(bf16[4,2,128,128]{3,2,1,0:T(8,128)(2,1)S(1)} %get-tuple-element.57), channel_id=1, source_target_pairs={{0,4},{4,0},{8,12},{12,8},{16,20},{20,16},{24,28},{28,24},{1,5},{5... | collective-permute-start | bytes 786440 | tf_op jit(solution)/shard_map/ppermute | solution.py:902
  11.7 10.3 %collective-permute-start.2 = (bf16[4,2,128,128]{3,2,1,0:T(8,128)(2,1)S(1)}, bf16[4,2,128,128]{3,2,1,0:T(8,128)(2,1)S(1)}, u32[]{:S(2)}, u32[]{:S(2)}) collective-permute-start(bf16[4,2,128,128]{3,2,1,0:T(8,128)(2,1)S(1)} %get-tuple-element.58), channel_id=1, source_target_pairs={{4,8},{12,16},{20,24},{8,4},{16,12},{24,20},{5,9},{13,17},{21,25},... | collective-permute-start | bytes 786440 | tf_op jit(solution)/shard_map/ppermute | solution.py:904
  22.5 8.3 %collective-permute-start.3 = (bf16[384,128]{1,0:T(8,128)(2,1)S(1)}, bf16[384,128]{1,0:T(8,128)(2,1)S(1)}, u32[]{:S(2)}, u32[]{:S(2)}) collective-permute-start(bf16[384,128]{1,0:T(8,128)(2,1)S(1)} %fusion.4), channel_id=1, source_target_pairs={{2,0},{3,1},{0,2},{1,3},{6,4},{7,5},{4,6},{5,7},{10,8},{11,9},{8,1... | collective-permute-start | bytes 294920 | tf_op jit(solution)/shard_map/ppermute | solution.py:803
  24.0 13.4 %all-to-all-start = ((f32[8,8,128]{2,1,0:T(8,128)}), f32[8,8,128]{2,1,0:T(8,128)S(1)}, u32[]{:S(2)}, u32[]{:S(2)}) async-start(f32[8,8,128]{2,1,0:T(8,128)} %get-tuple-element.59), calls=%async_computation | async-start | bytes 65536 | tf_op jit(solution)/shard_map/all_to_all | solution.py:819
  30.8 16.1 %collective-permute-start.4 = (bf16[384,128]{1,0:T(8,128)(2,1)S(1)}, bf16[384,128]{1,0:T(8,128)(2,1)S(1)}, u32[]{:S(2)}, u32[]{:S(2)}) collective-permute-start(bf16[384,128]{1,0:T(8,128)(2,1)S(1)} %fusion.4), channel_id=1, source_target_pairs={{0,1},{1,0},{2,3},{3,2},{4,5},{5,4},{6,7},{7,6},{8,9},{9,8},{10,11... | collective-permute-start | bytes 294920 | tf_op jit(solution)/shard_map/ppermute | solution.py:828
  30.8 16.1 %collective-permute-start.5 = (bf16[384,128]{1,0:T(8,128)(2,1)S(1)}, bf16[384,128]{1,0:T(8,128)(2,1)S(1)}, u32[]{:S(2)}, u32[]{:S(2)}) collective-permute-start(bf16[384,128]{1,0:T(8,128)(2,1)S(1)} %collective-permute-done.3), channel_id=1, source_target_pairs={{0,1},{1,0},{2,3},{3,2},{4,5},{5,4},{6,7},{7,6},{8,9},{9,8},{10,11... | collective-permute-start | bytes 294920 | tf_op jit(solution)/shard_map/ppermute | solution.py:828
  37.5 16.0 %copy-start.2 = (f32[128]{0:T(128)S(1)}, f32[128]{0:T(128)}, u32[]{:S(2)}) copy-start(f32[128]{0:T(128)} %param.20) | copy-start | bytes 1540
  37.5 16.0 %copy-start.3 = (f32[128]{0:T(128)S(1)}, f32[128]{0:T(128)}, u32[]{:S(2)}) copy-start(f32[128]{0:T(128)} %param.21) | copy-start | bytes 1540
  37.5 16.0 %copy-start.5 = (bf16[128,64]{0,1:T(8,128)(2,1)S(1)}, bf16[128,64]{0,1:T(8,128)(2,1)}, u32[]{:S(2)}) copy-start(bf16[128,64]{0,1:T(8,128)(2,1)} %param.22) | copy-start | bytes 49156
  37.5 16.0 %copy-start.6 = (f32[16,4]{0,1:T(4,128)S(1)}, f32[16,4]{0,1:T(4,128)}, u32[]{:S(2)}) copy-start(f32[16,4]{0,1:T(4,128)} %param.23) | copy-start | bytes 772
  37.5 16.0 %copy-start.7 = (s32[16]{0:T(128)S(1)}, s32[16]{0:T(128)}, u32[]{:S(2)}) copy-start(s32[16]{0:T(128)} %refs_0_.1) | copy-start | bytes 196
  43.4 20.9 %copy-start = (bf16[4,8,128,128]{3,2,1,0:T(8,128)(2,1)S(1)}, bf16[4,8,128,128]{3,2,1,0:T(8,128)(2,1)}, u32[]{:S(2)}) copy-start(bf16[4,8,128,128]{3,2,1,0:T(8,128)(2,1)} %get-tuple-element.65.refs_1_.refs_5_.refs_2_) | copy-start | bytes 3145732
  43.4 10.1 %all-to-all-start.1 = ((f32[8,8,128]{2,1,0:T(8,128)}), f32[8,8,128]{2,1,0:T(8,128)S(1)}, u32[]{:S(2)}, u32[]{:S(2)}) async-start(f32[8,8,128]{2,1,0:T(8,128)} %get-tuple-element.66), calls=%async_computation.1 | async-start | bytes 65536 | tf_op jit(solution)/shard_map/all_to_all | solution.py:819
  84.2 10.0 %all-to-all-start.3 = ((f32[8,8,128]{2,1,0:T(8,128)}), f32[8,8,128]{2,1,0:T(8,128)S(1)}, u32[]{:S(2)}, u32[]{:S(2)}) async-start(f32[8,8,128]{2,1,0:T(8,128)} %get-tuple-element.82), calls=%async_computation.3 | async-start | bytes 65536 | tf_op jit(solution)/shard_map/all_to_all | solution.py:819
  98.4 19.7 %copy-start.9 = (bf16[4,8,32,128]{3,2,1,0:T(8,128)(2,1)S(1)}, bf16[4,8,32,128]{3,2,1,0:T(8,128)(2,1)}, u32[]{:S(2)}) copy-start(bf16[4,8,32,128]{3,2,1,0:T(8,128)(2,1)} %get-tuple-element.92) | copy-start | bytes 786436
  98.4 1.6 %collective-permute-start.6 = (bf16[1024,128]{1,0:T(8,128)(2,1)S(1)}, bf16[1024,128]{1,0:T(8,128)(2,1)S(1)}, u32[]{:S(2)}, u32[]{:S(2)}) collective-permute-start(bf16[1024,128]{1,0:T(8,128)(2,1)S(1)} %get-tuple-element.91), channel_id=1, source_target_pairs={{0,1},{1,0},{2,3},{3,2},{4,5},{5,4},{6,7},{7,6},{8,9},{9,8},{10,11... | collective-permute-start | bytes 786440 | tf_op jit(solution)/shard_map/ppermute | solution.py:828
  114.5 13.0 %all-to-all-start.5 = ((bf16[16,64,128]{2,1,0:T(8,128)(2,1)}), bf16[16,64,128]{2,1,0:T(8,128)(2,1)S(1)}, u32[]{:S(2)}, u32[]{:S(2)}) async-start(bf16[16,64,128]{2,1,0:T(8,128)(2,1)} %shard_map.195), calls=%async_computation.5 | async-start | bytes 524288 | tf_op jit(solution)/shard_map/all_to_all | solution.py:835
  118.1 9.3 %collective-permute-start.7 = (bf16[8,32,128]{2,1,0:T(8,128)(2,1)S(1)}, bf16[8,32,128]{2,1,0:T(8,128)(2,1)S(1)}, u32[]{:S(2)}, u32[]{:S(2)}) collective-permute-start(bf16[8,32,128]{2,1,0:T(8,128)(2,1)S(1)} %get-tuple-element.103), channel_id=1, source_target_pairs={{0,1},{1,2},{2,3},{3,0},{4,5},{5,6},{6,7},{7,4},{8,9},{9,10},{10,1... | collective-permute-start | bytes 196616 | tf_op jit(solution)/shard_map/ppermute | solution.py:814
  118.2 9.3 %collective-permute-start.8 = (bf16[8,32,128]{2,1,0:T(8,128)(2,1)S(1)}, bf16[8,32,128]{2,1,0:T(8,128)(2,1)S(1)}, u32[]{:S(2)}, u32[]{:S(2)}) collective-permute-start(bf16[8,32,128]{2,1,0:T(8,128)(2,1)S(1)} %get-tuple-element.105), channel_id=1, source_target_pairs={{0,2},{1,3},{2,0},{3,1},{4,6},{5,7},{6,4},{7,5},{8,10},{9,11},{10,... | collective-permute-start | bytes 196616 | tf_op jit(solution)/shard_map/ppermute | solution.py:814
  120.1 7.4 %collective-permute-start.9 = (bf16[8,32,128]{2,1,0:T(8,128)(2,1)S(1)}, bf16[8,32,128]{2,1,0:T(8,128)(2,1)S(1)}, u32[]{:S(2)}, u32[]{:S(2)}) collective-permute-start(bf16[8,32,128]{2,1,0:T(8,128)(2,1)S(1)} %get-tuple-element.104), channel_id=1, source_target_pairs={{0,3},{1,0},{2,1},{3,2},{4,7},{5,4},{6,5},{7,6},{8,11},{9,8},{10,9... | collective-permute-start | bytes 196616 | tf_op jit(solution)/shard_map/ppermute | solution.py:814
  127.5 1.5 %collective-permute-start.10 = (bf16[1024,128]{1,0:T(8,128)(2,1)S(1)}, bf16[1024,128]{1,0:T(8,128)(2,1)S(1)}, u32[]{:S(2)}, u32[]{:S(2)}) collective-permute-start(bf16[1024,128]{1,0:T(8,128)(2,1)S(1)} %bitcast.39), channel_id=1, source_target_pairs={{0,1},{1,0},{2,3},{3,2},{4,5},{5,4},{6,7},{7,6},{8,9},{9,8},{10,11... | collective-permute-start | bytes 786440 | tf_op jit(solution)/shard_map/ppermute | solution.py:828

commit v8 on v7

--- a/solution.py
+++ b/solution.py
@@ -132,6 +132,49 @@
     def _():
         high_ref[...] = outer_ref[...]
         below_ref[...] = inner_ref[...]
+
+
+def load_kernel(
+    place_ref,
+    last_ref,
+    img_hbm,
+    grad_hbm,
+    valid_hbm,
+    img_ref,
+    inner_ref,
+    outer_ref,
+    packed_ref,
+    valid_ref,
+    ready,
+):
+    blocks = grad_hbm.shape[0]
+    moves = [
+        pltpu.make_async_copy(grad_hbm, packed_ref.at[pl.ds(0, blocks)], ready.at[0]),
+        pltpu.make_async_copy(valid_hbm, valid_ref, ready.at[1]),
+        pltpu.make_async_copy(img_hbm, img_ref, ready.at[2]),
+    ]
+    for move in moves:
+        move.start()
+    for move in moves:
+        move.wait()
+    rows = img_ref.shape[1]
+    odd = place_ref[0] % 2 == 1
+
+    @pl.when(odd)
+    def _():
+        inner_ref[...] = img_ref[:, :2]
+        outer_ref[...] = img_ref[:, rows - 3 : rows - 1]
+
+    @pl.when(jnp.logical_not(odd))
+    def _():
+        inner_ref[...] = img_ref[:, rows - 3 : rows - 1]
+        outer_ref[...] = img_ref[:, :2]
+
+    piece, width = packed_ref.shape[1:]
+    dates, rows, cols = valid_ref.shape
+    values = valid_ref[...].astype(F32).reshape(dates * rows, cols)
+    values = jnp.concatenate([values, jnp.zeros((dates * rows, width - cols), F32)], axis=1)
+    packed_ref[blocks:] = values.astype(BF16).reshape(-1, piece, width)
 
 
 def edge_kernel(
@@ -162,6 +205,22 @@
     down_ref[...] = stored[dates:]
 
 
+def activate_rows(date, dates, edge_flags, conv_refs, norm_refs, hidden_ref):
+    conv_ref, up_ref, down_ref = conv_refs
+    norm_ref, gain_ref, shift_ref = norm_refs
+    scale = norm_ref[pl.ds(dates + date, 1), :] * gain_ref[...]
+    shift = shift_ref[...] - norm_ref[pl.ds(date, 1), :] * scale
+
+    def activate(values):
+        linear = values.astype(F32) * scale + shift
+        return linear * sigmoid(linear)
+
+    rows = conv_ref.shape[1]
+    hidden_ref[0, 0] = (activate(up_ref[0]) * edge_flags[0]).astype(BF16)
+    hidden_ref[0, rows + 1] = (activate(down_ref[0]) * edge_flags[1]).astype(BF16)
+    hidden_ref[0, 1 : rows + 1] = activate(conv_ref[0]).astype(BF16)
+
+
 def block_kernel(
     date,
     dates,
@@ -174,10 +233,10 @@
     shift_ref,
     weight_ref,
     out_ref,
-    hidden_ref,
     norm_ref,
     sums_ref,
     table,
+    hidden_ref,
     *,
     norm_count,
     row_devs,
@@ -192,18 +251,15 @@
                     row_tap * width : (row_tap + 1) * width, col_tap * width : (col_tap + 1) * width
                 ] = weight_ref[row_tap, col_tap]
 
-    scale = norm_ref[pl.ds(dates + date, 1), :] * gain_ref[...]
-    shift = shift_ref[...] - norm_ref[pl.ds(date, 1), :] * scale
-
-    def activate(values):
-        linear = values.astype(F32) * scale + shift
-        return linear * sigmoid(linear)
-
     rows, cols = conv_ref.shape[1:3]
-    above_edge, below_edge = edges(edge_ref, row_devs)
-    hidden_ref[0, 0] = (activate(up_ref[0]) * above_edge).astype(BF16)
-    hidden_ref[0, rows + 1] = (activate(down_ref[0]) * below_edge).astype(BF16)
-    hidden_ref[0, 1 : rows + 1] = activate(conv_ref[0]).astype(BF16)
+    activate_rows(
+        date,
+        dates,
+        edges(edge_ref, row_devs),
+        (conv_ref, up_ref, down_ref),
+        (norm_ref, gain_ref, shift_ref),
+        hidden_ref,
+    )
     taps = jnp.concatenate(
         [hidden_ref[0, tap : tap + rows] for tap in range(3)], axis=-1
     ).reshape(rows * cols, 3 * width)
@@ -530,13 +586,36 @@
 
 
 def block_grad_kernel(
-    date, dates, hidden_ref, pre_ref, key_ref, out_ref, total
+    date,
+    dates,
+    edge_ref,
+    conv_ref,
+    up_ref,
+    down_ref,
+    norm_ref,
+    gain_ref,
+    shift_ref,
+    pre_ref,
+    key_ref,
+    out_ref,
+    total,
+    hidden_ref,
+    *,
+    row_devs,
 ):
     rows, cols, width = pre_ref.shape[1:]
 
     if date == 0:
         total[...] = jnp.zeros_like(total)
 
+    activate_rows(
+        date,
+        dates,
+        edges(edge_ref, row_devs),
+        (conv_ref, up_ref, down_ref),
+        (norm_ref, gain_ref, shift_ref),
+        hidden_ref,
+    )
     grads = pre_ref[0].astype(F32)
     grads = jnp.concatenate(
         [from_right(grads).astype(BF16), pre_ref[0], from_left(grads).astype(BF16)], axis=-1
@@ -795,13 +874,13 @@
     return lax.ppermute(array, "rows", pairs)
 
 
-def turned(array):
+def same_core(array):
     devices = lax.axis_size("dates")
     pieces = [array]
     for step in range(2, devices, 2):
         pairs = [((i + step) % devices, i) for i in range(devices)]
         pieces.append(lax.ppermute(array, "dates", pairs))
-    return jnp.stack(pieces + [other_core(piece) for piece in pieces])
+    return pieces
 
 
 def sum_of_parts(parts):
@@ -891,13 +970,28 @@
     last = images[:, -1]
     above = shifted(last, 1)
     grad_rows = out_grad.size // width
-    valid_rows = valid.astype(BF16).reshape(valid.shape[0] * rows, -1)
-    valid_rows = jnp.pad(valid_rows, ((0, 0), (0, width - valid_rows.shape[1])))
-    packed = jnp.concatenate([out_grad.reshape(grad_rows, width), valid_rows])
     row_place = lax.axis_index("rows")
-    odd = row_place % 2 == 1
-    inner = jnp.where(odd, images[:, :2], images[:, -3:-1])
-    outer = jnp.where(odd, images[:, -3:-1], images[:, :2])
+    place = row_place.reshape(1)
+    valid_count = valid.shape[0] * rows
+    piece = out_grad.shape[1]
+    packed_shape = ((grad_rows + valid_count) // piece, piece, width)
+    in_hbm, in_vmem = pl.BlockSpec(memory_space=pltpu.HBM), pl.BlockSpec(memory_space=pltpu.VMEM)
+    images_near, inner, outer, packed = pl.pallas_call(
+        load_kernel,
+        in_specs=[pl.BlockSpec(memory_space=pltpu.SMEM), in_vmem, in_hbm, in_hbm, in_hbm],
+        out_specs=[in_vmem] * 4,
+        out_shape=[
+            jax.ShapeDtypeStruct(shape, BF16)
+            for shape in (images.shape,) + ((dates, 2, cols, pair_width),) * 2 + (packed_shape,)
+        ],
+        scratch_shapes=[pltpu.VMEM(valid.shape, valid.dtype), pltpu.SemaphoreType.DMA((3,))],
+        compiler_params=pltpu.CompilerParams(vmem_limit_bytes=16 * MIB),
+    )(
+        place,
+        last,
+        *[pltpu.with_memory_space_constraint(x, pltpu.HBM) for x in (images, out_grad, valid)],
+    )
+    packed = packed.reshape(grad_rows + valid_count, width)
     inner, outer, above, packed = lax.optimization_barrier((inner, outer, above, packed))
     inner = lax.ppermute(inner, "rows", [(i, i ^ 1) for i in range(row_devs)])
     pairs = [(i, i + 1) for i in range(1, row_devs - 1, 2)]
@@ -906,14 +1000,17 @@
     conv_out, sums = call(
         down_kernel,
         dates,
-        [("date far", paired), ("date", above), ("all far", conv_weight)],
+        [
+            ("date", images_near.reshape(paired.shape)),
+            ("date", above),
+            ("all far", conv_weight),
+        ],
         [("date far", frame, BF16), ("all", (row_devs, 2 * dates, width), F32)],
         [pltpu.VMEM((3 * pair_width, 2 * width), BF16)],
         6 * flops,
     )
     stats = exchange(sums, "rows")
     inner, outer, last, _ = lax.optimization_barrier((inner, outer, last, sums))
-    place = row_place.reshape(1)
     halo_up, halo_down = call(
         edge_kernel,
         1,
@@ -933,12 +1030,10 @@
         ],
         6 * flops // rows,
     )
+    turn = lax.axis_index("dates").reshape(1)
     packed, _ = lax.optimization_barrier((packed, halo_up))
-    sources = turned(packed)
-    clear = lax.dynamic_slice_in_dim(sources, grad_rows + date_start * rows, dates * rows, 1)
-    clear = clear.astype(F32)
-    turn = lax.axis_index("dates").reshape(1)
-    block_out, hidden, first_norm, sums = call(
+    pieces = same_core(packed)
+    block_out, first_norm, sums = call(
         functools.partial(block_kernel, norm_count=norm_count, row_devs=row_devs),
         dates,
         [
@@ -953,14 +1048,20 @@
         ],
         [
             ("date far", frame, BF16),
-            ("date far", (dates, rows + 2, cols, width), BF16),
             ("all", (2 * dates, width), F32),
             ("all", (row_devs, 2 * dates, width), F32),
         ],
-        [pltpu.VMEM((3 * width, 3 * width), BF16)],
+        [
+            pltpu.VMEM((3 * width, 3 * width), BF16),
+            pltpu.VMEM((1, rows + 2, cols, width), BF16),
+        ],
         9 * flops,
     )
     stats = exchange(sums, "rows")
+    pieces, _ = lax.optimization_barrier((pieces, sums))
+    sources = jnp.stack(pieces + [other_core(piece) for piece in pieces])
+    clear = lax.dynamic_slice_in_dim(sources, grad_rows + date_start * rows, dates * rows, 1)
+    clear = clear.astype(F32)
     features, exponent, attn, norm, packed, own_total, key_wide, query_wide = call(
         functools.partial(score_kernel, norm_count=norm_count, grad_scale=grad_scale),
         dates,
@@ -1056,11 +1157,24 @@
     )
     tails = exchange(sums, "rows")
     (block_rows,) = call(
-        block_grad_kernel,
+        functools.partial(block_grad_kernel, row_devs=row_devs),
         dates,
-        [("date far", hidden), ("date far", pre_grad), ("all far", key_part)],
+        [
+            ("scalar", place),
+            ("date far", conv_out),
+            ("date", halo_up),
+            ("date", halo_down),
+            ("all", first_norm),
+            ("all", first_gain),
+            ("all", first_shift),
+            ("date far", pre_grad),
+            ("all far", key_part),
+        ],
         [("all far", (10 * width, width), BF16)],
-        [pltpu.VMEM((3 * width, 3 * width), F32)],
+        [
+            pltpu.VMEM((3 * width, 3 * width), F32),
+            pltpu.VMEM((1, rows + 2, cols, width), BF16),
+        ],
         9 * flops,
     )
     tails, block_rows = lax.optimization_barrier((tails, block_rows))

time: 131 us -> 125 us (0.954)
  waiting for transfers between devices: 27.9 us -> 22.6 us
  other arithmetic: 3.65 us -> 0.81 us
    ppermute x1, waiting for transfers between devices: 4.26 us -> 0.01 us  [local(): inner = lax.ppermute(inner, 'rows', [(i, i ^ 1) for i in range(row_devs)])]
    all_to_all x3, waiting for transfers between devices: 15.3 us -> 13.3 us  [exchange(): return lax.all_to_all(pieces, axes, split_axis=0, concat_axis=0, tiled=True)]
    pallas_call x0 -> x1, Pallas kernels: none -> 1.74 us  [local(): pl.pallas_call(load_kernel, in_specs=[pl.BlockSpec(memory_space=pltpu.SME...]
    pallas_call x8, Pallas kernels: 35.1 us -> 33.8 us  [call(): pl.pallas_call(body, in_specs=in_specs, out_specs=out_specs, out_shape=ou...]
  transfers between devices with their start and end apart: 15 -> 15, of which waited for: 7 -> 7; matrix products, arithmetic and copies ran while one was open for 3% -> 1% of each run, Pallas kernels for 12% -> 13%
where the time goes in v8:
time: 125 us; the launch traced here: 124 us
  Pallas kernels  37.3 us (30%)
  starting transfers between devices  31.4 us (25%)
  blocking collectives  30.2 us (24%)
  waiting for transfers between devices  22.6 us (18%)
    pallas_call x8, Pallas kernels, call(): pl.pallas_call(body, in_specs=in_specs, out_specs=out_specs, out_shape=ou...  33.8 us
    all_to_all x1, blocking collectives, exchange_cores(): lax.all_to_all(pieces, axes, split_axis=0, concat_axis=0, axis_index_grou...  14.4 us
    all_to_all x3, starting transfers between devices, exchange(): return lax.all_to_all(pieces, axes, split_axis=0, concat_axis=0, tiled=True)  14.3 us
    all_to_all x3, waiting for transfers between devices, exchange(): return lax.all_to_all(pieces, axes, split_axis=0, concat_axis=0, tiled=True)  13.3 us
    all_to_all x1, blocking collectives, exchange(): return lax.all_to_all(pieces, axes, split_axis=0, concat_axis=0, tiled=True)  9.24 us
    all_gather x1, blocking collectives, gather(): return lax.all_gather(array, axis, axis=0, tiled=True)  6.47 us
    all_to_all x1, waiting for transfers between devices, exchange_cores(): lax.all_to_all(pieces, axes, split_axis=0, concat_axis=0, axis_index_grou...  5.95 us
    ppermute x1, starting transfers between devices, shifted(): return lax.ppermute(array, 'rows', pairs)  4.88 us
  transfers between devices with their start and end apart: 15, of which 7 were waited for; matrix products, arithmetic and copies ran while one was open for 1% of the time, Pallas kernels for 13%

profile of v8, /device:TPU:0, one launch (start us, length us, event | category | flops | bytes accessed | tf_op | source)
XLA Modules:
  0.0 124.3 jit_solution(18186351339786324515)
XLA Ops:
  0.6 0.9 slice_bitcast_fusion.last_ref.refs_4_
  1.6 4.9 %collective-permute-start = (bf16[4,128,128]{2,1,0:T(8,128)(2,1)S(1)}, bf16[4,128,128]{2,1,0:T(8,128)(2,1)S(1)}, u32[]{:S(2)}, u32[]{:S(2)}) collective-permute-start(bf16[4,128,128]{2,1,0:T(8,128)(2,1)S(1)} %slice_bitcast_fusion.last_ref.refs_4_), channel_id=1, source_target_pairs={{0,4},{4,8},{8,12},{12,16},{16,20},{20,24},{24,28},{1,5},{5,9},{9,... | collective-permute-start | bytes 393224 | tf_op jit(solution)/shard_map/ppermute | solution.py:874
  6.5 1.7 %shard_map.187 = (bf16[4,16,128,128]{3,2,1,0:T(8,128)(2,1)S(1)}, bf16[4,2,128,128]{3,2,1,0:T(8,128)(2,1)S(1)}, bf16[4,2,128,128]{3,2,1,0:T(8,128)(2,1)S(1)}, bf16[12,32,128]{2,1,0:T(8,128)(2,1)S(1)}) custom-call(s32[1]{0:T(128)} %bitcast.place_ref.refs_0_.refs_4_, bf16[4,128,128]{2,1,0:T(8,128)(2,1)S(1)} %slice_bitcast_fusion.last_ref.refs_4_, ...), custom_call_target="tpu_custom_call" | custom-call | tf_op jit(solution)/shard_map/pallas_call | solution.py:979
  8.2 0.0 copy-start.1
  8.2 0.0 copy-start.4
  8.2 0.0 copy-start.8
  8.2 0.9 collective-permute-done.refs_1_.refs_3_
  9.2 2.5 %collective-permute-start.1 = (bf16[4,2,128,128]{3,2,1,0:T(8,128)(2,1)S(1)}, bf16[4,2,128,128]{3,2,1,0:T(8,128)(2,1)S(1)}, u32[]{:S(2)}, u32[]{:S(2)}) collective-permute-start(bf16[4,2,128,128]{3,2,1,0:T(8,128)(2,1)S(1)} %get-tuple-element.66), channel_id=1, source_target_pairs={{0,4},{4,0},{8,12},{12,8},{16,20},{20,16},{24,28},{28,24},{1,5},{5... | collective-permute-start | bytes 786440 | tf_op jit(solution)/shard_map/ppermute | solution.py:996
  11.7 0.7 collective-permute-start.2
  12.3 3.7 %shard_map.188 = (bf16[4,8,128,128]{3,2,1,0:T(8,128)(2,1)}, f32[8,8,128]{2,1,0:T(8,128)}) custom-call(bf16[4,8,2,128,128]{4,3,2,1,0:T(8,128)(2,1)S(1)} %bitcast.51, bf16[4,128,128]{2,1,0:T(8,128)(2,1)S(1)} %collective-permute-done.refs_1_.refs_3_, bf16[3,3,64,128]{3,2,1,0:T(8,128)(2,1)} %refs_5_.2), custom_call_target="tpu_custom_call" | custom-call | flops 805306368 | bytes 4751360 | tf_op jit(solution)/shard_map/pallas_call | solution.py:860
  16.0 7.6 %all-to-all-start = ((f32[8,8,128]{2,1,0:T(8,128)}), f32[8,8,128]{2,1,0:T(8,128)S(1)}, u32[]{:S(2)}, u32[]{:S(2)}) async-start(f32[8,8,128]{2,1,0:T(8,128)} %get-tuple-element.68), calls=%async_computation | async-start | bytes 65536 | tf_op jit(solution)/shard_map/all_to_all | solution.py:898
  23.6 0.0 collective-permute-done.1.refs_1_.refs_2_
  23.6 0.5 shard_map.189
  24.2 1.5 %collective-permute-start.3 = (bf16[384,128]{1,0:T(8,128)(2,1)S(1)}, bf16[384,128]{1,0:T(8,128)(2,1)S(1)}, u32[]{:S(2)}, u32[]{:S(2)}) collective-permute-start(bf16[384,128]{1,0:T(8,128)(2,1)S(1)} %bitcast.40), channel_id=1, source_target_pairs={{2,0},{3,1},{0,2},{1,3},{6,4},{7,5},{4,6},{5,7},{10,8},{11,9},{8,1... | collective-permute-start | bytes 294920 | tf_op jit(solution)/shard_map/ppermute | solution.py:882
  25.7 4.6 %all-to-all-done.refs_4_ = f32[8,8,128]{2,1,0:T(8,128)S(1)} async-done(((f32[8,8,128]{2,1,0:T(8,128)}), f32[8,8,128]{2,1,0:T(8,128)S(1)}, u32[]{:S(2)}, u32[]{:S(2)}) %all-to-all-start) | async-done | bytes 32800 | tf_op jit(solution)/shard_map/all_to_all | solution.py:898
  30.3 0.0 copy-start.5
  30.3 0.0 copy-start.6
  30.3 0.0 copy-start.7
  30.4 5.7 %shard_map.190 = (bf16[4,8,128,128]{3,2,1,0:T(8,128)(2,1)}, f32[8,128]{1,0:T(8,128)S(1)}, f32[8,8,128]{2,1,0:T(8,128)}) custom-call(s32[1]{0:T(128)} %bitcast.place_ref.refs_0_.refs_4_, bf16[4,8,128,128]{3,2,1,0:T(8,128)(2,1)} %get-tuple-element.65.refs_1_.refs_6_.refs_5_, bf16[4,128,128]{2,1,0:T(8,128)(2,1)S(1)} %get-tuple-element.72.refs_2_.refs_7_, ...), custom_call_target="tpu_custom_call" | custom-call | flops 1207959552 | bytes 3278856 | tf_op jit(solution)/shard_map/pallas_call | solution.py:860
  36.0 0.1 collective-permute-start.4
  36.1 0.5 collective-permute-start.5
  36.6 3.3 %all-to-all-start.1 = ((f32[8,8,128]{2,1,0:T(8,128)}), f32[8,8,128]{2,1,0:T(8,128)S(1)}, u32[]{:S(2)}, u32[]{:S(2)}) async-start(f32[8,8,128]{2,1,0:T(8,128)} %get-tuple-element.75), calls=%async_computation.1 | async-start | bytes 65536 | tf_op jit(solution)/shard_map/all_to_all | solution.py:898
  40.0 0.0 collective-permute-done.5
  40.0 0.1 pad_maximum_fusion.refs_5_.refs_10_
  40.1 6.5 %all-to-all-done.1.refs_2_ = f32[8,8,128]{2,1,0:T(8,128)S(1)} async-done(((f32[8,8,128]{2,1,0:T(8,128)}), f32[8,8,128]{2,1,0:T(8,128)S(1)}, u32[]{:S(2)}, u32[]{:S(2)}) %all-to-all-start.1) | async-done | bytes 32800 | tf_op jit(solution)/shard_map/all_to_all | solution.py:898
  46.6 4.4 %shard_map.191 = (bf16[4,8,128,128]{3,2,1,0:T(8,128)(2,1)S(1)}, f32[4,8,128,128]{3,2,1,0:T(8,128)S(1)}, f32[4,8,128,128]{3,2,1,0:T(8,128)S(1)}, f32[8,128]{1,0:T...) custom-call(s32[16]{0:T(128)S(1)} %copy-done.7, ...), custom_call_target="tpu_custom_call" | custom-call | flops 671088640 | bytes 3115656 | tf_op jit(solution)/shard_map/pallas_call | solution.py:860
  51.0 6.5 %all_gather.3.refs_0_ = bf16[4,3,128,128]{3,2,1,0:T(8,128)(2,1)S(1)} all-gather(bf16[1,3,128,128]{3,2,1,0:T(8,128)(2,1)S(1)} %get-tuple-element.80), channel_id=1, replica_groups=mesh['rows'=8,'dates'=4] {'dates'}, dimensions={0}, use_global_device_ids=true | all-gather | bytes 491520 | tf_op jit(solution)/shard_map/all_gather | solution.py:902
  57.5 4.0 %shard_map.192 = (bf16[4,8,128,128]{3,2,1,0:T(8,128)(2,1)}, bf16[4,8,32,128]{3,2,1,0:T(8,128)(2,1)}, f32[128,128]{1,0:T(8,128)}, f32[8,128]{1,0:T(8,128)S(1)}, f32[8,8,128]{2,1,0:T(8,128)S(1)}) custom-call(bf16[4,3,128,128]{3,2,1,0:T(8,128)(2,1)S(1)} %all_gather.3.refs_0_, f32[128,128]{1,0:T(8,128)S(1)} %get-tuple-element.81.refs_1_, ...), custom_call_target="tpu_custom_call" | custom-call | flops 671088640 | bytes 14370824 | tf_op jit(solution)/shard_map/pallas_call | solution.py:860
  61.5 9.2 %all_to_all.30.refs_3_ = f32[8,8,128]{2,1,0:T(8,128)S(1)} all-to-all(f32[8,8,128]{2,1,0:T(8,128)S(1)} %get-tuple-element.90), channel_id=1, replica_groups=mesh['rows'=8,'dates'=4] {'rows'}, dimensions={0} | all-to-all | bytes 65536 | tf_op jit(solution)/shard_map/all_to_all | solution.py:898
  70.7 7.0 %shard_map.193 = (bf16[4,8,128,128]{3,2,1,0:T(8,128)(2,1)}, bf16[4,10,128,128]{3,2,1,0:T(8,128)(2,1)}, f32[8,128]{1,0:T(8,128)S(1)}, f32[8,8,128]{2,1,0:T(8,128)}) custom-call(s32[1]{0:T(128)} %bitcast.place_ref.refs_0_.refs_4_, bf16[4,8,128,128]{3,2,1,0:T(8,128)(2,1)} %get-tuple-element.89.refs_1_, ...), custom_call_target="tpu_custom_call" | custom-call | flops 1207959552 | bytes 7489544 | tf_op jit(solution)/shard_map/pallas_call | solution.py:860
  77.7 3.4 %all-to-all-start.3 = ((f32[8,8,128]{2,1,0:T(8,128)}), f32[8,8,128]{2,1,0:T(8,128)S(1)}, u32[]{:S(2)}, u32[]{:S(2)}) async-start(f32[8,8,128]{2,1,0:T(8,128)} %get-tuple-element.93), calls=%async_computation.3 | async-start | bytes 65536 | tf_op jit(solution)/shard_map/all_to_all | solution.py:898
  81.0 4.4 %shard_map.194.refs_12_ = bf16[1280,128]{1,0:T(8,128)(2,1)} custom-call(s32[1]{0:T(128)} %bitcast.place_ref.refs_0_.refs_4_, bf16[4,8,128,128]{3,2,1,0:T(8,128)(2,1)} %get-tuple-element.65.refs_1_.refs_6_.refs_5_, bf16[4,128,128]{2,1,0:T(8,128)(2,1)S(1)} %get-tuple-element.72.refs_2_.refs_7_, bf16[4,128,128]{2,1,0:T(8,128)(2,1)S(1)} %get-tuple-element.73.refs_3_.refs_8_, ...), custom_call_target="tpu_custom_call" | custom-call | flops 1207959552 | bytes 4859912 | tf_op jit(solution)/shard_map/pallas_call | solution.py:860
  85.5 2.2 %all-to-all-done.3.refs_7_ = f32[8,8,128]{2,1,0:T(8,128)S(1)} async-done(((f32[8,8,128]{2,1,0:T(8,128)}), f32[8,8,128]{2,1,0:T(8,128)S(1)}, u32[]{:S(2)}, u32[]{:S(2)}) %all-to-all-start.3) | async-done | bytes 32800 | tf_op jit(solution)/shard_map/all_to_all | solution.py:898
  87.7 4.1 %shard_map.195 = (bf16[1024,128]{1,0:T(8,128)(2,1)S(1)}, bf16[1024,128]{1,0:T(8,128)(2,1)S(1)}) custom-call(bf16[4,8,2,128,128]{4,3,2,1,0:T(8,128)(2,1)} %bitcast.57, bf16[4,128,128]{2,1,0:T(8,128)(2,1)S(1)} %collective-permute-done.refs_1_.refs_3_, bf16[4,2,128,128]{3,2,1,0:T(8,128)(2,1)S(1)} %collective-permute-done.1.refs_1_.refs_2_, ...), custom_call_target="tpu_custom_call" | custom-call | flops 805306368 | bytes 10970128 | tf_op jit(solution)/shard_map/pallas_call | solution.py:860
  91.8 0.0 copy-start.9
  91.8 0.1 collective-permute-start.6
  91.9 1.5 %collective-permute-done.6 = bf16[1024,128]{1,0:T(8,128)(2,1)S(1)} collective-permute-done((bf16[1024,128]{1,0:T(8,128)(2,1)S(1)}, bf16[1024,128]{1,0:T(8,128)(2,1)S(1)}, u32[]{:S(2)}, u32[]{:S(2)}) %collective-permute-start.6) | collective-permute-done | bytes 262176 | tf_op jit(solution)/shard_map/ppermute | solution.py:907
  93.4 0.1 add_convert_fusion
  93.5 14.4 %all_to_all.31.in_ref = bf16[16,64,128]{2,1,0:T(8,128)(2,1)S(1)} all-to-all(bf16[16,64,128]{2,1,0:T(8,128)(2,1)S(1)} %bitcast.58), channel_id=1, replica_groups={{0,2,4,6,8,10,12,14,16,18,20,22,24,26,28,30},{1,3,5,7,9,11,13,15,17,19,..., dimensions={0} | all-to-all | bytes 524288 | tf_op jit(solution)/shard_map/all_to_all | solution.py:914
  108.0 0.8 shard_map.196
  108.7 3.5 %all-to-all-start.5 = ((bf16[16,64,128]{2,1,0:T(8,128)(2,1)}), bf16[16,64,128]{2,1,0:T(8,128)(2,1)S(1)}, u32[]{:S(2)}, u32[]{:S(2)}) async-start(bf16[16,64,128]{2,1,0:T(8,128)(2,1)} %shard_map.196), calls=%async_computation.5 | async-start | bytes 524288 | tf_op jit(solution)/shard_map/all_to_all | solution.py:914
  112.3 0.1 collective-permute-start.7
  112.4 1.9 %collective-permute-start.8 = (bf16[8,32,128]{2,1,0:T(8,128)(2,1)S(1)}, bf16[8,32,128]{2,1,0:T(8,128)(2,1)S(1)}, u32[]{:S(2)}, u32[]{:S(2)}) collective-permute-start(bf16[8,32,128]{2,1,0:T(8,128)(2,1)S(1)} %get-tuple-element.113), channel_id=1, source_target_pairs={{0,2},{1,3},{2,0},{3,1},{4,6},{5,7},{6,4},{7,5},{8,10},{9,11},{10,... | collective-permute-start | bytes 196616 | tf_op jit(solution)/shard_map/ppermute | solution.py:893
  114.3 1.4 %collective-permute-start.9 = (bf16[8,32,128]{2,1,0:T(8,128)(2,1)S(1)}, bf16[8,32,128]{2,1,0:T(8,128)(2,1)S(1)}, u32[]{:S(2)}, u32[]{:S(2)}) collective-permute-start(bf16[8,32,128]{2,1,0:T(8,128)(2,1)S(1)} %get-tuple-element.112), channel_id=1, source_target_pairs={{0,3},{1,0},{2,1},{3,2},{4,7},{5,4},{6,5},{7,6},{8,11},{9,8},{10,9... | collective-permute-start | bytes 196616 | tf_op jit(solution)/shard_map/ppermute | solution.py:893
  115.7 5.9 %all-to-all-done.5 = bf16[16,64,128]{2,1,0:T(8,128)(2,1)S(1)} async-done(((bf16[16,64,128]{2,1,0:T(8,128)(2,1)}), bf16[16,64,128]{2,1,0:T(8,128)(2,1)S(1)}, u32[]{:S(2)}, u32[]{:S(2)}) %all-to-all-start.5) | async-done | bytes 262176 | tf_op jit(solution)/shard_map/all_to_all | solution.py:914
  121.7 0.7 fusion.2
  122.4 0.8 collective-permute-done.10.other_ref
  123.2 1.0 shard_map.197
  (22 shorter events, 0.1 us)
Async XLA Ops:
  1.6 7.6 %collective-permute-start = (bf16[4,128,128]{2,1,0:T(8,128)(2,1)S(1)}, bf16[4,128,128]{2,1,0:T(8,128)(2,1)S(1)}, u32[]{:S(2)}, u32[]{:S(2)}) collective-permute-start(bf16[4,128,128]{2,1,0:T(8,128)(2,1)S(1)} %slice_bitcast_fusion.last_ref.refs_4_), channel_id=1, source_target_pairs={{0,4},{4,8},{8,12},{12,16},{16,20},{20,24},{24,28},{1,5},{5,9},{9,... | collective-permute-start | bytes 393224 | tf_op jit(solution)/shard_map/ppermute | solution.py:874
  8.2 15.4 %copy-start.1 = (bf16[3,3,64,128]{3,2,1,0:T(8,128)(2,1)S(1)}, bf16[3,3,64,128]{3,2,1,0:T(8,128)(2,1)}, u32[]{:S(2)}) copy-start(bf16[3,3,64,128]{3,2,1,0:T(8,128)(2,1)} %refs_5_.2) | copy-start | bytes 442372
  8.2 22.1 %copy-start.4 = (f32[128]{0:T(128)S(1)}, f32[128]{0:T(128)}, u32[]{:S(2)}) copy-start(f32[128]{0:T(128)} %param.17) | copy-start | bytes 1540
  8.2 22.1 %copy-start.8 = (f32[128]{0:T(128)S(1)}, f32[128]{0:T(128)}, u32[]{:S(2)}) copy-start(f32[128]{0:T(128)} %param.18) | copy-start | bytes 1540
  9.2 14.4 %collective-permute-start.1 = (bf16[4,2,128,128]{3,2,1,0:T(8,128)(2,1)S(1)}, bf16[4,2,128,128]{3,2,1,0:T(8,128)(2,1)S(1)}, u32[]{:S(2)}, u32[]{:S(2)}) collective-permute-start(bf16[4,2,128,128]{3,2,1,0:T(8,128)(2,1)S(1)} %get-tuple-element.66), channel_id=1, source_target_pairs={{0,4},{4,0},{8,12},{12,8},{16,20},{20,16},{24,28},{28,24},{1,5},{5... | collective-permute-start | bytes 786440 | tf_op jit(solution)/shard_map/ppermute | solution.py:996
  11.7 12.0 %collective-permute-start.2 = (bf16[4,2,128,128]{3,2,1,0:T(8,128)(2,1)S(1)}, bf16[4,2,128,128]{3,2,1,0:T(8,128)(2,1)S(1)}, u32[]{:S(2)}, u32[]{:S(2)}) collective-permute-start(bf16[4,2,128,128]{3,2,1,0:T(8,128)(2,1)S(1)} %get-tuple-element.67), channel_id=1, source_target_pairs={{4,8},{12,16},{20,24},{8,4},{16,12},{24,20},{5,9},{13,17},{21,25},... | collective-permute-start | bytes 786440 | tf_op jit(solution)/shard_map/ppermute | solution.py:998
  16.0 14.3 %all-to-all-start = ((f32[8,8,128]{2,1,0:T(8,128)}), f32[8,8,128]{2,1,0:T(8,128)S(1)}, u32[]{:S(2)}, u32[]{:S(2)}) async-start(f32[8,8,128]{2,1,0:T(8,128)} %get-tuple-element.68), calls=%async_computation | async-start | bytes 65536 | tf_op jit(solution)/shard_map/all_to_all | solution.py:898
  24.2 11.9 %collective-permute-start.3 = (bf16[384,128]{1,0:T(8,128)(2,1)S(1)}, bf16[384,128]{1,0:T(8,128)(2,1)S(1)}, u32[]{:S(2)}, u32[]{:S(2)}) collective-permute-start(bf16[384,128]{1,0:T(8,128)(2,1)S(1)} %bitcast.40), channel_id=1, source_target_pairs={{2,0},{3,1},{0,2},{1,3},{6,4},{7,5},{4,6},{5,7},{10,8},{11,9},{8,1... | collective-permute-start | bytes 294920 | tf_op jit(solution)/shard_map/ppermute | solution.py:882
  30.3 16.3 %copy-start.2 = (f32[128]{0:T(128)S(1)}, f32[128]{0:T(128)}, u32[]{:S(2)}) copy-start(f32[128]{0:T(128)} %param.20) | copy-start | bytes 1540
  30.3 16.3 %copy-start.3 = (f32[128]{0:T(128)S(1)}, f32[128]{0:T(128)}, u32[]{:S(2)}) copy-start(f32[128]{0:T(128)} %param.21) | copy-start | bytes 1540
  30.3 16.3 %copy-start.5 = (bf16[128,64]{0,1:T(8,128)(2,1)S(1)}, bf16[128,64]{0,1:T(8,128)(2,1)}, u32[]{:S(2)}) copy-start(bf16[128,64]{0,1:T(8,128)(2,1)} %param.22) | copy-start | bytes 49156
  30.3 16.3 %copy-start.6 = (f32[16,4]{0,1:T(4,128)S(1)}, f32[16,4]{0,1:T(4,128)}, u32[]{:S(2)}) copy-start(f32[16,4]{0,1:T(4,128)} %param.23) | copy-start | bytes 772
  30.3 16.3 %copy-start.7 = (s32[16]{0:T(128)S(1)}, s32[16]{0:T(128)}, u32[]{:S(2)}) copy-start(s32[16]{0:T(128)} %refs_0_.1) | copy-start | bytes 196
  36.0 21.4 %copy-start = (bf16[4,8,128,128]{3,2,1,0:T(8,128)(2,1)S(1)}, bf16[4,8,128,128]{3,2,1,0:T(8,128)(2,1)}, u32[]{:S(2)}) copy-start(bf16[4,8,128,128]{3,2,1,0:T(8,128)(2,1)} %get-tuple-element.74.refs_1_.refs_5_.refs_2_) | copy-start | bytes 3145732
  36.0 3.9 %collective-permute-start.4 = (bf16[384,128]{1,0:T(8,128)(2,1)S(1)}, bf16[384,128]{1,0:T(8,128)(2,1)S(1)}, u32[]{:S(2)}, u32[]{:S(2)}) collective-permute-start(bf16[384,128]{1,0:T(8,128)(2,1)S(1)} %bitcast.41), channel_id=1, source_target_pairs={{0,1},{1,0},{2,3},{3,2},{4,5},{5,4},{6,7},{7,6},{8,9},{9,8},{10,11... | collective-permute-start | bytes 294920 | tf_op jit(solution)/shard_map/ppermute | solution.py:907
  36.1 3.9 %collective-permute-start.5 = (bf16[384,128]{1,0:T(8,128)(2,1)S(1)}, bf16[384,128]{1,0:T(8,128)(2,1)S(1)}, u32[]{:S(2)}, u32[]{:S(2)}) collective-permute-start(bf16[384,128]{1,0:T(8,128)(2,1)S(1)} %collective-permute-done.3), channel_id=1, source_target_pairs={{0,1},{1,0},{2,3},{3,2},{4,5},{5,4},{6,7},{7,6},{8,9},{9,8},{10,11... | collective-permute-start | bytes 294920 | tf_op jit(solution)/shard_map/ppermute | solution.py:907
  36.6 10.0 %all-to-all-start.1 = ((f32[8,8,128]{2,1,0:T(8,128)}), f32[8,8,128]{2,1,0:T(8,128)S(1)}, u32[]{:S(2)}, u32[]{:S(2)}) async-start(f32[8,8,128]{2,1,0:T(8,128)} %get-tuple-element.75), calls=%async_computation.1 | async-start | bytes 65536 | tf_op jit(solution)/shard_map/all_to_all | solution.py:898
  77.7 10.0 %all-to-all-start.3 = ((f32[8,8,128]{2,1,0:T(8,128)}), f32[8,8,128]{2,1,0:T(8,128)S(1)}, u32[]{:S(2)}, u32[]{:S(2)}) async-start(f32[8,8,128]{2,1,0:T(8,128)} %get-tuple-element.93), calls=%async_computation.3 | async-start | bytes 65536 | tf_op jit(solution)/shard_map/all_to_all | solution.py:898
  91.8 20.5 %copy-start.9 = (bf16[4,8,32,128]{3,2,1,0:T(8,128)(2,1)S(1)}, bf16[4,8,32,128]{3,2,1,0:T(8,128)(2,1)}, u32[]{:S(2)}) copy-start(bf16[4,8,32,128]{3,2,1,0:T(8,128)(2,1)} %get-tuple-element.102) | copy-start | bytes 786436
  91.8 1.6 %collective-permute-start.6 = (bf16[1024,128]{1,0:T(8,128)(2,1)S(1)}, bf16[1024,128]{1,0:T(8,128)(2,1)S(1)}, u32[]{:S(2)}, u32[]{:S(2)}) collective-permute-start(bf16[1024,128]{1,0:T(8,128)(2,1)S(1)} %get-tuple-element.101), channel_id=1, source_target_pairs={{0,1},{1,0},{2,3},{3,2},{4,5},{5,4},{6,7},{7,6},{8,9},{9,8},{10,11... | collective-permute-start | bytes 786440 | tf_op jit(solution)/shard_map/ppermute | solution.py:907
  108.7 13.0 %all-to-all-start.5 = ((bf16[16,64,128]{2,1,0:T(8,128)(2,1)}), bf16[16,64,128]{2,1,0:T(8,128)(2,1)S(1)}, u32[]{:S(2)}, u32[]{:S(2)}) async-start(bf16[16,64,128]{2,1,0:T(8,128)(2,1)} %shard_map.196), calls=%async_computation.5 | async-start | bytes 524288 | tf_op jit(solution)/shard_map/all_to_all | solution.py:914
  112.3 9.3 %collective-permute-start.7 = (bf16[8,32,128]{2,1,0:T(8,128)(2,1)S(1)}, bf16[8,32,128]{2,1,0:T(8,128)(2,1)S(1)}, u32[]{:S(2)}, u32[]{:S(2)}) collective-permute-start(bf16[8,32,128]{2,1,0:T(8,128)(2,1)S(1)} %get-tuple-element.111), channel_id=1, source_target_pairs={{0,1},{1,2},{2,3},{3,0},{4,5},{5,6},{6,7},{7,4},{8,9},{9,10},{10,1... | collective-permute-start | bytes 196616 | tf_op jit(solution)/shard_map/ppermute | solution.py:893
  112.4 9.3 %collective-permute-start.8 = (bf16[8,32,128]{2,1,0:T(8,128)(2,1)S(1)}, bf16[8,32,128]{2,1,0:T(8,128)(2,1)S(1)}, u32[]{:S(2)}, u32[]{:S(2)}) collective-permute-start(bf16[8,32,128]{2,1,0:T(8,128)(2,1)S(1)} %get-tuple-element.113), channel_id=1, source_target_pairs={{0,2},{1,3},{2,0},{3,1},{4,6},{5,7},{6,4},{7,5},{8,10},{9,11},{10,... | collective-permute-start | bytes 196616 | tf_op jit(solution)/shard_map/ppermute | solution.py:893
  114.3 7.4 %collective-permute-start.9 = (bf16[8,32,128]{2,1,0:T(8,128)(2,1)S(1)}, bf16[8,32,128]{2,1,0:T(8,128)(2,1)S(1)}, u32[]{:S(2)}, u32[]{:S(2)}) collective-permute-start(bf16[8,32,128]{2,1,0:T(8,128)(2,1)S(1)} %get-tuple-element.112), channel_id=1, source_target_pairs={{0,3},{1,0},{2,1},{3,2},{4,7},{5,4},{6,5},{7,6},{8,11},{9,8},{10,9... | collective-permute-start | bytes 196616 | tf_op jit(solution)/shard_map/ppermute | solution.py:893
  121.7 1.5 %collective-permute-start.10 = (bf16[1024,128]{1,0:T(8,128)(2,1)S(1)}, bf16[1024,128]{1,0:T(8,128)(2,1)S(1)}, u32[]{:S(2)}, u32[]{:S(2)}) collective-permute-start(bf16[1024,128]{1,0:T(8,128)(2,1)S(1)} %bitcast.38), channel_id=1, source_target_pairs={{0,1},{1,0},{2,3},{3,2},{4,5},{5,4},{6,7},{7,6},{8,9},{9,8},{10,11... | collective-permute-start | bytes 786440 | tf_op jit(solution)/shard_map/ppermute | solution.py:907

commit v9 on v8

--- a/solution.py
+++ b/solution.py
@@ -992,7 +992,6 @@
         *[pltpu.with_memory_space_constraint(x, pltpu.HBM) for x in (images, out_grad, valid)],
     )
     packed = packed.reshape(grad_rows + valid_count, width)
-    inner, outer, above, packed = lax.optimization_barrier((inner, outer, above, packed))
     inner = lax.ppermute(inner, "rows", [(i, i ^ 1) for i in range(row_devs)])
     pairs = [(i, i + 1) for i in range(1, row_devs - 1, 2)]
     outer = lax.ppermute(outer, "rows", pairs + [(j, i) for i, j in pairs])
@@ -1003,7 +1002,7 @@
         [
             ("date", images_near.reshape(paired.shape)),
             ("date", above),
-            ("all far", conv_weight),
+            ("all", conv_weight),
         ],
         [("date far", frame, BF16), ("all", (row_devs, 2 * dates, width), F32)],
         [pltpu.VMEM((3 * pair_width, 2 * width), BF16)],

time: 125 us -> 130 us (1.040)
  waiting for transfers between devices: 22.6 us -> 28.7 us
    ppermute x1, waiting for transfers between devices: 0.94 us -> 7.13 us  [shifted(): return lax.ppermute(array, 'rows', pairs)]
    all_to_all x3, starting transfers between devices: 14.3 us -> 12.5 us  [exchange(): return lax.all_to_all(pieces, axes, split_axis=0, concat_axis=0, tiled=True)]
    ppermute x1, starting transfers between devices: 4.88 us -> 6.18 us  [shifted(): return lax.ppermute(array, 'rows', pairs)]
  transfers between devices with their start and end apart: 15 -> 15, of which waited for: 7 -> 7; matrix products, arithmetic and copies ran while one was open for 1% -> 1% of each run, Pallas kernels for 13% -> 10%
where the time goes in v9:
time: 130 us
  Pallas kernels  36.4 us (28%)
  starting transfers between devices  31.5 us (24%)
  blocking collectives  30.2 us (23%)
  waiting for transfers between devices  28.7 us (22%)
    pallas_call x8, Pallas kernels, call(): pl.pallas_call(body, in_specs=in_specs, out_specs=out_specs, out_shape=ou...  32.8 us
    all_to_all x1, blocking collectives, exchange_cores(): lax.all_to_all(pieces, axes, split_axis=0, concat_axis=0, axis_index_grou...  14.5 us
    all_to_all x3, waiting for transfers between devices, exchange(): return lax.all_to_all(pieces, axes, split_axis=0, concat_axis=0, tiled=True)  13.3 us
    all_to_all x3, starting transfers between devices, exchange(): return lax.all_to_all(pieces, axes, split_axis=0, concat_axis=0, tiled=True)  12.5 us
    all_to_all x1, blocking collectives, exchange(): return lax.all_to_all(pieces, axes, split_axis=0, concat_axis=0, tiled=True)  9.24 us
    ppermute x1, waiting for transfers between devices, shifted(): return lax.ppermute(array, 'rows', pairs)  7.13 us
    all_gather x1, blocking collectives, gather(): return lax.all_gather(array, axis, axis=0, tiled=True)  6.45 us
    ppermute x1, starting transfers between devices, shifted(): return lax.ppermute(array, 'rows', pairs)  6.18 us
  transfers between devices with their start and end apart: 15, of which 7 were waited for; matrix products, arithmetic and copies ran while one was open for 1% of the time, Pallas kernels for 10%

profile of v9, /device:TPU:0, one launch (start us, length us, event | category | flops | bytes accessed | tf_op | source)
XLA Modules:
  0.0 129.6 jit_solution(9032214843019048554)
XLA Ops:
  0.7 1.0 slice_bitcast_fusion.last_ref.refs_4_
  1.6 1.7 %shard_map.187 = (bf16[4,16,128,128]{3,2,1,0:T(8,128)(2,1)S(1)}, bf16[4,2,128,128]{3,2,1,0:T(8,128)(2,1)S(1)}, bf16[4,2,128,128]{3,2,1,0:T(8,128)(2,1)S(1)}, bf16[12,32,128]{2,1,0:T(8,128)(2,1)S(1)}) custom-call(s32[1]{0:T(128)} %bitcast.place_ref.refs_0_.refs_4_, bf16[4,128,128]{2,1,0:T(8,128)(2,1)S(1)} %slice_bitcast_fusion.last_ref.refs_4_, ...), custom_call_target="tpu_custom_call" | custom-call | tf_op jit(solution)/shard_map/pallas_call | solution.py:979
  3.4 0.0 copy-start.4
  3.4 0.0 copy-start.8
  3.4 3.0 %collective-permute-start.1 = (bf16[4,2,128,128]{3,2,1,0:T(8,128)(2,1)S(1)}, bf16[4,2,128,128]{3,2,1,0:T(8,128)(2,1)S(1)}, u32[]{:S(2)}, u32[]{:S(2)}) collective-permute-start(bf16[4,2,128,128]{3,2,1,0:T(8,128)(2,1)S(1)} %get-tuple-element.58), channel_id=1, source_target_pairs={{0,4},{4,0},{8,12},{12,8},{16,20},{20,16},{24,28},{28,24},{1,5},{5... | collective-permute-start | bytes 786440 | tf_op jit(solution)/shard_map/ppermute | solution.py:995
  6.4 0.7 collective-permute-start.2
  7.1 6.2 %collective-permute-start = (bf16[4,128,128]{2,1,0:T(8,128)(2,1)S(1)}, bf16[4,128,128]{2,1,0:T(8,128)(2,1)S(1)}, u32[]{:S(2)}, u32[]{:S(2)}) collective-permute-start(bf16[4,128,128]{2,1,0:T(8,128)(2,1)S(1)} %slice_bitcast_fusion.last_ref.refs_4_), channel_id=1, source_target_pairs={{0,4},{4,8},{8,12},{12,16},{16,20},{20,24},{24,28},{1,5},{5,9},{9,... | collective-permute-start | bytes 393224 | tf_op jit(solution)/shard_map/ppermute | solution.py:874
  13.3 7.1 %collective-permute-done.refs_1_.refs_3_ = bf16[4,128,128]{2,1,0:T(8,128)(2,1)S(1)} collective-permute-done((bf16[4,128,128]{2,1,0:T(8,128)(2,1)S(1)}, bf16[4,128,128]{2,1,0:T(8,128)(2,1)S(1)}, u32[]{:S(2)}, u32[]{:S(2)}) %collective-permute-start) | collective-permute-done | bytes 131104 | tf_op jit(solution)/shard_map/ppermute | solution.py:874
  20.4 2.7 %shard_map.188 = (bf16[4,8,128,128]{3,2,1,0:T(8,128)(2,1)}, f32[8,8,128]{2,1,0:T(8,128)}) custom-call(bf16[4,8,2,128,128]{4,3,2,1,0:T(8,128)(2,1)S(1)} %bitcast.51, bf16[4,128,128]{2,1,0:T(8,128)(2,1)S(1)} %collective-permute-done.refs_1_.refs_3_, bf16[3,3,64,128]{3,2,1,0:T(8,128)(2,1)S(1)} %copy-done.1), custom_call_target="tpu_custom_call" | custom-call | flops 805306368 | bytes 4751360 | tf_op jit(solution)/shard_map/pallas_call | solution.py:860
  23.2 5.8 %all-to-all-start = ((f32[8,8,128]{2,1,0:T(8,128)}), f32[8,8,128]{2,1,0:T(8,128)S(1)}, u32[]{:S(2)}, u32[]{:S(2)}) async-start(f32[8,8,128]{2,1,0:T(8,128)} %get-tuple-element.60), calls=%async_computation | async-start | bytes 65536 | tf_op jit(solution)/shard_map/all_to_all | solution.py:898
  29.0 0.0 collective-permute-done.2.refs_2_.refs_3_
  29.0 0.5 shard_map.189
  29.5 1.6 %collective-permute-start.3 = (bf16[384,128]{1,0:T(8,128)(2,1)S(1)}, bf16[384,128]{1,0:T(8,128)(2,1)S(1)}, u32[]{:S(2)}, u32[]{:S(2)}) collective-permute-start(bf16[384,128]{1,0:T(8,128)(2,1)S(1)} %bitcast.40), channel_id=1, source_target_pairs={{2,0},{3,1},{0,2},{1,3},{6,4},{7,5},{4,6},{5,7},{10,8},{11,9},{8,1... | collective-permute-start | bytes 294920 | tf_op jit(solution)/shard_map/ppermute | solution.py:882
  31.0 4.6 %all-to-all-done.refs_4_ = f32[8,8,128]{2,1,0:T(8,128)S(1)} async-done(((f32[8,8,128]{2,1,0:T(8,128)}), f32[8,8,128]{2,1,0:T(8,128)S(1)}, u32[]{:S(2)}, u32[]{:S(2)}) %all-to-all-start) | async-done | bytes 32800 | tf_op jit(solution)/shard_map/all_to_all | solution.py:898
  35.7 0.0 copy-start.5
  35.7 0.0 copy-start.6
  35.7 0.0 copy-start.7
  35.7 5.7 %shard_map.190 = (bf16[4,8,128,128]{3,2,1,0:T(8,128)(2,1)}, f32[8,128]{1,0:T(8,128)S(1)}, f32[8,8,128]{2,1,0:T(8,128)}) custom-call(s32[1]{0:T(128)} %bitcast.place_ref.refs_0_.refs_4_, bf16[4,8,128,128]{3,2,1,0:T(8,128)(2,1)} %get-tuple-element.57.refs_1_.refs_6_.refs_5_, bf16[4,128,128]{2,1,0:T(8,128)(2,1)S(1)} %get-tuple-element.64.refs_2_.refs_7_, ...), custom_call_target="tpu_custom_call" | custom-call | flops 1207959552 | bytes 3278856 | tf_op jit(solution)/shard_map/pallas_call | solution.py:860
  41.4 0.0 collective-permute-done.3
  41.4 0.1 collective-permute-start.4
  41.5 0.5 collective-permute-start.5
  42.0 3.3 %all-to-all-start.1 = ((f32[8,8,128]{2,1,0:T(8,128)}), f32[8,8,128]{2,1,0:T(8,128)S(1)}, u32[]{:S(2)}, u32[]{:S(2)}) async-start(f32[8,8,128]{2,1,0:T(8,128)} %get-tuple-element.67), calls=%async_computation.1 | async-start | bytes 65536 | tf_op jit(solution)/shard_map/all_to_all | solution.py:898
  45.3 0.0 collective-permute-done.4
  45.3 0.1 pad_maximum_fusion.refs_5_.refs_10_
  45.4 6.5 %all-to-all-done.1.refs_2_ = f32[8,8,128]{2,1,0:T(8,128)S(1)} async-done(((f32[8,8,128]{2,1,0:T(8,128)}), f32[8,8,128]{2,1,0:T(8,128)S(1)}, u32[]{:S(2)}, u32[]{:S(2)}) %all-to-all-start.1) | async-done | bytes 32800 | tf_op jit(solution)/shard_map/all_to_all | solution.py:898
  52.0 4.4 %shard_map.191 = (bf16[4,8,128,128]{3,2,1,0:T(8,128)(2,1)S(1)}, f32[4,8,128,128]{3,2,1,0:T(8,128)S(1)}, f32[4,8,128,128]{3,2,1,0:T(8,128)S(1)}, f32[8,128]{1,0:T...) custom-call(s32[16]{0:T(128)S(1)} %copy-done.7, ...), custom_call_target="tpu_custom_call" | custom-call | flops 671088640 | bytes 3115656 | tf_op jit(solution)/shard_map/pallas_call | solution.py:860
  56.4 6.4 %all_gather.3.refs_0_ = bf16[4,3,128,128]{3,2,1,0:T(8,128)(2,1)S(1)} all-gather(bf16[1,3,128,128]{3,2,1,0:T(8,128)(2,1)S(1)} %get-tuple-element.72), channel_id=1, replica_groups=mesh['rows'=8,'dates'=4] {'dates'}, dimensions={0}, use_global_device_ids=true | all-gather | bytes 491520 | tf_op jit(solution)/shard_map/all_gather | solution.py:902
  62.8 4.0 %shard_map.192 = (bf16[4,8,128,128]{3,2,1,0:T(8,128)(2,1)}, bf16[4,8,32,128]{3,2,1,0:T(8,128)(2,1)}, f32[128,128]{1,0:T(8,128)}, f32[8,128]{1,0:T(8,128)S(1)}, f32[8,8,128]{2,1,0:T(8,128)S(1)}) custom-call(bf16[4,3,128,128]{3,2,1,0:T(8,128)(2,1)S(1)} %all_gather.3.refs_0_, f32[128,128]{1,0:T(8,128)S(1)} %get-tuple-element.73.refs_1_, ...), custom_call_target="tpu_custom_call" | custom-call | flops 671088640 | bytes 14370824 | tf_op jit(solution)/shard_map/pallas_call | solution.py:860
  66.8 9.2 %all_to_all.30.refs_3_ = f32[8,8,128]{2,1,0:T(8,128)S(1)} all-to-all(f32[8,8,128]{2,1,0:T(8,128)S(1)} %get-tuple-element.82), channel_id=1, replica_groups=mesh['rows'=8,'dates'=4] {'rows'}, dimensions={0} | all-to-all | bytes 65536 | tf_op jit(solution)/shard_map/all_to_all | solution.py:898
  76.0 7.0 %shard_map.193 = (bf16[4,8,128,128]{3,2,1,0:T(8,128)(2,1)}, bf16[4,10,128,128]{3,2,1,0:T(8,128)(2,1)}, f32[8,128]{1,0:T(8,128)S(1)}, f32[8,8,128]{2,1,0:T(8,128)}) custom-call(s32[1]{0:T(128)} %bitcast.place_ref.refs_0_.refs_4_, bf16[4,8,128,128]{3,2,1,0:T(8,128)(2,1)} %get-tuple-element.81.refs_1_, ...), custom_call_target="tpu_custom_call" | custom-call | flops 1207959552 | bytes 7489544 | tf_op jit(solution)/shard_map/pallas_call | solution.py:860
  83.0 3.4 %all-to-all-start.3 = ((f32[8,8,128]{2,1,0:T(8,128)}), f32[8,8,128]{2,1,0:T(8,128)S(1)}, u32[]{:S(2)}, u32[]{:S(2)}) async-start(f32[8,8,128]{2,1,0:T(8,128)} %get-tuple-element.85), calls=%async_computation.3 | async-start | bytes 65536 | tf_op jit(solution)/shard_map/all_to_all | solution.py:898
  86.4 4.4 %shard_map.194.refs_12_ = bf16[1280,128]{1,0:T(8,128)(2,1)} custom-call(s32[1]{0:T(128)} %bitcast.place_ref.refs_0_.refs_4_, bf16[4,8,128,128]{3,2,1,0:T(8,128)(2,1)} %get-tuple-element.57.refs_1_.refs_6_.refs_5_, bf16[4,128,128]{2,1,0:T(8,128)(2,1)S(1)} %get-tuple-element.64.refs_2_.refs_7_, bf16[4,128,128]{2,1,0:T(8,128)(2,1)S(1)} %get-tuple-element.65.refs_3_.refs_8_, ...), custom_call_target="tpu_custom_call" | custom-call | flops 1207959552 | bytes 4859912 | tf_op jit(solution)/shard_map/pallas_call | solution.py:860
  90.8 2.2 %all-to-all-done.3.refs_7_ = f32[8,8,128]{2,1,0:T(8,128)S(1)} async-done(((f32[8,8,128]{2,1,0:T(8,128)}), f32[8,8,128]{2,1,0:T(8,128)S(1)}, u32[]{:S(2)}, u32[]{:S(2)}) %all-to-all-start.3) | async-done | bytes 32800 | tf_op jit(solution)/shard_map/all_to_all | solution.py:898
  93.0 4.1 %shard_map.195 = (bf16[1024,128]{1,0:T(8,128)(2,1)S(1)}, bf16[1024,128]{1,0:T(8,128)(2,1)S(1)}) custom-call(bf16[4,8,2,128,128]{4,3,2,1,0:T(8,128)(2,1)} %bitcast.57, bf16[4,128,128]{2,1,0:T(8,128)(2,1)S(1)} %collective-permute-done.refs_1_.refs_3_, bf16[4,2,128,128]{3,2,1,0:T(8,128)(2,1)S(1)} %collective-permute-done.1.refs_1_.refs_2_, ...), custom_call_target="tpu_custom_call" | custom-call | flops 805306368 | bytes 10970128 | tf_op jit(solution)/shard_map/pallas_call | solution.py:860
  97.2 0.0 copy-start.9
  97.2 0.1 collective-permute-start.6
  97.2 1.5 %collective-permute-done.6 = bf16[1024,128]{1,0:T(8,128)(2,1)S(1)} collective-permute-done((bf16[1024,128]{1,0:T(8,128)(2,1)S(1)}, bf16[1024,128]{1,0:T(8,128)(2,1)S(1)}, u32[]{:S(2)}, u32[]{:S(2)}) %collective-permute-start.6) | collective-permute-done | bytes 262176 | tf_op jit(solution)/shard_map/ppermute | solution.py:907
  98.8 0.1 add_convert_fusion
  98.8 14.5 %all_to_all.31.in_ref = bf16[16,64,128]{2,1,0:T(8,128)(2,1)S(1)} all-to-all(bf16[16,64,128]{2,1,0:T(8,128)(2,1)S(1)} %bitcast.58), channel_id=1, replica_groups={{0,2,4,6,8,10,12,14,16,18,20,22,24,26,28,30},{1,3,5,7,9,11,13,15,17,19,..., dimensions={0} | all-to-all | bytes 524288 | tf_op jit(solution)/shard_map/all_to_all | solution.py:914
  113.3 0.8 shard_map.196
  114.1 3.5 %all-to-all-start.5 = ((bf16[16,64,128]{2,1,0:T(8,128)(2,1)}), bf16[16,64,128]{2,1,0:T(8,128)(2,1)S(1)}, u32[]{:S(2)}, u32[]{:S(2)}) async-start(bf16[16,64,128]{2,1,0:T(8,128)(2,1)} %shard_map.196), calls=%async_computation.5 | async-start | bytes 524288 | tf_op jit(solution)/shard_map/all_to_all | solution.py:914
  117.7 0.1 collective-permute-start.7
  117.8 1.9 %collective-permute-start.8 = (bf16[8,32,128]{2,1,0:T(8,128)(2,1)S(1)}, bf16[8,32,128]{2,1,0:T(8,128)(2,1)S(1)}, u32[]{:S(2)}, u32[]{:S(2)}) collective-permute-start(bf16[8,32,128]{2,1,0:T(8,128)(2,1)S(1)} %get-tuple-element.105), channel_id=1, source_target_pairs={{0,2},{1,3},{2,0},{3,1},{4,6},{5,7},{6,4},{7,5},{8,10},{9,11},{10,... | collective-permute-start | bytes 196616 | tf_op jit(solution)/shard_map/ppermute | solution.py:893
  119.7 1.4 %collective-permute-start.9 = (bf16[8,32,128]{2,1,0:T(8,128)(2,1)S(1)}, bf16[8,32,128]{2,1,0:T(8,128)(2,1)S(1)}, u32[]{:S(2)}, u32[]{:S(2)}) collective-permute-start(bf16[8,32,128]{2,1,0:T(8,128)(2,1)S(1)} %get-tuple-element.104), channel_id=1, source_target_pairs={{0,3},{1,0},{2,1},{3,2},{4,7},{5,4},{6,5},{7,6},{8,11},{9,8},{10,9... | collective-permute-start | bytes 196616 | tf_op jit(solution)/shard_map/ppermute | solution.py:893
  121.1 5.9 %all-to-all-done.5 = bf16[16,64,128]{2,1,0:T(8,128)(2,1)S(1)} async-done(((bf16[16,64,128]{2,1,0:T(8,128)(2,1)}), bf16[16,64,128]{2,1,0:T(8,128)(2,1)S(1)}, u32[]{:S(2)}, u32[]{:S(2)}) %all-to-all-start.5) | async-done | bytes 262176 | tf_op jit(solution)/shard_map/all_to_all | solution.py:914
  127.1 0.7 fusion.2
  127.7 0.8 collective-permute-done.10.other_ref
  128.6 1.0 shard_map.197
  (22 shorter events, 0.1 us)
Async XLA Ops:
  0.6 19.8 %copy-start.1 = (bf16[3,3,64,128]{3,2,1,0:T(8,128)(2,1)S(1)}, bf16[3,3,64,128]{3,2,1,0:T(8,128)(2,1)}, u32[]{:S(2)}) copy-start(bf16[3,3,64,128]{3,2,1,0:T(8,128)(2,1)} %refs_5_.2) | copy-start | bytes 442372
  3.4 32.3 %copy-start.4 = (f32[128]{0:T(128)S(1)}, f32[128]{0:T(128)}, u32[]{:S(2)}) copy-start(f32[128]{0:T(128)} %param.17) | copy-start | bytes 1540
  3.4 32.3 %copy-start.8 = (f32[128]{0:T(128)S(1)}, f32[128]{0:T(128)}, u32[]{:S(2)}) copy-start(f32[128]{0:T(128)} %param.18) | copy-start | bytes 1540
  3.4 25.6 %collective-permute-start.1 = (bf16[4,2,128,128]{3,2,1,0:T(8,128)(2,1)S(1)}, bf16[4,2,128,128]{3,2,1,0:T(8,128)(2,1)S(1)}, u32[]{:S(2)}, u32[]{:S(2)}) collective-permute-start(bf16[4,2,128,128]{3,2,1,0:T(8,128)(2,1)S(1)} %get-tuple-element.58), channel_id=1, source_target_pairs={{0,4},{4,0},{8,12},{12,8},{16,20},{20,16},{24,28},{28,24},{1,5},{5... | collective-permute-start | bytes 786440 | tf_op jit(solution)/shard_map/ppermute | solution.py:995
  6.4 22.5 %collective-permute-start.2 = (bf16[4,2,128,128]{3,2,1,0:T(8,128)(2,1)S(1)}, bf16[4,2,128,128]{3,2,1,0:T(8,128)(2,1)S(1)}, u32[]{:S(2)}, u32[]{:S(2)}) collective-permute-start(bf16[4,2,128,128]{3,2,1,0:T(8,128)(2,1)S(1)} %get-tuple-element.59), channel_id=1, source_target_pairs={{4,8},{12,16},{20,24},{8,4},{16,12},{24,20},{5,9},{13,17},{21,25},... | collective-permute-start | bytes 786440 | tf_op jit(solution)/shard_map/ppermute | solution.py:997
  7.1 13.3 %collective-permute-start = (bf16[4,128,128]{2,1,0:T(8,128)(2,1)S(1)}, bf16[4,128,128]{2,1,0:T(8,128)(2,1)S(1)}, u32[]{:S(2)}, u32[]{:S(2)}) collective-permute-start(bf16[4,128,128]{2,1,0:T(8,128)(2,1)S(1)} %slice_bitcast_fusion.last_ref.refs_4_), channel_id=1, source_target_pairs={{0,4},{4,8},{8,12},{12,16},{16,20},{20,24},{24,28},{1,5},{5,9},{9,... | collective-permute-start | bytes 393224 | tf_op jit(solution)/shard_map/ppermute | solution.py:874
  23.2 12.5 %all-to-all-start = ((f32[8,8,128]{2,1,0:T(8,128)}), f32[8,8,128]{2,1,0:T(8,128)S(1)}, u32[]{:S(2)}, u32[]{:S(2)}) async-start(f32[8,8,128]{2,1,0:T(8,128)} %get-tuple-element.60), calls=%async_computation | async-start | bytes 65536 | tf_op jit(solution)/shard_map/all_to_all | solution.py:898
  29.5 11.9 %collective-permute-start.3 = (bf16[384,128]{1,0:T(8,128)(2,1)S(1)}, bf16[384,128]{1,0:T(8,128)(2,1)S(1)}, u32[]{:S(2)}, u32[]{:S(2)}) collective-permute-start(bf16[384,128]{1,0:T(8,128)(2,1)S(1)} %bitcast.40), channel_id=1, source_target_pairs={{2,0},{3,1},{0,2},{1,3},{6,4},{7,5},{4,6},{5,7},{10,8},{11,9},{8,1... | collective-permute-start | bytes 294920 | tf_op jit(solution)/shard_map/ppermute | solution.py:882
  35.6 16.3 %copy-start.2 = (f32[128]{0:T(128)S(1)}, f32[128]{0:T(128)}, u32[]{:S(2)}) copy-start(f32[128]{0:T(128)} %param.20) | copy-start | bytes 1540
  35.6 16.3 %copy-start.3 = (f32[128]{0:T(128)S(1)}, f32[128]{0:T(128)}, u32[]{:S(2)}) copy-start(f32[128]{0:T(128)} %param.21) | copy-start | bytes 1540
  35.7 16.3 %copy-start.5 = (bf16[128,64]{0,1:T(8,128)(2,1)S(1)}, bf16[128,64]{0,1:T(8,128)(2,1)}, u32[]{:S(2)}) copy-start(bf16[128,64]{0,1:T(8,128)(2,1)} %param.22) | copy-start | bytes 49156
  35.7 16.3 %copy-start.6 = (f32[16,4]{0,1:T(4,128)S(1)}, f32[16,4]{0,1:T(4,128)}, u32[]{:S(2)}) copy-start(f32[16,4]{0,1:T(4,128)} %param.23) | copy-start | bytes 772
  35.7 16.3 %copy-start.7 = (s32[16]{0:T(128)S(1)}, s32[16]{0:T(128)}, u32[]{:S(2)}) copy-start(s32[16]{0:T(128)} %refs_0_.1) | copy-start | bytes 196
  41.4 21.4 %copy-start = (bf16[4,8,128,128]{3,2,1,0:T(8,128)(2,1)S(1)}, bf16[4,8,128,128]{3,2,1,0:T(8,128)(2,1)}, u32[]{:S(2)}) copy-start(bf16[4,8,128,128]{3,2,1,0:T(8,128)(2,1)} %get-tuple-element.66.refs_1_.refs_5_.refs_2_) | copy-start | bytes 3145732
  41.4 3.9 %collective-permute-start.4 = (bf16[384,128]{1,0:T(8,128)(2,1)S(1)}, bf16[384,128]{1,0:T(8,128)(2,1)S(1)}, u32[]{:S(2)}, u32[]{:S(2)}) collective-permute-start(bf16[384,128]{1,0:T(8,128)(2,1)S(1)} %bitcast.41), channel_id=1, source_target_pairs={{0,1},{1,0},{2,3},{3,2},{4,5},{5,4},{6,7},{7,6},{8,9},{9,8},{10,11... | collective-permute-start | bytes 294920 | tf_op jit(solution)/shard_map/ppermute | solution.py:907
  41.5 3.9 %collective-permute-start.5 = (bf16[384,128]{1,0:T(8,128)(2,1)S(1)}, bf16[384,128]{1,0:T(8,128)(2,1)S(1)}, u32[]{:S(2)}, u32[]{:S(2)}) collective-permute-start(bf16[384,128]{1,0:T(8,128)(2,1)S(1)} %collective-permute-done.3), channel_id=1, source_target_pairs={{0,1},{1,0},{2,3},{3,2},{4,5},{5,4},{6,7},{7,6},{8,9},{9,8},{10,11... | collective-permute-start | bytes 294920 | tf_op jit(solution)/shard_map/ppermute | solution.py:907
  42.0 10.0 %all-to-all-start.1 = ((f32[8,8,128]{2,1,0:T(8,128)}), f32[8,8,128]{2,1,0:T(8,128)S(1)}, u32[]{:S(2)}, u32[]{:S(2)}) async-start(f32[8,8,128]{2,1,0:T(8,128)} %get-tuple-element.67), calls=%async_computation.1 | async-start | bytes 65536 | tf_op jit(solution)/shard_map/all_to_all | solution.py:898
  83.0 10.0 %all-to-all-start.3 = ((f32[8,8,128]{2,1,0:T(8,128)}), f32[8,8,128]{2,1,0:T(8,128)S(1)}, u32[]{:S(2)}, u32[]{:S(2)}) async-start(f32[8,8,128]{2,1,0:T(8,128)} %get-tuple-element.85), calls=%async_computation.3 | async-start | bytes 65536 | tf_op jit(solution)/shard_map/all_to_all | solution.py:898
  97.2 20.5 %copy-start.9 = (bf16[4,8,32,128]{3,2,1,0:T(8,128)(2,1)S(1)}, bf16[4,8,32,128]{3,2,1,0:T(8,128)(2,1)}, u32[]{:S(2)}) copy-start(bf16[4,8,32,128]{3,2,1,0:T(8,128)(2,1)} %get-tuple-element.94) | copy-start | bytes 786436
  97.2 1.6 %collective-permute-start.6 = (bf16[1024,128]{1,0:T(8,128)(2,1)S(1)}, bf16[1024,128]{1,0:T(8,128)(2,1)S(1)}, u32[]{:S(2)}, u32[]{:S(2)}) collective-permute-start(bf16[1024,128]{1,0:T(8,128)(2,1)S(1)} %get-tuple-element.93), channel_id=1, source_target_pairs={{0,1},{1,0},{2,3},{3,2},{4,5},{5,4},{6,7},{7,6},{8,9},{9,8},{10,11... | collective-permute-start | bytes 786440 | tf_op jit(solution)/shard_map/ppermute | solution.py:907
  114.1 13.0 %all-to-all-start.5 = ((bf16[16,64,128]{2,1,0:T(8,128)(2,1)}), bf16[16,64,128]{2,1,0:T(8,128)(2,1)S(1)}, u32[]{:S(2)}, u32[]{:S(2)}) async-start(bf16[16,64,128]{2,1,0:T(8,128)(2,1)} %shard_map.196), calls=%async_computation.5 | async-start | bytes 524288 | tf_op jit(solution)/shard_map/all_to_all | solution.py:914
  117.7 9.3 %collective-permute-start.7 = (bf16[8,32,128]{2,1,0:T(8,128)(2,1)S(1)}, bf16[8,32,128]{2,1,0:T(8,128)(2,1)S(1)}, u32[]{:S(2)}, u32[]{:S(2)}) collective-permute-start(bf16[8,32,128]{2,1,0:T(8,128)(2,1)S(1)} %get-tuple-element.103), channel_id=1, source_target_pairs={{0,1},{1,2},{2,3},{3,0},{4,5},{5,6},{6,7},{7,4},{8,9},{9,10},{10,1... | collective-permute-start | bytes 196616 | tf_op jit(solution)/shard_map/ppermute | solution.py:893
  117.8 9.3 %collective-permute-start.8 = (bf16[8,32,128]{2,1,0:T(8,128)(2,1)S(1)}, bf16[8,32,128]{2,1,0:T(8,128)(2,1)S(1)}, u32[]{:S(2)}, u32[]{:S(2)}) collective-permute-start(bf16[8,32,128]{2,1,0:T(8,128)(2,1)S(1)} %get-tuple-element.105), channel_id=1, source_target_pairs={{0,2},{1,3},{2,0},{3,1},{4,6},{5,7},{6,4},{7,5},{8,10},{9,11},{10,... | collective-permute-start | bytes 196616 | tf_op jit(solution)/shard_map/ppermute | solution.py:893
  119.7 7.4 %collective-permute-start.9 = (bf16[8,32,128]{2,1,0:T(8,128)(2,1)S(1)}, bf16[8,32,128]{2,1,0:T(8,128)(2,1)S(1)}, u32[]{:S(2)}, u32[]{:S(2)}) collective-permute-start(bf16[8,32,128]{2,1,0:T(8,128)(2,1)S(1)} %get-tuple-element.104), channel_id=1, source_target_pairs={{0,3},{1,0},{2,1},{3,2},{4,7},{5,4},{6,5},{7,6},{8,11},{9,8},{10,9... | collective-permute-start | bytes 196616 | tf_op jit(solution)/shard_map/ppermute | solution.py:893
  127.0 1.5 %collective-permute-start.10 = (bf16[1024,128]{1,0:T(8,128)(2,1)S(1)}, bf16[1024,128]{1,0:T(8,128)(2,1)S(1)}, u32[]{:S(2)}, u32[]{:S(2)}) collective-permute-start(bf16[1024,128]{1,0:T(8,128)(2,1)S(1)} %bitcast.38), channel_id=1, source_target_pairs={{0,1},{1,0},{2,3},{3,2},{4,5},{5,4},{6,7},{7,6},{8,9},{9,8},{10,11... | collective-permute-start | bytes 786440 | tf_op jit(solution)/shard_map/ppermute | solution.py:907

commit v10 on v9

--- a/solution.py
+++ b/solution.py
@@ -45,14 +45,52 @@
 
 
 def from_left(values):
-    column = lax.broadcasted_iota(jnp.int32, values.shape, 1)
-    return jnp.where(column > 0, pltpu.roll(values, 1, 1), 0.0)
+    moved = pltpu.roll(values, 1, 1)
+    first = moved[:, :8]
+    column = lax.broadcasted_iota(jnp.int32, first.shape, 1)
+    return jnp.concatenate([jnp.where(column > 0, first, 0.0), moved[:, 8:]], axis=1)
 
 
 def from_right(values):
     count = values.shape[1]
-    column = lax.broadcasted_iota(jnp.int32, values.shape, 1)
-    return jnp.where(column < count - 1, pltpu.roll(values, count - 1, 1), 0.0)
+    moved = pltpu.roll(values, count - 1, 1)
+    last = moved[:, count - 8 :]
+    column = lax.broadcasted_iota(jnp.int32, last.shape, 1)
+    return jnp.concatenate([moved[:, : count - 8], jnp.where(column < 7, last, 0.0)], axis=1)
+
+
+def pair_table(weight_ref, table, backward):
+    width = weight_ref.shape[-1]
+    for row in range(4):
+        for parity in range(2):
+            for col_tap in range(3):
+                deep = slice(row * width, (row + 1) * width)
+                start = (col_tap * 2 + parity) * width
+                wide = slice(start, start + width)
+                tap = row - parity
+                inside = 0 <= tap <= 2
+                if backward:
+                    block = weight_ref[2 - tap, col_tap] if inside else None
+                    where = (wide, deep)
+                else:
+                    block = weight_ref[tap, col_tap] if inside else None
+                    where = (deep, wide)
+                table[where] = block if inside else jnp.zeros((width, width), BF16)
+
+
+def pair_rows(padded, table, backward):
+    rows, cols, width = padded.shape
+    pairs = padded.reshape(rows // 2, 2, cols, width)
+    count = rows // 2 - 1
+    taps = [pairs[:count, 0], pairs[:count, 1], pairs[1:, 0], pairs[1:, 1]]
+    taps = jnp.concatenate(taps, axis=-1).reshape(count * cols, 4 * width)
+    terms = product(taps, table[...], 1, 1 if backward else 0).reshape(count, cols, 6 * width)
+    parts = [terms[..., place * width : (place + 1) * width] for place in range(6)]
+    first, last = (from_right, from_left) if backward else (from_left, from_right)
+    results = [
+        parts[2 + parity] + first(parts[parity]) + last(parts[4 + parity]) for parity in range(2)
+    ]
+    return jnp.stack(results, axis=1).reshape(2 * count, cols, width)
 
 
 def column_sum(values):
@@ -241,17 +279,11 @@
     norm_count,
     row_devs,
 ):
-    width = conv_ref.shape[-1]
 
     if date == 0:
         norm_table(stats_ref, norm_ref, dates, norm_count)
-        for row_tap in range(3):
-            for col_tap in range(3):
-                table[
-                    row_tap * width : (row_tap + 1) * width, col_tap * width : (col_tap + 1) * width
-                ] = weight_ref[row_tap, col_tap]
-
-    rows, cols = conv_ref.shape[1:3]
+        pair_table(weight_ref, table, False)
+
     activate_rows(
         date,
         dates,
@@ -260,15 +292,7 @@
         (norm_ref, gain_ref, shift_ref),
         hidden_ref,
     )
-    taps = jnp.concatenate(
-        [hidden_ref[0, tap : tap + rows] for tap in range(3)], axis=-1
-    ).reshape(rows * cols, 3 * width)
-    terms = product(taps, table[...], 1, 0).reshape(rows, cols, 3 * width)
-    stored = (
-        terms[..., width : 2 * width]
-        + from_left(terms[..., :width])
-        + from_right(terms[..., 2 * width :])
-    ).astype(BF16)
+    stored = pair_rows(hidden_ref[0], table, False).astype(BF16)
     out_ref[0] = stored
     values = stored.astype(F32)
     store_sums(sums_ref, date, dates, column_sum(values), column_sum(values * values))
@@ -535,11 +559,7 @@
         vector_ref[...] = jnp.zeros_like(vector_ref)
         padded[:2] = jnp.zeros_like(padded[:2])
         padded[rows + 2 :] = jnp.zeros_like(padded[rows + 2 :])
-        for row_tap in range(3):
-            for col_tap in range(3):
-                table[
-                    col_tap * width : (col_tap + 1) * width, row_tap * width : (row_tap + 1) * width
-                ] = weight_ref[2 - row_tap, col_tap]
+        pair_table(weight_ref, table, True)
 
     inverse = norm_ref[pl.ds(dates + date, 1), :]
     slope = factors[pl.ds(date, 1), :]
@@ -551,16 +571,7 @@
     ).astype(BF16)
     pre_ref[0] = stored
     padded[2 : rows + 2] = stored
-    reach = rows + 2
-    taps = jnp.concatenate([padded[tap : tap + reach] for tap in range(3)], axis=-1).reshape(
-        reach * cols, 3 * width
-    )
-    terms = product(taps, table[...], 1, 1).reshape(reach, cols, 3 * width)
-    hidden_grad = (
-        terms[..., width : 2 * width]
-        + from_right(terms[..., :width])
-        + from_left(terms[..., 2 * width :])
-    )
+    hidden_grad = pair_rows(padded[...], table, True)
     gain = gain_ref[...]
     conv = jnp.concatenate([up_ref[0][None], conv_ref[0], down_ref[0][None]], axis=0)
     centred = (conv.astype(F32) - first_norm_ref[pl.ds(date, 1), :]) * first_norm_ref[
@@ -992,6 +1003,7 @@
         *[pltpu.with_memory_space_constraint(x, pltpu.HBM) for x in (images, out_grad, valid)],
     )
     packed = packed.reshape(grad_rows + valid_count, width)
+    inner, outer, above, packed = lax.optimization_barrier((inner, outer, above, packed))
     inner = lax.ppermute(inner, "rows", [(i, i ^ 1) for i in range(row_devs)])
     pairs = [(i, i + 1) for i in range(1, row_devs - 1, 2)]
     outer = lax.ppermute(outer, "rows", pairs + [(j, i) for i, j in pairs])
@@ -1051,7 +1063,7 @@
             ("all", (row_devs, 2 * dates, width), F32),
         ],
         [
-            pltpu.VMEM((3 * width, 3 * width), BF16),
+            pltpu.VMEM((4 * width, 6 * width), BF16),
             pltpu.VMEM((1, rows + 2, cols, width), BF16),
         ],
         9 * flops,
@@ -1148,7 +1160,7 @@
             ("all", (row_devs, 2 * dates, width), F32),
         ],
         [
-            pltpu.VMEM((3 * width, 3 * width), BF16),
+            pltpu.VMEM((6 * width, 4 * width), BF16),
             pltpu.VMEM((2 * dates, width), F32),
             pltpu.VMEM((rows + 4, cols, width), BF16),
         ],

time: 130 us -> 124 us (0.954)
  waiting for transfers between devices: 28.7 us -> 22.6 us
    ppermute x1, waiting for transfers between devices: 7.13 us -> 0.95 us  [shifted(): return lax.ppermute(array, 'rows', pairs)]
    all_to_all x3, starting transfers between devices: 12.5 us -> 14.3 us  [exchange(): return lax.all_to_all(pieces, axes, split_axis=0, concat_axis=0, tiled=True)]
    ppermute x1, starting transfers between devices: 6.18 us -> 4.88 us  [shifted(): return lax.ppermute(array, 'rows', pairs)]
  transfers between devices with their start and end apart: 15 -> 15, of which waited for: 7 -> 7; matrix products, arithmetic and copies ran while one was open for 1% -> 1% of each run, Pallas kernels for 10% -> 12%
where the time goes in v10:
time: 124 us
  Pallas kernels  36.8 us (30%)
  starting transfers between devices  31.4 us (25%)
  blocking collectives  30 us (24%)
  waiting for transfers between devices  22.6 us (18%)
    pallas_call x8, Pallas kernels, call(): pl.pallas_call(body, in_specs=in_specs, out_specs=out_specs, out_shape=ou...  33.3 us
    all_to_all x1, blocking collectives, exchange_cores(): lax.all_to_all(pieces, axes, split_axis=0, concat_axis=0, axis_index_grou...  14.5 us
    all_to_all x3, starting transfers between devices, exchange(): return lax.all_to_all(pieces, axes, split_axis=0, concat_axis=0, tiled=True)  14.3 us
    all_to_all x3, waiting for transfers between devices, exchange(): return lax.all_to_all(pieces, axes, split_axis=0, concat_axis=0, tiled=True)  13.3 us
    all_to_all x1, blocking collectives, exchange(): return lax.all_to_all(pieces, axes, split_axis=0, concat_axis=0, tiled=True)  9.06 us
    all_gather x1, blocking collectives, gather(): return lax.all_gather(array, axis, axis=0, tiled=True)  6.45 us
    all_to_all x1, waiting for transfers between devices, exchange_cores(): lax.all_to_all(pieces, axes, split_axis=0, concat_axis=0, axis_index_grou...  5.95 us
    ppermute x1, starting transfers between devices, shifted(): return lax.ppermute(array, 'rows', pairs)  4.88 us
  transfers between devices with their start and end apart: 15, of which 7 were waited for; matrix products, arithmetic and copies ran while one was open for 1% of the time, Pallas kernels for 12%

profile of v10, /device:TPU:0, one launch (start us, length us, event | category | flops | bytes accessed | tf_op | source)
XLA Modules:
  0.0 123.7 jit_solution(13294171067607077907)
XLA Ops:
  0.7 1.0 slice_bitcast_fusion.last_ref.refs_4_
  1.6 4.9 %collective-permute-start = (bf16[4,128,128]{2,1,0:T(8,128)(2,1)S(1)}, bf16[4,128,128]{2,1,0:T(8,128)(2,1)S(1)}, u32[]{:S(2)}, u32[]{:S(2)}) collective-permute-start(bf16[4,128,128]{2,1,0:T(8,128)(2,1)S(1)} %slice_bitcast_fusion.last_ref.refs_4_), channel_id=1, source_target_pairs={{0,4},{4,8},{8,12},{12,16},{16,20},{20,24},{24,28},{1,5},{5,9},{9,... | collective-permute-start | bytes 393224 | tf_op jit(solution)/shard_map/ppermute | solution.py:885
  6.5 1.7 %shard_map.187 = (bf16[4,16,128,128]{3,2,1,0:T(8,128)(2,1)S(1)}, bf16[4,2,128,128]{3,2,1,0:T(8,128)(2,1)S(1)}, bf16[4,2,128,128]{3,2,1,0:T(8,128)(2,1)S(1)}, bf16[12,32,128]{2,1,0:T(8,128)(2,1)S(1)}) custom-call(s32[1]{0:T(128)} %bitcast.place_ref.refs_0_.refs_4_, bf16[4,128,128]{2,1,0:T(8,128)(2,1)S(1)} %slice_bitcast_fusion.last_ref.refs_4_, ...), custom_call_target="tpu_custom_call" | custom-call | tf_op jit(solution)/shard_map/pallas_call | solution.py:990
  8.3 0.0 copy-start.4
  8.3 0.0 copy-start.8
  8.3 1.0 collective-permute-done.refs_1_.refs_3_
  9.2 2.5 %collective-permute-start.1 = (bf16[4,2,128,128]{3,2,1,0:T(8,128)(2,1)S(1)}, bf16[4,2,128,128]{3,2,1,0:T(8,128)(2,1)S(1)}, u32[]{:S(2)}, u32[]{:S(2)}) collective-permute-start(bf16[4,2,128,128]{3,2,1,0:T(8,128)(2,1)S(1)} %get-tuple-element.66), channel_id=1, source_target_pairs={{0,4},{4,0},{8,12},{12,8},{16,20},{20,16},{24,28},{28,24},{1,5},{5... | collective-permute-start | bytes 786440 | tf_op jit(solution)/shard_map/ppermute | solution.py:1007
  11.7 0.7 collective-permute-start.2
  12.4 2.7 %shard_map.188 = (bf16[4,8,128,128]{3,2,1,0:T(8,128)(2,1)}, f32[8,8,128]{2,1,0:T(8,128)}) custom-call(bf16[4,8,2,128,128]{4,3,2,1,0:T(8,128)(2,1)S(1)} %bitcast.51, bf16[4,128,128]{2,1,0:T(8,128)(2,1)S(1)} %collective-permute-done.refs_1_.refs_3_, bf16[3,3,64,128]{3,2,1,0:T(8,128)(2,1)S(1)} %copy-done.1), custom_call_target="tpu_custom_call" | custom-call | flops 805306368 | bytes 4751360 | tf_op jit(solution)/shard_map/pallas_call | solution.py:871
  15.1 7.6 %all-to-all-start = ((f32[8,8,128]{2,1,0:T(8,128)}), f32[8,8,128]{2,1,0:T(8,128)S(1)}, u32[]{:S(2)}, u32[]{:S(2)}) async-start(f32[8,8,128]{2,1,0:T(8,128)} %get-tuple-element.68), calls=%async_computation | async-start | bytes 65536 | tf_op jit(solution)/shard_map/all_to_all | solution.py:909
  22.7 0.0 collective-permute-done.2.refs_2_.refs_3_
  22.7 0.5 shard_map.189
  23.3 1.6 %collective-permute-start.3 = (bf16[384,128]{1,0:T(8,128)(2,1)S(1)}, bf16[384,128]{1,0:T(8,128)(2,1)S(1)}, u32[]{:S(2)}, u32[]{:S(2)}) collective-permute-start(bf16[384,128]{1,0:T(8,128)(2,1)S(1)} %bitcast.40), channel_id=1, source_target_pairs={{2,0},{3,1},{0,2},{1,3},{6,4},{7,5},{4,6},{5,7},{10,8},{11,9},{8,1... | collective-permute-start | bytes 294920 | tf_op jit(solution)/shard_map/ppermute | solution.py:893
  24.8 4.6 %all-to-all-done.refs_4_ = f32[8,8,128]{2,1,0:T(8,128)S(1)} async-done(((f32[8,8,128]{2,1,0:T(8,128)}), f32[8,8,128]{2,1,0:T(8,128)S(1)}, u32[]{:S(2)}, u32[]{:S(2)}) %all-to-all-start) | async-done | bytes 32800 | tf_op jit(solution)/shard_map/all_to_all | solution.py:909
  29.4 0.0 copy-start.5
  29.4 0.0 copy-start.6
  29.4 0.0 copy-start.7
  29.5 5.8 %shard_map.190 = (bf16[4,8,128,128]{3,2,1,0:T(8,128)(2,1)}, f32[8,128]{1,0:T(8,128)S(1)}, f32[8,8,128]{2,1,0:T(8,128)}) custom-call(s32[1]{0:T(128)} %bitcast.place_ref.refs_0_.refs_4_, bf16[4,8,128,128]{3,2,1,0:T(8,128)(2,1)} %get-tuple-element.65.refs_1_.refs_6_.refs_5_, bf16[4,128,128]{2,1,0:T(8,128)(2,1)S(1)} %get-tuple-element.72.refs_2_.refs_7_, ...), custom_call_target="tpu_custom_call" | custom-call | flops 1207959552 | bytes 3278856 | tf_op jit(solution)/shard_map/pallas_call | solution.py:871
  35.2 0.0 collective-permute-done.3
  35.3 0.1 collective-permute-start.4
  35.3 0.5 collective-permute-start.5
  35.8 3.3 %all-to-all-start.1 = ((f32[8,8,128]{2,1,0:T(8,128)}), f32[8,8,128]{2,1,0:T(8,128)S(1)}, u32[]{:S(2)}, u32[]{:S(2)}) async-start(f32[8,8,128]{2,1,0:T(8,128)} %get-tuple-element.75), calls=%async_computation.1 | async-start | bytes 65536 | tf_op jit(solution)/shard_map/all_to_all | solution.py:909
  39.2 0.0 collective-permute-done.4
  39.2 0.1 pad_maximum_fusion.refs_5_.refs_10_
  39.3 6.5 %all-to-all-done.1.refs_2_ = f32[8,8,128]{2,1,0:T(8,128)S(1)} async-done(((f32[8,8,128]{2,1,0:T(8,128)}), f32[8,8,128]{2,1,0:T(8,128)S(1)}, u32[]{:S(2)}, u32[]{:S(2)}) %all-to-all-start.1) | async-done | bytes 32800 | tf_op jit(solution)/shard_map/all_to_all | solution.py:909
  45.8 4.4 %shard_map.191 = (bf16[4,8,128,128]{3,2,1,0:T(8,128)(2,1)S(1)}, f32[4,8,128,128]{3,2,1,0:T(8,128)S(1)}, f32[4,8,128,128]{3,2,1,0:T(8,128)S(1)}, f32[8,128]{1,0:T...) custom-call(s32[16]{0:T(128)S(1)} %copy-done.7, ...), custom_call_target="tpu_custom_call" | custom-call | flops 671088640 | bytes 3115656 | tf_op jit(solution)/shard_map/pallas_call | solution.py:871
  50.2 6.5 %all_gather.3.refs_0_ = bf16[4,3,128,128]{3,2,1,0:T(8,128)(2,1)S(1)} all-gather(bf16[1,3,128,128]{3,2,1,0:T(8,128)(2,1)S(1)} %get-tuple-element.80), channel_id=1, replica_groups=mesh['rows'=8,'dates'=4] {'dates'}, dimensions={0}, use_global_device_ids=true | all-gather | bytes 491520 | tf_op jit(solution)/shard_map/all_gather | solution.py:913
  56.7 4.0 %shard_map.192 = (bf16[4,8,128,128]{3,2,1,0:T(8,128)(2,1)}, bf16[4,8,32,128]{3,2,1,0:T(8,128)(2,1)}, f32[128,128]{1,0:T(8,128)}, f32[8,128]{1,0:T(8,128)S(1)}, f32[8,8,128]{2,1,0:T(8,128)S(1)}) custom-call(bf16[4,3,128,128]{3,2,1,0:T(8,128)(2,1)S(1)} %all_gather.3.refs_0_, f32[128,128]{1,0:T(8,128)S(1)} %get-tuple-element.81.refs_1_, ...), custom_call_target="tpu_custom_call" | custom-call | flops 671088640 | bytes 14370824 | tf_op jit(solution)/shard_map/pallas_call | solution.py:871
  60.7 9.1 %all_to_all.30.refs_3_ = f32[8,8,128]{2,1,0:T(8,128)S(1)} all-to-all(f32[8,8,128]{2,1,0:T(8,128)S(1)} %get-tuple-element.90), channel_id=1, replica_groups=mesh['rows'=8,'dates'=4] {'rows'}, dimensions={0} | all-to-all | bytes 65536 | tf_op jit(solution)/shard_map/all_to_all | solution.py:909
  69.7 7.3 %shard_map.193 = (bf16[4,8,128,128]{3,2,1,0:T(8,128)(2,1)}, bf16[4,10,128,128]{3,2,1,0:T(8,128)(2,1)}, f32[8,128]{1,0:T(8,128)S(1)}, f32[8,8,128]{2,1,0:T(8,128)}) custom-call(s32[1]{0:T(128)} %bitcast.place_ref.refs_0_.refs_4_, bf16[4,8,128,128]{3,2,1,0:T(8,128)(2,1)} %get-tuple-element.89.refs_1_, ...), custom_call_target="tpu_custom_call" | custom-call | flops 1207959552 | bytes 7489544 | tf_op jit(solution)/shard_map/pallas_call | solution.py:871
  77.1 3.4 %all-to-all-start.3 = ((f32[8,8,128]{2,1,0:T(8,128)}), f32[8,8,128]{2,1,0:T(8,128)S(1)}, u32[]{:S(2)}, u32[]{:S(2)}) async-start(f32[8,8,128]{2,1,0:T(8,128)} %get-tuple-element.93), calls=%async_computation.3 | async-start | bytes 65536 | tf_op jit(solution)/shard_map/all_to_all | solution.py:909
  80.4 4.4 %shard_map.194.refs_12_ = bf16[1280,128]{1,0:T(8,128)(2,1)} custom-call(s32[1]{0:T(128)} %bitcast.place_ref.refs_0_.refs_4_, bf16[4,8,128,128]{3,2,1,0:T(8,128)(2,1)} %get-tuple-element.65.refs_1_.refs_6_.refs_5_, bf16[4,128,128]{2,1,0:T(8,128)(2,1)S(1)} %get-tuple-element.72.refs_2_.refs_7_, bf16[4,128,128]{2,1,0:T(8,128)(2,1)S(1)} %get-tuple-element.73.refs_3_.refs_8_, ...), custom_call_target="tpu_custom_call" | custom-call | flops 1207959552 | bytes 4859912 | tf_op jit(solution)/shard_map/pallas_call | solution.py:871
  84.9 2.2 %all-to-all-done.3.refs_7_ = f32[8,8,128]{2,1,0:T(8,128)S(1)} async-done(((f32[8,8,128]{2,1,0:T(8,128)}), f32[8,8,128]{2,1,0:T(8,128)S(1)}, u32[]{:S(2)}, u32[]{:S(2)}) %all-to-all-start.3) | async-done | bytes 32800 | tf_op jit(solution)/shard_map/all_to_all | solution.py:909
  87.1 4.1 %shard_map.195 = (bf16[1024,128]{1,0:T(8,128)(2,1)S(1)}, bf16[1024,128]{1,0:T(8,128)(2,1)S(1)}) custom-call(bf16[4,8,2,128,128]{4,3,2,1,0:T(8,128)(2,1)} %bitcast.57, bf16[4,128,128]{2,1,0:T(8,128)(2,1)S(1)} %collective-permute-done.refs_1_.refs_3_, bf16[4,2,128,128]{3,2,1,0:T(8,128)(2,1)S(1)} %collective-permute-done.1.refs_1_.refs_2_, ...), custom_call_target="tpu_custom_call" | custom-call | flops 805306368 | bytes 10970128 | tf_op jit(solution)/shard_map/pallas_call | solution.py:871
  91.2 0.0 copy-start.9
  91.2 0.1 collective-permute-start.6
  91.3 1.5 %collective-permute-done.6 = bf16[1024,128]{1,0:T(8,128)(2,1)S(1)} collective-permute-done((bf16[1024,128]{1,0:T(8,128)(2,1)S(1)}, bf16[1024,128]{1,0:T(8,128)(2,1)S(1)}, u32[]{:S(2)}, u32[]{:S(2)}) %collective-permute-start.6) | collective-permute-done | bytes 262176 | tf_op jit(solution)/shard_map/ppermute | solution.py:918
  92.8 0.1 add_convert_fusion
  92.9 14.5 %all_to_all.31.in_ref = bf16[16,64,128]{2,1,0:T(8,128)(2,1)S(1)} all-to-all(bf16[16,64,128]{2,1,0:T(8,128)(2,1)S(1)} %bitcast.58), channel_id=1, replica_groups={{0,2,4,6,8,10,12,14,16,18,20,22,24,26,28,30},{1,3,5,7,9,11,13,15,17,19,..., dimensions={0} | all-to-all | bytes 524288 | tf_op jit(solution)/shard_map/all_to_all | solution.py:925
  107.4 0.8 shard_map.196
  108.1 3.5 %all-to-all-start.5 = ((bf16[16,64,128]{2,1,0:T(8,128)(2,1)}), bf16[16,64,128]{2,1,0:T(8,128)(2,1)S(1)}, u32[]{:S(2)}, u32[]{:S(2)}) async-start(bf16[16,64,128]{2,1,0:T(8,128)(2,1)} %shard_map.196), calls=%async_computation.5 | async-start | bytes 524288 | tf_op jit(solution)/shard_map/all_to_all | solution.py:925
  111.8 0.1 collective-permute-start.7
  111.8 1.9 %collective-permute-start.8 = (bf16[8,32,128]{2,1,0:T(8,128)(2,1)S(1)}, bf16[8,32,128]{2,1,0:T(8,128)(2,1)S(1)}, u32[]{:S(2)}, u32[]{:S(2)}) collective-permute-start(bf16[8,32,128]{2,1,0:T(8,128)(2,1)S(1)} %get-tuple-element.113), channel_id=1, source_target_pairs={{0,2},{1,3},{2,0},{3,1},{4,6},{5,7},{6,4},{7,5},{8,10},{9,11},{10,... | collective-permute-start | bytes 196616 | tf_op jit(solution)/shard_map/ppermute | solution.py:904
  113.8 1.4 %collective-permute-start.9 = (bf16[8,32,128]{2,1,0:T(8,128)(2,1)S(1)}, bf16[8,32,128]{2,1,0:T(8,128)(2,1)S(1)}, u32[]{:S(2)}, u32[]{:S(2)}) collective-permute-start(bf16[8,32,128]{2,1,0:T(8,128)(2,1)S(1)} %get-tuple-element.112), channel_id=1, source_target_pairs={{0,3},{1,0},{2,1},{3,2},{4,7},{5,4},{6,5},{7,6},{8,11},{9,8},{10,9... | collective-permute-start | bytes 196616 | tf_op jit(solution)/shard_map/ppermute | solution.py:904
  115.2 5.9 %all-to-all-done.5 = bf16[16,64,128]{2,1,0:T(8,128)(2,1)S(1)} async-done(((bf16[16,64,128]{2,1,0:T(8,128)(2,1)}), bf16[16,64,128]{2,1,0:T(8,128)(2,1)S(1)}, u32[]{:S(2)}, u32[]{:S(2)}) %all-to-all-start.5) | async-done | bytes 262176 | tf_op jit(solution)/shard_map/all_to_all | solution.py:925
  121.1 0.7 fusion.2
  121.8 0.8 collective-permute-done.10.other_ref
  122.6 1.0 shard_map.197
  (22 shorter events, 0.1 us)
Async XLA Ops:
  0.6 11.7 %copy-start.1 = (bf16[3,3,64,128]{3,2,1,0:T(8,128)(2,1)S(1)}, bf16[3,3,64,128]{3,2,1,0:T(8,128)(2,1)}, u32[]{:S(2)}) copy-start(bf16[3,3,64,128]{3,2,1,0:T(8,128)(2,1)} %refs_5_.2) | copy-start | bytes 442372
  1.6 7.6 %collective-permute-start = (bf16[4,128,128]{2,1,0:T(8,128)(2,1)S(1)}, bf16[4,128,128]{2,1,0:T(8,128)(2,1)S(1)}, u32[]{:S(2)}, u32[]{:S(2)}) collective-permute-start(bf16[4,128,128]{2,1,0:T(8,128)(2,1)S(1)} %slice_bitcast_fusion.last_ref.refs_4_), channel_id=1, source_target_pairs={{0,4},{4,8},{8,12},{12,16},{16,20},{20,24},{24,28},{1,5},{5,9},{9,... | collective-permute-start | bytes 393224 | tf_op jit(solution)/shard_map/ppermute | solution.py:885
  8.3 21.2 %copy-start.4 = (f32[128]{0:T(128)S(1)}, f32[128]{0:T(128)}, u32[]{:S(2)}) copy-start(f32[128]{0:T(128)} %param.17) | copy-start | bytes 1540
  8.3 21.1 %copy-start.8 = (f32[128]{0:T(128)S(1)}, f32[128]{0:T(128)}, u32[]{:S(2)}) copy-start(f32[128]{0:T(128)} %param.18) | copy-start | bytes 1540
  9.2 13.5 %collective-permute-start.1 = (bf16[4,2,128,128]{3,2,1,0:T(8,128)(2,1)S(1)}, bf16[4,2,128,128]{3,2,1,0:T(8,128)(2,1)S(1)}, u32[]{:S(2)}, u32[]{:S(2)}) collective-permute-start(bf16[4,2,128,128]{3,2,1,0:T(8,128)(2,1)S(1)} %get-tuple-element.66), channel_id=1, source_target_pairs={{0,4},{4,0},{8,12},{12,8},{16,20},{20,16},{24,28},{28,24},{1,5},{5... | collective-permute-start | bytes 786440 | tf_op jit(solution)/shard_map/ppermute | solution.py:1007
  11.7 11.0 %collective-permute-start.2 = (bf16[4,2,128,128]{3,2,1,0:T(8,128)(2,1)S(1)}, bf16[4,2,128,128]{3,2,1,0:T(8,128)(2,1)S(1)}, u32[]{:S(2)}, u32[]{:S(2)}) collective-permute-start(bf16[4,2,128,128]{3,2,1,0:T(8,128)(2,1)S(1)} %get-tuple-element.67), channel_id=1, source_target_pairs={{4,8},{12,16},{20,24},{8,4},{16,12},{24,20},{5,9},{13,17},{21,25},... | collective-permute-start | bytes 786440 | tf_op jit(solution)/shard_map/ppermute | solution.py:1009
  15.1 14.3 %all-to-all-start = ((f32[8,8,128]{2,1,0:T(8,128)}), f32[8,8,128]{2,1,0:T(8,128)S(1)}, u32[]{:S(2)}, u32[]{:S(2)}) async-start(f32[8,8,128]{2,1,0:T(8,128)} %get-tuple-element.68), calls=%async_computation | async-start | bytes 65536 | tf_op jit(solution)/shard_map/all_to_all | solution.py:909
  23.3 12.0 %collective-permute-start.3 = (bf16[384,128]{1,0:T(8,128)(2,1)S(1)}, bf16[384,128]{1,0:T(8,128)(2,1)S(1)}, u32[]{:S(2)}, u32[]{:S(2)}) collective-permute-start(bf16[384,128]{1,0:T(8,128)(2,1)S(1)} %bitcast.40), channel_id=1, source_target_pairs={{2,0},{3,1},{0,2},{1,3},{6,4},{7,5},{4,6},{5,7},{10,8},{11,9},{8,1... | collective-permute-start | bytes 294920 | tf_op jit(solution)/shard_map/ppermute | solution.py:893
  29.4 16.4 %copy-start.2 = (f32[128]{0:T(128)S(1)}, f32[128]{0:T(128)}, u32[]{:S(2)}) copy-start(f32[128]{0:T(128)} %param.20) | copy-start | bytes 1540
  29.4 16.4 %copy-start.3 = (f32[128]{0:T(128)S(1)}, f32[128]{0:T(128)}, u32[]{:S(2)}) copy-start(f32[128]{0:T(128)} %param.21) | copy-start | bytes 1540
  29.4 16.4 %copy-start.5 = (bf16[128,64]{0,1:T(8,128)(2,1)S(1)}, bf16[128,64]{0,1:T(8,128)(2,1)}, u32[]{:S(2)}) copy-start(bf16[128,64]{0,1:T(8,128)(2,1)} %param.22) | copy-start | bytes 49156
  29.4 16.4 %copy-start.6 = (f32[16,4]{0,1:T(4,128)S(1)}, f32[16,4]{0,1:T(4,128)}, u32[]{:S(2)}) copy-start(f32[16,4]{0,1:T(4,128)} %param.23) | copy-start | bytes 772
  29.4 16.4 %copy-start.7 = (s32[16]{0:T(128)S(1)}, s32[16]{0:T(128)}, u32[]{:S(2)}) copy-start(s32[16]{0:T(128)} %refs_0_.1) | copy-start | bytes 196
  35.2 21.4 %copy-start = (bf16[4,8,128,128]{3,2,1,0:T(8,128)(2,1)S(1)}, bf16[4,8,128,128]{3,2,1,0:T(8,128)(2,1)}, u32[]{:S(2)}) copy-start(bf16[4,8,128,128]{3,2,1,0:T(8,128)(2,1)} %get-tuple-element.74.refs_1_.refs_5_.refs_2_) | copy-start | bytes 3145732
  35.3 3.9 %collective-permute-start.4 = (bf16[384,128]{1,0:T(8,128)(2,1)S(1)}, bf16[384,128]{1,0:T(8,128)(2,1)S(1)}, u32[]{:S(2)}, u32[]{:S(2)}) collective-permute-start(bf16[384,128]{1,0:T(8,128)(2,1)S(1)} %bitcast.41), channel_id=1, source_target_pairs={{0,1},{1,0},{2,3},{3,2},{4,5},{5,4},{6,7},{7,6},{8,9},{9,8},{10,11... | collective-permute-start | bytes 294920 | tf_op jit(solution)/shard_map/ppermute | solution.py:918
  35.3 3.9 %collective-permute-start.5 = (bf16[384,128]{1,0:T(8,128)(2,1)S(1)}, bf16[384,128]{1,0:T(8,128)(2,1)S(1)}, u32[]{:S(2)}, u32[]{:S(2)}) collective-permute-start(bf16[384,128]{1,0:T(8,128)(2,1)S(1)} %collective-permute-done.3), channel_id=1, source_target_pairs={{0,1},{1,0},{2,3},{3,2},{4,5},{5,4},{6,7},{7,6},{8,9},{9,8},{10,11... | collective-permute-start | bytes 294920 | tf_op jit(solution)/shard_map/ppermute | solution.py:918
  35.8 10.0 %all-to-all-start.1 = ((f32[8,8,128]{2,1,0:T(8,128)}), f32[8,8,128]{2,1,0:T(8,128)S(1)}, u32[]{:S(2)}, u32[]{:S(2)}) async-start(f32[8,8,128]{2,1,0:T(8,128)} %get-tuple-element.75), calls=%async_computation.1 | async-start | bytes 65536 | tf_op jit(solution)/shard_map/all_to_all | solution.py:909
  77.1 10.0 %all-to-all-start.3 = ((f32[8,8,128]{2,1,0:T(8,128)}), f32[8,8,128]{2,1,0:T(8,128)S(1)}, u32[]{:S(2)}, u32[]{:S(2)}) async-start(f32[8,8,128]{2,1,0:T(8,128)} %get-tuple-element.93), calls=%async_computation.3 | async-start | bytes 65536 | tf_op jit(solution)/shard_map/all_to_all | solution.py:909
  91.2 20.5 %copy-start.9 = (bf16[4,8,32,128]{3,2,1,0:T(8,128)(2,1)S(1)}, bf16[4,8,32,128]{3,2,1,0:T(8,128)(2,1)}, u32[]{:S(2)}) copy-start(bf16[4,8,32,128]{3,2,1,0:T(8,128)(2,1)} %get-tuple-element.102) | copy-start | bytes 786436
  91.2 1.6 %collective-permute-start.6 = (bf16[1024,128]{1,0:T(8,128)(2,1)S(1)}, bf16[1024,128]{1,0:T(8,128)(2,1)S(1)}, u32[]{:S(2)}, u32[]{:S(2)}) collective-permute-start(bf16[1024,128]{1,0:T(8,128)(2,1)S(1)} %get-tuple-element.101), channel_id=1, source_target_pairs={{0,1},{1,0},{2,3},{3,2},{4,5},{5,4},{6,7},{7,6},{8,9},{9,8},{10,11... | collective-permute-start | bytes 786440 | tf_op jit(solution)/shard_map/ppermute | solution.py:918
  108.1 13.0 %all-to-all-start.5 = ((bf16[16,64,128]{2,1,0:T(8,128)(2,1)}), bf16[16,64,128]{2,1,0:T(8,128)(2,1)S(1)}, u32[]{:S(2)}, u32[]{:S(2)}) async-start(bf16[16,64,128]{2,1,0:T(8,128)(2,1)} %shard_map.196), calls=%async_computation.5 | async-start | bytes 524288 | tf_op jit(solution)/shard_map/all_to_all | solution.py:925
  111.8 9.3 %collective-permute-start.7 = (bf16[8,32,128]{2,1,0:T(8,128)(2,1)S(1)}, bf16[8,32,128]{2,1,0:T(8,128)(2,1)S(1)}, u32[]{:S(2)}, u32[]{:S(2)}) collective-permute-start(bf16[8,32,128]{2,1,0:T(8,128)(2,1)S(1)} %get-tuple-element.111), channel_id=1, source_target_pairs={{0,1},{1,2},{2,3},{3,0},{4,5},{5,6},{6,7},{7,4},{8,9},{9,10},{10,1... | collective-permute-start | bytes 196616 | tf_op jit(solution)/shard_map/ppermute | solution.py:904
  111.8 9.3 %collective-permute-start.8 = (bf16[8,32,128]{2,1,0:T(8,128)(2,1)S(1)}, bf16[8,32,128]{2,1,0:T(8,128)(2,1)S(1)}, u32[]{:S(2)}, u32[]{:S(2)}) collective-permute-start(bf16[8,32,128]{2,1,0:T(8,128)(2,1)S(1)} %get-tuple-element.113), channel_id=1, source_target_pairs={{0,2},{1,3},{2,0},{3,1},{4,6},{5,7},{6,4},{7,5},{8,10},{9,11},{10,... | collective-permute-start | bytes 196616 | tf_op jit(solution)/shard_map/ppermute | solution.py:904
  113.8 7.4 %collective-permute-start.9 = (bf16[8,32,128]{2,1,0:T(8,128)(2,1)S(1)}, bf16[8,32,128]{2,1,0:T(8,128)(2,1)S(1)}, u32[]{:S(2)}, u32[]{:S(2)}) collective-permute-start(bf16[8,32,128]{2,1,0:T(8,128)(2,1)S(1)} %get-tuple-element.112), channel_id=1, source_target_pairs={{0,3},{1,0},{2,1},{3,2},{4,7},{5,4},{6,5},{7,6},{8,11},{9,8},{10,9... | collective-permute-start | bytes 196616 | tf_op jit(solution)/shard_map/ppermute | solution.py:904
  121.1 1.5 %collective-permute-start.10 = (bf16[1024,128]{1,0:T(8,128)(2,1)S(1)}, bf16[1024,128]{1,0:T(8,128)(2,1)S(1)}, u32[]{:S(2)}, u32[]{:S(2)}) collective-permute-start(bf16[1024,128]{1,0:T(8,128)(2,1)S(1)} %bitcast.38), channel_id=1, source_target_pairs={{0,1},{1,0},{2,3},{3,2},{4,5},{5,4},{6,7},{7,6},{8,9},{9,8},{10,11... | collective-permute-start | bytes 786440 | tf_op jit(solution)/shard_map/ppermute | solution.py:918

commit v11 on v10

--- a/solution.py
+++ b/solution.py
@@ -59,38 +59,29 @@
     return jnp.concatenate([moved[:, : count - 8], jnp.where(column < 7, last, 0.0)], axis=1)
 
 
-def pair_table(weight_ref, table, backward):
+def tap_table(weight_ref, table, backward):
     width = weight_ref.shape[-1]
-    for row in range(4):
-        for parity in range(2):
-            for col_tap in range(3):
-                deep = slice(row * width, (row + 1) * width)
-                start = (col_tap * 2 + parity) * width
-                wide = slice(start, start + width)
-                tap = row - parity
-                inside = 0 <= tap <= 2
-                if backward:
-                    block = weight_ref[2 - tap, col_tap] if inside else None
-                    where = (wide, deep)
-                else:
-                    block = weight_ref[tap, col_tap] if inside else None
-                    where = (deep, wide)
-                table[where] = block if inside else jnp.zeros((width, width), BF16)
-
-
-def pair_rows(padded, table, backward):
-    rows, cols, width = padded.shape
-    pairs = padded.reshape(rows // 2, 2, cols, width)
-    count = rows // 2 - 1
-    taps = [pairs[:count, 0], pairs[:count, 1], pairs[1:, 0], pairs[1:, 1]]
-    taps = jnp.concatenate(taps, axis=-1).reshape(count * cols, 4 * width)
-    terms = product(taps, table[...], 1, 1 if backward else 0).reshape(count, cols, 6 * width)
-    parts = [terms[..., place * width : (place + 1) * width] for place in range(6)]
+    for row_tap in range(3):
+        for col_tap in range(3):
+            deep = slice(row_tap * width, (row_tap + 1) * width)
+            wide = slice(col_tap * width, (col_tap + 1) * width)
+            if backward:
+                table[wide, deep] = weight_ref[2 - row_tap, col_tap]
+            else:
+                table[deep, wide] = weight_ref[row_tap, col_tap]
+
+
+def tap_rows(padded, table, backward):
+    rows, cols, width = padded.shape[0] - 2, *padded.shape[1:]
+    taps = jnp.concatenate([padded[tap : tap + rows] for tap in range(3)], axis=-1)
+    taps = taps.reshape(rows * cols, 3 * width)
+    terms = product(taps, table[...], 1, 1 if backward else 0).reshape(rows, cols, 3 * width)
     first, last = (from_right, from_left) if backward else (from_left, from_right)
-    results = [
-        parts[2 + parity] + first(parts[parity]) + last(parts[4 + parity]) for parity in range(2)
-    ]
-    return jnp.stack(results, axis=1).reshape(2 * count, cols, width)
+    return (
+        terms[..., width : 2 * width]
+        + first(terms[..., :width])
+        + last(terms[..., 2 * width :])
+    )
 
 
 def column_sum(values):
@@ -282,7 +273,7 @@
 
     if date == 0:
         norm_table(stats_ref, norm_ref, dates, norm_count)
-        pair_table(weight_ref, table, False)
+        tap_table(weight_ref, table, False)
 
     activate_rows(
         date,
@@ -292,7 +283,7 @@
         (norm_ref, gain_ref, shift_ref),
         hidden_ref,
     )
-    stored = pair_rows(hidden_ref[0], table, False).astype(BF16)
+    stored = tap_rows(hidden_ref[0], table, False).astype(BF16)
     out_ref[0] = stored
     values = stored.astype(F32)
     store_sums(sums_ref, date, dates, column_sum(values), column_sum(values * values))
@@ -559,7 +550,7 @@
         vector_ref[...] = jnp.zeros_like(vector_ref)
         padded[:2] = jnp.zeros_like(padded[:2])
         padded[rows + 2 :] = jnp.zeros_like(padded[rows + 2 :])
-        pair_table(weight_ref, table, True)
+        tap_table(weight_ref, table, True)
 
     inverse = norm_ref[pl.ds(dates + date, 1), :]
     slope = factors[pl.ds(date, 1), :]
@@ -571,7 +562,7 @@
     ).astype(BF16)
     pre_ref[0] = stored
     padded[2 : rows + 2] = stored
-    hidden_grad = pair_rows(padded[...], table, True)
+    hidden_grad = tap_rows(padded[...], table, True)
     gain = gain_ref[...]
     conv = jnp.concatenate([up_ref[0][None], conv_ref[0], down_ref[0][None]], axis=0)
     centred = (conv.astype(F32) - first_norm_ref[pl.ds(date, 1), :]) * first_norm_ref[
@@ -841,10 +832,13 @@
             copies_of(len(inputs) + place, len(loads) + index, False)
             for index, place in enumerate(stores)
         ]
-        for date in range(dates):
+        def fetch(date):
             for moves in incoming:
                 if date < len(moves):
                     moves[date].start()
+
+        fetch(0)
+        fetch(1)
         for index, place in enumerate(loads):
             views[place] = buffer_refs[index]
         for index, place in enumerate(stores):
@@ -853,6 +847,7 @@
             for moves in incoming:
                 if date < len(moves):
                     moves[date].wait()
+            fetch(date + 2)
             here = [
                 view.at[pl.ds(date, 1)] if "date" in kind else view
                 for view, kind in zip(views, kinds)
@@ -1063,7 +1058,7 @@
             ("all", (row_devs, 2 * dates, width), F32),
         ],
         [
-            pltpu.VMEM((4 * width, 6 * width), BF16),
+            pltpu.VMEM((3 * width, 3 * width), BF16),
             pltpu.VMEM((1, rows + 2, cols, width), BF16),
         ],
         9 * flops,
@@ -1160,7 +1155,7 @@
             ("all", (row_devs, 2 * dates, width), F32),
         ],
         [
-            pltpu.VMEM((6 * width, 4 * width), BF16),
+            pltpu.VMEM((3 * width, 3 * width), BF16),
             pltpu.VMEM((2 * dates, width), F32),
             pltpu.VMEM((rows + 4, cols, width), BF16),
         ],

time: 124 us -> 124 us (level)
  no operation moved by 1% of the time
where the time goes in v11:
time: 124 us; the launch traced here: 123 us
  Pallas kernels  36.4 us (29%)
  starting transfers between devices  31.4 us (25%)
  blocking collectives  30.2 us (24%)
  waiting for transfers between devices  22.6 us (18%)
    pallas_call x8, Pallas kernels, call(): pl.pallas_call(body, in_specs=in_specs, out_specs=out_specs, out_shape=ou...  32.8 us
    all_to_all x1, blocking collectives, exchange_cores(): lax.all_to_all(pieces, axes, split_axis=0, concat_axis=0, axis_index_grou...  14.5 us
    all_to_all x3, starting transfers between devices, exchange(): return lax.all_to_all(pieces, axes, split_axis=0, concat_axis=0, tiled=True)  14.3 us
    all_to_all x3, waiting for transfers between devices, exchange(): return lax.all_to_all(pieces, axes, split_axis=0, concat_axis=0, tiled=True)  13.3 us
    all_to_all x1, blocking collectives, exchange(): return lax.all_to_all(pieces, axes, split_axis=0, concat_axis=0, tiled=True)  9.24 us
    all_gather x1, blocking collectives, gather(): return lax.all_gather(array, axis, axis=0, tiled=True)  6.46 us
    all_to_all x1, waiting for transfers between devices, exchange_cores(): lax.all_to_all(pieces, axes, split_axis=0, concat_axis=0, axis_index_grou...  5.95 us
    ppermute x1, starting transfers between devices, shifted(): return lax.ppermute(array, 'rows', pairs)  4.88 us
  transfers between devices with their start and end apart: 15, of which 7 were waited for; matrix products, arithmetic and copies ran while one was open for 1% of the time, Pallas kernels for 12%

profile of v11, /device:TPU:0, one launch (start us, length us, event | category | flops | bytes accessed | tf_op | source)
XLA Modules:
  0.0 123.4 jit_solution(9252189309386438133)
XLA Ops:
  0.7 1.0 slice_bitcast_fusion.last_ref.refs_4_
  1.6 4.9 %collective-permute-start = (bf16[4,128,128]{2,1,0:T(8,128)(2,1)S(1)}, bf16[4,128,128]{2,1,0:T(8,128)(2,1)S(1)}, u32[]{:S(2)}, u32[]{:S(2)}) collective-permute-start(bf16[4,128,128]{2,1,0:T(8,128)(2,1)S(1)} %slice_bitcast_fusion.last_ref.refs_4_), channel_id=1, source_target_pairs={{0,4},{4,8},{8,12},{12,16},{16,20},{20,24},{24,28},{1,5},{5,9},{9,... | collective-permute-start | bytes 393224 | tf_op jit(solution)/shard_map/ppermute | solution.py:880
  6.5 1.7 %shard_map.187 = (bf16[4,16,128,128]{3,2,1,0:T(8,128)(2,1)S(1)}, bf16[4,2,128,128]{3,2,1,0:T(8,128)(2,1)S(1)}, bf16[4,2,128,128]{3,2,1,0:T(8,128)(2,1)S(1)}, bf16[12,32,128]{2,1,0:T(8,128)(2,1)S(1)}) custom-call(s32[1]{0:T(128)} %bitcast.place_ref.refs_0_.refs_4_, bf16[4,128,128]{2,1,0:T(8,128)(2,1)S(1)} %slice_bitcast_fusion.last_ref.refs_4_, ...), custom_call_target="tpu_custom_call" | custom-call | tf_op jit(solution)/shard_map/pallas_call | solution.py:985
  8.3 0.0 copy-start.4
  8.3 0.0 copy-start.8
  8.3 1.0 collective-permute-done.refs_1_.refs_3_
  9.2 2.5 %collective-permute-start.1 = (bf16[4,2,128,128]{3,2,1,0:T(8,128)(2,1)S(1)}, bf16[4,2,128,128]{3,2,1,0:T(8,128)(2,1)S(1)}, u32[]{:S(2)}, u32[]{:S(2)}) collective-permute-start(bf16[4,2,128,128]{3,2,1,0:T(8,128)(2,1)S(1)} %get-tuple-element.66), channel_id=1, source_target_pairs={{0,4},{4,0},{8,12},{12,8},{16,20},{20,16},{24,28},{28,24},{1,5},{5... | collective-permute-start | bytes 786440 | tf_op jit(solution)/shard_map/ppermute | solution.py:1002
  11.7 0.7 collective-permute-start.2
  12.4 2.7 %shard_map.188 = (bf16[4,8,128,128]{3,2,1,0:T(8,128)(2,1)}, f32[8,8,128]{2,1,0:T(8,128)}) custom-call(bf16[4,8,2,128,128]{4,3,2,1,0:T(8,128)(2,1)S(1)} %bitcast.51, bf16[4,128,128]{2,1,0:T(8,128)(2,1)S(1)} %collective-permute-done.refs_1_.refs_3_, bf16[3,3,64,128]{3,2,1,0:T(8,128)(2,1)S(1)} %copy-done.1), custom_call_target="tpu_custom_call" | custom-call | flops 805306368 | bytes 4751360 | tf_op jit(solution)/shard_map/pallas_call | solution.py:866
  15.1 7.6 %all-to-all-start = ((f32[8,8,128]{2,1,0:T(8,128)}), f32[8,8,128]{2,1,0:T(8,128)S(1)}, u32[]{:S(2)}, u32[]{:S(2)}) async-start(f32[8,8,128]{2,1,0:T(8,128)} %get-tuple-element.68), calls=%async_computation | async-start | bytes 65536 | tf_op jit(solution)/shard_map/all_to_all | solution.py:904
  22.7 0.0 collective-permute-done.2.refs_2_.refs_3_
  22.7 0.5 shard_map.189
  23.3 1.6 %collective-permute-start.3 = (bf16[384,128]{1,0:T(8,128)(2,1)S(1)}, bf16[384,128]{1,0:T(8,128)(2,1)S(1)}, u32[]{:S(2)}, u32[]{:S(2)}) collective-permute-start(bf16[384,128]{1,0:T(8,128)(2,1)S(1)} %bitcast.40), channel_id=1, source_target_pairs={{2,0},{3,1},{0,2},{1,3},{6,4},{7,5},{4,6},{5,7},{10,8},{11,9},{8,1... | collective-permute-start | bytes 294920 | tf_op jit(solution)/shard_map/ppermute | solution.py:888
  24.8 4.6 %all-to-all-done.refs_4_ = f32[8,8,128]{2,1,0:T(8,128)S(1)} async-done(((f32[8,8,128]{2,1,0:T(8,128)}), f32[8,8,128]{2,1,0:T(8,128)S(1)}, u32[]{:S(2)}, u32[]{:S(2)}) %all-to-all-start) | async-done | bytes 32800 | tf_op jit(solution)/shard_map/all_to_all | solution.py:904
  29.4 0.0 copy-start.5
  29.4 0.0 copy-start.6
  29.4 0.0 copy-start.7
  29.5 5.7 %shard_map.190 = (bf16[4,8,128,128]{3,2,1,0:T(8,128)(2,1)}, f32[8,128]{1,0:T(8,128)S(1)}, f32[8,8,128]{2,1,0:T(8,128)}) custom-call(s32[1]{0:T(128)} %bitcast.place_ref.refs_0_.refs_4_, bf16[4,8,128,128]{3,2,1,0:T(8,128)(2,1)} %get-tuple-element.65.refs_1_.refs_6_.refs_5_, bf16[4,128,128]{2,1,0:T(8,128)(2,1)S(1)} %get-tuple-element.72.refs_2_.refs_7_, ...), custom_call_target="tpu_custom_call" | custom-call | flops 1207959552 | bytes 3278856 | tf_op jit(solution)/shard_map/pallas_call | solution.py:866
  35.1 0.0 collective-permute-done.3
  35.1 0.1 collective-permute-start.4
  35.2 0.5 collective-permute-start.5
  35.7 3.3 %all-to-all-start.1 = ((f32[8,8,128]{2,1,0:T(8,128)}), f32[8,8,128]{2,1,0:T(8,128)S(1)}, u32[]{:S(2)}, u32[]{:S(2)}) async-start(f32[8,8,128]{2,1,0:T(8,128)} %get-tuple-element.75), calls=%async_computation.1 | async-start | bytes 65536 | tf_op jit(solution)/shard_map/all_to_all | solution.py:904
  39.1 0.0 collective-permute-done.4
  39.1 0.1 pad_maximum_fusion.refs_5_.refs_10_
  39.2 6.5 %all-to-all-done.1.refs_2_ = f32[8,8,128]{2,1,0:T(8,128)S(1)} async-done(((f32[8,8,128]{2,1,0:T(8,128)}), f32[8,8,128]{2,1,0:T(8,128)S(1)}, u32[]{:S(2)}, u32[]{:S(2)}) %all-to-all-start.1) | async-done | bytes 32800 | tf_op jit(solution)/shard_map/all_to_all | solution.py:904
  45.7 4.4 %shard_map.191 = (bf16[4,8,128,128]{3,2,1,0:T(8,128)(2,1)S(1)}, f32[4,8,128,128]{3,2,1,0:T(8,128)S(1)}, f32[4,8,128,128]{3,2,1,0:T(8,128)S(1)}, f32[8,128]{1,0:T...) custom-call(s32[16]{0:T(128)S(1)} %copy-done.7, ...), custom_call_target="tpu_custom_call" | custom-call | flops 671088640 | bytes 3115656 | tf_op jit(solution)/shard_map/pallas_call | solution.py:866
  50.1 6.5 %all_gather.3.refs_0_ = bf16[4,3,128,128]{3,2,1,0:T(8,128)(2,1)S(1)} all-gather(bf16[1,3,128,128]{3,2,1,0:T(8,128)(2,1)S(1)} %get-tuple-element.80), channel_id=1, replica_groups=mesh['rows'=8,'dates'=4] {'dates'}, dimensions={0}, use_global_device_ids=true | all-gather | bytes 491520 | tf_op jit(solution)/shard_map/all_gather | solution.py:908
  56.6 4.0 %shard_map.192 = (bf16[4,8,128,128]{3,2,1,0:T(8,128)(2,1)}, bf16[4,8,32,128]{3,2,1,0:T(8,128)(2,1)}, f32[128,128]{1,0:T(8,128)}, f32[8,128]{1,0:T(8,128)S(1)}, f32[8,8,128]{2,1,0:T(8,128)S(1)}) custom-call(bf16[4,3,128,128]{3,2,1,0:T(8,128)(2,1)S(1)} %all_gather.3.refs_0_, f32[128,128]{1,0:T(8,128)S(1)} %get-tuple-element.81.refs_1_, ...), custom_call_target="tpu_custom_call" | custom-call | flops 671088640 | bytes 14370824 | tf_op jit(solution)/shard_map/pallas_call | solution.py:866
  60.6 9.2 %all_to_all.30.refs_3_ = f32[8,8,128]{2,1,0:T(8,128)S(1)} all-to-all(f32[8,8,128]{2,1,0:T(8,128)S(1)} %get-tuple-element.90), channel_id=1, replica_groups=mesh['rows'=8,'dates'=4] {'rows'}, dimensions={0} | all-to-all | bytes 65536 | tf_op jit(solution)/shard_map/all_to_all | solution.py:904
  69.8 7.0 %shard_map.193 = (bf16[4,8,128,128]{3,2,1,0:T(8,128)(2,1)}, bf16[4,10,128,128]{3,2,1,0:T(8,128)(2,1)}, f32[8,128]{1,0:T(8,128)S(1)}, f32[8,8,128]{2,1,0:T(8,128)}) custom-call(s32[1]{0:T(128)} %bitcast.place_ref.refs_0_.refs_4_, bf16[4,8,128,128]{3,2,1,0:T(8,128)(2,1)} %get-tuple-element.89.refs_1_, ...), custom_call_target="tpu_custom_call" | custom-call | flops 1207959552 | bytes 7489544 | tf_op jit(solution)/shard_map/pallas_call | solution.py:866
  76.8 3.4 %all-to-all-start.3 = ((f32[8,8,128]{2,1,0:T(8,128)}), f32[8,8,128]{2,1,0:T(8,128)S(1)}, u32[]{:S(2)}, u32[]{:S(2)}) async-start(f32[8,8,128]{2,1,0:T(8,128)} %get-tuple-element.93), calls=%async_computation.3 | async-start | bytes 65536 | tf_op jit(solution)/shard_map/all_to_all | solution.py:904
  80.1 4.4 %shard_map.194.refs_12_ = bf16[1280,128]{1,0:T(8,128)(2,1)} custom-call(s32[1]{0:T(128)} %bitcast.place_ref.refs_0_.refs_4_, bf16[4,8,128,128]{3,2,1,0:T(8,128)(2,1)} %get-tuple-element.65.refs_1_.refs_6_.refs_5_, bf16[4,128,128]{2,1,0:T(8,128)(2,1)S(1)} %get-tuple-element.72.refs_2_.refs_7_, bf16[4,128,128]{2,1,0:T(8,128)(2,1)S(1)} %get-tuple-element.73.refs_3_.refs_8_, ...), custom_call_target="tpu_custom_call" | custom-call | flops 1207959552 | bytes 4859912 | tf_op jit(solution)/shard_map/pallas_call | solution.py:866
  84.6 2.2 %all-to-all-done.3.refs_7_ = f32[8,8,128]{2,1,0:T(8,128)S(1)} async-done(((f32[8,8,128]{2,1,0:T(8,128)}), f32[8,8,128]{2,1,0:T(8,128)S(1)}, u32[]{:S(2)}, u32[]{:S(2)}) %all-to-all-start.3) | async-done | bytes 32800 | tf_op jit(solution)/shard_map/all_to_all | solution.py:904
  86.8 4.2 %shard_map.195 = (bf16[1024,128]{1,0:T(8,128)(2,1)S(1)}, bf16[1024,128]{1,0:T(8,128)(2,1)S(1)}) custom-call(bf16[4,8,2,128,128]{4,3,2,1,0:T(8,128)(2,1)} %bitcast.57, bf16[4,128,128]{2,1,0:T(8,128)(2,1)S(1)} %collective-permute-done.refs_1_.refs_3_, bf16[4,2,128,128]{3,2,1,0:T(8,128)(2,1)S(1)} %collective-permute-done.1.refs_1_.refs_2_, ...), custom_call_target="tpu_custom_call" | custom-call | flops 805306368 | bytes 10970128 | tf_op jit(solution)/shard_map/pallas_call | solution.py:866
  90.9 0.0 copy-start.9
  91.0 0.1 collective-permute-start.6
  91.0 1.5 %collective-permute-done.6 = bf16[1024,128]{1,0:T(8,128)(2,1)S(1)} collective-permute-done((bf16[1024,128]{1,0:T(8,128)(2,1)S(1)}, bf16[1024,128]{1,0:T(8,128)(2,1)S(1)}, u32[]{:S(2)}, u32[]{:S(2)}) %collective-permute-start.6) | collective-permute-done | bytes 262176 | tf_op jit(solution)/shard_map/ppermute | solution.py:913
  92.6 0.1 add_convert_fusion
  92.6 14.5 %all_to_all.31.in_ref = bf16[16,64,128]{2,1,0:T(8,128)(2,1)S(1)} all-to-all(bf16[16,64,128]{2,1,0:T(8,128)(2,1)S(1)} %bitcast.58), channel_id=1, replica_groups={{0,2,4,6,8,10,12,14,16,18,20,22,24,26,28,30},{1,3,5,7,9,11,13,15,17,19,..., dimensions={0} | all-to-all | bytes 524288 | tf_op jit(solution)/shard_map/all_to_all | solution.py:920
  107.1 0.8 shard_map.196
  107.8 3.5 %all-to-all-start.5 = ((bf16[16,64,128]{2,1,0:T(8,128)(2,1)}), bf16[16,64,128]{2,1,0:T(8,128)(2,1)S(1)}, u32[]{:S(2)}, u32[]{:S(2)}) async-start(bf16[16,64,128]{2,1,0:T(8,128)(2,1)} %shard_map.196), calls=%async_computation.5 | async-start | bytes 524288 | tf_op jit(solution)/shard_map/all_to_all | solution.py:920
  111.5 0.1 collective-permute-start.7
  111.5 1.9 %collective-permute-start.8 = (bf16[8,32,128]{2,1,0:T(8,128)(2,1)S(1)}, bf16[8,32,128]{2,1,0:T(8,128)(2,1)S(1)}, u32[]{:S(2)}, u32[]{:S(2)}) collective-permute-start(bf16[8,32,128]{2,1,0:T(8,128)(2,1)S(1)} %get-tuple-element.113), channel_id=1, source_target_pairs={{0,2},{1,3},{2,0},{3,1},{4,6},{5,7},{6,4},{7,5},{8,10},{9,11},{10,... | collective-permute-start | bytes 196616 | tf_op jit(solution)/shard_map/ppermute | solution.py:899
  113.5 1.4 %collective-permute-start.9 = (bf16[8,32,128]{2,1,0:T(8,128)(2,1)S(1)}, bf16[8,32,128]{2,1,0:T(8,128)(2,1)S(1)}, u32[]{:S(2)}, u32[]{:S(2)}) collective-permute-start(bf16[8,32,128]{2,1,0:T(8,128)(2,1)S(1)} %get-tuple-element.112), channel_id=1, source_target_pairs={{0,3},{1,0},{2,1},{3,2},{4,7},{5,4},{6,5},{7,6},{8,11},{9,8},{10,9... | collective-permute-start | bytes 196616 | tf_op jit(solution)/shard_map/ppermute | solution.py:899
  114.9 5.9 %all-to-all-done.5 = bf16[16,64,128]{2,1,0:T(8,128)(2,1)S(1)} async-done(((bf16[16,64,128]{2,1,0:T(8,128)(2,1)}), bf16[16,64,128]{2,1,0:T(8,128)(2,1)S(1)}, u32[]{:S(2)}, u32[]{:S(2)}) %all-to-all-start.5) | async-done | bytes 262176 | tf_op jit(solution)/shard_map/all_to_all | solution.py:920
  120.8 0.7 fusion.2
  121.5 0.8 collective-permute-done.10.other_ref
  122.4 1.0 shard_map.197
  (22 shorter events, 0.1 us)
Async XLA Ops:
  0.6 11.7 %copy-start.1 = (bf16[3,3,64,128]{3,2,1,0:T(8,128)(2,1)S(1)}, bf16[3,3,64,128]{3,2,1,0:T(8,128)(2,1)}, u32[]{:S(2)}) copy-start(bf16[3,3,64,128]{3,2,1,0:T(8,128)(2,1)} %refs_5_.2) | copy-start | bytes 442372
  1.6 7.6 %collective-permute-start = (bf16[4,128,128]{2,1,0:T(8,128)(2,1)S(1)}, bf16[4,128,128]{2,1,0:T(8,128)(2,1)S(1)}, u32[]{:S(2)}, u32[]{:S(2)}) collective-permute-start(bf16[4,128,128]{2,1,0:T(8,128)(2,1)S(1)} %slice_bitcast_fusion.last_ref.refs_4_), channel_id=1, source_target_pairs={{0,4},{4,8},{8,12},{12,16},{16,20},{20,24},{24,28},{1,5},{5,9},{9,... | collective-permute-start | bytes 393224 | tf_op jit(solution)/shard_map/ppermute | solution.py:880
  8.3 21.2 %copy-start.4 = (f32[128]{0:T(128)S(1)}, f32[128]{0:T(128)}, u32[]{:S(2)}) copy-start(f32[128]{0:T(128)} %param.17) | copy-start | bytes 1540
  8.3 21.1 %copy-start.8 = (f32[128]{0:T(128)S(1)}, f32[128]{0:T(128)}, u32[]{:S(2)}) copy-start(f32[128]{0:T(128)} %param.18) | copy-start | bytes 1540
  9.2 13.5 %collective-permute-start.1 = (bf16[4,2,128,128]{3,2,1,0:T(8,128)(2,1)S(1)}, bf16[4,2,128,128]{3,2,1,0:T(8,128)(2,1)S(1)}, u32[]{:S(2)}, u32[]{:S(2)}) collective-permute-start(bf16[4,2,128,128]{3,2,1,0:T(8,128)(2,1)S(1)} %get-tuple-element.66), channel_id=1, source_target_pairs={{0,4},{4,0},{8,12},{12,8},{16,20},{20,16},{24,28},{28,24},{1,5},{5... | collective-permute-start | bytes 786440 | tf_op jit(solution)/shard_map/ppermute | solution.py:1002
  11.7 11.0 %collective-permute-start.2 = (bf16[4,2,128,128]{3,2,1,0:T(8,128)(2,1)S(1)}, bf16[4,2,128,128]{3,2,1,0:T(8,128)(2,1)S(1)}, u32[]{:S(2)}, u32[]{:S(2)}) collective-permute-start(bf16[4,2,128,128]{3,2,1,0:T(8,128)(2,1)S(1)} %get-tuple-element.67), channel_id=1, source_target_pairs={{4,8},{12,16},{20,24},{8,4},{16,12},{24,20},{5,9},{13,17},{21,25},... | collective-permute-start | bytes 786440 | tf_op jit(solution)/shard_map/ppermute | solution.py:1004
  15.1 14.3 %all-to-all-start = ((f32[8,8,128]{2,1,0:T(8,128)}), f32[8,8,128]{2,1,0:T(8,128)S(1)}, u32[]{:S(2)}, u32[]{:S(2)}) async-start(f32[8,8,128]{2,1,0:T(8,128)} %get-tuple-element.68), calls=%async_computation | async-start | bytes 65536 | tf_op jit(solution)/shard_map/all_to_all | solution.py:904
  23.3 11.9 %collective-permute-start.3 = (bf16[384,128]{1,0:T(8,128)(2,1)S(1)}, bf16[384,128]{1,0:T(8,128)(2,1)S(1)}, u32[]{:S(2)}, u32[]{:S(2)}) collective-permute-start(bf16[384,128]{1,0:T(8,128)(2,1)S(1)} %bitcast.40), channel_id=1, source_target_pairs={{2,0},{3,1},{0,2},{1,3},{6,4},{7,5},{4,6},{5,7},{10,8},{11,9},{8,1... | collective-permute-start | bytes 294920 | tf_op jit(solution)/shard_map/ppermute | solution.py:888
  29.4 16.3 %copy-start.2 = (f32[128]{0:T(128)S(1)}, f32[128]{0:T(128)}, u32[]{:S(2)}) copy-start(f32[128]{0:T(128)} %param.20) | copy-start | bytes 1540
  29.4 16.3 %copy-start.3 = (f32[128]{0:T(128)S(1)}, f32[128]{0:T(128)}, u32[]{:S(2)}) copy-start(f32[128]{0:T(128)} %param.21) | copy-start | bytes 1540
  29.4 16.3 %copy-start.5 = (bf16[128,64]{0,1:T(8,128)(2,1)S(1)}, bf16[128,64]{0,1:T(8,128)(2,1)}, u32[]{:S(2)}) copy-start(bf16[128,64]{0,1:T(8,128)(2,1)} %param.22) | copy-start | bytes 49156
  29.4 16.3 %copy-start.6 = (f32[16,4]{0,1:T(4,128)S(1)}, f32[16,4]{0,1:T(4,128)}, u32[]{:S(2)}) copy-start(f32[16,4]{0,1:T(4,128)} %param.23) | copy-start | bytes 772
  29.4 16.3 %copy-start.7 = (s32[16]{0:T(128)S(1)}, s32[16]{0:T(128)}, u32[]{:S(2)}) copy-start(s32[16]{0:T(128)} %refs_0_.1) | copy-start | bytes 196
  35.1 21.4 %copy-start = (bf16[4,8,128,128]{3,2,1,0:T(8,128)(2,1)S(1)}, bf16[4,8,128,128]{3,2,1,0:T(8,128)(2,1)}, u32[]{:S(2)}) copy-start(bf16[4,8,128,128]{3,2,1,0:T(8,128)(2,1)} %get-tuple-element.74.refs_1_.refs_5_.refs_2_) | copy-start | bytes 3145732
  35.1 3.9 %collective-permute-start.4 = (bf16[384,128]{1,0:T(8,128)(2,1)S(1)}, bf16[384,128]{1,0:T(8,128)(2,1)S(1)}, u32[]{:S(2)}, u32[]{:S(2)}) collective-permute-start(bf16[384,128]{1,0:T(8,128)(2,1)S(1)} %bitcast.41), channel_id=1, source_target_pairs={{0,1},{1,0},{2,3},{3,2},{4,5},{5,4},{6,7},{7,6},{8,9},{9,8},{10,11... | collective-permute-start | bytes 294920 | tf_op jit(solution)/shard_map/ppermute | solution.py:913
  35.2 3.9 %collective-permute-start.5 = (bf16[384,128]{1,0:T(8,128)(2,1)S(1)}, bf16[384,128]{1,0:T(8,128)(2,1)S(1)}, u32[]{:S(2)}, u32[]{:S(2)}) collective-permute-start(bf16[384,128]{1,0:T(8,128)(2,1)S(1)} %collective-permute-done.3), channel_id=1, source_target_pairs={{0,1},{1,0},{2,3},{3,2},{4,5},{5,4},{6,7},{7,6},{8,9},{9,8},{10,11... | collective-permute-start | bytes 294920 | tf_op jit(solution)/shard_map/ppermute | solution.py:913
  35.7 10.0 %all-to-all-start.1 = ((f32[8,8,128]{2,1,0:T(8,128)}), f32[8,8,128]{2,1,0:T(8,128)S(1)}, u32[]{:S(2)}, u32[]{:S(2)}) async-start(f32[8,8,128]{2,1,0:T(8,128)} %get-tuple-element.75), calls=%async_computation.1 | async-start | bytes 65536 | tf_op jit(solution)/shard_map/all_to_all | solution.py:904
  76.8 10.0 %all-to-all-start.3 = ((f32[8,8,128]{2,1,0:T(8,128)}), f32[8,8,128]{2,1,0:T(8,128)S(1)}, u32[]{:S(2)}, u32[]{:S(2)}) async-start(f32[8,8,128]{2,1,0:T(8,128)} %get-tuple-element.93), calls=%async_computation.3 | async-start | bytes 65536 | tf_op jit(solution)/shard_map/all_to_all | solution.py:904
  90.9 20.5 %copy-start.9 = (bf16[4,8,32,128]{3,2,1,0:T(8,128)(2,1)S(1)}, bf16[4,8,32,128]{3,2,1,0:T(8,128)(2,1)}, u32[]{:S(2)}) copy-start(bf16[4,8,32,128]{3,2,1,0:T(8,128)(2,1)} %get-tuple-element.102) | copy-start | bytes 786436
  91.0 1.6 %collective-permute-start.6 = (bf16[1024,128]{1,0:T(8,128)(2,1)S(1)}, bf16[1024,128]{1,0:T(8,128)(2,1)S(1)}, u32[]{:S(2)}, u32[]{:S(2)}) collective-permute-start(bf16[1024,128]{1,0:T(8,128)(2,1)S(1)} %get-tuple-element.101), channel_id=1, source_target_pairs={{0,1},{1,0},{2,3},{3,2},{4,5},{5,4},{6,7},{7,6},{8,9},{9,8},{10,11... | collective-permute-start | bytes 786440 | tf_op jit(solution)/shard_map/ppermute | solution.py:913
  107.8 13.0 %all-to-all-start.5 = ((bf16[16,64,128]{2,1,0:T(8,128)(2,1)}), bf16[16,64,128]{2,1,0:T(8,128)(2,1)S(1)}, u32[]{:S(2)}, u32[]{:S(2)}) async-start(bf16[16,64,128]{2,1,0:T(8,128)(2,1)} %shard_map.196), calls=%async_computation.5 | async-start | bytes 524288 | tf_op jit(solution)/shard_map/all_to_all | solution.py:920
  111.5 9.3 %collective-permute-start.7 = (bf16[8,32,128]{2,1,0:T(8,128)(2,1)S(1)}, bf16[8,32,128]{2,1,0:T(8,128)(2,1)S(1)}, u32[]{:S(2)}, u32[]{:S(2)}) collective-permute-start(bf16[8,32,128]{2,1,0:T(8,128)(2,1)S(1)} %get-tuple-element.111), channel_id=1, source_target_pairs={{0,1},{1,2},{2,3},{3,0},{4,5},{5,6},{6,7},{7,4},{8,9},{9,10},{10,1... | collective-permute-start | bytes 196616 | tf_op jit(solution)/shard_map/ppermute | solution.py:899
  111.5 9.3 %collective-permute-start.8 = (bf16[8,32,128]{2,1,0:T(8,128)(2,1)S(1)}, bf16[8,32,128]{2,1,0:T(8,128)(2,1)S(1)}, u32[]{:S(2)}, u32[]{:S(2)}) collective-permute-start(bf16[8,32,128]{2,1,0:T(8,128)(2,1)S(1)} %get-tuple-element.113), channel_id=1, source_target_pairs={{0,2},{1,3},{2,0},{3,1},{4,6},{5,7},{6,4},{7,5},{8,10},{9,11},{10,... | collective-permute-start | bytes 196616 | tf_op jit(solution)/shard_map/ppermute | solution.py:899
  113.5 7.4 %collective-permute-start.9 = (bf16[8,32,128]{2,1,0:T(8,128)(2,1)S(1)}, bf16[8,32,128]{2,1,0:T(8,128)(2,1)S(1)}, u32[]{:S(2)}, u32[]{:S(2)}) collective-permute-start(bf16[8,32,128]{2,1,0:T(8,128)(2,1)S(1)} %get-tuple-element.112), channel_id=1, source_target_pairs={{0,3},{1,0},{2,1},{3,2},{4,7},{5,4},{6,5},{7,6},{8,11},{9,8},{10,9... | collective-permute-start | bytes 196616 | tf_op jit(solution)/shard_map/ppermute | solution.py:899
  120.8 1.5 %collective-permute-start.10 = (bf16[1024,128]{1,0:T(8,128)(2,1)S(1)}, bf16[1024,128]{1,0:T(8,128)(2,1)S(1)}, u32[]{:S(2)}, u32[]{:S(2)}) collective-permute-start(bf16[1024,128]{1,0:T(8,128)(2,1)S(1)} %bitcast.38), channel_id=1, source_target_pairs={{0,1},{1,0},{2,3},{3,2},{4,5},{5,4},{6,7},{7,6},{8,9},{9,8},{10,11... | collective-permute-start | bytes 786440 | tf_op jit(solution)/shard_map/ppermute | solution.py:913

commit v12 on v11

--- a/solution.py
+++ b/solution.py
@@ -138,8 +138,9 @@
     date, dates, img_ref, above_ref, weight_ref, out_ref, sums_ref, table
 ):
 
-    if date == 0:
+    if date is None:
         down_table(weight_ref, table)
+        return
 
     even, odd = img_ref[0, :, 0], img_ref[0, :, 1]
     above = jnp.concatenate([above_ref[0][None], odd[:-1]], axis=0)
@@ -221,6 +222,8 @@
     high_ref,
     below_ref,
 ):
+    if step is None:
+        return
     dates = above_ref.shape[0]
     sort_halos(place_ref, inner_ref, outer_ref, high_ref, below_ref)
     down_table(weight_ref, table)
@@ -271,9 +274,10 @@
     row_devs,
 ):
 
-    if date == 0:
+    if date is None:
         norm_table(stats_ref, norm_ref, dates, norm_count)
         tap_table(weight_ref, table, False)
+        return
 
     activate_rows(
         date,
@@ -370,11 +374,12 @@
 ):
     rows, cols, width = block_ref.shape[1:]
 
-    if date == 0:
+    if date is None:
         norm_table(stats_ref, norm_ref, dates, norm_count)
         fold_keys(key_ref, query_ref, wide_ref, vector_ref, spread_ref, score_ref)
         total[...] = jnp.zeros_like(total)
         mean[...] = jnp.zeros_like(mean)
+        return
 
     scale = norm_ref[pl.ds(dates + date, 1), :] * gain_ref[...]
     shift = shift_ref[...] - norm_ref[pl.ds(date, 1), :] * scale
@@ -452,7 +457,7 @@
 ):
     rows, cols, width = block_ref.shape[1:]
 
-    if date == 0:
+    if date is None:
         totals = packed_ref[:, 0].astype(F32)
         reciprocal = 1.0 / jnp.sum(totals, axis=0)
         means = packed_ref[:, 1].astype(F32) + packed_ref[:, 2].astype(F32)
@@ -471,6 +476,7 @@
         attended[...] = jnp.zeros_like(attended)
         key_out_ref[...] = jnp.zeros_like(key_out_ref)
         vector_ref[...] = jnp.zeros_like(vector_ref)
+        return
 
     features = feat_ref[0]
     weights = exp_ref[0] * inverse[...]
@@ -541,7 +547,7 @@
 ):
     rows, cols, width = block_ref.shape[1:]
 
-    if date == 0:
+    if date is None:
         tails = group_sum(jnp.sum(tails_ref[...], axis=0)) / norm_count
         mean, inverse = norm_ref[:dates], norm_ref[dates:]
         slope = -inverse * inverse * tails[dates:]
@@ -551,6 +557,7 @@
         padded[:2] = jnp.zeros_like(padded[:2])
         padded[rows + 2 :] = jnp.zeros_like(padded[rows + 2 :])
         tap_table(weight_ref, table, True)
+        return
 
     inverse = norm_ref[pl.ds(dates + date, 1), :]
     slope = factors[pl.ds(date, 1), :]
@@ -607,8 +614,9 @@
 ):
     rows, cols, width = pre_ref.shape[1:]
 
-    if date == 0:
+    if date is None:
         total[...] = jnp.zeros_like(total)
+        return
 
     activate_rows(
         date,
@@ -675,7 +683,7 @@
     rows, cols, width = conv_ref.shape[1:]
     half = width // 2
 
-    if date == 0:
+    if date is None:
         sort_halos(place_ref, inner_ref, outer_ref, high_ref, below_ref)
         tails = group_sum(jnp.sum(tails_ref[...], axis=0)) / norm_count
         mean, inverse = norm_ref[:dates], norm_ref[dates:]
@@ -683,6 +691,7 @@
         factors[0:dates] = slope
         factors[dates : 2 * dates] = -inverse * tails[:dates] - mean * slope
         total[...] = jnp.zeros_like(total)
+        return
 
     scale = norm_ref[pl.ds(dates + date, 1), :] * gain_ref[...]
     slope = factors[pl.ds(date, 1), :]
@@ -832,22 +841,30 @@
             copies_of(len(inputs) + place, len(loads) + index, False)
             for index, place in enumerate(stores)
         ]
-        def fetch(date):
-            for moves in incoming:
-                if date < len(moves):
-                    moves[date].start()
-
-        fetch(0)
-        fetch(1)
+        def per_date(date):
+            for place, moves in zip(loads, incoming):
+                if date < len(moves) and "date" in kinds[place]:
+                    yield moves[date]
+
+        early = [m[0] for p, m in zip(loads, incoming) if kinds[p] == "all far"]
+        late = [m[0] for p, m in zip(loads, incoming) if kinds[p] == "late far"]
+        for move in early + list(per_date(0)) + list(per_date(1)) + late:
+            move.start()
         for index, place in enumerate(loads):
             views[place] = buffer_refs[index]
         for index, place in enumerate(stores):
             views[len(inputs) + place] = buffer_refs[len(loads) + index]
+        for move in early:
+            move.wait()
+        kernel(None, dates, *views, *rest)
         for date in range(dates):
-            for moves in incoming:
-                if date < len(moves):
-                    moves[date].wait()
-            fetch(date + 2)
+            for move in per_date(date):
+                move.wait()
+            for move in per_date(date + 2):
+                move.start()
+            if date == dates - 1:
+                for move in late:
+                    move.wait()
             here = [
                 view.at[pl.ds(date, 1)] if "date" in kind else view
                 for view, kind in zip(views, kinds)
@@ -1174,7 +1191,7 @@
             ("all", first_gain),
             ("all", first_shift),
             ("date far", pre_grad),
-            ("all far", key_part),
+            ("late far", key_part),
         ],
         [("all far", (10 * width, width), BF16)],
         [
@@ -1202,7 +1219,7 @@
             ("all", first_gain),
             ("all", first_vectors),
             ("all", vectors),
-            ("all far", block_rows),
+            ("late far", block_rows),
             ("scalar", turn),
         ],
         [("all", (half_rows, width), BF16)] * 2,

time: 124 us -> 124 us (level)
  no operation moved by 1% of the time
where the time goes in v12:
time: 124 us; the launch traced here: 123 us
  Pallas kernels  36.1 us (29%)
  starting transfers between devices  31.4 us (25%)
  blocking collectives  30.2 us (24%)
  waiting for transfers between devices  22.6 us (18%)
    pallas_call x8, Pallas kernels, call(): pl.pallas_call(body, in_specs=in_specs, out_specs=out_specs, out_shape=ou...  32.5 us
    all_to_all x1, blocking collectives, exchange_cores(): lax.all_to_all(pieces, axes, split_axis=0, concat_axis=0, axis_index_grou...  14.5 us
    all_to_all x3, starting transfers between devices, exchange(): return lax.all_to_all(pieces, axes, split_axis=0, concat_axis=0, tiled=True)  14.3 us
    all_to_all x3, waiting for transfers between devices, exchange(): return lax.all_to_all(pieces, axes, split_axis=0, concat_axis=0, tiled=True)  13.3 us
    all_to_all x1, blocking collectives, exchange(): return lax.all_to_all(pieces, axes, split_axis=0, concat_axis=0, tiled=True)  9.06 us
    all_gather x1, blocking collectives, gather(): return lax.all_gather(array, axis, axis=0, tiled=True)  6.63 us
    all_to_all x1, waiting for transfers between devices, exchange_cores(): lax.all_to_all(pieces, axes, split_axis=0, concat_axis=0, axis_index_grou...  5.95 us
    ppermute x1, starting transfers between devices, shifted(): return lax.ppermute(array, 'rows', pairs)  4.88 us
  transfers between devices with their start and end apart: 15, of which 7 were waited for; matrix products, arithmetic and copies ran while one was open for 1% of the time, Pallas kernels for 12%

profile of v12, /device:TPU:0, one launch (start us, length us, event | category | flops | bytes accessed | tf_op | source)
XLA Modules:
  0.0 123.1 jit_solution(6389684974911505037)
XLA Ops:
  0.7 1.0 slice_bitcast_fusion.last_ref.refs_4_
  1.6 4.9 %collective-permute-start = (bf16[4,128,128]{2,1,0:T(8,128)(2,1)S(1)}, bf16[4,128,128]{2,1,0:T(8,128)(2,1)S(1)}, u32[]{:S(2)}, u32[]{:S(2)}) collective-permute-start(bf16[4,128,128]{2,1,0:T(8,128)(2,1)S(1)} %slice_bitcast_fusion.last_ref.refs_4_), channel_id=1, source_target_pairs={{0,4},{4,8},{8,12},{12,16},{16,20},{20,24},{24,28},{1,5},{5,9},{9,... | collective-permute-start | bytes 393224 | tf_op jit(solution)/shard_map/ppermute | solution.py:897
  6.5 1.7 %shard_map.187 = (bf16[4,16,128,128]{3,2,1,0:T(8,128)(2,1)S(1)}, bf16[4,2,128,128]{3,2,1,0:T(8,128)(2,1)S(1)}, bf16[4,2,128,128]{3,2,1,0:T(8,128)(2,1)S(1)}, bf16[12,32,128]{2,1,0:T(8,128)(2,1)S(1)}) custom-call(s32[1]{0:T(128)} %bitcast.place_ref.refs_0_.refs_4_, bf16[4,128,128]{2,1,0:T(8,128)(2,1)S(1)} %slice_bitcast_fusion.last_ref.refs_4_, ...), custom_call_target="tpu_custom_call" | custom-call | tf_op jit(solution)/shard_map/pallas_call | solution.py:1002
  8.3 0.0 copy-start.4
  8.3 0.0 copy-start.8
  8.3 1.0 collective-permute-done.refs_1_.refs_3_
  9.2 2.5 %collective-permute-start.1 = (bf16[4,2,128,128]{3,2,1,0:T(8,128)(2,1)S(1)}, bf16[4,2,128,128]{3,2,1,0:T(8,128)(2,1)S(1)}, u32[]{:S(2)}, u32[]{:S(2)}) collective-permute-start(bf16[4,2,128,128]{3,2,1,0:T(8,128)(2,1)S(1)} %get-tuple-element.66), channel_id=1, source_target_pairs={{0,4},{4,0},{8,12},{12,8},{16,20},{20,16},{24,28},{28,24},{1,5},{5... | collective-permute-start | bytes 786440 | tf_op jit(solution)/shard_map/ppermute | solution.py:1019
  11.7 0.7 collective-permute-start.2
  12.4 2.7 %shard_map.188 = (bf16[4,8,128,128]{3,2,1,0:T(8,128)(2,1)}, f32[8,8,128]{2,1,0:T(8,128)}) custom-call(bf16[4,8,2,128,128]{4,3,2,1,0:T(8,128)(2,1)S(1)} %bitcast.51, bf16[4,128,128]{2,1,0:T(8,128)(2,1)S(1)} %collective-permute-done.refs_1_.refs_3_, bf16[3,3,64,128]{3,2,1,0:T(8,128)(2,1)S(1)} %copy-done.1), custom_call_target="tpu_custom_call" | custom-call | flops 805306368 | bytes 4751360 | tf_op jit(solution)/shard_map/pallas_call | solution.py:883
  15.1 7.6 %all-to-all-start = ((f32[8,8,128]{2,1,0:T(8,128)}), f32[8,8,128]{2,1,0:T(8,128)S(1)}, u32[]{:S(2)}, u32[]{:S(2)}) async-start(f32[8,8,128]{2,1,0:T(8,128)} %get-tuple-element.68), calls=%async_computation | async-start | bytes 65536 | tf_op jit(solution)/shard_map/all_to_all | solution.py:921
  22.7 0.0 collective-permute-done.2.refs_2_.refs_3_
  22.7 0.5 shard_map.189
  23.3 1.6 %collective-permute-start.3 = (bf16[384,128]{1,0:T(8,128)(2,1)S(1)}, bf16[384,128]{1,0:T(8,128)(2,1)S(1)}, u32[]{:S(2)}, u32[]{:S(2)}) collective-permute-start(bf16[384,128]{1,0:T(8,128)(2,1)S(1)} %bitcast.40), channel_id=1, source_target_pairs={{2,0},{3,1},{0,2},{1,3},{6,4},{7,5},{4,6},{5,7},{10,8},{11,9},{8,1... | collective-permute-start | bytes 294920 | tf_op jit(solution)/shard_map/ppermute | solution.py:905
  24.8 4.6 %all-to-all-done.refs_4_ = f32[8,8,128]{2,1,0:T(8,128)S(1)} async-done(((f32[8,8,128]{2,1,0:T(8,128)}), f32[8,8,128]{2,1,0:T(8,128)S(1)}, u32[]{:S(2)}, u32[]{:S(2)}) %all-to-all-start) | async-done | bytes 32800 | tf_op jit(solution)/shard_map/all_to_all | solution.py:921
  29.4 0.0 copy-start.5
  29.4 0.0 copy-start.6
  29.4 0.0 copy-start.7
  29.5 5.6 %shard_map.190 = (bf16[4,8,128,128]{3,2,1,0:T(8,128)(2,1)}, f32[8,128]{1,0:T(8,128)S(1)}, f32[8,8,128]{2,1,0:T(8,128)}) custom-call(s32[1]{0:T(128)} %bitcast.place_ref.refs_0_.refs_4_, bf16[4,8,128,128]{3,2,1,0:T(8,128)(2,1)} %get-tuple-element.65.refs_1_.refs_6_.refs_5_, bf16[4,128,128]{2,1,0:T(8,128)(2,1)S(1)} %get-tuple-element.72.refs_2_.refs_7_, ...), custom_call_target="tpu_custom_call" | custom-call | flops 1207959552 | bytes 3278856 | tf_op jit(solution)/shard_map/pallas_call | solution.py:883
  35.1 0.0 collective-permute-done.3
  35.1 0.1 collective-permute-start.4
  35.2 0.5 collective-permute-start.5
  35.7 3.3 %all-to-all-start.1 = ((f32[8,8,128]{2,1,0:T(8,128)}), f32[8,8,128]{2,1,0:T(8,128)S(1)}, u32[]{:S(2)}, u32[]{:S(2)}) async-start(f32[8,8,128]{2,1,0:T(8,128)} %get-tuple-element.75), calls=%async_computation.1 | async-start | bytes 65536 | tf_op jit(solution)/shard_map/all_to_all | solution.py:921
  39.1 0.0 collective-permute-done.4
  39.1 0.1 pad_maximum_fusion.refs_5_.refs_10_
  39.2 6.5 %all-to-all-done.1.refs_2_ = f32[8,8,128]{2,1,0:T(8,128)S(1)} async-done(((f32[8,8,128]{2,1,0:T(8,128)}), f32[8,8,128]{2,1,0:T(8,128)S(1)}, u32[]{:S(2)}, u32[]{:S(2)}) %all-to-all-start.1) | async-done | bytes 32800 | tf_op jit(solution)/shard_map/all_to_all | solution.py:921
  45.7 4.4 %shard_map.191 = (bf16[4,8,128,128]{3,2,1,0:T(8,128)(2,1)S(1)}, f32[4,8,128,128]{3,2,1,0:T(8,128)S(1)}, f32[4,8,128,128]{3,2,1,0:T(8,128)S(1)}, f32[8,128]{1,0:T...) custom-call(s32[16]{0:T(128)S(1)} %copy-done.7, ...), custom_call_target="tpu_custom_call" | custom-call | flops 671088640 | bytes 3115656 | tf_op jit(solution)/shard_map/pallas_call | solution.py:883
  50.1 6.6 %all_gather.3.refs_0_ = bf16[4,3,128,128]{3,2,1,0:T(8,128)(2,1)S(1)} all-gather(bf16[1,3,128,128]{3,2,1,0:T(8,128)(2,1)S(1)} %get-tuple-element.80), channel_id=1, replica_groups=mesh['rows'=8,'dates'=4] {'dates'}, dimensions={0}, use_global_device_ids=true | all-gather | bytes 491520 | tf_op jit(solution)/shard_map/all_gather | solution.py:925
  56.7 4.0 %shard_map.192 = (bf16[4,8,128,128]{3,2,1,0:T(8,128)(2,1)}, bf16[4,8,32,128]{3,2,1,0:T(8,128)(2,1)}, f32[128,128]{1,0:T(8,128)}, f32[8,128]{1,0:T(8,128)S(1)}, f32[8,8,128]{2,1,0:T(8,128)S(1)}) custom-call(bf16[4,3,128,128]{3,2,1,0:T(8,128)(2,1)S(1)} %all_gather.3.refs_0_, f32[128,128]{1,0:T(8,128)S(1)} %get-tuple-element.81.refs_1_, ...), custom_call_target="tpu_custom_call" | custom-call | flops 671088640 | bytes 14370824 | tf_op jit(solution)/shard_map/pallas_call | solution.py:883
  60.7 9.1 %all_to_all.30.refs_3_ = f32[8,8,128]{2,1,0:T(8,128)S(1)} all-to-all(f32[8,8,128]{2,1,0:T(8,128)S(1)} %get-tuple-element.90), channel_id=1, replica_groups=mesh['rows'=8,'dates'=4] {'rows'}, dimensions={0} | all-to-all | bytes 65536 | tf_op jit(solution)/shard_map/all_to_all | solution.py:921
  69.8 6.9 %shard_map.193 = (bf16[4,8,128,128]{3,2,1,0:T(8,128)(2,1)}, bf16[4,10,128,128]{3,2,1,0:T(8,128)(2,1)}, f32[8,128]{1,0:T(8,128)S(1)}, f32[8,8,128]{2,1,0:T(8,128)}) custom-call(s32[1]{0:T(128)} %bitcast.place_ref.refs_0_.refs_4_, bf16[4,8,128,128]{3,2,1,0:T(8,128)(2,1)} %get-tuple-element.89.refs_1_, ...), custom_call_target="tpu_custom_call" | custom-call | flops 1207959552 | bytes 7489544 | tf_op jit(solution)/shard_map/pallas_call | solution.py:883
  76.6 3.4 %all-to-all-start.3 = ((f32[8,8,128]{2,1,0:T(8,128)}), f32[8,8,128]{2,1,0:T(8,128)S(1)}, u32[]{:S(2)}, u32[]{:S(2)}) async-start(f32[8,8,128]{2,1,0:T(8,128)} %get-tuple-element.93), calls=%async_computation.3 | async-start | bytes 65536 | tf_op jit(solution)/shard_map/all_to_all | solution.py:921
  80.0 4.4 %shard_map.194.refs_12_ = bf16[1280,128]{1,0:T(8,128)(2,1)} custom-call(s32[1]{0:T(128)} %bitcast.place_ref.refs_0_.refs_4_, bf16[4,8,128,128]{3,2,1,0:T(8,128)(2,1)} %get-tuple-element.65.refs_1_.refs_6_.refs_5_, bf16[4,128,128]{2,1,0:T(8,128)(2,1)S(1)} %get-tuple-element.72.refs_2_.refs_7_, bf16[4,128,128]{2,1,0:T(8,128)(2,1)S(1)} %get-tuple-element.73.refs_3_.refs_8_, ...), custom_call_target="tpu_custom_call" | custom-call | flops 1207959552 | bytes 4859912 | tf_op jit(solution)/shard_map/pallas_call | solution.py:883
  84.4 2.2 %all-to-all-done.3.refs_7_ = f32[8,8,128]{2,1,0:T(8,128)S(1)} async-done(((f32[8,8,128]{2,1,0:T(8,128)}), f32[8,8,128]{2,1,0:T(8,128)S(1)}, u32[]{:S(2)}, u32[]{:S(2)}) %all-to-all-start.3) | async-done | bytes 32800 | tf_op jit(solution)/shard_map/all_to_all | solution.py:921
  86.6 4.0 %shard_map.195 = (bf16[1024,128]{1,0:T(8,128)(2,1)S(1)}, bf16[1024,128]{1,0:T(8,128)(2,1)S(1)}) custom-call(bf16[4,8,2,128,128]{4,3,2,1,0:T(8,128)(2,1)} %bitcast.57, bf16[4,128,128]{2,1,0:T(8,128)(2,1)S(1)} %collective-permute-done.refs_1_.refs_3_, bf16[4,2,128,128]{3,2,1,0:T(8,128)(2,1)S(1)} %collective-permute-done.1.refs_1_.refs_2_, ...), custom_call_target="tpu_custom_call" | custom-call | flops 805306368 | bytes 10970128 | tf_op jit(solution)/shard_map/pallas_call | solution.py:883
  90.6 0.0 copy-start.9
  90.7 0.1 collective-permute-start.6
  90.7 1.5 %collective-permute-done.6 = bf16[1024,128]{1,0:T(8,128)(2,1)S(1)} collective-permute-done((bf16[1024,128]{1,0:T(8,128)(2,1)S(1)}, bf16[1024,128]{1,0:T(8,128)(2,1)S(1)}, u32[]{:S(2)}, u32[]{:S(2)}) %collective-permute-start.6) | collective-permute-done | bytes 262176 | tf_op jit(solution)/shard_map/ppermute | solution.py:930
  92.3 0.1 add_convert_fusion
  92.3 14.5 %all_to_all.31.in_ref = bf16[16,64,128]{2,1,0:T(8,128)(2,1)S(1)} all-to-all(bf16[16,64,128]{2,1,0:T(8,128)(2,1)S(1)} %bitcast.58), channel_id=1, replica_groups={{0,2,4,6,8,10,12,14,16,18,20,22,24,26,28,30},{1,3,5,7,9,11,13,15,17,19,..., dimensions={0} | all-to-all | bytes 524288 | tf_op jit(solution)/shard_map/all_to_all | solution.py:937
  106.8 0.8 shard_map.196
  107.6 3.5 %all-to-all-start.5 = ((bf16[16,64,128]{2,1,0:T(8,128)(2,1)}), bf16[16,64,128]{2,1,0:T(8,128)(2,1)S(1)}, u32[]{:S(2)}, u32[]{:S(2)}) async-start(bf16[16,64,128]{2,1,0:T(8,128)(2,1)} %shard_map.196), calls=%async_computation.5 | async-start | bytes 524288 | tf_op jit(solution)/shard_map/all_to_all | solution.py:937
  111.2 0.1 collective-permute-start.7
  111.3 1.9 %collective-permute-start.8 = (bf16[8,32,128]{2,1,0:T(8,128)(2,1)S(1)}, bf16[8,32,128]{2,1,0:T(8,128)(2,1)S(1)}, u32[]{:S(2)}, u32[]{:S(2)}) collective-permute-start(bf16[8,32,128]{2,1,0:T(8,128)(2,1)S(1)} %get-tuple-element.113), channel_id=1, source_target_pairs={{0,2},{1,3},{2,0},{3,1},{4,6},{5,7},{6,4},{7,5},{8,10},{9,11},{10,... | collective-permute-start | bytes 196616 | tf_op jit(solution)/shard_map/ppermute | solution.py:916
  113.2 1.4 %collective-permute-start.9 = (bf16[8,32,128]{2,1,0:T(8,128)(2,1)S(1)}, bf16[8,32,128]{2,1,0:T(8,128)(2,1)S(1)}, u32[]{:S(2)}, u32[]{:S(2)}) collective-permute-start(bf16[8,32,128]{2,1,0:T(8,128)(2,1)S(1)} %get-tuple-element.112), channel_id=1, source_target_pairs={{0,3},{1,0},{2,1},{3,2},{4,7},{5,4},{6,5},{7,6},{8,11},{9,8},{10,9... | collective-permute-start | bytes 196616 | tf_op jit(solution)/shard_map/ppermute | solution.py:916
  114.6 5.9 %all-to-all-done.5 = bf16[16,64,128]{2,1,0:T(8,128)(2,1)S(1)} async-done(((bf16[16,64,128]{2,1,0:T(8,128)(2,1)}), bf16[16,64,128]{2,1,0:T(8,128)(2,1)S(1)}, u32[]{:S(2)}, u32[]{:S(2)}) %all-to-all-start.5) | async-done | bytes 262176 | tf_op jit(solution)/shard_map/all_to_all | solution.py:937
  120.6 0.7 fusion.2
  121.2 0.8 collective-permute-done.10.other_ref
  122.1 1.0 shard_map.197
  (22 shorter events, 0.1 us)
Async XLA Ops:
  0.6 11.7 %copy-start.1 = (bf16[3,3,64,128]{3,2,1,0:T(8,128)(2,1)S(1)}, bf16[3,3,64,128]{3,2,1,0:T(8,128)(2,1)}, u32[]{:S(2)}) copy-start(bf16[3,3,64,128]{3,2,1,0:T(8,128)(2,1)} %refs_5_.2) | copy-start | bytes 442372
  1.6 7.6 %collective-permute-start = (bf16[4,128,128]{2,1,0:T(8,128)(2,1)S(1)}, bf16[4,128,128]{2,1,0:T(8,128)(2,1)S(1)}, u32[]{:S(2)}, u32[]{:S(2)}) collective-permute-start(bf16[4,128,128]{2,1,0:T(8,128)(2,1)S(1)} %slice_bitcast_fusion.last_ref.refs_4_), channel_id=1, source_target_pairs={{0,4},{4,8},{8,12},{12,16},{16,20},{20,24},{24,28},{1,5},{5,9},{9,... | collective-permute-start | bytes 393224 | tf_op jit(solution)/shard_map/ppermute | solution.py:897
  8.3 21.2 %copy-start.4 = (f32[128]{0:T(128)S(1)}, f32[128]{0:T(128)}, u32[]{:S(2)}) copy-start(f32[128]{0:T(128)} %param.17) | copy-start | bytes 1540
  8.3 21.1 %copy-start.8 = (f32[128]{0:T(128)S(1)}, f32[128]{0:T(128)}, u32[]{:S(2)}) copy-start(f32[128]{0:T(128)} %param.18) | copy-start | bytes 1540
  9.2 13.5 %collective-permute-start.1 = (bf16[4,2,128,128]{3,2,1,0:T(8,128)(2,1)S(1)}, bf16[4,2,128,128]{3,2,1,0:T(8,128)(2,1)S(1)}, u32[]{:S(2)}, u32[]{:S(2)}) collective-permute-start(bf16[4,2,128,128]{3,2,1,0:T(8,128)(2,1)S(1)} %get-tuple-element.66), channel_id=1, source_target_pairs={{0,4},{4,0},{8,12},{12,8},{16,20},{20,16},{24,28},{28,24},{1,5},{5... | collective-permute-start | bytes 786440 | tf_op jit(solution)/shard_map/ppermute | solution.py:1019
  11.7 11.0 %collective-permute-start.2 = (bf16[4,2,128,128]{3,2,1,0:T(8,128)(2,1)S(1)}, bf16[4,2,128,128]{3,2,1,0:T(8,128)(2,1)S(1)}, u32[]{:S(2)}, u32[]{:S(2)}) collective-permute-start(bf16[4,2,128,128]{3,2,1,0:T(8,128)(2,1)S(1)} %get-tuple-element.67), channel_id=1, source_target_pairs={{4,8},{12,16},{20,24},{8,4},{16,12},{24,20},{5,9},{13,17},{21,25},... | collective-permute-start | bytes 786440 | tf_op jit(solution)/shard_map/ppermute | solution.py:1021
  15.1 14.3 %all-to-all-start = ((f32[8,8,128]{2,1,0:T(8,128)}), f32[8,8,128]{2,1,0:T(8,128)S(1)}, u32[]{:S(2)}, u32[]{:S(2)}) async-start(f32[8,8,128]{2,1,0:T(8,128)} %get-tuple-element.68), calls=%async_computation | async-start | bytes 65536 | tf_op jit(solution)/shard_map/all_to_all | solution.py:921
  23.3 11.9 %collective-permute-start.3 = (bf16[384,128]{1,0:T(8,128)(2,1)S(1)}, bf16[384,128]{1,0:T(8,128)(2,1)S(1)}, u32[]{:S(2)}, u32[]{:S(2)}) collective-permute-start(bf16[384,128]{1,0:T(8,128)(2,1)S(1)} %bitcast.40), channel_id=1, source_target_pairs={{2,0},{3,1},{0,2},{1,3},{6,4},{7,5},{4,6},{5,7},{10,8},{11,9},{8,1... | collective-permute-start | bytes 294920 | tf_op jit(solution)/shard_map/ppermute | solution.py:905
  29.4 16.3 %copy-start.2 = (f32[128]{0:T(128)S(1)}, f32[128]{0:T(128)}, u32[]{:S(2)}) copy-start(f32[128]{0:T(128)} %param.20) | copy-start | bytes 1540
  29.4 16.3 %copy-start.3 = (f32[128]{0:T(128)S(1)}, f32[128]{0:T(128)}, u32[]{:S(2)}) copy-start(f32[128]{0:T(128)} %param.21) | copy-start | bytes 1540
  29.4 16.3 %copy-start.5 = (bf16[128,64]{0,1:T(8,128)(2,1)S(1)}, bf16[128,64]{0,1:T(8,128)(2,1)}, u32[]{:S(2)}) copy-start(bf16[128,64]{0,1:T(8,128)(2,1)} %param.22) | copy-start | bytes 49156
  29.4 16.3 %copy-start.6 = (f32[16,4]{0,1:T(4,128)S(1)}, f32[16,4]{0,1:T(4,128)}, u32[]{:S(2)}) copy-start(f32[16,4]{0,1:T(4,128)} %param.23) | copy-start | bytes 772
  29.4 16.3 %copy-start.7 = (s32[16]{0:T(128)S(1)}, s32[16]{0:T(128)}, u32[]{:S(2)}) copy-start(s32[16]{0:T(128)} %refs_0_.1) | copy-start | bytes 196
  35.1 21.6 %copy-start = (bf16[4,8,128,128]{3,2,1,0:T(8,128)(2,1)S(1)}, bf16[4,8,128,128]{3,2,1,0:T(8,128)(2,1)}, u32[]{:S(2)}) copy-start(bf16[4,8,128,128]{3,2,1,0:T(8,128)(2,1)} %get-tuple-element.74.refs_1_.refs_5_.refs_2_) | copy-start | bytes 3145732
  35.1 3.9 %collective-permute-start.4 = (bf16[384,128]{1,0:T(8,128)(2,1)S(1)}, bf16[384,128]{1,0:T(8,128)(2,1)S(1)}, u32[]{:S(2)}, u32[]{:S(2)}) collective-permute-start(bf16[384,128]{1,0:T(8,128)(2,1)S(1)} %bitcast.41), channel_id=1, source_target_pairs={{0,1},{1,0},{2,3},{3,2},{4,5},{5,4},{6,7},{7,6},{8,9},{9,8},{10,11... | collective-permute-start | bytes 294920 | tf_op jit(solution)/shard_map/ppermute | solution.py:930
  35.2 3.9 %collective-permute-start.5 = (bf16[384,128]{1,0:T(8,128)(2,1)S(1)}, bf16[384,128]{1,0:T(8,128)(2,1)S(1)}, u32[]{:S(2)}, u32[]{:S(2)}) collective-permute-start(bf16[384,128]{1,0:T(8,128)(2,1)S(1)} %collective-permute-done.3), channel_id=1, source_target_pairs={{0,1},{1,0},{2,3},{3,2},{4,5},{5,4},{6,7},{7,6},{8,9},{9,8},{10,11... | collective-permute-start | bytes 294920 | tf_op jit(solution)/shard_map/ppermute | solution.py:930
  35.7 10.0 %all-to-all-start.1 = ((f32[8,8,128]{2,1,0:T(8,128)}), f32[8,8,128]{2,1,0:T(8,128)S(1)}, u32[]{:S(2)}, u32[]{:S(2)}) async-start(f32[8,8,128]{2,1,0:T(8,128)} %get-tuple-element.75), calls=%async_computation.1 | async-start | bytes 65536 | tf_op jit(solution)/shard_map/all_to_all | solution.py:921
  76.6 10.0 %all-to-all-start.3 = ((f32[8,8,128]{2,1,0:T(8,128)}), f32[8,8,128]{2,1,0:T(8,128)S(1)}, u32[]{:S(2)}, u32[]{:S(2)}) async-start(f32[8,8,128]{2,1,0:T(8,128)} %get-tuple-element.93), calls=%async_computation.3 | async-start | bytes 65536 | tf_op jit(solution)/shard_map/all_to_all | solution.py:921
  90.6 20.5 %copy-start.9 = (bf16[4,8,32,128]{3,2,1,0:T(8,128)(2,1)S(1)}, bf16[4,8,32,128]{3,2,1,0:T(8,128)(2,1)}, u32[]{:S(2)}) copy-start(bf16[4,8,32,128]{3,2,1,0:T(8,128)(2,1)} %get-tuple-element.102) | copy-start | bytes 786436
  90.7 1.6 %collective-permute-start.6 = (bf16[1024,128]{1,0:T(8,128)(2,1)S(1)}, bf16[1024,128]{1,0:T(8,128)(2,1)S(1)}, u32[]{:S(2)}, u32[]{:S(2)}) collective-permute-start(bf16[1024,128]{1,0:T(8,128)(2,1)S(1)} %get-tuple-element.101), channel_id=1, source_target_pairs={{0,1},{1,0},{2,3},{3,2},{4,5},{5,4},{6,7},{7,6},{8,9},{9,8},{10,11... | collective-permute-start | bytes 786440 | tf_op jit(solution)/shard_map/ppermute | solution.py:930
  107.6 13.0 %all-to-all-start.5 = ((bf16[16,64,128]{2,1,0:T(8,128)(2,1)}), bf16[16,64,128]{2,1,0:T(8,128)(2,1)S(1)}, u32[]{:S(2)}, u32[]{:S(2)}) async-start(bf16[16,64,128]{2,1,0:T(8,128)(2,1)} %shard_map.196), calls=%async_computation.5 | async-start | bytes 524288 | tf_op jit(solution)/shard_map/all_to_all | solution.py:937
  111.2 9.3 %collective-permute-start.7 = (bf16[8,32,128]{2,1,0:T(8,128)(2,1)S(1)}, bf16[8,32,128]{2,1,0:T(8,128)(2,1)S(1)}, u32[]{:S(2)}, u32[]{:S(2)}) collective-permute-start(bf16[8,32,128]{2,1,0:T(8,128)(2,1)S(1)} %get-tuple-element.111), channel_id=1, source_target_pairs={{0,1},{1,2},{2,3},{3,0},{4,5},{5,6},{6,7},{7,4},{8,9},{9,10},{10,1... | collective-permute-start | bytes 196616 | tf_op jit(solution)/shard_map/ppermute | solution.py:916
  111.3 9.3 %collective-permute-start.8 = (bf16[8,32,128]{2,1,0:T(8,128)(2,1)S(1)}, bf16[8,32,128]{2,1,0:T(8,128)(2,1)S(1)}, u32[]{:S(2)}, u32[]{:S(2)}) collective-permute-start(bf16[8,32,128]{2,1,0:T(8,128)(2,1)S(1)} %get-tuple-element.113), channel_id=1, source_target_pairs={{0,2},{1,3},{2,0},{3,1},{4,6},{5,7},{6,4},{7,5},{8,10},{9,11},{10,... | collective-permute-start | bytes 196616 | tf_op jit(solution)/shard_map/ppermute | solution.py:916
  113.2 7.4 %collective-permute-start.9 = (bf16[8,32,128]{2,1,0:T(8,128)(2,1)S(1)}, bf16[8,32,128]{2,1,0:T(8,128)(2,1)S(1)}, u32[]{:S(2)}, u32[]{:S(2)}) collective-permute-start(bf16[8,32,128]{2,1,0:T(8,128)(2,1)S(1)} %get-tuple-element.112), channel_id=1, source_target_pairs={{0,3},{1,0},{2,1},{3,2},{4,7},{5,4},{6,5},{7,6},{8,11},{9,8},{10,9... | collective-permute-start | bytes 196616 | tf_op jit(solution)/shard_map/ppermute | solution.py:916
  120.5 1.5 %collective-permute-start.10 = (bf16[1024,128]{1,0:T(8,128)(2,1)S(1)}, bf16[1024,128]{1,0:T(8,128)(2,1)S(1)}, u32[]{:S(2)}, u32[]{:S(2)}) collective-permute-start(bf16[1024,128]{1,0:T(8,128)(2,1)S(1)} %bitcast.38), channel_id=1, source_target_pairs={{0,1},{1,0},{2,3},{3,2},{4,5},{5,4},{6,7},{7,6},{8,9},{9,8},{10,11... | collective-permute-start | bytes 786440 | tf_op jit(solution)/shard_map/ppermute | solution.py:930

commit v13 on v12

--- a/solution.py
+++ b/solution.py
@@ -134,20 +134,46 @@
     return (both[..., :width] + from_left(both[..., width:])).astype(BF16)
 
 
-def down_kernel(
-    date, dates, img_ref, above_ref, weight_ref, out_ref, sums_ref, table
-):
-
+def inner_kernel(date, dates, img_ref, weight_ref, main_ref, sums_ref, table):
     if date is None:
         down_table(weight_ref, table)
         return
 
     even, odd = img_ref[0, :, 0], img_ref[0, :, 1]
-    above = jnp.concatenate([above_ref[0][None], odd[:-1]], axis=0)
-    stored = down_rows([above, even, odd], table)
-    out_ref[0] = stored
+    stored = down_rows([odd[:-1], even[1:], odd[1:]], table)
+    main_ref[0, 1:] = stored
     values = stored.astype(F32)
     store_sums(sums_ref, date, dates, column_sum(values), column_sum(values * values))
+
+
+def first_row_kernel(
+    img_ref,
+    above_ref,
+    weight_ref,
+    main_ref,
+    part_ref,
+    out_hbm,
+    sums_ref,
+    table,
+    row_ref,
+    ready,
+):
+    rows = main_ref.shape[1]
+    rest = pl.ds(1, rows - 1)
+    main_move = pltpu.make_async_copy(main_ref.at[:, rest], out_hbm.at[:, rest], ready.at[0])
+    main_move.start()
+    down_table(weight_ref, table)
+    stored = down_rows([above_ref[...], img_ref[:, 0], img_ref[:, 1]], table)
+    row_ref[:, 0] = stored
+    row_move = pltpu.make_async_copy(row_ref, out_hbm.at[:, pl.ds(0, 1)], ready.at[1])
+    row_move.start()
+    values = stored.astype(F32)
+    both = [jnp.sum(values, axis=1), jnp.sum(values * values, axis=1)]
+    total = part_ref[0] + jnp.concatenate(both, axis=0)
+    for copy in range(sums_ref.shape[0]):
+        sums_ref[copy] = total
+    main_move.wait()
+    row_move.wait()
 
 
 def sort_halos(place_ref, inner_ref, outer_ref, high_ref, below_ref):
@@ -1015,23 +1041,36 @@
         *[pltpu.with_memory_space_constraint(x, pltpu.HBM) for x in (images, out_grad, valid)],
     )
     packed = packed.reshape(grad_rows + valid_count, width)
-    inner, outer, above, packed = lax.optimization_barrier((inner, outer, above, packed))
+    paired = images.reshape(dates, rows, 2, cols, pair_width)
+    conv_main, part = call(
+        inner_kernel,
+        dates,
+        [("date", images_near.reshape(paired.shape)), ("all", conv_weight)],
+        [("date", frame, BF16), ("all", (1, 2 * dates, width), F32)],
+        [pltpu.VMEM((3 * pair_width, 2 * width), BF16)],
+        6 * flops,
+    )
+    inner, outer, above, packed, part = lax.optimization_barrier(
+        (inner, outer, above, packed, part)
+    )
     inner = lax.ppermute(inner, "rows", [(i, i ^ 1) for i in range(row_devs)])
     pairs = [(i, i + 1) for i in range(1, row_devs - 1, 2)]
     outer = lax.ppermute(outer, "rows", pairs + [(j, i) for i, j in pairs])
-    paired = images.reshape(dates, rows, 2, cols, pair_width)
-    conv_out, sums = call(
-        down_kernel,
-        dates,
-        [
-            ("date", images_near.reshape(paired.shape)),
-            ("date", above),
-            ("all", conv_weight),
-        ],
-        [("date far", frame, BF16), ("all", (row_devs, 2 * dates, width), F32)],
-        [pltpu.VMEM((3 * pair_width, 2 * width), BF16)],
-        6 * flops,
-    )
+    conv_out, sums = pl.pallas_call(
+        first_row_kernel,
+        in_specs=[in_vmem] * 5,
+        out_specs=[in_hbm, in_vmem],
+        out_shape=[
+            pltpu.HBM(frame, BF16),
+            jax.ShapeDtypeStruct((row_devs, 2 * dates, width), F32),
+        ],
+        scratch_shapes=[
+            pltpu.VMEM((3 * pair_width, 2 * width), BF16),
+            pltpu.VMEM((dates, 1, cols, width), BF16),
+            pltpu.SemaphoreType.DMA((2,)),
+        ],
+        compiler_params=pltpu.CompilerParams(vmem_limit_bytes=16 * MIB),
+    )(images_near, above, conv_weight, conv_main, part)
     stats = exchange(sums, "rows")
     inner, outer, last, _ = lax.optimization_barrier((inner, outer, last, sums))
     halo_up, halo_down = call(

time: 124 us -> 123 us (level)
    pallas_call x0 -> x1, Pallas kernels: none -> 1.72 us  [local(): pl.pallas_call(first_row_kernel, in_specs=[in_vmem] * 5, out_specs=[in_hb...]
    pallas_call x8, Pallas kernels: 32.5 us -> 31 us  [call(): pl.pallas_call(body, in_specs=in_specs, out_specs=out_specs, out_shape=ou...]
where the time goes in v13:
time: 123 us; the launch traced here: 122 us
  Pallas kernels  36.3 us (30%)
  starting transfers between devices  31.1 us (25%)
  blocking collectives  30.2 us (25%)
  waiting for transfers between devices  21.7 us (18%)
    pallas_call x8, Pallas kernels, call(): pl.pallas_call(body, in_specs=in_specs, out_specs=out_specs, out_shape=ou...  31 us
    all_to_all x1, blocking collectives, exchange_cores(): lax.all_to_all(pieces, axes, split_axis=0, concat_axis=0, axis_index_grou...  14.5 us
    all_to_all x3, starting transfers between devices, exchange(): return lax.all_to_all(pieces, axes, split_axis=0, concat_axis=0, tiled=True)  14.3 us
    all_to_all x3, waiting for transfers between devices, exchange(): return lax.all_to_all(pieces, axes, split_axis=0, concat_axis=0, tiled=True)  12.9 us
    all_to_all x1, blocking collectives, exchange(): return lax.all_to_all(pieces, axes, split_axis=0, concat_axis=0, tiled=True)  9.06 us
    all_gather x1, blocking collectives, gather(): return lax.all_gather(array, axis, axis=0, tiled=True)  6.65 us
    all_to_all x1, waiting for transfers between devices, exchange_cores(): lax.all_to_all(pieces, axes, split_axis=0, concat_axis=0, axis_index_grou...  5.95 us
    ppermute x1, starting transfers between devices, shifted(): return lax.ppermute(array, 'rows', pairs)  4.88 us
  transfers between devices with their start and end apart: 15, of which 7 were waited for; matrix products, arithmetic and copies ran while one was open for 1% of the time, Pallas kernels for 12%

profile of v13, /device:TPU:0, one launch (start us, length us, event | category | flops | bytes accessed | tf_op | source)
XLA Modules:
  0.0 122.1 jit_solution(12208624379677011380)
XLA Ops:
  0.7 1.0 slice_bitcast_fusion.last_ref.refs_4_
  1.6 4.9 %collective-permute-start = (bf16[4,128,128]{2,1,0:T(8,128)(2,1)S(1)}, bf16[4,128,128]{2,1,0:T(8,128)(2,1)S(1)}, u32[]{:S(2)}, u32[]{:S(2)}) collective-permute-start(bf16[4,128,128]{2,1,0:T(8,128)(2,1)S(1)} %slice_bitcast_fusion.last_ref.refs_4_), channel_id=1, source_target_pairs={{0,4},{4,8},{8,12},{12,16},{16,20},{20,24},{24,28},{1,5},{5,9},{9,... | collective-permute-start | bytes 393224 | tf_op jit(solution)/shard_map/ppermute | solution.py:923
  6.5 1.7 %shard_map.187 = (bf16[4,16,128,128]{3,2,1,0:T(8,128)(2,1)S(1)}, bf16[4,2,128,128]{3,2,1,0:T(8,128)(2,1)S(1)}, bf16[4,2,128,128]{3,2,1,0:T(8,128)(2,1)S(1)}, bf16[12,32,128]{2,1,0:T(8,128)(2,1)S(1)}) custom-call(s32[1]{0:T(128)} %bitcast.place_ref.refs_0_.refs_4_, bf16[4,128,128]{2,1,0:T(8,128)(2,1)S(1)} %slice_bitcast_fusion.last_ref.refs_4_, ...), custom_call_target="tpu_custom_call" | custom-call | tf_op jit(solution)/shard_map/pallas_call | solution.py:1028
  8.3 1.2 %shard_map.188 = (bf16[4,8,128,128]{3,2,1,0:T(8,128)(2,1)S(1)}, f32[1,8,128]{2,1,0:T(8,128)S(1)}) custom-call(bf16[4,8,2,128,128]{4,3,2,1,0:T(8,128)(2,1)S(1)} %bitcast.38, bf16[3,3,64,128]{3,2,1,0:T(8,128)(2,1)S(1)} %copy-done.1), custom_call_target="tpu_custom_call" | custom-call | flops 805306368 | bytes 4489216 | tf_op jit(solution)/shard_map/pallas_call | solution.py:909
  9.5 2.2 %collective-permute-start.1 = (bf16[4,2,128,128]{3,2,1,0:T(8,128)(2,1)S(1)}, bf16[4,2,128,128]{3,2,1,0:T(8,128)(2,1)S(1)}, u32[]{:S(2)}, u32[]{:S(2)}) collective-permute-start(bf16[4,2,128,128]{3,2,1,0:T(8,128)(2,1)S(1)} %get-tuple-element.72), channel_id=1, source_target_pairs={{0,4},{4,0},{8,12},{12,8},{16,20},{20,16},{24,28},{28,24},{1,5},{5... | collective-permute-start | bytes 786440 | tf_op jit(solution)/shard_map/ppermute | solution.py:1056
  11.7 0.7 collective-permute-start.2
  12.4 0.0 copy-start.4
  12.4 0.0 copy-start.8
  12.4 1.7 %shard_map.189 = (bf16[4,8,128,128]{3,2,1,0:T(8,128)(2,1)}, f32[8,8,128]{2,1,0:T(8,128)}) custom-call(bf16[4,16,128,128]{3,2,1,0:T(8,128)(2,1)S(1)} %get-tuple-element.63.img_ref, bf16[4,128,128]{2,1,0:T(8,128)(2,1)S(1)} %collective-permute-done.above_ref.refs_3_.refs_1_, bf16[3,3,64,128]{3,2,1,0:T(8,128)(2,1)S(1)} %copy-done.1, ...), custom_call_target="tpu_custom_call" | custom-call | tf_op jit(solution)/shard_map/pallas_call | solution.py:1059
  14.1 7.6 %all-to-all-start = ((f32[8,8,128]{2,1,0:T(8,128)}), f32[8,8,128]{2,1,0:T(8,128)S(1)}, u32[]{:S(2)}, u32[]{:S(2)}) async-start(f32[8,8,128]{2,1,0:T(8,128)} %get-tuple-element.74), calls=%async_computation | async-start | bytes 65536 | tf_op jit(solution)/shard_map/all_to_all | solution.py:947
  21.7 0.4 collective-permute-done.1.refs_1_.refs_2_
  22.1 0.0 collective-permute-done.2.refs_2_.refs_3_
  22.1 0.5 shard_map.190
  22.6 1.6 %collective-permute-start.3 = (bf16[384,128]{1,0:T(8,128)(2,1)S(1)}, bf16[384,128]{1,0:T(8,128)(2,1)S(1)}, u32[]{:S(2)}, u32[]{:S(2)}) collective-permute-start(bf16[384,128]{1,0:T(8,128)(2,1)S(1)} %bitcast.41), channel_id=1, source_target_pairs={{2,0},{3,1},{0,2},{1,3},{6,4},{7,5},{4,6},{5,7},{10,8},{11,9},{8,1... | collective-permute-start | bytes 294920 | tf_op jit(solution)/shard_map/ppermute | solution.py:931
  24.2 4.2 %all-to-all-done.refs_4_ = f32[8,8,128]{2,1,0:T(8,128)S(1)} async-done(((f32[8,8,128]{2,1,0:T(8,128)}), f32[8,8,128]{2,1,0:T(8,128)S(1)}, u32[]{:S(2)}, u32[]{:S(2)}) %all-to-all-start) | async-done | bytes 32800 | tf_op jit(solution)/shard_map/all_to_all | solution.py:947
  28.4 0.0 copy-start.5
  28.4 0.0 copy-start.6
  28.4 0.0 copy-start.7
  28.5 5.6 %shard_map.191 = (bf16[4,8,128,128]{3,2,1,0:T(8,128)(2,1)}, f32[8,128]{1,0:T(8,128)S(1)}, f32[8,8,128]{2,1,0:T(8,128)}) custom-call(s32[1]{0:T(128)} %bitcast.place_ref.refs_0_.refs_4_, bf16[4,8,128,128]{3,2,1,0:T(8,128)(2,1)} %get-tuple-element.71.refs_1_.refs_6_.refs_5_, bf16[4,128,128]{2,1,0:T(8,128)(2,1)S(1)} %get-tuple-element.78.refs_2_.refs_7_, ...), custom_call_target="tpu_custom_call" | custom-call | flops 1207959552 | bytes 3278856 | tf_op jit(solution)/shard_map/pallas_call | solution.py:909
  34.1 0.0 collective-permute-done.3
  34.1 0.1 collective-permute-start.4
  34.2 0.5 collective-permute-start.5
  34.7 3.3 %all-to-all-start.1 = ((f32[8,8,128]{2,1,0:T(8,128)}), f32[8,8,128]{2,1,0:T(8,128)S(1)}, u32[]{:S(2)}, u32[]{:S(2)}) async-start(f32[8,8,128]{2,1,0:T(8,128)} %get-tuple-element.81), calls=%async_computation.1 | async-start | bytes 65536 | tf_op jit(solution)/shard_map/all_to_all | solution.py:947
  38.1 0.1 pad_maximum_fusion.refs_5_.refs_10_
  38.2 6.5 %all-to-all-done.1.refs_2_ = f32[8,8,128]{2,1,0:T(8,128)S(1)} async-done(((f32[8,8,128]{2,1,0:T(8,128)}), f32[8,8,128]{2,1,0:T(8,128)S(1)}, u32[]{:S(2)}, u32[]{:S(2)}) %all-to-all-start.1) | async-done | bytes 32800 | tf_op jit(solution)/shard_map/all_to_all | solution.py:947
  44.7 4.4 %shard_map.192 = (bf16[4,8,128,128]{3,2,1,0:T(8,128)(2,1)S(1)}, f32[4,8,128,128]{3,2,1,0:T(8,128)S(1)}, f32[4,8,128,128]{3,2,1,0:T(8,128)S(1)}, f32[8,128]{1,0:T...) custom-call(s32[16]{0:T(128)S(1)} %copy-done.7, ...), custom_call_target="tpu_custom_call" | custom-call | flops 671088640 | bytes 3115656 | tf_op jit(solution)/shard_map/pallas_call | solution.py:909
  49.1 6.7 %all_gather.3.refs_0_ = bf16[4,3,128,128]{3,2,1,0:T(8,128)(2,1)S(1)} all-gather(bf16[1,3,128,128]{3,2,1,0:T(8,128)(2,1)S(1)} %get-tuple-element.86), channel_id=1, replica_groups=mesh['rows'=8,'dates'=4] {'dates'}, dimensions={0}, use_global_device_ids=true | all-gather | bytes 491520 | tf_op jit(solution)/shard_map/all_gather | solution.py:951
  55.7 4.0 %shard_map.193 = (bf16[4,8,128,128]{3,2,1,0:T(8,128)(2,1)}, bf16[4,8,32,128]{3,2,1,0:T(8,128)(2,1)}, f32[128,128]{1,0:T(8,128)}, f32[8,128]{1,0:T(8,128)S(1)}, f32[8,8,128]{2,1,0:T(8,128)S(1)}) custom-call(bf16[4,3,128,128]{3,2,1,0:T(8,128)(2,1)S(1)} %all_gather.3.refs_0_, f32[128,128]{1,0:T(8,128)S(1)} %get-tuple-element.87.refs_1_, ...), custom_call_target="tpu_custom_call" | custom-call | flops 671088640 | bytes 14370824 | tf_op jit(solution)/shard_map/pallas_call | solution.py:909
  59.7 9.1 %all_to_all.30.refs_3_ = f32[8,8,128]{2,1,0:T(8,128)S(1)} all-to-all(f32[8,8,128]{2,1,0:T(8,128)S(1)} %get-tuple-element.96), channel_id=1, replica_groups=mesh['rows'=8,'dates'=4] {'rows'}, dimensions={0} | all-to-all | bytes 65536 | tf_op jit(solution)/shard_map/all_to_all | solution.py:947
  68.8 6.9 %shard_map.194 = (bf16[4,8,128,128]{3,2,1,0:T(8,128)(2,1)}, bf16[4,10,128,128]{3,2,1,0:T(8,128)(2,1)}, f32[8,128]{1,0:T(8,128)S(1)}, f32[8,8,128]{2,1,0:T(8,128)}) custom-call(s32[1]{0:T(128)} %bitcast.place_ref.refs_0_.refs_4_, bf16[4,8,128,128]{3,2,1,0:T(8,128)(2,1)} %get-tuple-element.95.refs_1_, ...), custom_call_target="tpu_custom_call" | custom-call | flops 1207959552 | bytes 7489544 | tf_op jit(solution)/shard_map/pallas_call | solution.py:909
  75.7 3.4 %all-to-all-start.3 = ((f32[8,8,128]{2,1,0:T(8,128)}), f32[8,8,128]{2,1,0:T(8,128)S(1)}, u32[]{:S(2)}, u32[]{:S(2)}) async-start(f32[8,8,128]{2,1,0:T(8,128)} %get-tuple-element.99), calls=%async_computation.3 | async-start | bytes 65536 | tf_op jit(solution)/shard_map/all_to_all | solution.py:947
  79.0 4.4 %shard_map.195.refs_12_ = bf16[1280,128]{1,0:T(8,128)(2,1)} custom-call(s32[1]{0:T(128)} %bitcast.place_ref.refs_0_.refs_4_, bf16[4,8,128,128]{3,2,1,0:T(8,128)(2,1)} %get-tuple-element.71.refs_1_.refs_6_.refs_5_, bf16[4,128,128]{2,1,0:T(8,128)(2,1)S(1)} %get-tuple-element.78.refs_2_.refs_7_, bf16[4,128,128]{2,1,0:T(8,128)(2,1)S(1)} %get-tuple-element.79.refs_3_.refs_8_, ...), custom_call_target="tpu_custom_call" | custom-call | flops 1207959552 | bytes 4859912 | tf_op jit(solution)/shard_map/pallas_call | solution.py:909
  83.4 2.2 %all-to-all-done.3.refs_7_ = f32[8,8,128]{2,1,0:T(8,128)S(1)} async-done(((f32[8,8,128]{2,1,0:T(8,128)}), f32[8,8,128]{2,1,0:T(8,128)S(1)}, u32[]{:S(2)}, u32[]{:S(2)}) %all-to-all-start.3) | async-done | bytes 32800 | tf_op jit(solution)/shard_map/all_to_all | solution.py:947
  85.6 4.0 %shard_map.196 = (bf16[1024,128]{1,0:T(8,128)(2,1)S(1)}, bf16[1024,128]{1,0:T(8,128)(2,1)S(1)}) custom-call(bf16[4,8,2,128,128]{4,3,2,1,0:T(8,128)(2,1)} %bitcast.57, bf16[4,128,128]{2,1,0:T(8,128)(2,1)S(1)} %collective-permute-done.above_ref.refs_3_.refs_1_, bf16[4,2,128,128]{3,2,1,0:T(8,128)(2,1)S(1)} %collective-permute-done.1.refs_1_.refs_2_, ...), custom_call_target="tpu_custom_call" | custom-call | flops 805306368 | bytes 10970128 | tf_op jit(solution)/shard_map/pallas_call | solution.py:909
  89.7 0.0 copy-start.9
  89.7 0.1 collective-permute-start.6
  89.8 1.5 %collective-permute-done.6 = bf16[1024,128]{1,0:T(8,128)(2,1)S(1)} collective-permute-done((bf16[1024,128]{1,0:T(8,128)(2,1)S(1)}, bf16[1024,128]{1,0:T(8,128)(2,1)S(1)}, u32[]{:S(2)}, u32[]{:S(2)}) %collective-permute-start.6) | collective-permute-done | bytes 262176 | tf_op jit(solution)/shard_map/ppermute | solution.py:956
  91.3 0.1 add_convert_fusion
  91.4 14.5 %all_to_all.31.in_ref = bf16[16,64,128]{2,1,0:T(8,128)(2,1)S(1)} all-to-all(bf16[16,64,128]{2,1,0:T(8,128)(2,1)S(1)} %bitcast.58), channel_id=1, replica_groups={{0,2,4,6,8,10,12,14,16,18,20,22,24,26,28,30},{1,3,5,7,9,11,13,15,17,19,..., dimensions={0} | all-to-all | bytes 524288 | tf_op jit(solution)/shard_map/all_to_all | solution.py:963
  105.8 0.8 shard_map.197
  106.6 3.5 %all-to-all-start.5 = ((bf16[16,64,128]{2,1,0:T(8,128)(2,1)}), bf16[16,64,128]{2,1,0:T(8,128)(2,1)S(1)}, u32[]{:S(2)}, u32[]{:S(2)}) async-start(bf16[16,64,128]{2,1,0:T(8,128)(2,1)} %shard_map.197), calls=%async_computation.5 | async-start | bytes 524288 | tf_op jit(solution)/shard_map/all_to_all | solution.py:963
  110.2 0.1 collective-permute-start.7
  110.3 1.9 %collective-permute-start.8 = (bf16[8,32,128]{2,1,0:T(8,128)(2,1)S(1)}, bf16[8,32,128]{2,1,0:T(8,128)(2,1)S(1)}, u32[]{:S(2)}, u32[]{:S(2)}) collective-permute-start(bf16[8,32,128]{2,1,0:T(8,128)(2,1)S(1)} %get-tuple-element.119), channel_id=1, source_target_pairs={{0,2},{1,3},{2,0},{3,1},{4,6},{5,7},{6,4},{7,5},{8,10},{9,11},{10,... | collective-permute-start | bytes 196616 | tf_op jit(solution)/shard_map/ppermute | solution.py:942
  112.2 1.4 %collective-permute-start.9 = (bf16[8,32,128]{2,1,0:T(8,128)(2,1)S(1)}, bf16[8,32,128]{2,1,0:T(8,128)(2,1)S(1)}, u32[]{:S(2)}, u32[]{:S(2)}) collective-permute-start(bf16[8,32,128]{2,1,0:T(8,128)(2,1)S(1)} %get-tuple-element.118), channel_id=1, source_target_pairs={{0,3},{1,0},{2,1},{3,2},{4,7},{5,4},{6,5},{7,6},{8,11},{9,8},{10,9... | collective-permute-start | bytes 196616 | tf_op jit(solution)/shard_map/ppermute | solution.py:942
  113.6 5.9 %all-to-all-done.5 = bf16[16,64,128]{2,1,0:T(8,128)(2,1)S(1)} async-done(((bf16[16,64,128]{2,1,0:T(8,128)(2,1)}), bf16[16,64,128]{2,1,0:T(8,128)(2,1)S(1)}, u32[]{:S(2)}, u32[]{:S(2)}) %all-to-all-start.5) | async-done | bytes 262176 | tf_op jit(solution)/shard_map/all_to_all | solution.py:963
  119.6 0.7 fusion.2
  120.2 0.8 collective-permute-done.10.other_ref
  121.1 1.0 shard_map.198
  (23 shorter events, 0.1 us)
Async XLA Ops:
  0.6 7.6 %copy-start.1 = (bf16[3,3,64,128]{3,2,1,0:T(8,128)(2,1)S(1)}, bf16[3,3,64,128]{3,2,1,0:T(8,128)(2,1)}, u32[]{:S(2)}) copy-start(bf16[3,3,64,128]{3,2,1,0:T(8,128)(2,1)} %refs_5_.2) | copy-start | bytes 442372
  1.6 7.9 %collective-permute-start = (bf16[4,128,128]{2,1,0:T(8,128)(2,1)S(1)}, bf16[4,128,128]{2,1,0:T(8,128)(2,1)S(1)}, u32[]{:S(2)}, u32[]{:S(2)}) collective-permute-start(bf16[4,128,128]{2,1,0:T(8,128)(2,1)S(1)} %slice_bitcast_fusion.last_ref.refs_4_), channel_id=1, source_target_pairs={{0,4},{4,8},{8,12},{12,16},{16,20},{20,24},{24,28},{1,5},{5,9},{9,... | collective-permute-start | bytes 393224 | tf_op jit(solution)/shard_map/ppermute | solution.py:923
  9.5 12.6 %collective-permute-start.1 = (bf16[4,2,128,128]{3,2,1,0:T(8,128)(2,1)S(1)}, bf16[4,2,128,128]{3,2,1,0:T(8,128)(2,1)S(1)}, u32[]{:S(2)}, u32[]{:S(2)}) collective-permute-start(bf16[4,2,128,128]{3,2,1,0:T(8,128)(2,1)S(1)} %get-tuple-element.72), channel_id=1, source_target_pairs={{0,4},{4,0},{8,12},{12,8},{16,20},{20,16},{24,28},{28,24},{1,5},{5... | collective-permute-start | bytes 786440 | tf_op jit(solution)/shard_map/ppermute | solution.py:1056
  11.7 10.4 %collective-permute-start.2 = (bf16[4,2,128,128]{3,2,1,0:T(8,128)(2,1)S(1)}, bf16[4,2,128,128]{3,2,1,0:T(8,128)(2,1)S(1)}, u32[]{:S(2)}, u32[]{:S(2)}) collective-permute-start(bf16[4,2,128,128]{3,2,1,0:T(8,128)(2,1)S(1)} %get-tuple-element.73), channel_id=1, source_target_pairs={{4,8},{12,16},{20,24},{8,4},{16,12},{24,20},{5,9},{13,17},{21,25},... | collective-permute-start | bytes 786440 | tf_op jit(solution)/shard_map/ppermute | solution.py:1058
  12.4 16.0 %copy-start.4 = (f32[128]{0:T(128)S(1)}, f32[128]{0:T(128)}, u32[]{:S(2)}) copy-start(f32[128]{0:T(128)} %param.17) | copy-start | bytes 1540
  12.4 16.0 %copy-start.8 = (f32[128]{0:T(128)S(1)}, f32[128]{0:T(128)}, u32[]{:S(2)}) copy-start(f32[128]{0:T(128)} %param.18) | copy-start | bytes 1540
  14.1 14.3 %all-to-all-start = ((f32[8,8,128]{2,1,0:T(8,128)}), f32[8,8,128]{2,1,0:T(8,128)S(1)}, u32[]{:S(2)}, u32[]{:S(2)}) async-start(f32[8,8,128]{2,1,0:T(8,128)} %get-tuple-element.74), calls=%async_computation | async-start | bytes 65536 | tf_op jit(solution)/shard_map/all_to_all | solution.py:947
  22.6 11.5 %collective-permute-start.3 = (bf16[384,128]{1,0:T(8,128)(2,1)S(1)}, bf16[384,128]{1,0:T(8,128)(2,1)S(1)}, u32[]{:S(2)}, u32[]{:S(2)}) collective-permute-start(bf16[384,128]{1,0:T(8,128)(2,1)S(1)} %bitcast.41), channel_id=1, source_target_pairs={{2,0},{3,1},{0,2},{1,3},{6,4},{7,5},{4,6},{5,7},{10,8},{11,9},{8,1... | collective-permute-start | bytes 294920 | tf_op jit(solution)/shard_map/ppermute | solution.py:931
  28.4 16.3 %copy-start.2 = (f32[128]{0:T(128)S(1)}, f32[128]{0:T(128)}, u32[]{:S(2)}) copy-start(f32[128]{0:T(128)} %param.20) | copy-start | bytes 1540
  28.4 16.3 %copy-start.3 = (f32[128]{0:T(128)S(1)}, f32[128]{0:T(128)}, u32[]{:S(2)}) copy-start(f32[128]{0:T(128)} %param.21) | copy-start | bytes 1540
  28.4 16.3 %copy-start.5 = (bf16[128,64]{0,1:T(8,128)(2,1)S(1)}, bf16[128,64]{0,1:T(8,128)(2,1)}, u32[]{:S(2)}) copy-start(bf16[128,64]{0,1:T(8,128)(2,1)} %param.22) | copy-start | bytes 49156
  28.4 16.2 %copy-start.6 = (f32[16,4]{0,1:T(4,128)S(1)}, f32[16,4]{0,1:T(4,128)}, u32[]{:S(2)}) copy-start(f32[16,4]{0,1:T(4,128)} %param.23) | copy-start | bytes 772
  28.4 16.2 %copy-start.7 = (s32[16]{0:T(128)S(1)}, s32[16]{0:T(128)}, u32[]{:S(2)}) copy-start(s32[16]{0:T(128)} %refs_0_.1) | copy-start | bytes 196
  34.1 21.6 %copy-start = (bf16[4,8,128,128]{3,2,1,0:T(8,128)(2,1)S(1)}, bf16[4,8,128,128]{3,2,1,0:T(8,128)(2,1)}, u32[]{:S(2)}) copy-start(bf16[4,8,128,128]{3,2,1,0:T(8,128)(2,1)} %get-tuple-element.80.refs_1_.refs_5_.refs_2_) | copy-start | bytes 3145732
  34.1 3.9 %collective-permute-start.4 = (bf16[384,128]{1,0:T(8,128)(2,1)S(1)}, bf16[384,128]{1,0:T(8,128)(2,1)S(1)}, u32[]{:S(2)}, u32[]{:S(2)}) collective-permute-start(bf16[384,128]{1,0:T(8,128)(2,1)S(1)} %bitcast.42), channel_id=1, source_target_pairs={{0,1},{1,0},{2,3},{3,2},{4,5},{5,4},{6,7},{7,6},{8,9},{9,8},{10,11... | collective-permute-start | bytes 294920 | tf_op jit(solution)/shard_map/ppermute | solution.py:956
  34.2 3.9 %collective-permute-start.5 = (bf16[384,128]{1,0:T(8,128)(2,1)S(1)}, bf16[384,128]{1,0:T(8,128)(2,1)S(1)}, u32[]{:S(2)}, u32[]{:S(2)}) collective-permute-start(bf16[384,128]{1,0:T(8,128)(2,1)S(1)} %collective-permute-done.3), channel_id=1, source_target_pairs={{0,1},{1,0},{2,3},{3,2},{4,5},{5,4},{6,7},{7,6},{8,9},{9,8},{10,11... | collective-permute-start | bytes 294920 | tf_op jit(solution)/shard_map/ppermute | solution.py:956
  34.7 10.0 %all-to-all-start.1 = ((f32[8,8,128]{2,1,0:T(8,128)}), f32[8,8,128]{2,1,0:T(8,128)S(1)}, u32[]{:S(2)}, u32[]{:S(2)}) async-start(f32[8,8,128]{2,1,0:T(8,128)} %get-tuple-element.81), calls=%async_computation.1 | async-start | bytes 65536 | tf_op jit(solution)/shard_map/all_to_all | solution.py:947
  75.7 10.0 %all-to-all-start.3 = ((f32[8,8,128]{2,1,0:T(8,128)}), f32[8,8,128]{2,1,0:T(8,128)S(1)}, u32[]{:S(2)}, u32[]{:S(2)}) async-start(f32[8,8,128]{2,1,0:T(8,128)} %get-tuple-element.99), calls=%async_computation.3 | async-start | bytes 65536 | tf_op jit(solution)/shard_map/all_to_all | solution.py:947
  89.7 20.5 %copy-start.9 = (bf16[4,8,32,128]{3,2,1,0:T(8,128)(2,1)S(1)}, bf16[4,8,32,128]{3,2,1,0:T(8,128)(2,1)}, u32[]{:S(2)}) copy-start(bf16[4,8,32,128]{3,2,1,0:T(8,128)(2,1)} %get-tuple-element.108) | copy-start | bytes 786436
  89.7 1.6 %collective-permute-start.6 = (bf16[1024,128]{1,0:T(8,128)(2,1)S(1)}, bf16[1024,128]{1,0:T(8,128)(2,1)S(1)}, u32[]{:S(2)}, u32[]{:S(2)}) collective-permute-start(bf16[1024,128]{1,0:T(8,128)(2,1)S(1)} %get-tuple-element.107), channel_id=1, source_target_pairs={{0,1},{1,0},{2,3},{3,2},{4,5},{5,4},{6,7},{7,6},{8,9},{9,8},{10,11... | collective-permute-start | bytes 786440 | tf_op jit(solution)/shard_map/ppermute | solution.py:956
  106.6 13.0 %all-to-all-start.5 = ((bf16[16,64,128]{2,1,0:T(8,128)(2,1)}), bf16[16,64,128]{2,1,0:T(8,128)(2,1)S(1)}, u32[]{:S(2)}, u32[]{:S(2)}) async-start(bf16[16,64,128]{2,1,0:T(8,128)(2,1)} %shard_map.197), calls=%async_computation.5 | async-start | bytes 524288 | tf_op jit(solution)/shard_map/all_to_all | solution.py:963
  110.2 9.3 %collective-permute-start.7 = (bf16[8,32,128]{2,1,0:T(8,128)(2,1)S(1)}, bf16[8,32,128]{2,1,0:T(8,128)(2,1)S(1)}, u32[]{:S(2)}, u32[]{:S(2)}) collective-permute-start(bf16[8,32,128]{2,1,0:T(8,128)(2,1)S(1)} %get-tuple-element.117), channel_id=1, source_target_pairs={{0,1},{1,2},{2,3},{3,0},{4,5},{5,6},{6,7},{7,4},{8,9},{9,10},{10,1... | collective-permute-start | bytes 196616 | tf_op jit(solution)/shard_map/ppermute | solution.py:942
  110.3 9.3 %collective-permute-start.8 = (bf16[8,32,128]{2,1,0:T(8,128)(2,1)S(1)}, bf16[8,32,128]{2,1,0:T(8,128)(2,1)S(1)}, u32[]{:S(2)}, u32[]{:S(2)}) collective-permute-start(bf16[8,32,128]{2,1,0:T(8,128)(2,1)S(1)} %get-tuple-element.119), channel_id=1, source_target_pairs={{0,2},{1,3},{2,0},{3,1},{4,6},{5,7},{6,4},{7,5},{8,10},{9,11},{10,... | collective-permute-start | bytes 196616 | tf_op jit(solution)/shard_map/ppermute | solution.py:942
  112.2 7.4 %collective-permute-start.9 = (bf16[8,32,128]{2,1,0:T(8,128)(2,1)S(1)}, bf16[8,32,128]{2,1,0:T(8,128)(2,1)S(1)}, u32[]{:S(2)}, u32[]{:S(2)}) collective-permute-start(bf16[8,32,128]{2,1,0:T(8,128)(2,1)S(1)} %get-tuple-element.118), channel_id=1, source_target_pairs={{0,3},{1,0},{2,1},{3,2},{4,7},{5,4},{6,5},{7,6},{8,11},{9,8},{10,9... | collective-permute-start | bytes 196616 | tf_op jit(solution)/shard_map/ppermute | solution.py:942
  119.5 1.5 %collective-permute-start.10 = (bf16[1024,128]{1,0:T(8,128)(2,1)S(1)}, bf16[1024,128]{1,0:T(8,128)(2,1)S(1)}, u32[]{:S(2)}, u32[]{:S(2)}) collective-permute-start(bf16[1024,128]{1,0:T(8,128)(2,1)S(1)} %bitcast.39), channel_id=1, source_target_pairs={{0,1},{1,0},{2,3},{3,2},{4,5},{5,4},{6,7},{7,6},{8,9},{9,8},{10,11... | collective-permute-start | bytes 786440 | tf_op jit(solution)/shard_map/ppermute | solution.py:956
